TPU v7x, 32 devices: a whole 2x2x4 slice. The times are simulated.
32 devices in a mesh: layer: 4 (over y, x), front: 8 (over z, core).
Axes of the slice: x: 2, y: 2, z: 4, core: 2. Of those that a mesh axis runs over, the one named last changes fastest.
Arguments:
- right_sides: float32 [4, 2, 4, 1024], P('layer', None, None, 'front'), may hold values from -6 to 6
- leaf_inverse: bfloat16 [4, 2, 1024, 128], P('layer', None, 'front'), may hold values from -0.375 to 0.375
- couple_above: bfloat16 [4, 2, 1024, 128], P('layer', None, 'front'), may hold values from -0.1875 to 0.1875
- couple_below: bfloat16 [4, 2, 1024, 128], P('layer', None, 'front'), may hold values from -0.1875 to 0.1875
- sep_gather: bfloat16 [4, 2, 5120, 1024], P('layer', None, None, 'front'), may hold values from -0.125 to 0.125
- sep_inverse: bfloat16 [4, 2, 5120, 5120], P('layer', None, 'front'), may hold values from -0.0625 to 0.0625
- sep_spread: bfloat16 [4, 2, 1024, 5120], P('layer', None, 'front'), may hold values from -0.0625 to 0.0625
- panel_owner: int32 [4, 8], P('layer'), may hold values from 0 to 7, each once within a row
Outputs:
- solution: float32 [4, 2, 4, 1024], P('layer', None, None, 'front')
Inputs may be any that keep to these rules, and one draw needn't show every extreme that they name: Each row of panel_owner names every slot 0 to 7 once.
All inputs are finite; a program needn't handle non-finite values.
Results may differ from a plain program's by a relative error of at most 0.023.
Values may be sent and summed in bfloat16 or wider, within the bound.
No kernel may reach another device: no remote copies, remote signals or barrier semaphores. Data moves between devices by JAX's collectives and lax.ppermute only.
A program may use at most 128 MiB of HBM per device.

v0:
```python
import jax
import jax.numpy as jnp
from jax import lax
from jax.sharding import PartitionSpec as P


def from_behind(block, axis, distance):
    devices = range(lax.axis_size(axis))
    route = [(i - distance, i) for i in devices if i - distance in devices]
    return lax.ppermute(block, axis, route)


def dense_apply(matrix, vector):

    def single(left, right):
        return jnp.dot(right, left.T, preferred_element_type=jnp.float32)

    real_part = single(matrix[0], vector[0]) - single(matrix[1], vector[1])
    imag_part = single(matrix[0], vector[1]) + single(matrix[1], vector[0])
    return jnp.stack([real_part, imag_part])


def layer_solve(source, leaf, gather_map, sep_panel, spread, owner_row):
    leaf_values = dense_apply(leaf, source.astype(jnp.bfloat16))
    partial_sums = dense_apply(gather_map, leaf_values.astype(jnp.bfloat16))
    sep_rounded = lax.psum(partial_sums, "front").astype(jnp.bfloat16)
    own_rows = dense_apply(sep_panel, sep_rounded).astype(jnp.bfloat16)
    stored = lax.all_gather(own_rows, "front", axis=2, tiled=True)
    count = stored.shape[1]
    panels = stored.reshape(2, count, owner_row.shape[0], own_rows.shape[2])
    sep_values = jnp.take(panels, owner_row, axis=2).reshape(2, count, stored.shape[2])
    return leaf_values - dense_apply(spread, sep_values)


def local(
    right_sides,
    leaf_inverse,
    couple_above,
    couple_below,
    sep_gather,
    sep_inverse,
    sep_spread,
    panel_owner,
):
    depth = lax.axis_size("layer")
    owner_row = panel_owner[0]
    sources = right_sides[0]

    def solve(source):
        return layer_solve(
            source, leaf_inverse[0], sep_gather[0], sep_inverse[0], sep_spread[0], owner_row
        )

    forward = solve(sources)
    for step_index in range(depth - 1):
        from_prev = from_behind(forward.astype(jnp.bfloat16), "layer", 1)
        forward = solve(sources - dense_apply(couple_above[0], from_prev))
    solution = forward
    for step_index in range(depth - 1):
        from_next = from_behind(solution.astype(jnp.bfloat16), "layer", -1)
        solution = forward - solve(dense_apply(couple_below[0], from_next))
    return solution[None]


def solution(mesh):
    return jax.shard_map(
        local,
        mesh=mesh,
        in_specs=(
            P("layer", None, None, "front"),
            P("layer", None, "front", None),
            P("layer", None, "front", None),
            P("layer", None, "front", None),
            P("layer", None, None, "front"),
            P("layer", None, "front", None),
            P("layer", None, "front", None),
            P("layer", None),
        ),
        out_specs=P("layer", None, None, "front"),
        check_vma=False,
    )
```

profile of v0, /device:TPU:0, one launch (start us, length us, event | category | flops | bytes accessed | tf_op | source)
XLA Modules:
  0.0 523.8 jit_solution(4343662699394242140)
XLA Ops:
  10.3 31.9 %all-reduce.7 = bf16[2,4,5120]{2,1,0:T(4,128)(2,1)S(1)} all-reduce(f32[2,4,5120]{2,1,0:T(4,128)S(1)} %pad_maximum_fusion), channel_id=1, replica_groups=mesh['layer'=4,'front'=8] {'front'}, use_global_device_ids=true, to_apply=%region_0.0 | all-reduce | flops 40960 | bytes 245760 | tf_op jit(solution)/shard_map/psum | solution.py:26
  42.2 4.8 fusion.24
  47.0 5.4 %fusion.26 = f32[4,640]{1,0:T(4,128)S(1)} fusion(bf16[2,4,5120]{2,1,0:T(4,128)(2,1)S(1)} %all-reduce.7, bf16[1,2,640,5120]{3,2,1,0:T(8,128)(2,1)} %param.15), kind=kOutput, calls=%fused_computation.33 | convolution fusion | flops 26214400 | bytes 6604800 | tf_op jit(solution)/shard_map/dot_general | solution.py:16
  56.1 14.0 %all_gather.21 = bf16[2,4,5120]{2,1,0:T(4,128)(2,1)S(1)} all-gather(bf16[2,4,640]{2,1,0:T(4,128)(2,1)S(1)} %pad_maximum_fusion.7), channel_id=1, replica_groups=mesh['layer'=4,'front'=8] {'front'}, dimensions={2}, use_global_device_ids=true | all-gather | bytes 92160 | tf_op jit(solution)/shard_map/all_gather | solution.py:28
  70.9 1.9 fusion.94
  75.5 3.4 collective-permute-start
  83.3 28.2 %all-reduce.8 = bf16[2,4,5120]{2,1,0:T(4,128)(2,1)S(1)} all-reduce(f32[2,4,5120]{2,1,0:T(4,128)S(1)} %pad_maximum_fusion.1), channel_id=1, replica_groups=mesh['layer'=4,'front'=8] {'front'}, use_global_device_ids=true, to_apply=%region_1.0 | all-reduce | flops 40960 | bytes 245760 | tf_op jit(solution)/shard_map/psum | solution.py:26
  111.5 4.6 fusion.20
  116.1 4.7 fusion.22
  120.8 4.7 fusion.282
  125.5 4.7 fusion.285
  130.2 14.0 %all_gather.22 = bf16[2,4,5120]{2,1,0:T(4,128)(2,1)S(1)} all-gather(bf16[2,4,640]{2,1,0:T(4,128)(2,1)S(1)} %pad_maximum_fusion.8), channel_id=1, replica_groups=mesh['layer'=4,'front'=8] {'front'}, dimensions={2}, use_global_device_ids=true | all-gather | bytes 92160 | tf_op jit(solution)/shard_map/all_gather | solution.py:28
  149.6 4.2 collective-permute-start.1
  158.1 27.8 %all-reduce.9 = bf16[2,4,5120]{2,1,0:T(4,128)(2,1)S(1)} all-reduce(f32[2,4,5120]{2,1,0:T(4,128)S(1)} %pad_maximum_fusion.2), channel_id=1, replica_groups=mesh['layer'=4,'front'=8] {'front'}, use_global_device_ids=true, to_apply=%region_2.4 | all-reduce | flops 40960 | bytes 245760 | tf_op jit(solution)/shard_map/psum | solution.py:26
  186.0 4.6 fusion.16
  190.6 4.7 fusion.18
  195.3 4.7 fusion.276
  200.0 4.7 fusion.279
  204.7 14.0 %all_gather.23 = bf16[2,4,5120]{2,1,0:T(4,128)(2,1)S(1)} all-gather(bf16[2,4,640]{2,1,0:T(4,128)(2,1)S(1)} %pad_maximum_fusion.9), channel_id=1, replica_groups=mesh['layer'=4,'front'=8] {'front'}, dimensions={2}, use_global_device_ids=true | all-gather | bytes 92160 | tf_op jit(solution)/shard_map/all_gather | solution.py:28
  224.0 4.3 collective-permute-start.2
  232.7 27.9 %all-reduce.10 = bf16[2,4,5120]{2,1,0:T(4,128)(2,1)S(1)} all-reduce(f32[2,4,5120]{2,1,0:T(4,128)S(1)} %pad_maximum_fusion.3), channel_id=1, replica_groups=mesh['layer'=4,'front'=8] {'front'}, use_global_device_ids=true, to_apply=%region_3.5 | all-reduce | flops 40960 | bytes 245760 | tf_op jit(solution)/shard_map/psum | solution.py:26
  260.6 4.6 fusion.12
  265.2 4.7 fusion.14
  269.9 4.7 fusion.270
  274.6 4.7 fusion.273
  279.3 14.0 %all_gather.24 = bf16[2,4,5120]{2,1,0:T(4,128)(2,1)S(1)} all-gather(bf16[2,4,640]{2,1,0:T(4,128)(2,1)S(1)} %pad_maximum_fusion.10), channel_id=1, replica_groups=mesh['layer'=4,'front'=8] {'front'}, dimensions={2}, use_global_device_ids=true | all-gather | bytes 92160 | tf_op jit(solution)/shard_map/all_gather | solution.py:28
  294.1 1.9 fusion.82
  300.0 5.3 %collective-permute-done.3 = bf16[2,4,128]{2,1,0:T(4,128)(2,1)S(1)} collective-permute-done((bf16[2,4,128]{2,1,0:T(4,128)(2,1)S(1)}, bf16[2,4,128]{2,1,0:T(4,128)(2,1)S(1)}, u32[]{:S(2)}, u32[]{:S(2)}) %collective-permute-start.3) | collective-permute-done | bytes 2080 | tf_op jit(solution)/shard_map/ppermute | solution.py:10
  308.4 27.9 %all-reduce.11 = bf16[2,4,5120]{2,1,0:T(4,128)(2,1)S(1)} all-reduce(f32[2,4,5120]{2,1,0:T(4,128)S(1)} %pad_maximum_fusion.4), channel_id=1, replica_groups=mesh['layer'=4,'front'=8] {'front'}, use_global_device_ids=true, to_apply=%region_4.6 | all-reduce | flops 40960 | bytes 245760 | tf_op jit(solution)/shard_map/psum | solution.py:26
  336.3 4.6 fusion.8
  340.9 4.7 fusion.10
  345.6 4.7 fusion.264
  350.3 4.7 fusion.267
  355.0 14.0 %all_gather.25 = bf16[2,4,5120]{2,1,0:T(4,128)(2,1)S(1)} all-gather(bf16[2,4,640]{2,1,0:T(4,128)(2,1)S(1)} %pad_maximum_fusion.11), channel_id=1, replica_groups=mesh['layer'=4,'front'=8] {'front'}, dimensions={2}, use_global_device_ids=true | all-gather | bytes 92160 | tf_op jit(solution)/shard_map/all_gather | solution.py:28
  375.7 5.3 %collective-permute-done.4 = bf16[2,4,128]{2,1,0:T(4,128)(2,1)S(1)} collective-permute-done((bf16[2,4,128]{2,1,0:T(4,128)(2,1)S(1)}, bf16[2,4,128]{2,1,0:T(4,128)(2,1)S(1)}, u32[]{:S(2)}, u32[]{:S(2)}) %collective-permute-start.4) | collective-permute-done | bytes 2080 | tf_op jit(solution)/shard_map/ppermute | solution.py:10
  384.1 28.1 %all-reduce.12 = bf16[2,4,5120]{2,1,0:T(4,128)(2,1)S(1)} all-reduce(f32[2,4,5120]{2,1,0:T(4,128)S(1)} %pad_maximum_fusion.5), channel_id=1, replica_groups=mesh['layer'=4,'front'=8] {'front'}, use_global_device_ids=true, to_apply=%region_5.7 | all-reduce | flops 40960 | bytes 245760 | tf_op jit(solution)/shard_map/psum | solution.py:26
  412.2 4.6 fusion.4
  416.9 4.7 fusion.6
  421.5 4.7 fusion.258
  426.2 4.7 fusion.261
  430.9 14.0 %all_gather.26 = bf16[2,4,5120]{2,1,0:T(4,128)(2,1)S(1)} all-gather(bf16[2,4,640]{2,1,0:T(4,128)(2,1)S(1)} %pad_maximum_fusion.12), channel_id=1, replica_groups=mesh['layer'=4,'front'=8] {'front'}, dimensions={2}, use_global_device_ids=true | all-gather | bytes 92160 | tf_op jit(solution)/shard_map/all_gather | solution.py:28
  451.6 5.1 collective-permute-done.5
  459.7 27.8 %all-reduce.13 = bf16[2,4,5120]{2,1,0:T(4,128)(2,1)S(1)} all-reduce(f32[2,4,5120]{2,1,0:T(4,128)S(1)} %pad_maximum_fusion.6), channel_id=1, replica_groups=mesh['layer'=4,'front'=8] {'front'}, use_global_device_ids=true, to_apply=%region_6.8 | all-reduce | flops 40960 | bytes 245760 | tf_op jit(solution)/shard_map/psum | solution.py:26
  487.6 4.6 fusion
  492.2 4.7 fusion.2
  496.9 4.7 fusion.252
  501.5 4.8 fusion.255
  506.4 14.0 %all_gather.27 = bf16[2,4,5120]{2,1,0:T(4,128)(2,1)S(1)} all-gather(bf16[2,4,640]{2,1,0:T(4,128)(2,1)S(1)} %pad_maximum_fusion.13), channel_id=1, replica_groups=mesh['layer'=4,'front'=8] {'front'}, dimensions={2}, use_global_device_ids=true | all-gather | bytes 92160 | tf_op jit(solution)/shard_map/all_gather | solution.py:28
  (195 shorter events, 71.7 us)
Async XLA Ops:
  0.0 9.3 %copy-start.1 = (bf16[1,2,5120,128]{3,2,1,0:T(8,128)(2,1)S(1)}, bf16[1,2,5120,128]{3,2,1,0:T(8,128)(2,1)}, u32[]{:S(2)}) copy-start(bf16[1,2,5120,128]{3,2,1,0:T(8,128)(2,1)} %param.14) | copy-start | bytes 7864324
  42.2 10.2 %copy-start = (bf16[1,2,640,5120]{3,2,1,0:T(8,128)(2,1)S(1)}, bf16[1,2,640,5120]{3,2,1,0:T(8,128)(2,1)}, u32[]{:S(2)}) copy-start(bf16[1,2,640,5120]{3,2,1,0:T(8,128)(2,1)} %param.15) | copy-start | bytes 39321604
  70.7 3.9 copy-start.2
  70.9 9.3 %copy-start.10 = (bf16[1,2,128,128]{3,2,1,0:T(8,128)(2,1)S(1)}, bf16[1,2,128,128]{3,2,1,0:T(8,128)(2,1)}, u32[]{:S(2)}) copy-start(bf16[1,2,128,128]{3,2,1,0:T(8,128)(2,1)} %param.12) | copy-start | bytes 196612
  70.9 9.9 %copy-start.12 = (f32[1,2,4,128]{3,2,1,0:T(4,128)S(1)}, f32[1,2,4,128]{3,2,1,0:T(4,128)}, u32[]{:S(2)}) copy-start(f32[1,2,4,128]{3,2,1,0:T(4,128)} %param.10) | copy-start | bytes 12292
  70.9 9.9 %copy-start.9 = (bf16[1,2,128,128]{3,2,1,0:T(8,128)(2,1)S(1)}, bf16[1,2,128,128]{3,2,1,0:T(8,128)(2,1)}, u32[]{:S(2)}) copy-start(bf16[1,2,128,128]{3,2,1,0:T(8,128)(2,1)} %param.11) | copy-start | bytes 196612
  75.5 4.7 collective-permute-start
  144.8 3.8 copy-start.3
  149.6 5.5 %collective-permute-start.1 = (bf16[2,4,128]{2,1,0:T(4,128)(2,1)S(1)}, bf16[2,4,128]{2,1,0:T(4,128)(2,1)S(1)}, u32[]{:S(2)}, u32[]{:S(2)}) collective-permute-start(bf16[2,4,128]{2,1,0:T(4,128)(2,1)S(1)} %fusion.498), channel_id=1, source_target_pairs={{0,8},{8,16},{16,24},{1,9},{9,17},{17,25},{2,10},{10,18},{18,26},{... | collective-permute-start | bytes 6152 | tf_op jit(solution)/shard_map/ppermute | solution.py:10
  219.3 3.8 copy-start.4
  224.0 5.6 %collective-permute-start.2 = (bf16[2,4,128]{2,1,0:T(4,128)(2,1)S(1)}, bf16[2,4,128]{2,1,0:T(4,128)(2,1)S(1)}, u32[]{:S(2)}, u32[]{:S(2)}) collective-permute-start(bf16[2,4,128]{2,1,0:T(4,128)(2,1)S(1)} %fusion.500), channel_id=1, source_target_pairs={{0,8},{8,16},{16,24},{1,9},{9,17},{17,25},{2,10},{10,18},{18,26},{... | collective-permute-start | bytes 6152 | tf_op jit(solution)/shard_map/ppermute | solution.py:10
  293.9 3.8 copy-start.5
  294.1 11.3 %copy-start.11 = (bf16[1,2,128,128]{3,2,1,0:T(8,128)(2,1)S(1)}, bf16[1,2,128,128]{3,2,1,0:T(8,128)(2,1)}, u32[]{:S(2)}) copy-start(bf16[1,2,128,128]{3,2,1,0:T(8,128)(2,1)} %param.13) | copy-start | bytes 196612
  298.7 6.6 %collective-permute-start.3 = (bf16[2,4,128]{2,1,0:T(4,128)(2,1)S(1)}, bf16[2,4,128]{2,1,0:T(4,128)(2,1)S(1)}, u32[]{:S(2)}, u32[]{:S(2)}) collective-permute-start(bf16[2,4,128]{2,1,0:T(4,128)(2,1)S(1)} %get-tuple-element.6), channel_id=1, source_target_pairs={{8,0},{16,8},{24,16},{9,1},{17,9},{25,17},{10,2},{18,10},{26,18},{... | collective-permute-start | bytes 6152 | tf_op jit(solution)/shard_map/ppermute | solution.py:10
  369.6 3.8 copy-start.6
  374.4 6.6 %collective-permute-start.4 = (bf16[2,4,128]{2,1,0:T(4,128)(2,1)S(1)}, bf16[2,4,128]{2,1,0:T(4,128)(2,1)S(1)}, u32[]{:S(2)}, u32[]{:S(2)}) collective-permute-start(bf16[2,4,128]{2,1,0:T(4,128)(2,1)S(1)} %fusion.504), channel_id=1, source_target_pairs={{8,0},{16,8},{24,16},{9,1},{17,9},{25,17},{10,2},{18,10},{26,18},{... | collective-permute-start | bytes 6152 | tf_op jit(solution)/shard_map/ppermute | solution.py:10
  445.5 3.8 copy-start.7
  450.3 6.4 %collective-permute-start.5 = (bf16[2,4,128]{2,1,0:T(4,128)(2,1)S(1)}, bf16[2,4,128]{2,1,0:T(4,128)(2,1)S(1)}, u32[]{:S(2)}, u32[]{:S(2)}) collective-permute-start(bf16[2,4,128]{2,1,0:T(4,128)(2,1)S(1)} %fusion.506), channel_id=1, source_target_pairs={{8,0},{16,8},{24,16},{9,1},{17,9},{25,17},{10,2},{18,10},{26,18},{... | collective-permute-start | bytes 6152 | tf_op jit(solution)/shard_map/ppermute | solution.py:10
  501.5 19.6 %copy-start.8 = (bf16[1,2,128,5120]{3,2,1,0:T(8,128)(2,1)S(1)}, bf16[1,2,128,5120]{3,2,1,0:T(8,128)(2,1)}, u32[]{:S(2)}) copy-start(bf16[1,2,128,5120]{3,2,1,0:T(8,128)(2,1)} %param.16) | copy-start | bytes 7864324
where the time goes:
time: 532 us; the launch traced here: 524 us
  blocking collectives  298 us (56%)
  matrix products  181 us (34%)
  waiting for transfers between devices  19.6 us (4%)
  starting transfers between devices  15.8 us (3%)
    psum x7, blocking collectives, layer_solve(): sep_rounded = lax.psum(partial_sums, 'front').astype(jnp.bfloat16)  200 us
    dot_general x136, matrix products, single(): return jnp.dot(right, left.T, preferred_element_type=jnp.float32)  181 us
    all_gather x7, blocking collectives, layer_solve(): stored = lax.all_gather(own_rows, 'front', axis=2, tiled=True)  98 us
    ppermute x6, waiting for transfers between devices, from_behind(): return lax.ppermute(block, axis, route)  19.6 us
    ppermute x6, starting transfers between devices, from_behind(): return lax.ppermute(block, axis, route)  15.8 us
  transfers between devices with their start and end apart: 6, of which 6 were waited for; matrix products, arithmetic and copies ran while one was open for 0% of the time, Pallas kernels for 0%

commit v1 on v0

v1 whole, which is shorter than its diff:
```python
import jax
import jax.numpy as jnp
from jax import lax
from jax.sharding import PartitionSpec as P


def xor_route(axis, distance):
    return [(i, i ^ distance) for i in range(lax.axis_size(axis))]


def pair(block):
    return lax.ppermute(block, "front", xor_route("front", 1))


FEW_CHIPS = 8


def same_core_groups():
    slots = lax.axis_size("front")
    return [list(range(core, slots, 2)) for core in range(2)]


def arrival_order(chip, chips):
    steps = jnp.arange(chips, dtype=jnp.int32)
    return chip ^ steps if chips <= FEW_CHIPS else steps


def gather_chips(block):
    chips = lax.axis_size("front") // 2
    if chips > FEW_CHIPS:
        return lax.all_gather(
            block, "front", axis=2, tiled=True, axis_index_groups=same_core_groups()
        )
    return jnp.concatenate(from_chips(block, chips), axis=2)


def sum_chips(block):
    chips = lax.axis_size("front") // 2
    if chips > FEW_CHIPS:
        return lax.psum(block, "front", axis_index_groups=same_core_groups())
    parts = from_chips(block.astype(jnp.bfloat16), chips)
    return sum(part.astype(jnp.float32) for part in parts)


def from_chips(block, chips):
    return [block] + [
        lax.ppermute(block, "front", xor_route("front", 2 * step)) for step in range(1, chips)
    ]


def combine(real_rows, imag_rows, count):
    real_part = real_rows[:count] - imag_rows[count:]
    imag_part = real_rows[count:] + imag_rows[:count]
    return jnp.stack([real_part, imag_part])


def dense_apply(matrix, vector):
    count = vector.shape[1]
    rows = vector.reshape(2 * count, vector.shape[2])
    both = lax.dot_general(
        rows, matrix, (((1,), (2,)), ((), ())), preferred_element_type=jnp.float32
    )
    return combine(both[:, 0], both[:, 1], count)


def block_apply(blocks, vector):
    size = blocks.shape[2]
    return jnp.concatenate(
        [dense_apply(blocks[:, i], vector[:, :, i * size : (i + 1) * size]) for i in range(2)],
        axis=2,
    )


def local(
    right_sides,
    leaf_inverse,
    couple_above,
    couple_below,
    sep_gather,
    sep_inverse,
    sep_spread,
    panel_owner,
):
    depth = lax.axis_size("layer")
    slots = lax.axis_size("front")
    chips = slots // 2
    layer = lax.axis_index("layer")
    place = lax.axis_index("front")
    core = place % 2
    sep = sep_inverse[0]
    cells = leaf_inverse.shape[2]
    total = sep_gather.shape[2]

    def with_partner(block, axis):
        return jnp.concatenate([block, pair(block)], axis=axis)

    halves = sep_gather[0].reshape(2, 2, total // 2, cells)
    own_half = lax.dynamic_index_in_dim(halves, core, 1, keepdims=False)
    other_half = lax.dynamic_index_in_dim(halves, 1 - core, 1, keepdims=False)
    gather_half = jnp.concatenate([own_half, pair(other_half)], axis=2)

    slot_ids = jnp.arange(slots, dtype=jnp.int32)
    panel_of = jnp.sum(
        jnp.where(panel_owner[0][None, :] == slot_ids[:, None], slot_ids[None, :], 0), axis=1
    )
    arrive = arrival_order(place // 2, chips)
    panels = sep_spread[0].reshape(2, cells, slots, total // slots)

    def columns(which):
        chosen = jnp.take(panels, panel_of[2 * arrive + which], axis=2)
        return chosen.reshape(2, cells, total // 2)

    spread_half = jnp.concatenate([columns(core), pair(columns(1 - core))], axis=1)

    leaf = jnp.stack([leaf_inverse[0], pair(leaf_inverse[0])], axis=1)
    above = jnp.stack([couple_above[0], pair(couple_above[0])], axis=1)
    below = jnp.stack([couple_below[0], pair(couple_below[0])], axis=1)
    sources = with_partner(right_sides[0], 2)

    def solve(source):
        leaf_values = block_apply(leaf, source.astype(jnp.bfloat16))
        partial_sums = dense_apply(gather_half, leaf_values.astype(jnp.bfloat16))
        half_sums = sum_chips(partial_sums).astype(jnp.bfloat16)
        other_sums = pair(half_sums)
        first = jnp.where(core == 0, half_sums, other_sums)
        second = jnp.where(core == 0, other_sums, half_sums)
        own_rows = dense_apply(sep, jnp.concatenate([first, second], axis=2)).astype(jnp.bfloat16)
        stored = gather_chips(own_rows)
        spread = dense_apply(spread_half, stored)
        theirs = pair(spread)
        spread = spread + jnp.concatenate([theirs[:, :, cells:], theirs[:, :, :cells]], axis=2)
        return leaf_values - spread

    def hop(value, source_layer, target_layer):
        return lax.ppermute(
            value.astype(jnp.bfloat16), "layer", xor_route("layer", source_layer ^ target_layer)
        )

    value = jnp.zeros_like(sources)
    value = lax.cond(layer == 0, lambda old: solve(sources), lambda old: old, value)
    for level in range(1, depth):
        arrived = hop(value, level - 1, level)
        value = lax.cond(
            layer == level,
            lambda old, got: solve(sources - block_apply(above, got)),
            lambda old, got: old,
            value,
            arrived,
        )
    for level in range(depth - 2, -1, -1):
        arrived = hop(value, level + 1, level)
        value = lax.cond(
            layer == level,
            lambda old, got: old - solve(block_apply(below, got)),
            lambda old, got: old,
            value,
            arrived,
        )
    return value[None, :, :, :cells]


def solution(mesh):
    return jax.shard_map(
        local,
        mesh=mesh,
        in_specs=(
            P("layer", None, None, "front"),
            P("layer", None, "front", None),
            P("layer", None, "front", None),
            P("layer", None, "front", None),
            P("layer", None, None, "front"),
            P("layer", None, "front", None),
            P("layer", None, "front", None),
            P("layer", None),
        ),
        out_specs=P("layer", None, None, "front"),
        check_vma=False,
    )
```

time: 532 us -> 261 us (0.49); the launches traced: 524 us -> 261 us
  blocking collectives: 298 us -> 0 us
  starting transfers between devices: 15.8 us -> 178 us
  matrix products: 181 us -> 21.5 us
  waiting for transfers between devices: 19.6 us -> 34.6 us
  local copies, waits for them, and re-layouts: 4.69 us -> 18 us
    psum x7 -> x0, blocking collectives: 200 us -> none  [layer_solve(): sep_rounded = lax.psum(partial_sums, 'front').astype(jnp.bfloat16)]
    ppermute x6 -> x28, starting transfers between devices: 15.8 us -> 178 us  [the longest x6 157 us: hop(): lax.ppermute(value.astype(jnp.bfloat16), 'layer', xor_route('layer', sour...]
    dot_general x136 -> x12, matrix products: 181 us -> 21.5 us  [dense_apply(): lax.dot_general(rows, matrix, (((1,), (2,)), ((), ())), preferred_element...]
    all_gather x7 -> x0, blocking collectives: 98 us -> none  [layer_solve(): stored = lax.all_gather(own_rows, 'front', axis=2, tiled=True)]
    ppermute x6 -> x28, waiting for transfers between devices: 19.6 us -> 34.6 us  [the longest x12 15.5 us: from_chips(): lax.ppermute(block, 'front', xor_route('front', 2 * step))]
  transfers between devices with their start and end apart: 6 -> 28, of which waited for: 6 -> 18; matrix products, arithmetic and copies ran while one was open for 0% -> 9% of each run, Pallas kernels for 0% -> 0%
where the time goes in v1:
time: 261 us
  starting transfers between devices  178 us (68%)
  waiting for transfers between devices  34.6 us (13%)
  matrix products  21.5 us (8%)
  local copies, waits for them, and re-layouts  18 us (7%)
  other arithmetic  8.13 us (3%)
    ppermute x6, starting transfers between devices, hop(): lax.ppermute(value.astype(jnp.bfloat16), 'layer', xor_route('layer', sour...  157 us
    dot_general x12, matrix products, dense_apply(): lax.dot_general(rows, matrix, (((1,), (2,)), ((), ())), preferred_element...  21.5 us
    ppermute x12, starting transfers between devices, from_chips(): lax.ppermute(block, 'front', xor_route('front', 2 * step))  19 us
    ppermute x12, waiting for transfers between devices, from_chips(): lax.ppermute(block, 'front', xor_route('front', 2 * step))  15.5 us
    ppermute x6, waiting for transfers between devices, hop(): lax.ppermute(value.astype(jnp.bfloat16), 'layer', xor_route('layer', sour...  14.4 us
    gather x4, local copies, waits for them, and re-layouts, columns(): chosen = jnp.take(panels, panel_of[2 * arrive + which], axis=2)  5.6 us
  transfers between devices with their start and end apart: 28, of which 18 were waited for; matrix products, arithmetic and copies ran while one was open for 9% of the time, Pallas kernels for 0%

profile of v1, /device:TPU:0, one launch (start us, length us, event | category | flops | bytes accessed | tf_op | source)
XLA Modules:
  0.0 260.9 jit_solution(13193516724369134185)
XLA Ops:
  0.0 0.8 select_reduce_fusion
  0.8 0.6 gather_fusion.1
  1.4 0.6 gather_fusion
  2.1 3.2 %copy.31 = bf16[1,2,128,5120]{2,3,1,0:T(8,128)(2,1)S(1)} copy(bf16[1,2,128,5120]{3,2,1,0:T(8,128)(2,1)} %param.30) | data formatting | bytes 5242880 | tf_op args[6]
  5.4 2.6 copy.32
  7.9 2.5 gather_fusion.3
  10.7 1.5 copy.35
  12.6 3.6 %dynamic-slice_bitcast_fusion.1 = (bf16[2,2560,128]{2,1,0:T(8,128)(2,1)}, bf16[2,2560,128]{2,1,0:T(8,128)(2,1)}) fusion(bf16[2,2,2560,128]{3,2,1,0:T(8,128)(2,1)} %bitcast.482, s32[]{:T(128)S(6)} %select_n.122, s32[]{:T(128)S(6)} %select_n.123), kind=kLoop, calls=%fused_computation.406 | loop fusion | bytes 5242888 | tf_op jit(solution)/shard_map/jit(dynamic_index_in_dim)/squeeze | solution.py:98
  17.2 1.8 gather_fusion.2
  19.0 1.6 select_bitcast_fusion.1
  20.6 0.8 copy.33
  21.6 3.2 %pad_maximum_fusion.45 = bf16[2,256,2560]{1,2,0:T(8,128)(2,1)} fusion(bf16[2,128,2560]{1,2,0:T(8,128)(2,1)} %collective-permute-done.59, bf16[2,128,2560]{1,2,0:T(8,128)(2,1)S(1)} %bitcast.480), kind=kLoop, calls=%fused_computation.402 | loop fusion | flops 5242880 | bytes 5242880 | tf_op jit(solution)/shard_map/concatenate | solution.py:113
  24.8 1.6 pad_maximum_fusion.44
  26.4 32.6 %conditional.7 = (f32[2,4,256]{2,1,0:T(4,128)S(1)}) conditional(s32[]{:T(128)} %convert_element_type.181, () %tuple.50, (f32[2,4,256]{2,1,0:T(4,128)S(1)}, bf16[1,2,128,128]{3,2,1,0:T(8,128)(2,1)S(1)}, bf16[2,128,128]{2,1,0:T(8,128)(2,1)S(1)}, s32[]{:T(128)}, bf16[2,2560,256]{2,1,0:T(8,128)(2,1)S(1)}, /*index=5*/bf16[2,640,5120]{2,1,0:T(8,128)(2,1)}, ...), branch_computations={%region_1.3_spmd, %region_2.4_spmd} | conditional | flops 148552704 | bytes 21027154 | solution.py:140
  26.8 0.8 fusion.12
  27.7 3.1 %collective-permute-start = (bf16[2,4,2560]{2,1,0:T(4,128)(2,1)S(1)}, bf16[2,4,2560]{2,1,0:T(4,128)(2,1)S(1)}, u32[]{:S(2)}, u32[]{:S(2)}) collective-permute-start(bf16[2,4,2560]{2,1,0:T(4,128)(2,1)S(1)} %pad_maximum_fusion.1), channel_id=1, source_target_pairs={{0,2},{1,3},{2,0},{3,1},{4,6},{5,7},{6,4},{7,5},{8,10},{9,11},{10,... | collective-permute-start | bytes 122888 | tf_op jit(solution)/shard_map/cond/branch_1_fun/ppermute | solution.py:47
  30.8 2.6 collective-permute-start.1
  33.4 3.2 %collective-permute-done.1 = bf16[2,4,2560]{2,1,0:T(4,128)(2,1)S(1)} collective-permute-done((bf16[2,4,2560]{2,1,0:T(4,128)(2,1)S(1)}, bf16[2,4,2560]{2,1,0:T(4,128)(2,1)S(1)}, u32[]{:S(2)}, u32[]{:S(2)}) %collective-permute-start.1) | collective-permute-done | bytes 40992 | tf_op jit(solution)/shard_map/cond/branch_1_fun/ppermute | solution.py:47
  36.5 2.6 %collective-permute-done.2 = bf16[2,4,2560]{2,1,0:T(4,128)(2,1)S(1)} collective-permute-done((bf16[2,4,2560]{2,1,0:T(4,128)(2,1)S(1)}, bf16[2,4,2560]{2,1,0:T(4,128)(2,1)S(1)}, u32[]{:S(2)}, u32[]{:S(2)}) %collective-permute-start.2) | collective-permute-done | bytes 40992 | tf_op jit(solution)/shard_map/cond/branch_1_fun/ppermute | solution.py:47
  39.3 1.2 collective-permute-done.3
  40.6 8.2 %fusion.220 = f32[8,2,640]{2,0,1:T(8,128)S(1)} fusion(bf16[8,5120,1]{1,0,2:T(8,128)(2,1)S(1)} %reshape.2164, bf16[2,640,5120]{2,1,0:T(8,128)(2,1)} %get-tuple-element.174), kind=kOutput, calls=%fused_computation.441 | convolution fusion | flops 104857600 | bytes 13230080 | tf_op jit(solution)/shard_map/cond/branch_1_fun/dot_general | solution.py:60
  48.9 1.1 collective-permute-start.5
  50.0 3.2 %collective-permute-start.6 = (bf16[2,4,640]{2,1,0:T(4,128)(2,1)S(1)}, bf16[2,4,640]{2,1,0:T(4,128)(2,1)S(1)}, u32[]{:S(2)}, u32[]{:S(2)}) collective-permute-start(bf16[2,4,640]{2,1,0:T(4,128)(2,1)S(1)} %pad_maximum_fusion.3), channel_id=1, source_target_pairs={{0,6},{1,7},{2,4},{3,5},{4,2},{5,3},{6,0},{7,1},{8,14},{9,15},{10,... | collective-permute-start | bytes 30728 | tf_op jit(solution)/shard_map/cond/branch_1_fun/ppermute | solution.py:47
  53.5 2.0 collective-permute-done.6
  55.6 2.2 fusion.221
  57.8 1.2 collective-permute-done.7
  59.1 3.6 %collective-permute-done.60 = bf16[2,4,256]{2,1,0:T(4,128)(2,1)S(1)} collective-permute-done((bf16[2,4,256]{2,1,0:T(4,128)(2,1)S(1)}, bf16[2,4,256]{2,1,0:T(4,128)(2,1)S(1)}, u32[]{:S(2)}, u32[]{:S(2)}) %collective-permute-start.60) | collective-permute-done | bytes 4128 | tf_op jit(solution)/shard_map/ppermute | solution.py:135
  62.7 4.5 %collective-permute-done.62 = bf16[2,4,256]{2,1,0:T(4,128)(2,1)S(1)} collective-permute-done((bf16[2,4,256]{2,1,0:T(4,128)(2,1)S(1)}, bf16[2,4,256]{2,1,0:T(4,128)(2,1)S(1)}, u32[]{:S(2)}, u32[]{:S(2)}) %collective-permute-start.62) | collective-permute-done | bytes 4128 | tf_op jit(solution)/shard_map/ppermute | solution.py:135
  67.2 30.6 %collective-permute-start.63 = (bf16[2,4,256]{2,1,0:T(4,128)(2,1)S(1)}, bf16[2,4,256]{2,1,0:T(4,128)(2,1)S(1)}, u32[]{:S(2)}, u32[]{:S(2)}) collective-permute-start(bf16[2,4,256]{2,1,0:T(4,128)(2,1)S(1)} %convert_element_type.187), channel_id=1, source_target_pairs={{0,8},{8,0},{16,24},{24,16},{1,9},{9,1},{17,25},{25,17},{2,10},{10... | collective-permute-start | bytes 12296 | tf_op jit(solution)/shard_map/ppermute | solution.py:135
  97.8 1.6 collective-permute-done.63
  99.4 2.0 collective-permute-start.64
  101.4 1.6 collective-permute-done.64
  103.0 62.3 %collective-permute-start.66 = (bf16[2,4,256]{2,1,0:T(4,128)(2,1)S(1)}, bf16[2,4,256]{2,1,0:T(4,128)(2,1)S(1)}, u32[]{:S(2)}, u32[]{:S(2)}) collective-permute-start(bf16[2,4,256]{2,1,0:T(4,128)(2,1)S(1)} %convert_element_type.189), channel_id=1, source_target_pairs={{0,24},{8,16},{16,8},{24,0},{1,25},{9,17},{17,9},{25,1},{2,26},{10... | collective-permute-start | bytes 12296 | tf_op jit(solution)/shard_map/ppermute | solution.py:135
  165.3 1.6 collective-permute-done.66
  166.9 62.3 %collective-permute-start.67 = (bf16[2,4,256]{2,1,0:T(4,128)(2,1)S(1)}, bf16[2,4,256]{2,1,0:T(4,128)(2,1)S(1)}, u32[]{:S(2)}, u32[]{:S(2)}) collective-permute-start(bf16[2,4,256]{2,1,0:T(4,128)(2,1)S(1)} %convert_element_type.190), channel_id=1, source_target_pairs={{0,8},{8,0},{16,24},{24,16},{1,9},{9,1},{17,25},{25,17},{2,10},{10... | collective-permute-start | bytes 12296 | tf_op jit(solution)/shard_map/ppermute | solution.py:135
  229.2 1.6 collective-permute-done.67
  230.8 29.5 %conditional.13 = (f32[1,2,4,128]{3,2,1,0:T(4,128)S(1)}) conditional(s32[]{:T(128)} %convert_element_type.181, f32[2,4,256]{2,1,0:T(4,128)S(1)} %get-tuple-element.554, (bf16[2,4,256]{2,1,0:T(4,128)(2,1)S(1)}, bf16[1,2,128,128]{3,2,1,0:T(8,128)(2,1)S(1)}, bf16[1,2,128,128]{3,2,1,0:T(8,128)(2,1)S(1)}, bf16[2,128,128]{2,1,0:T(8,128)(2,1)S(1)}, ...), branch_computations={%region_13.15_spmd, %region_14.16_spmd} | conditional | flops 149599232 | bytes 31680878 | solution.py:152
  231.5 0.8 fusion.183
  232.4 3.0 %collective-permute-start.49 = (bf16[2,4,2560]{2,1,0:T(4,128)(2,1)S(1)}, bf16[2,4,2560]{2,1,0:T(4,128)(2,1)S(1)}, u32[]{:S(2)}, u32[]{:S(2)}) collective-permute-start(bf16[2,4,2560]{2,1,0:T(4,128)(2,1)S(1)} %pad_maximum_fusion.35), channel_id=1, source_target_pairs={{0,4},{1,5},{2,6},{3,7},{4,0},{5,1},{6,2},{7,3},{8,12},{9,13},{10,... | collective-permute-start | bytes 122888 | tf_op jit(solution)/shard_map/cond/branch_1_fun/ppermute | solution.py:47
  235.4 1.4 collective-permute-start.50
  236.8 1.0 collective-permute-done.49
  237.8 3.4 %collective-permute-done.50 = bf16[2,4,2560]{2,1,0:T(4,128)(2,1)S(1)} collective-permute-done((bf16[2,4,2560]{2,1,0:T(4,128)(2,1)S(1)}, bf16[2,4,2560]{2,1,0:T(4,128)(2,1)S(1)}, u32[]{:S(2)}, u32[]{:S(2)}) %collective-permute-start.50) | collective-permute-done | bytes 40992 | tf_op jit(solution)/shard_map/cond/branch_1_fun/ppermute | solution.py:47
  241.4 1.2 collective-permute-done.51
  242.7 8.3 %fusion.244 = f32[8,2,640]{2,0,1:T(8,128)S(1)} fusion(bf16[8,5120,1]{1,0,2:T(8,128)(2,1)S(1)} %reshape.2206, bf16[2,640,5120]{2,1,0:T(8,128)(2,1)} %get-tuple-element.234), kind=kOutput, calls=%fused_computation.465 | convolution fusion | flops 104857600 | bytes 13230080 | tf_op jit(solution)/shard_map/cond/branch_1_fun/dot_general | solution.py:60
  251.1 1.9 collective-permute-start.53
  253.1 2.4 collective-permute-start.54
  255.8 2.8 %collective-permute-done.54 = bf16[2,4,640]{2,1,0:T(4,128)(2,1)S(1)} collective-permute-done((bf16[2,4,640]{2,1,0:T(4,128)(2,1)S(1)}, bf16[2,4,640]{2,1,0:T(4,128)(2,1)S(1)}, u32[]{:S(2)}, u32[]{:S(2)}) %collective-permute-start.54) | collective-permute-done | bytes 10272 | tf_op jit(solution)/shard_map/cond/branch_1_fun/ppermute | solution.py:47
  259.2 1.2 collective-permute-done.55
  (113 shorter events, 5.7 us)
Async XLA Ops:
  12.2 9.4 %collective-permute-start.59 = (bf16[2,128,2560]{1,2,0:T(8,128)(2,1)}, bf16[2,128,2560]{1,2,0:T(8,128)(2,1)}, u32[]{:S(2)}, u32[]{:S(2)}) collective-permute-start(bf16[2,128,2560]{1,2,0:T(8,128)(2,1)} %bitcast.195), channel_id=1, source_target_pairs={{0,1},{1,0},{2,3},{3,2},{4,5},{5,4},{6,7},{7,6},{8,9},{9,8},{10,11... | collective-permute-start | bytes 3932168 | tf_op jit(solution)/shard_map/ppermute | solution.py:12
  12.6 3.6 %copy-start.3 = (bf16[1,2,128,128]{3,2,1,0:T(8,128)(2,1)S(1)}, bf16[1,2,128,128]{3,2,1,0:T(8,128)(2,1)}, u32[]{:S(2)}) copy-start(bf16[1,2,128,128]{3,2,1,0:T(8,128)(2,1)} %param.25) | copy-start | bytes 196612
  12.6 4.1 %copy-start.7 = (f32[1,2,4,128]{3,2,1,0:T(4,128)S(1)}, f32[1,2,4,128]{3,2,1,0:T(4,128)}, u32[]{:S(2)}) copy-start(f32[1,2,4,128]{3,2,1,0:T(4,128)} %param.24) | copy-start | bytes 12292
  12.6 4.2 %copy-start.4 = (bf16[1,2,128,128]{3,2,1,0:T(8,128)(2,1)S(1)}, bf16[1,2,128,128]{3,2,1,0:T(8,128)(2,1)}, u32[]{:S(2)}) copy-start(bf16[1,2,128,128]{3,2,1,0:T(8,128)(2,1)} %param.26) | copy-start | bytes 196612
  12.6 4.6 %copy-start.1 = (bf16[2,128,8,640]{3,1,2,0:T(8,128)(2,1)S(1)}, bf16[2,128,8,640]{3,1,2,0:T(8,128)(2,1)}, u32[]{:S(2)}) copy-start(bf16[2,128,8,640]{3,1,2,0:T(8,128)(2,1)} %copy.32) | copy-start | bytes 7864324
  16.2 8.6 %collective-permute-start.58 = (bf16[2,2560,128]{2,1,0:T(8,128)(2,1)}, bf16[2,2560,128]{2,1,0:T(8,128)(2,1)}, u32[]{:S(2)}, u32[]{:S(2)}) collective-permute-start(bf16[2,2560,128]{2,1,0:T(8,128)(2,1)} %get-tuple-element.528), channel_id=1, source_target_pairs={{0,1},{1,0},{2,3},{3,2},{4,5},{5,4},{6,7},{7,6},{8,9},{9,8},{10,11... | collective-permute-start | bytes 3932168 | tf_op jit(solution)/shard_map/ppermute | solution.py:12
  16.3 10.2 %collective-permute-start.57 = (bf16[2,128,128]{2,1,0:T(8,128)(2,1)S(1)}, bf16[2,128,128]{2,1,0:T(8,128)(2,1)S(1)}, u32[]{:S(2)}, u32[]{:S(2)}) collective-permute-start(bf16[2,128,128]{2,1,0:T(8,128)(2,1)S(1)} %bitcast.481), channel_id=1, source_target_pairs={{0,1},{1,0},{2,3},{3,2},{4,5},{5,4},{6,7},{7,6},{8,9},{9,8},{10,11... | collective-permute-start | bytes 196616 | tf_op jit(solution)/shard_map/ppermute | solution.py:12
  16.7 4.7 %collective-permute-start.56 = (f32[2,4,128]{2,1,0:T(4,128)S(1)}, f32[2,4,128]{2,1,0:T(4,128)S(1)}, u32[]{:S(2)}, u32[]{:S(2)}) collective-permute-start(f32[2,4,128]{2,1,0:T(4,128)S(1)} %bitcast.553), channel_id=1, source_target_pairs={{0,1},{1,0},{2,3},{3,2},{4,5},{5,4},{6,7},{7,6},{8,9},{9,8},{10,11... | collective-permute-start | bytes 12296 | tf_op jit(solution)/shard_map/ppermute | solution.py:12
  16.8 42.3 %collective-permute-start.61 = (bf16[2,128,128]{2,1,0:T(8,128)(2,1)S(1)}, bf16[2,128,128]{2,1,0:T(8,128)(2,1)S(1)}, u32[]{:S(2)}, u32[]{:S(2)}) collective-permute-start(bf16[2,128,128]{2,1,0:T(8,128)(2,1)S(1)} %bitcast.483), channel_id=1, source_target_pairs={{0,1},{1,0},{2,3},{3,2},{4,5},{5,4},{6,7},{7,6},{8,9},{9,8},{10,11... | collective-permute-start | bytes 196616 | tf_op jit(solution)/shard_map/ppermute | solution.py:12
  19.0 2.4 copy-start.5
  21.4 80.0 %collective-permute-start.65 = (bf16[2,128,128]{2,1,0:T(8,128)(2,1)S(1)}, bf16[2,128,128]{2,1,0:T(8,128)(2,1)S(1)}, u32[]{:S(2)}, u32[]{:S(2)}) collective-permute-start(bf16[2,128,128]{2,1,0:T(8,128)(2,1)S(1)} %bitcast.484), channel_id=1, source_target_pairs={{0,1},{1,0},{2,3},{3,2},{4,5},{5,4},{6,7},{7,6},{8,9},{9,8},{10,11... | collective-permute-start | bytes 196616 | tf_op jit(solution)/shard_map/ppermute | solution.py:12
  21.6 3.2 %copy-start.2 = (bf16[2,2560,128]{2,1,0:T(8,128)(2,1)S(1)}, bf16[2,2560,128]{2,1,0:T(8,128)(2,1)}, u32[]{:S(2)}) copy-start(bf16[2,2560,128]{2,1,0:T(8,128)(2,1)} %get-tuple-element.527) | copy-start | bytes 3932164
  27.7 5.7 %collective-permute-start = (bf16[2,4,2560]{2,1,0:T(4,128)(2,1)S(1)}, bf16[2,4,2560]{2,1,0:T(4,128)(2,1)S(1)}, u32[]{:S(2)}, u32[]{:S(2)}) collective-permute-start(bf16[2,4,2560]{2,1,0:T(4,128)(2,1)S(1)} %pad_maximum_fusion.1), channel_id=1, source_target_pairs={{0,2},{1,3},{2,0},{3,1},{4,6},{5,7},{6,4},{7,5},{8,10},{9,11},{10,... | collective-permute-start | bytes 122888 | tf_op jit(solution)/shard_map/cond/branch_1_fun/ppermute | solution.py:47
  30.8 5.8 %collective-permute-start.1 = (bf16[2,4,2560]{2,1,0:T(4,128)(2,1)S(1)}, bf16[2,4,2560]{2,1,0:T(4,128)(2,1)S(1)}, u32[]{:S(2)}, u32[]{:S(2)}) collective-permute-start(bf16[2,4,2560]{2,1,0:T(4,128)(2,1)S(1)} %pad_maximum_fusion.1), channel_id=1, source_target_pairs={{0,4},{1,5},{2,6},{3,7},{4,0},{5,1},{6,2},{7,3},{8,12},{9,13},{10,... | collective-permute-start | bytes 122888 | tf_op jit(solution)/shard_map/cond/branch_1_fun/ppermute | solution.py:47
  33.3 5.8 %collective-permute-start.2 = (bf16[2,4,2560]{2,1,0:T(4,128)(2,1)S(1)}, bf16[2,4,2560]{2,1,0:T(4,128)(2,1)S(1)}, u32[]{:S(2)}, u32[]{:S(2)}) collective-permute-start(bf16[2,4,2560]{2,1,0:T(4,128)(2,1)S(1)} %pad_maximum_fusion.1), channel_id=1, source_target_pairs={{0,6},{1,7},{2,4},{3,5},{4,2},{5,3},{6,0},{7,1},{8,14},{9,15},{10,... | collective-permute-start | bytes 122888 | tf_op jit(solution)/shard_map/cond/branch_1_fun/ppermute | solution.py:47
  39.2 1.3 collective-permute-start.3
  48.8 4.5 %collective-permute-start.4 = (bf16[2,4,640]{2,1,0:T(4,128)(2,1)S(1)}, bf16[2,4,640]{2,1,0:T(4,128)(2,1)S(1)}, u32[]{:S(2)}, u32[]{:S(2)}) collective-permute-start(bf16[2,4,640]{2,1,0:T(4,128)(2,1)S(1)} %pad_maximum_fusion.3), channel_id=1, source_target_pairs={{0,2},{1,3},{2,0},{3,1},{4,6},{5,7},{6,4},{7,5},{8,10},{9,11},{10,... | collective-permute-start | bytes 30728 | tf_op jit(solution)/shard_map/cond/branch_1_fun/ppermute | solution.py:47
  48.9 4.6 %collective-permute-start.5 = (bf16[2,4,640]{2,1,0:T(4,128)(2,1)S(1)}, bf16[2,4,640]{2,1,0:T(4,128)(2,1)S(1)}, u32[]{:S(2)}, u32[]{:S(2)}) collective-permute-start(bf16[2,4,640]{2,1,0:T(4,128)(2,1)S(1)} %pad_maximum_fusion.3), channel_id=1, source_target_pairs={{0,4},{1,5},{2,6},{3,7},{4,0},{5,1},{6,2},{7,3},{8,12},{9,13},{10,... | collective-permute-start | bytes 30728 | tf_op jit(solution)/shard_map/cond/branch_1_fun/ppermute | solution.py:47
  50.0 5.5 %collective-permute-start.6 = (bf16[2,4,640]{2,1,0:T(4,128)(2,1)S(1)}, bf16[2,4,640]{2,1,0:T(4,128)(2,1)S(1)}, u32[]{:S(2)}, u32[]{:S(2)}) collective-permute-start(bf16[2,4,640]{2,1,0:T(4,128)(2,1)S(1)} %pad_maximum_fusion.3), channel_id=1, source_target_pairs={{0,6},{1,7},{2,4},{3,5},{4,2},{5,3},{6,0},{7,1},{8,14},{9,15},{10,... | collective-permute-start | bytes 30728 | tf_op jit(solution)/shard_map/cond/branch_1_fun/ppermute | solution.py:47
  57.8 1.2 collective-permute-start.7
  59.0 3.7 %collective-permute-start.60 = (bf16[2,4,256]{2,1,0:T(4,128)(2,1)S(1)}, bf16[2,4,256]{2,1,0:T(4,128)(2,1)S(1)}, u32[]{:S(2)}, u32[]{:S(2)}) collective-permute-start(bf16[2,4,256]{2,1,0:T(4,128)(2,1)S(1)} %convert_element_type.185), channel_id=1, source_target_pairs={{0,8},{8,0},{16,24},{24,16},{1,9},{9,1},{17,25},{25,17},{2,10},{10... | collective-permute-start | bytes 12296 | tf_op jit(solution)/shard_map/ppermute | solution.py:135
  62.7 4.5 %collective-permute-start.62 = (bf16[2,4,256]{2,1,0:T(4,128)(2,1)S(1)}, bf16[2,4,256]{2,1,0:T(4,128)(2,1)S(1)}, u32[]{:S(2)}, u32[]{:S(2)}) collective-permute-start(bf16[2,4,256]{2,1,0:T(4,128)(2,1)S(1)} %convert_element_type.186), channel_id=1, source_target_pairs={{0,24},{8,16},{16,8},{24,0},{1,25},{9,17},{17,9},{25,1},{2,26},{10... | collective-permute-start | bytes 12296 | tf_op jit(solution)/shard_map/ppermute | solution.py:135
  67.2 32.2 %collective-permute-start.63 = (bf16[2,4,256]{2,1,0:T(4,128)(2,1)S(1)}, bf16[2,4,256]{2,1,0:T(4,128)(2,1)S(1)}, u32[]{:S(2)}, u32[]{:S(2)}) collective-permute-start(bf16[2,4,256]{2,1,0:T(4,128)(2,1)S(1)} %convert_element_type.187), channel_id=1, source_target_pairs={{0,8},{8,0},{16,24},{24,16},{1,9},{9,1},{17,25},{25,17},{2,10},{10... | collective-permute-start | bytes 12296 | tf_op jit(solution)/shard_map/ppermute | solution.py:135
  99.4 3.6 %collective-permute-start.64 = (bf16[2,4,256]{2,1,0:T(4,128)(2,1)S(1)}, bf16[2,4,256]{2,1,0:T(4,128)(2,1)S(1)}, u32[]{:S(2)}, u32[]{:S(2)}) collective-permute-start(bf16[2,4,256]{2,1,0:T(4,128)(2,1)S(1)} %convert_element_type.188), channel_id=1, source_target_pairs={{0,8},{8,0},{16,24},{24,16},{1,9},{9,1},{17,25},{25,17},{2,10},{10... | collective-permute-start | bytes 12296 | tf_op jit(solution)/shard_map/ppermute | solution.py:135
  103.0 63.9 %collective-permute-start.66 = (bf16[2,4,256]{2,1,0:T(4,128)(2,1)S(1)}, bf16[2,4,256]{2,1,0:T(4,128)(2,1)S(1)}, u32[]{:S(2)}, u32[]{:S(2)}) collective-permute-start(bf16[2,4,256]{2,1,0:T(4,128)(2,1)S(1)} %convert_element_type.189), channel_id=1, source_target_pairs={{0,24},{8,16},{16,8},{24,0},{1,25},{9,17},{17,9},{25,1},{2,26},{10... | collective-permute-start | bytes 12296 | tf_op jit(solution)/shard_map/ppermute | solution.py:135
  166.9 63.9 %collective-permute-start.67 = (bf16[2,4,256]{2,1,0:T(4,128)(2,1)S(1)}, bf16[2,4,256]{2,1,0:T(4,128)(2,1)S(1)}, u32[]{:S(2)}, u32[]{:S(2)}) collective-permute-start(bf16[2,4,256]{2,1,0:T(4,128)(2,1)S(1)} %convert_element_type.190), channel_id=1, source_target_pairs={{0,8},{8,0},{16,24},{24,16},{1,9},{9,1},{17,25},{25,17},{2,10},{10... | collective-permute-start | bytes 12296 | tf_op jit(solution)/shard_map/ppermute | solution.py:135
  232.4 4.5 %collective-permute-start.48 = (bf16[2,4,2560]{2,1,0:T(4,128)(2,1)S(1)}, bf16[2,4,2560]{2,1,0:T(4,128)(2,1)S(1)}, u32[]{:S(2)}, u32[]{:S(2)}) collective-permute-start(bf16[2,4,2560]{2,1,0:T(4,128)(2,1)S(1)} %pad_maximum_fusion.35), channel_id=1, source_target_pairs={{0,2},{1,3},{2,0},{3,1},{4,6},{5,7},{6,4},{7,5},{8,10},{9,11},{10,... | collective-permute-start | bytes 122888 | tf_op jit(solution)/shard_map/cond/branch_1_fun/ppermute | solution.py:47
  232.4 5.3 %collective-permute-start.49 = (bf16[2,4,2560]{2,1,0:T(4,128)(2,1)S(1)}, bf16[2,4,2560]{2,1,0:T(4,128)(2,1)S(1)}, u32[]{:S(2)}, u32[]{:S(2)}) collective-permute-start(bf16[2,4,2560]{2,1,0:T(4,128)(2,1)S(1)} %pad_maximum_fusion.35), channel_id=1, source_target_pairs={{0,4},{1,5},{2,6},{3,7},{4,0},{5,1},{6,2},{7,3},{8,12},{9,13},{10,... | collective-permute-start | bytes 122888 | tf_op jit(solution)/shard_map/cond/branch_1_fun/ppermute | solution.py:47
  235.4 5.8 %collective-permute-start.50 = (bf16[2,4,2560]{2,1,0:T(4,128)(2,1)S(1)}, bf16[2,4,2560]{2,1,0:T(4,128)(2,1)S(1)}, u32[]{:S(2)}, u32[]{:S(2)}) collective-permute-start(bf16[2,4,2560]{2,1,0:T(4,128)(2,1)S(1)} %pad_maximum_fusion.35), channel_id=1, source_target_pairs={{0,6},{1,7},{2,4},{3,5},{4,2},{5,3},{6,0},{7,1},{8,14},{9,15},{10,... | collective-permute-start | bytes 122888 | tf_op jit(solution)/shard_map/cond/branch_1_fun/ppermute | solution.py:47
  241.3 1.3 collective-permute-start.51
  242.7 15.9 %copy-start = (bf16[2,256,2560]{1,2,0:T(8,128)(2,1)S(1)}, bf16[2,256,2560]{1,2,0:T(8,128)(2,1)}, u32[]{:S(2)}) copy-start(bf16[2,256,2560]{1,2,0:T(8,128)(2,1)} %get-tuple-element.369) | copy-start | bytes 7864324 | tf_op jit(solution)/shard_map/cond
  251.1 4.5 %collective-permute-start.52 = (bf16[2,4,640]{2,1,0:T(4,128)(2,1)S(1)}, bf16[2,4,640]{2,1,0:T(4,128)(2,1)S(1)}, u32[]{:S(2)}, u32[]{:S(2)}) collective-permute-start(bf16[2,4,640]{2,1,0:T(4,128)(2,1)S(1)} %pad_maximum_fusion.37), channel_id=1, source_target_pairs={{0,2},{1,3},{2,0},{3,1},{4,6},{5,7},{6,4},{7,5},{8,10},{9,11},{10,... | collective-permute-start | bytes 30728 | tf_op jit(solution)/shard_map/cond/branch_1_fun/ppermute | solution.py:47
  251.1 4.6 %collective-permute-start.53 = (bf16[2,4,640]{2,1,0:T(4,128)(2,1)S(1)}, bf16[2,4,640]{2,1,0:T(4,128)(2,1)S(1)}, u32[]{:S(2)}, u32[]{:S(2)}) collective-permute-start(bf16[2,4,640]{2,1,0:T(4,128)(2,1)S(1)} %pad_maximum_fusion.37), channel_id=1, source_target_pairs={{0,4},{1,5},{2,6},{3,7},{4,0},{5,1},{6,2},{7,3},{8,12},{9,13},{10,... | collective-permute-start | bytes 30728 | tf_op jit(solution)/shard_map/cond/branch_1_fun/ppermute | solution.py:47
  253.1 5.5 %collective-permute-start.54 = (bf16[2,4,640]{2,1,0:T(4,128)(2,1)S(1)}, bf16[2,4,640]{2,1,0:T(4,128)(2,1)S(1)}, u32[]{:S(2)}, u32[]{:S(2)}) collective-permute-start(bf16[2,4,640]{2,1,0:T(4,128)(2,1)S(1)} %pad_maximum_fusion.37), channel_id=1, source_target_pairs={{0,6},{1,7},{2,4},{3,5},{4,2},{5,3},{6,0},{7,1},{8,14},{9,15},{10,... | collective-permute-start | bytes 30728 | tf_op jit(solution)/shard_map/cond/branch_1_fun/ppermute | solution.py:47
  259.1 1.2 collective-permute-start.55
  260.3 0.6 copy-start.6

commit v2 on v0

v2 whole, which is shorter than its diff:
```python
import jax
import jax.numpy as jnp
from jax import lax
from jax.experimental import pallas as pl
from jax.experimental.pallas import tpu as pltpu
from jax.sharding import PartitionSpec as P

FEW_CHIPS = 8
BF16, F32 = jnp.bfloat16, jnp.float32
VMEM = pl.BlockSpec(memory_space=pltpu.VMEM)
MIB = 2**20


def xor_route(axis, distance):
    return [(i, i ^ distance) for i in range(lax.axis_size(axis))]


def pair(block):
    return lax.ppermute(block, "front", xor_route("front", 1))


def same_core_groups():
    slots = lax.axis_size("front")
    return [list(range(core, slots, 2)) for core in range(2)]


def arrival_order(chip, chips):
    steps = jnp.arange(chips, dtype=jnp.int32)
    return chip ^ steps if chips <= FEW_CHIPS else steps


def from_chips(block, chips):
    return [block] + [
        lax.ppermute(block, "front", xor_route("front", 2 * step)) for step in range(1, chips)
    ]


def gather_chips(block):
    chips = lax.axis_size("front") // 2
    if chips > FEW_CHIPS:
        groups = same_core_groups()
        return lax.all_gather(block, "front", axis=1, tiled=True, axis_index_groups=groups)
    return jnp.concatenate(from_chips(block, chips), axis=1)


def sum_chips(block):
    chips = lax.axis_size("front") // 2
    if chips > FEW_CHIPS:
        return lax.psum(block.astype(F32), "front", axis_index_groups=same_core_groups())
    return sum(part.astype(F32) for part in from_chips(block, chips))


def in_vmem(block):
    return pltpu.with_memory_space_constraint(block, pltpu.VMEM)


def params(mib):
    return pltpu.CompilerParams(vmem_limit_bytes=mib * MIB)


def cost(flops, nbytes):
    return pl.CostEstimate(flops=flops, bytes_accessed=nbytes, transcendentals=0)


def turned(vector):
    count = vector.shape[0] // 2
    return jnp.concatenate([-vector[count:], vector[:count]], axis=0)


def operands(vector):
    return vector.astype(BF16), turned(vector).astype(BF16)


def times(vector, real_matrix, imag_matrix, contract):
    straight, cross = operands(vector)
    dims = (((1,), (contract,)), ((), ()))
    return lax.dot_general(
        straight, real_matrix, dims, preferred_element_type=F32
    ) + lax.dot_general(cross, imag_matrix, dims, preferred_element_type=F32)


def transpose_sep(sep):
    _, rows, total = sep.shape
    step = 512

    def kernel(block, out):
        at = pl.multiple_of(pl.program_id(0) * step, step)
        for part in range(2):
            out[part, pl.ds(at, step), :] = block[part].T

    return pl.pallas_call(
        kernel,
        grid=(total // step,),
        in_specs=[pl.BlockSpec((2, rows, step), lambda i: (0, 0, i))],
        out_specs=VMEM,
        out_shape=pltpu.VMEM((2, total, rows), BF16),
        compiler_params=params(16),
        cost_estimate=cost(0, 4 * sep.size),
        name="transpose_sep",
    )(sep)


def transpose_gather(gather):
    _, total, cells = gather.shape
    half = total // 2
    step = 512

    def kernel(block, keep, give):
        core = lax.axis_index("front") % 2
        for out, start in ((keep, core * half), (give, (1 - core) * half)):
            for part in range(2):
                for at in range(0, half, step):
                    rows = pl.ds(pl.multiple_of(start + at, step), step)
                    out[part, :, pl.ds(at, step)] = block[part, rows, :].T

    shape = jax.ShapeDtypeStruct((2, cells, half), BF16)
    return pl.pallas_call(
        kernel,
        in_specs=[VMEM],
        out_specs=[VMEM, VMEM],
        out_shape=[shape, shape],
        compiler_params=params(16),
        cost_estimate=cost(0, 4 * gather.size),
        name="transpose_gather",
    )(gather)


def transpose_spread(spread, keep_panels, give_panels, rows):
    _, cells, total = spread.shape
    chips = keep_panels.shape[0]

    def kernel(order, keep_block, give_block, keep, give):
        for part in range(2):
            keep[part] = keep_block[part].T
            give[part] = give_block[part].T

    shape = jax.ShapeDtypeStruct((2, total // 2, cells), BF16)
    out_block = pl.BlockSpec((2, rows, cells), lambda i, order: (0, i, 0))
    return pl.pallas_call(
        kernel,
        grid_spec=pltpu.PrefetchScalarGridSpec(
            num_scalar_prefetch=1,
            grid=(chips,),
            in_specs=[
                pl.BlockSpec((2, cells, rows), lambda i, order: (0, 0, order[i])),
                pl.BlockSpec((2, cells, rows), lambda i, order: (0, 0, order[chips + i])),
            ],
            out_specs=[out_block, out_block],
        ),
        out_shape=[shape, shape],
        compiler_params=params(16),
        cost_estimate=cost(0, 4 * spread.size),
        name="transpose_spread",
    )(jnp.concatenate([keep_panels, give_panels]), spread, spread)


def join(keep, got, axis):
    shape = list(keep.shape)
    size = shape[axis]
    shape[axis] = 2 * size

    def kernel(keep_ref, got_ref, out):
        if axis == 1:
            out[:, :size, :] = keep_ref[...]
            out[:, size:, :] = got_ref[...]
        else:
            out[:, :, :size] = keep_ref[...]
            out[:, :, size:] = got_ref[...]

    return pl.pallas_call(
        kernel,
        in_specs=[VMEM, VMEM],
        out_specs=VMEM,
        out_shape=pltpu.VMEM(tuple(shape), BF16),
        compiler_params=params(16),
        cost_estimate=cost(0, 8 * keep.size),
        name="join",
    )(keep, got)


def leaf_and_gather(level, leaf, gather, sources=None, couple=None, arrived=None):
    cells = leaf[0].shape[1]
    width = gather.shape[2]
    given = [block for block in (arrived, sources) if block is not None]
    mats = list(couple or []) + list(leaf)

    def kernel(*refs):
        vectors = list(refs[: len(given)])
        matrices = list(refs[len(given) : len(given) + len(mats)])
        gather_ref, leaf_out, sums_out = refs[-3:]

        def blocks(vector, pair_of):
            return jnp.concatenate(
                [
                    times(vector[:, i * cells : (i + 1) * cells], pair_of[i][0], pair_of[i][1], 1)
                    for i in range(2)
                ],
                axis=1,
            )

        @pl.when(lax.axis_index("layer") == level)
        def _():
            if couple is None:
                source = vectors[0][...]
            else:
                source = blocks(vectors[0][...].astype(F32), matrices[:2])
                if sources is not None:
                    source = vectors[1][...] - source
            leaf_values = blocks(source, matrices[-2:])
            leaf_out[...] = leaf_values
            sums_out[...] = times(leaf_values, gather_ref[0], gather_ref[1], 0).astype(BF16)

    return pl.pallas_call(
        kernel,
        in_specs=[VMEM] * (len(given) + len(mats) + 1),
        out_specs=[VMEM, VMEM],
        out_shape=[
            jax.ShapeDtypeStruct((8, 2 * cells), F32),
            jax.ShapeDtypeStruct((8, width), BF16),
        ],
        compiler_params=params(16),
        cost_estimate=cost(32 * gather.size, 2 * gather.size),
        name="leaf_and_gather",
    )(*given, *mats, in_vmem(gather))


def sep_rows(level, sums, sep, other, before=None):
    half = sums.shape[1]
    rows = sep.shape[2]
    given = [sums] if before is None else [sums, before]

    def kernel(*refs):
        sums_ref, sep_ref, out = refs[0], refs[-2], refs[-1]

        @pl.when(lax.axis_index("layer") == level)
        def _():
            core = lax.axis_index("front") % 2
            side = 1 - core if other else core
            at = pl.ds(pl.multiple_of(side * half, half), half)
            value = times(sums_ref[...].astype(F32), sep_ref[0, at, :], sep_ref[1, at, :], 0)
            if before is not None:
                value = value + refs[1][...]
            out[...] = value.astype(out.dtype)

    return pl.pallas_call(
        kernel,
        in_specs=[VMEM] * (len(given) + 1),
        out_specs=VMEM,
        out_shape=jax.ShapeDtypeStruct((8, rows), F32 if before is None else BF16),
        compiler_params=params(16),
        cost_estimate=cost(16 * sep.size, sep.size),
        name="sep_rows",
    )(*given, in_vmem(sep))


def spread_cells(level, stored, spread):
    def kernel(stored_ref, spread_ref, out):
        @pl.when(lax.axis_index("layer") == level)
        def _():
            out[...] = times(stored_ref[...].astype(F32), spread_ref[0], spread_ref[1], 0)

    return pl.pallas_call(
        kernel,
        in_specs=[VMEM, VMEM],
        out_specs=VMEM,
        out_shape=jax.ShapeDtypeStruct((8, spread.shape[2]), F32),
        compiler_params=params(16),
        cost_estimate=cost(32 * spread.size, 2 * spread.size),
        name="spread_cells",
    )(stored, in_vmem(spread))


def local(
    right_sides,
    leaf_inverse,
    couple_above,
    couple_below,
    sep_gather,
    sep_inverse,
    sep_spread,
    panel_owner,
):
    depth = lax.axis_size("layer")
    slots = lax.axis_size("front")
    chips = slots // 2
    layer = lax.axis_index("layer")
    place = lax.axis_index("front")
    core = place % 2
    cells = leaf_inverse.shape[2]
    total = sep_gather.shape[2]
    rows = sep_inverse.shape[2]

    def with_partner(block):
        return [block, pair(block)]

    leaf = with_partner(leaf_inverse[0])
    sources = jnp.concatenate(with_partner(right_sides[0].reshape(8, cells)), axis=1)

    gather_keep, gather_give = transpose_gather(sep_gather[0])
    gather = join(gather_keep, pair(gather_give), 1)

    above = with_partner(couple_above[0])
    below = with_partner(couple_below[0])

    slot_ids = jnp.arange(slots, dtype=jnp.int32)
    panel_of = jnp.sum(
        jnp.where(panel_owner[0][None, :] == slot_ids[:, None], slot_ids[None, :], 0), axis=1
    )
    arrive = arrival_order(place // 2, chips)
    keep_panels, give_panels = panel_of[2 * arrive + core], panel_of[2 * arrive + 1 - core]
    if rows % 128 == 0:
        spread_keep, spread_give = transpose_spread(sep_spread[0], keep_panels, give_panels, rows)
    else:
        panels = sep_spread[0].reshape(2, cells, slots, rows)
        spread_keep, spread_give = (
            jnp.swapaxes(jnp.take(panels, which, axis=2).reshape(2, cells, total // 2), 1, 2)
            for which in (keep_panels, give_panels)
        )
    spread = join(spread_keep, pair(spread_give), 2)

    sep = transpose_sep(sep_inverse[0])

    def solve(level, **given):
        leaf_values, sums = leaf_and_gather(level, leaf, gather, **given)
        half_sums = sum_chips(sums).astype(BF16)
        other_sums = pair(half_sums)
        own_rows = sep_rows(level, half_sums, sep, False)
        own_rows = sep_rows(level, other_sums, sep, True, own_rows)
        part = spread_cells(level, gather_chips(own_rows), spread)
        theirs = pair(part)
        part = part + jnp.concatenate([theirs[:, cells:], theirs[:, :cells]], axis=1)
        return leaf_values - part

    def hop(value, source_layer, target_layer):
        route = xor_route("layer", source_layer ^ target_layer)
        return lax.ppermute(value.astype(BF16), "layer", route)

    value = solve(0, sources=sources)
    for level in range(1, depth):
        arrived = hop(value, level - 1, level)
        solved = solve(level, sources=sources, couple=above, arrived=arrived)
        value = jnp.where(layer == level, solved, value)
    for level in range(depth - 2, -1, -1):
        arrived = hop(value, level + 1, level)
        solved = solve(level, couple=below, arrived=arrived)
        value = jnp.where(layer == level, value - solved, value)
    return value[:, :cells].reshape(1, 2, 4, cells)


def solution(mesh):
    return jax.shard_map(
        local,
        mesh=mesh,
        in_specs=(
            P("layer", None, None, "front"),
            P("layer", None, "front", None),
            P("layer", None, "front", None),
            P("layer", None, "front", None),
            P("layer", None, None, "front"),
            P("layer", None, "front", None),
            P("layer", None, "front", None),
            P("layer", None),
        ),
        out_specs=P("layer", None, None, "front"),
        check_vma=False,
    )
```

time: 532 us -> 183 us (0.34); the launches traced: 524 us -> 183 us
  blocking collectives: 298 us -> 0 us
  matrix products: 181 us -> 0 us
  starting transfers between devices: 15.8 us -> 81.6 us
  waiting for transfers between devices: 19.6 us -> 62.9 us
  Pallas kernels: 0 us -> 16.9 us
  local copies, waits for them, and re-layouts: 4.69 us -> 19.8 us
    psum x7 -> x0, blocking collectives: 200 us -> none  [layer_solve(): sep_rounded = lax.psum(partial_sums, 'front').astype(jnp.bfloat16)]
    dot_general x136 -> x0, matrix products: 181 us -> none  [single(): return jnp.dot(right, left.T, preferred_element_type=jnp.float32)]
    all_gather x7 -> x0, blocking collectives: 98 us -> none  [layer_solve(): stored = lax.all_gather(own_rows, 'front', axis=2, tiled=True)]
    ppermute x6 -> x68, starting transfers between devices: 15.8 us -> 81.6 us  [the longest x42 62.7 us: from_chips(): lax.ppermute(block, 'front', xor_route('front', 2 * step))]
    ppermute x6 -> x68, waiting for transfers between devices: 19.6 us -> 62.9 us  [the longest x42 36.3 us: from_chips(): lax.ppermute(block, 'front', xor_route('front', 2 * step))]
    unnamed x26 -> x44, local copies, waits for them, and re-layouts: 0.09 us -> 18.5 us
    pallas_call x0 -> x33, Pallas kernels: none -> 16.9 us  [the longest x1 4.87 us: transpose_sep(): pl.pallas_call(kernel, grid=(total // step,), in_specs=[pl.BlockSpec((2,...]
  transfers between devices with their start and end apart: 6 -> 68, of which waited for: 6 -> 53; matrix products, arithmetic and copies ran while one was open for 0% -> 1% of each run, Pallas kernels for 0% -> 7%
where the time goes in v2:
time: 183 us
  starting transfers between devices  81.6 us (45%)
  waiting for transfers between devices  62.9 us (34%)
  local copies, waits for them, and re-layouts  19.8 us (11%)
  Pallas kernels  16.9 us (9%)
    ppermute x42, starting transfers between devices, from_chips(): lax.ppermute(block, 'front', xor_route('front', 2 * step))  62.7 us
    ppermute x42, waiting for transfers between devices, from_chips(): lax.ppermute(block, 'front', xor_route('front', 2 * step))  36.3 us
    unnamed x44, local copies, waits for them, and re-layouts  18.5 us
    ppermute x6, starting transfers between devices, hop(): return lax.ppermute(value.astype(BF16), 'layer', route)  15.9 us
    ppermute x6, waiting for transfers between devices, hop(): return lax.ppermute(value.astype(BF16), 'layer', route)  14.3 us
    ppermute x20, waiting for transfers between devices, pair(): return lax.ppermute(block, 'front', xor_route('front', 1))  12.3 us
    pallas_call x1, Pallas kernels, transpose_sep(): pl.pallas_call(kernel, grid=(total // step,), in_specs=[pl.BlockSpec((2,...  4.87 us
    pallas_call x14, Pallas kernels, sep_rows(): pl.pallas_call(kernel, in_specs=[VMEM] * (len(given) + 1), out_specs=VMEM...  3.93 us
  transfers between devices with their start and end apart: 68, of which 53 were waited for; matrix products, arithmetic and copies ran while one was open for 1% of the time, Pallas kernels for 7%

profile of v2, /device:TPU:0, one launch (start us, length us, event | category | flops | bytes accessed | tf_op | source)
XLA Modules:
  0.0 182.9 jit_solution(2139554039956301082)
XLA Ops:
  0.0 1.9 %copy-done.11 = bf16[1,2,5120,128]{3,2,1,0:T(8,128)(2,1)S(1)} copy-done((bf16[1,2,5120,128]{3,2,1,0:T(8,128)(2,1)S(1)}, bf16[1,2,5120,128]{3,2,1,0:T(8,128)(2,1)}, u32[]{:S(2)}) %copy-start.11) | copy-done | bytes 2621464
  1.9 1.8 transpose_gather.1
  6.8 2.0 %transpose_spread.1 = (bf16[2,2560,128]{2,1,0:T(8,128)(2,1)S(1)}, bf16[2,2560,128]{2,1,0:T(8,128)(2,1)S(1)}) custom-call(s32[8]{0:T(128)S(1)} %pad_add_fusion.order, bf16[2,128,5120]{2,1,0:T(8,128)(2,1)S(1)} %bitcast.16, bf16[2,128,5120]{2,1,0:T(8,128)(2,1)S(1)} %bitcast.17), custom_call_target="tpu_custom_call" | custom-call | bytes 5242880 | tf_op jit(solution)/shard_map/transpose_spread/pallas_call | solution.py:139
  9.4 2.4 %collective-permute-done = f32[8,128]{1,0:T(8,128)S(1)} collective-permute-done((f32[8,128]{1,0:T(8,128)S(1)}, f32[8,128]{1,0:T(8,128)S(1)}, u32[]{:S(2)}, u32[]{:S(2)}) %collective-permute-start) | collective-permute-done | bytes 4128 | tf_op jit(solution)/shard_map/ppermute | solution.py:19
  13.2 1.5 join.2.refs_3_.refs_6_.refs_5_
  15.3 4.8 %collective-permute-start.5 = (bf16[8,2560]{1,0:T(8,128)(2,1)S(1)}, bf16[8,2560]{1,0:T(8,128)(2,1)S(1)}, u32[]{:S(2)}, u32[]{:S(2)}) collective-permute-start(bf16[8,2560]{1,0:T(8,128)(2,1)S(1)} %get-tuple-element.26), channel_id=1, source_target_pairs={{0,6},{1,7},{2,4},{3,5},{4,2},{5,3},{6,0},{7,1},{8,14},{9,15},{10,... | collective-permute-start | bytes 122888 | tf_op jit(solution)/shard_map/ppermute | solution.py:34
  20.7 1.6 collective-permute-done.5
  22.3 2.7 %collective-permute-done.4 = bf16[8,2560]{1,0:T(8,128)(2,1)S(1)} collective-permute-done((bf16[8,2560]{1,0:T(8,128)(2,1)S(1)}, bf16[8,2560]{1,0:T(8,128)(2,1)S(1)}, u32[]{:S(2)}, u32[]{:S(2)}) %collective-permute-start.4) | collective-permute-done | bytes 40992 | tf_op jit(solution)/shard_map/ppermute | solution.py:34
  25.1 4.9 %transpose_sep.1.refs_1_.refs_2_ = bf16[2,5120,640]{2,1,0:T(8,128)(2,1)S(1)} custom-call(bf16[2,640,5120]{2,1,0:T(8,128)(2,1)S(1)} %bitcast.15), custom_call_target="tpu_custom_call" | custom-call | bytes 26214400 | tf_op jit(solution)/shard_map/transpose_sep/pallas_call | solution.py:91
  31.9 1.9 %collective-permute-start.9 = (bf16[8,640]{1,0:T(8,128)(2,1)S(1)}, bf16[8,640]{1,0:T(8,128)(2,1)S(1)}, u32[]{:S(2)}, u32[]{:S(2)}) collective-permute-start(bf16[8,640]{1,0:T(8,128)(2,1)S(1)} %sep_rows.15), channel_id=1, source_target_pairs={{0,6},{1,7},{2,4},{3,5},{4,2},{5,3},{6,0},{7,1},{8,14},{9,15},{10,... | collective-permute-start | bytes 30728 | tf_op jit(solution)/shard_map/ppermute | solution.py:34
  34.2 2.2 %collective-permute-start.7 = (bf16[8,640]{1,0:T(8,128)(2,1)S(1)}, bf16[8,640]{1,0:T(8,128)(2,1)S(1)}, u32[]{:S(2)}, u32[]{:S(2)}) collective-permute-start(bf16[8,640]{1,0:T(8,128)(2,1)S(1)} %sep_rows.15), channel_id=1, source_target_pairs={{0,2},{1,3},{2,0},{3,1},{4,6},{5,7},{6,4},{7,5},{8,10},{9,11},{10,... | collective-permute-start | bytes 30728 | tf_op jit(solution)/shard_map/ppermute | solution.py:34
  40.3 3.4 %collective-permute-done.12.refs_0_ = bf16[8,256]{1,0:T(8,128)(2,1)S(1)} collective-permute-done((bf16[8,256]{1,0:T(8,128)(2,1)S(1)}, bf16[8,256]{1,0:T(8,128)(2,1)S(1)}, u32[]{:S(2)}, u32[]{:S(2)}) %collective-permute-start.12) | collective-permute-done | bytes 4128 | tf_op jit(solution)/shard_map/ppermute | solution.py:336
  43.7 2.2 %collective-permute-start.16 = (bf16[8,2560]{1,0:T(8,128)(2,1)S(1)}, bf16[8,2560]{1,0:T(8,128)(2,1)S(1)}, u32[]{:S(2)}, u32[]{:S(2)}) collective-permute-start(bf16[8,2560]{1,0:T(8,128)(2,1)S(1)} %get-tuple-element.30), channel_id=1, source_target_pairs={{0,6},{1,7},{2,4},{3,5},{4,2},{5,3},{6,0},{7,1},{8,14},{9,15},{10,... | collective-permute-start | bytes 122888 | tf_op jit(solution)/shard_map/ppermute | solution.py:34
  48.1 1.6 collective-permute-done.16
  52.6 1.6 collective-permute-start.20
  54.9 2.1 %collective-permute-start.18 = (bf16[8,640]{1,0:T(8,128)(2,1)S(1)}, bf16[8,640]{1,0:T(8,128)(2,1)S(1)}, u32[]{:S(2)}, u32[]{:S(2)}) collective-permute-start(bf16[8,640]{1,0:T(8,128)(2,1)S(1)} %sep_rows.17), channel_id=1, source_target_pairs={{0,2},{1,3},{2,0},{3,1},{4,6},{5,7},{6,4},{7,5},{8,10},{9,11},{10,... | collective-permute-start | bytes 30728 | tf_op jit(solution)/shard_map/ppermute | solution.py:34
  60.2 4.5 %collective-permute-done.22.refs_0_ = bf16[8,256]{1,0:T(8,128)(2,1)S(1)} collective-permute-done((bf16[8,256]{1,0:T(8,128)(2,1)S(1)}, bf16[8,256]{1,0:T(8,128)(2,1)S(1)}, u32[]{:S(2)}, u32[]{:S(2)}) %collective-permute-start.22) | collective-permute-done | bytes 4128 | tf_op jit(solution)/shard_map/ppermute | solution.py:336
  64.7 2.1 %collective-permute-start.25 = (bf16[8,2560]{1,0:T(8,128)(2,1)S(1)}, bf16[8,2560]{1,0:T(8,128)(2,1)S(1)}, u32[]{:S(2)}, u32[]{:S(2)}) collective-permute-start(bf16[8,2560]{1,0:T(8,128)(2,1)S(1)} %get-tuple-element.32), channel_id=1, source_target_pairs={{0,6},{1,7},{2,4},{3,5},{4,2},{5,3},{6,0},{7,1},{8,14},{9,15},{10,... | collective-permute-start | bytes 122888 | tf_op jit(solution)/shard_map/ppermute | solution.py:34
  69.1 1.7 collective-permute-done.25
  72.5 4.7 %copy-done.1 = bf16[2,5120,640]{2,1,0:T(8,128)(2,1)S(1)} copy-done((bf16[2,5120,640]{2,1,0:T(8,128)(2,1)S(1)}, bf16[2,5120,640]{2,1,0:T(8,128)(2,1)}, u32[]{:S(2)}) %copy-start.1) | copy-done | bytes 13107224
  77.3 1.5 collective-permute-start.29
  79.4 2.2 %collective-permute-start.27 = (bf16[8,640]{1,0:T(8,128)(2,1)S(1)}, bf16[8,640]{1,0:T(8,128)(2,1)S(1)}, u32[]{:S(2)}, u32[]{:S(2)}) collective-permute-start(bf16[8,640]{1,0:T(8,128)(2,1)S(1)} %sep_rows.19), channel_id=1, source_target_pairs={{0,2},{1,3},{2,0},{3,1},{4,6},{5,7},{6,4},{7,5},{8,10},{9,11},{10,... | collective-permute-start | bytes 30728 | tf_op jit(solution)/shard_map/ppermute | solution.py:34
  84.7 2.2 %collective-permute-start.31 = (bf16[8,256]{1,0:T(8,128)(2,1)S(1)}, bf16[8,256]{1,0:T(8,128)(2,1)S(1)}, u32[]{:S(2)}, u32[]{:S(2)}) collective-permute-start(bf16[8,256]{1,0:T(8,128)(2,1)S(1)} %get-tuple-element.47), channel_id=1, source_target_pairs={{0,8},{8,0},{16,24},{24,16},{1,9},{9,1},{17,25},{25,17},{2,10},{10... | collective-permute-start | bytes 12296 | tf_op jit(solution)/shard_map/ppermute | solution.py:336
  86.9 1.6 collective-permute-done.31.refs_0_
  88.5 2.3 %collective-permute-start.34 = (bf16[8,2560]{1,0:T(8,128)(2,1)S(1)}, bf16[8,2560]{1,0:T(8,128)(2,1)S(1)}, u32[]{:S(2)}, u32[]{:S(2)}) collective-permute-start(bf16[8,2560]{1,0:T(8,128)(2,1)S(1)} %get-tuple-element.34), channel_id=1, source_target_pairs={{0,6},{1,7},{2,4},{3,5},{4,2},{5,3},{6,0},{7,1},{8,14},{9,15},{10,... | collective-permute-start | bytes 122888 | tf_op jit(solution)/shard_map/ppermute | solution.py:34
  92.9 1.5 collective-permute-done.34
  96.3 4.7 %copy-done.2 = bf16[2,5120,640]{2,1,0:T(8,128)(2,1)S(1)} copy-done((bf16[2,5120,640]{2,1,0:T(8,128)(2,1)S(1)}, bf16[2,5120,640]{2,1,0:T(8,128)(2,1)}, u32[]{:S(2)}) %copy-start.2) | copy-done | bytes 13107224
  101.1 1.6 collective-permute-start.38
  103.3 2.2 %collective-permute-start.36 = (bf16[8,640]{1,0:T(8,128)(2,1)S(1)}, bf16[8,640]{1,0:T(8,128)(2,1)S(1)}, u32[]{:S(2)}, u32[]{:S(2)}) collective-permute-start(bf16[8,640]{1,0:T(8,128)(2,1)S(1)} %sep_rows.21), channel_id=1, source_target_pairs={{0,2},{1,3},{2,0},{3,1},{4,6},{5,7},{6,4},{7,5},{8,10},{9,11},{10,... | collective-permute-start | bytes 30728 | tf_op jit(solution)/shard_map/ppermute | solution.py:34
  108.6 2.0 %collective-permute-start.40 = (bf16[8,256]{1,0:T(8,128)(2,1)S(1)}, bf16[8,256]{1,0:T(8,128)(2,1)S(1)}, u32[]{:S(2)}, u32[]{:S(2)}) collective-permute-start(bf16[8,256]{1,0:T(8,128)(2,1)S(1)} %get-tuple-element.45), channel_id=1, source_target_pairs={{0,8},{8,0},{16,24},{24,16},{1,9},{9,1},{17,25},{25,17},{2,10},{10... | collective-permute-start | bytes 12296 | tf_op jit(solution)/shard_map/ppermute | solution.py:336
  110.6 1.6 collective-permute-done.40.refs_0_
  112.3 2.2 %collective-permute-start.44 = (bf16[8,2560]{1,0:T(8,128)(2,1)S(1)}, bf16[8,2560]{1,0:T(8,128)(2,1)S(1)}, u32[]{:S(2)}, u32[]{:S(2)}) collective-permute-start(bf16[8,2560]{1,0:T(8,128)(2,1)S(1)} %get-tuple-element.36), channel_id=1, source_target_pairs={{0,6},{1,7},{2,4},{3,5},{4,2},{5,3},{6,0},{7,1},{8,14},{9,15},{10,... | collective-permute-start | bytes 122888 | tf_op jit(solution)/shard_map/ppermute | solution.py:34
  116.7 1.5 collective-permute-done.44
  120.1 4.7 %copy-done.3 = bf16[2,5120,640]{2,1,0:T(8,128)(2,1)S(1)} copy-done((bf16[2,5120,640]{2,1,0:T(8,128)(2,1)S(1)}, bf16[2,5120,640]{2,1,0:T(8,128)(2,1)}, u32[]{:S(2)}) %copy-start.3) | copy-done | bytes 13107224
  124.9 1.5 collective-permute-start.48
  127.1 2.3 %collective-permute-start.46 = (bf16[8,640]{1,0:T(8,128)(2,1)S(1)}, bf16[8,640]{1,0:T(8,128)(2,1)S(1)}, u32[]{:S(2)}, u32[]{:S(2)}) collective-permute-start(bf16[8,640]{1,0:T(8,128)(2,1)S(1)} %sep_rows.23), channel_id=1, source_target_pairs={{0,2},{1,3},{2,0},{3,1},{4,6},{5,7},{6,4},{7,5},{8,10},{9,11},{10,... | collective-permute-start | bytes 30728 | tf_op jit(solution)/shard_map/ppermute | solution.py:34
  132.4 6.2 %collective-permute-start.50 = (bf16[8,256]{1,0:T(8,128)(2,1)S(1)}, bf16[8,256]{1,0:T(8,128)(2,1)S(1)}, u32[]{:S(2)}, u32[]{:S(2)}) collective-permute-start(bf16[8,256]{1,0:T(8,128)(2,1)S(1)} %get-tuple-element.43), channel_id=1, source_target_pairs={{0,24},{8,16},{16,8},{24,0},{1,25},{9,17},{17,9},{25,1},{2,26},{10... | collective-permute-start | bytes 12296 | tf_op jit(solution)/shard_map/ppermute | solution.py:336
  138.7 1.6 collective-permute-done.50.refs_0_
  140.3 2.3 %collective-permute-start.53 = (bf16[8,2560]{1,0:T(8,128)(2,1)S(1)}, bf16[8,2560]{1,0:T(8,128)(2,1)S(1)}, u32[]{:S(2)}, u32[]{:S(2)}) collective-permute-start(bf16[8,2560]{1,0:T(8,128)(2,1)S(1)} %get-tuple-element.38), channel_id=1, source_target_pairs={{0,6},{1,7},{2,4},{3,5},{4,2},{5,3},{6,0},{7,1},{8,14},{9,15},{10,... | collective-permute-start | bytes 122888 | tf_op jit(solution)/shard_map/ppermute | solution.py:34
  144.7 1.6 collective-permute-done.53
  149.3 1.6 collective-permute-start.57
  151.4 2.3 %collective-permute-start.55 = (bf16[8,640]{1,0:T(8,128)(2,1)S(1)}, bf16[8,640]{1,0:T(8,128)(2,1)S(1)}, u32[]{:S(2)}, u32[]{:S(2)}) collective-permute-start(bf16[8,640]{1,0:T(8,128)(2,1)S(1)} %sep_rows.25), channel_id=1, source_target_pairs={{0,2},{1,3},{2,0},{3,1},{4,6},{5,7},{6,4},{7,5},{8,10},{9,11},{10,... | collective-permute-start | bytes 30728 | tf_op jit(solution)/shard_map/ppermute | solution.py:34
  156.7 5.3 %collective-permute-start.59 = (bf16[8,256]{1,0:T(8,128)(2,1)S(1)}, bf16[8,256]{1,0:T(8,128)(2,1)S(1)}, u32[]{:S(2)}, u32[]{:S(2)}) collective-permute-start(bf16[8,256]{1,0:T(8,128)(2,1)S(1)} %get-tuple-element.41), channel_id=1, source_target_pairs={{0,8},{8,0},{16,24},{24,16},{1,9},{9,1},{17,25},{25,17},{2,10},{10... | collective-permute-start | bytes 12296 | tf_op jit(solution)/shard_map/ppermute | solution.py:336
  162.0 1.6 collective-permute-done.59.refs_0_
  164.4 2.3 %collective-permute-start.62 = (bf16[8,2560]{1,0:T(8,128)(2,1)S(1)}, bf16[8,2560]{1,0:T(8,128)(2,1)S(1)}, u32[]{:S(2)}, u32[]{:S(2)}) collective-permute-start(bf16[8,2560]{1,0:T(8,128)(2,1)S(1)} %get-tuple-element.40), channel_id=1, source_target_pairs={{0,6},{1,7},{2,4},{3,5},{4,2},{5,3},{6,0},{7,1},{8,14},{9,15},{10,... | collective-permute-start | bytes 122888 | tf_op jit(solution)/shard_map/ppermute | solution.py:34
  170.2 1.5 collective-permute-done.61
  174.4 1.6 collective-permute-start.66
  176.6 2.3 %collective-permute-start.64 = (bf16[8,640]{1,0:T(8,128)(2,1)S(1)}, bf16[8,640]{1,0:T(8,128)(2,1)S(1)}, u32[]{:S(2)}, u32[]{:S(2)}) collective-permute-start(bf16[8,640]{1,0:T(8,128)(2,1)S(1)} %sep_rows.27), channel_id=1, source_target_pairs={{0,2},{1,3},{2,0},{3,1},{4,6},{5,7},{6,4},{7,5},{8,10},{9,11},{10,... | collective-permute-start | bytes 30728 | tf_op jit(solution)/shard_map/ppermute | solution.py:34
  (202 shorter events, 64.9 us)
Async XLA Ops:
  4.8 7.1 %collective-permute-start.2 = (bf16[2,128,2560]{2,1,0:T(8,128)(2,1)}, bf16[2,128,2560]{2,1,0:T(8,128)(2,1)}, u32[]{:S(2)}, u32[]{:S(2)}) collective-permute-start(bf16[2,128,2560]{2,1,0:T(8,128)(2,1)} %get-tuple-element.24), channel_id=1, source_target_pairs={{0,1},{1,0},{2,3},{3,2},{4,5},{5,4},{6,7},{7,6},{8,9},{9,8},{10,11... | collective-permute-start | bytes 3932168 | tf_op jit(solution)/shard_map/ppermute | solution.py:19
  8.8 27.6 %collective-permute-start.10 = (bf16[2,2560,128]{2,1,0:T(8,128)(2,1)S(1)}, bf16[2,2560,128]{2,1,0:T(8,128)(2,1)S(1)}, u32[]{:S(2)}, u32[]{:S(2)}) collective-permute-start(bf16[2,2560,128]{2,1,0:T(8,128)(2,1)S(1)} %get-tuple-element.28), channel_id=1, source_target_pairs={{0,1},{1,0},{2,3},{3,2},{4,5},{5,4},{6,7},{7,6},{8,9},{9,8},{10,11... | collective-permute-start | bytes 3932168 | tf_op jit(solution)/shard_map/ppermute | solution.py:19
  9.4 5.3 %collective-permute-start.1 = (bf16[2,128,128]{2,1,0:T(8,128)(2,1)S(1)}, bf16[2,128,128]{2,1,0:T(8,128)(2,1)S(1)}, u32[]{:S(2)}, u32[]{:S(2)}) collective-permute-start(bf16[2,128,128]{2,1,0:T(8,128)(2,1)S(1)} %bitcast.18), channel_id=1, source_target_pairs={{0,1},{1,0},{2,3},{3,2},{4,5},{5,4},{6,7},{7,6},{8,9},{9,8},{10,11... | collective-permute-start | bytes 196616 | tf_op jit(solution)/shard_map/ppermute | solution.py:19
  15.3 7.0 %collective-permute-start.5 = (bf16[8,2560]{1,0:T(8,128)(2,1)S(1)}, bf16[8,2560]{1,0:T(8,128)(2,1)S(1)}, u32[]{:S(2)}, u32[]{:S(2)}) collective-permute-start(bf16[8,2560]{1,0:T(8,128)(2,1)S(1)} %get-tuple-element.26), channel_id=1, source_target_pairs={{0,6},{1,7},{2,4},{3,5},{4,2},{5,3},{6,0},{7,1},{8,14},{9,15},{10,... | collective-permute-start | bytes 122888 | tf_op jit(solution)/shard_map/ppermute | solution.py:34
  20.1 4.9 %collective-permute-start.4 = (bf16[8,2560]{1,0:T(8,128)(2,1)S(1)}, bf16[8,2560]{1,0:T(8,128)(2,1)S(1)}, u32[]{:S(2)}, u32[]{:S(2)}) collective-permute-start(bf16[8,2560]{1,0:T(8,128)(2,1)S(1)} %get-tuple-element.26), channel_id=1, source_target_pairs={{0,4},{1,5},{2,6},{3,7},{4,0},{5,1},{6,2},{7,3},{8,12},{9,13},{10,... | collective-permute-start | bytes 122888 | tf_op jit(solution)/shard_map/ppermute | solution.py:34
  20.1 4.9 %collective-permute-start.3 = (bf16[8,2560]{1,0:T(8,128)(2,1)S(1)}, bf16[8,2560]{1,0:T(8,128)(2,1)S(1)}, u32[]{:S(2)}, u32[]{:S(2)}) collective-permute-start(bf16[8,2560]{1,0:T(8,128)(2,1)S(1)} %get-tuple-element.26), channel_id=1, source_target_pairs={{0,2},{1,3},{2,0},{3,1},{4,6},{5,7},{6,4},{7,5},{8,10},{9,11},{10,... | collective-permute-start | bytes 122888 | tf_op jit(solution)/shard_map/ppermute | solution.py:34
  25.0 5.9 %collective-permute-start.6 = (bf16[8,2560]{1,0:T(8,128)(2,1)S(1)}, bf16[8,2560]{1,0:T(8,128)(2,1)S(1)}, u32[]{:S(2)}, u32[]{:S(2)}) collective-permute-start(bf16[8,2560]{1,0:T(8,128)(2,1)S(1)} %add_convert_fusion.6.refs_0_), channel_id=1, source_target_pairs={{0,1},{1,0},{2,3},{3,2},{4,5},{5,4},{6,7},{7,6},{8,9},{9,8},{10,11... | collective-permute-start | bytes 122888 | tf_op jit(solution)/shard_map/ppermute | solution.py:19
  31.9 5.5 %collective-permute-start.9 = (bf16[8,640]{1,0:T(8,128)(2,1)S(1)}, bf16[8,640]{1,0:T(8,128)(2,1)S(1)}, u32[]{:S(2)}, u32[]{:S(2)}) collective-permute-start(bf16[8,640]{1,0:T(8,128)(2,1)S(1)} %sep_rows.15), channel_id=1, source_target_pairs={{0,6},{1,7},{2,4},{3,5},{4,2},{5,3},{6,0},{7,1},{8,14},{9,15},{10,... | collective-permute-start | bytes 30728 | tf_op jit(solution)/shard_map/ppermute | solution.py:34
  33.8 4.6 %collective-permute-start.8 = (bf16[8,640]{1,0:T(8,128)(2,1)S(1)}, bf16[8,640]{1,0:T(8,128)(2,1)S(1)}, u32[]{:S(2)}, u32[]{:S(2)}) collective-permute-start(bf16[8,640]{1,0:T(8,128)(2,1)S(1)} %sep_rows.15), channel_id=1, source_target_pairs={{0,4},{1,5},{2,6},{3,7},{4,0},{5,1},{6,2},{7,3},{8,12},{9,13},{10,... | collective-permute-start | bytes 30728 | tf_op jit(solution)/shard_map/ppermute | solution.py:34
  34.2 4.2 %collective-permute-start.7 = (bf16[8,640]{1,0:T(8,128)(2,1)S(1)}, bf16[8,640]{1,0:T(8,128)(2,1)S(1)}, u32[]{:S(2)}, u32[]{:S(2)}) collective-permute-start(bf16[8,640]{1,0:T(8,128)(2,1)S(1)} %sep_rows.15), channel_id=1, source_target_pairs={{0,2},{1,3},{2,0},{3,1},{4,6},{5,7},{6,4},{7,5},{8,10},{9,11},{10,... | collective-permute-start | bytes 30728 | tf_op jit(solution)/shard_map/ppermute | solution.py:34
  43.7 6.0 %collective-permute-start.16 = (bf16[8,2560]{1,0:T(8,128)(2,1)S(1)}, bf16[8,2560]{1,0:T(8,128)(2,1)S(1)}, u32[]{:S(2)}, u32[]{:S(2)}) collective-permute-start(bf16[8,2560]{1,0:T(8,128)(2,1)S(1)} %get-tuple-element.30), channel_id=1, source_target_pairs={{0,6},{1,7},{2,4},{3,5},{4,2},{5,3},{6,0},{7,1},{8,14},{9,15},{10,... | collective-permute-start | bytes 122888 | tf_op jit(solution)/shard_map/ppermute | solution.py:34
  45.9 5.3 %collective-permute-start.15 = (bf16[8,2560]{1,0:T(8,128)(2,1)S(1)}, bf16[8,2560]{1,0:T(8,128)(2,1)S(1)}, u32[]{:S(2)}, u32[]{:S(2)}) collective-permute-start(bf16[8,2560]{1,0:T(8,128)(2,1)S(1)} %get-tuple-element.30), channel_id=1, source_target_pairs={{0,4},{1,5},{2,6},{3,7},{4,0},{5,1},{6,2},{7,3},{8,12},{9,13},{10,... | collective-permute-start | bytes 122888 | tf_op jit(solution)/shard_map/ppermute | solution.py:34
  46.8 4.4 %collective-permute-start.14 = (bf16[8,2560]{1,0:T(8,128)(2,1)S(1)}, bf16[8,2560]{1,0:T(8,128)(2,1)S(1)}, u32[]{:S(2)}, u32[]{:S(2)}) collective-permute-start(bf16[8,2560]{1,0:T(8,128)(2,1)S(1)} %get-tuple-element.30), channel_id=1, source_target_pairs={{0,2},{1,3},{2,0},{3,1},{4,6},{5,7},{6,4},{7,5},{8,10},{9,11},{10,... | collective-permute-start | bytes 122888 | tf_op jit(solution)/shard_map/ppermute | solution.py:34
  52.6 5.5 %collective-permute-start.20 = (bf16[8,640]{1,0:T(8,128)(2,1)S(1)}, bf16[8,640]{1,0:T(8,128)(2,1)S(1)}, u32[]{:S(2)}, u32[]{:S(2)}) collective-permute-start(bf16[8,640]{1,0:T(8,128)(2,1)S(1)} %sep_rows.17), channel_id=1, source_target_pairs={{0,6},{1,7},{2,4},{3,5},{4,2},{5,3},{6,0},{7,1},{8,14},{9,15},{10,... | collective-permute-start | bytes 30728 | tf_op jit(solution)/shard_map/ppermute | solution.py:34
  54.2 4.6 %collective-permute-start.19 = (bf16[8,640]{1,0:T(8,128)(2,1)S(1)}, bf16[8,640]{1,0:T(8,128)(2,1)S(1)}, u32[]{:S(2)}, u32[]{:S(2)}) collective-permute-start(bf16[8,640]{1,0:T(8,128)(2,1)S(1)} %sep_rows.17), channel_id=1, source_target_pairs={{0,4},{1,5},{2,6},{3,7},{4,0},{5,1},{6,2},{7,3},{8,12},{9,13},{10,... | collective-permute-start | bytes 30728 | tf_op jit(solution)/shard_map/ppermute | solution.py:34
  60.2 4.6 %collective-permute-start.22 = (bf16[8,256]{1,0:T(8,128)(2,1)S(1)}, bf16[8,256]{1,0:T(8,128)(2,1)S(1)}, u32[]{:S(2)}, u32[]{:S(2)}) collective-permute-start(bf16[8,256]{1,0:T(8,128)(2,1)S(1)} %get-tuple-element.49), channel_id=1, source_target_pairs={{0,24},{8,16},{16,8},{24,0},{1,25},{9,17},{17,9},{25,1},{2,26},{10... | collective-permute-start | bytes 12296 | tf_op jit(solution)/shard_map/ppermute | solution.py:336
  64.7 6.1 %collective-permute-start.25 = (bf16[8,2560]{1,0:T(8,128)(2,1)S(1)}, bf16[8,2560]{1,0:T(8,128)(2,1)S(1)}, u32[]{:S(2)}, u32[]{:S(2)}) collective-permute-start(bf16[8,2560]{1,0:T(8,128)(2,1)S(1)} %get-tuple-element.32), channel_id=1, source_target_pairs={{0,6},{1,7},{2,4},{3,5},{4,2},{5,3},{6,0},{7,1},{8,14},{9,15},{10,... | collective-permute-start | bytes 122888 | tf_op jit(solution)/shard_map/ppermute | solution.py:34
  66.9 5.3 %collective-permute-start.24 = (bf16[8,2560]{1,0:T(8,128)(2,1)S(1)}, bf16[8,2560]{1,0:T(8,128)(2,1)S(1)}, u32[]{:S(2)}, u32[]{:S(2)}) collective-permute-start(bf16[8,2560]{1,0:T(8,128)(2,1)S(1)} %get-tuple-element.32), channel_id=1, source_target_pairs={{0,4},{1,5},{2,6},{3,7},{4,0},{5,1},{6,2},{7,3},{8,12},{9,13},{10,... | collective-permute-start | bytes 122888 | tf_op jit(solution)/shard_map/ppermute | solution.py:34
  68.0 4.4 %collective-permute-start.23 = (bf16[8,2560]{1,0:T(8,128)(2,1)S(1)}, bf16[8,2560]{1,0:T(8,128)(2,1)S(1)}, u32[]{:S(2)}, u32[]{:S(2)}) collective-permute-start(bf16[8,2560]{1,0:T(8,128)(2,1)S(1)} %get-tuple-element.32), channel_id=1, source_target_pairs={{0,2},{1,3},{2,0},{3,1},{4,6},{5,7},{6,4},{7,5},{8,10},{9,11},{10,... | collective-permute-start | bytes 122888 | tf_op jit(solution)/shard_map/ppermute | solution.py:34
  72.5 4.8 %collective-permute-start.26 = (bf16[8,2560]{1,0:T(8,128)(2,1)S(1)}, bf16[8,2560]{1,0:T(8,128)(2,1)S(1)}, u32[]{:S(2)}, u32[]{:S(2)}) collective-permute-start(bf16[8,2560]{1,0:T(8,128)(2,1)S(1)} %add_convert_fusion.4.refs_0_), channel_id=1, source_target_pairs={{0,1},{1,0},{2,3},{3,2},{4,5},{5,4},{6,7},{7,6},{8,9},{9,8},{10,11... | collective-permute-start | bytes 122888 | tf_op jit(solution)/shard_map/ppermute | solution.py:19
  77.3 5.5 %collective-permute-start.29 = (bf16[8,640]{1,0:T(8,128)(2,1)S(1)}, bf16[8,640]{1,0:T(8,128)(2,1)S(1)}, u32[]{:S(2)}, u32[]{:S(2)}) collective-permute-start(bf16[8,640]{1,0:T(8,128)(2,1)S(1)} %sep_rows.19), channel_id=1, source_target_pairs={{0,6},{1,7},{2,4},{3,5},{4,2},{5,3},{6,0},{7,1},{8,14},{9,15},{10,... | collective-permute-start | bytes 30728 | tf_op jit(solution)/shard_map/ppermute | solution.py:34
  78.7 4.6 %collective-permute-start.28 = (bf16[8,640]{1,0:T(8,128)(2,1)S(1)}, bf16[8,640]{1,0:T(8,128)(2,1)S(1)}, u32[]{:S(2)}, u32[]{:S(2)}) collective-permute-start(bf16[8,640]{1,0:T(8,128)(2,1)S(1)} %sep_rows.19), channel_id=1, source_target_pairs={{0,4},{1,5},{2,6},{3,7},{4,0},{5,1},{6,2},{7,3},{8,12},{9,13},{10,... | collective-permute-start | bytes 30728 | tf_op jit(solution)/shard_map/ppermute | solution.py:34
  88.5 5.9 %collective-permute-start.34 = (bf16[8,2560]{1,0:T(8,128)(2,1)S(1)}, bf16[8,2560]{1,0:T(8,128)(2,1)S(1)}, u32[]{:S(2)}, u32[]{:S(2)}) collective-permute-start(bf16[8,2560]{1,0:T(8,128)(2,1)S(1)} %get-tuple-element.34), channel_id=1, source_target_pairs={{0,6},{1,7},{2,4},{3,5},{4,2},{5,3},{6,0},{7,1},{8,14},{9,15},{10,... | collective-permute-start | bytes 122888 | tf_op jit(solution)/shard_map/ppermute | solution.py:34
  90.8 5.0 %collective-permute-start.33 = (bf16[8,2560]{1,0:T(8,128)(2,1)S(1)}, bf16[8,2560]{1,0:T(8,128)(2,1)S(1)}, u32[]{:S(2)}, u32[]{:S(2)}) collective-permute-start(bf16[8,2560]{1,0:T(8,128)(2,1)S(1)} %get-tuple-element.34), channel_id=1, source_target_pairs={{0,4},{1,5},{2,6},{3,7},{4,0},{5,1},{6,2},{7,3},{8,12},{9,13},{10,... | collective-permute-start | bytes 122888 | tf_op jit(solution)/shard_map/ppermute | solution.py:34
  91.9 4.3 %collective-permute-start.32 = (bf16[8,2560]{1,0:T(8,128)(2,1)S(1)}, bf16[8,2560]{1,0:T(8,128)(2,1)S(1)}, u32[]{:S(2)}, u32[]{:S(2)}) collective-permute-start(bf16[8,2560]{1,0:T(8,128)(2,1)S(1)} %get-tuple-element.34), channel_id=1, source_target_pairs={{0,2},{1,3},{2,0},{3,1},{4,6},{5,7},{6,4},{7,5},{8,10},{9,11},{10,... | collective-permute-start | bytes 122888 | tf_op jit(solution)/shard_map/ppermute | solution.py:34
  96.2 4.8 %collective-permute-start.35 = (bf16[8,2560]{1,0:T(8,128)(2,1)S(1)}, bf16[8,2560]{1,0:T(8,128)(2,1)S(1)}, u32[]{:S(2)}, u32[]{:S(2)}) collective-permute-start(bf16[8,2560]{1,0:T(8,128)(2,1)S(1)} %add_convert_fusion.3.refs_0_), channel_id=1, source_target_pairs={{0,1},{1,0},{2,3},{3,2},{4,5},{5,4},{6,7},{7,6},{8,9},{9,8},{10,11... | collective-permute-start | bytes 122888 | tf_op jit(solution)/shard_map/ppermute | solution.py:19
  101.1 5.6 %collective-permute-start.38 = (bf16[8,640]{1,0:T(8,128)(2,1)S(1)}, bf16[8,640]{1,0:T(8,128)(2,1)S(1)}, u32[]{:S(2)}, u32[]{:S(2)}) collective-permute-start(bf16[8,640]{1,0:T(8,128)(2,1)S(1)} %sep_rows.21), channel_id=1, source_target_pairs={{0,6},{1,7},{2,4},{3,5},{4,2},{5,3},{6,0},{7,1},{8,14},{9,15},{10,... | collective-permute-start | bytes 30728 | tf_op jit(solution)/shard_map/ppermute | solution.py:34
  102.7 4.6 %collective-permute-start.37 = (bf16[8,640]{1,0:T(8,128)(2,1)S(1)}, bf16[8,640]{1,0:T(8,128)(2,1)S(1)}, u32[]{:S(2)}, u32[]{:S(2)}) collective-permute-start(bf16[8,640]{1,0:T(8,128)(2,1)S(1)} %sep_rows.21), channel_id=1, source_target_pairs={{0,4},{1,5},{2,6},{3,7},{4,0},{5,1},{6,2},{7,3},{8,12},{9,13},{10,... | collective-permute-start | bytes 30728 | tf_op jit(solution)/shard_map/ppermute | solution.py:34
  112.3 5.9 %collective-permute-start.44 = (bf16[8,2560]{1,0:T(8,128)(2,1)S(1)}, bf16[8,2560]{1,0:T(8,128)(2,1)S(1)}, u32[]{:S(2)}, u32[]{:S(2)}) collective-permute-start(bf16[8,2560]{1,0:T(8,128)(2,1)S(1)} %get-tuple-element.36), channel_id=1, source_target_pairs={{0,6},{1,7},{2,4},{3,5},{4,2},{5,3},{6,0},{7,1},{8,14},{9,15},{10,... | collective-permute-start | bytes 122888 | tf_op jit(solution)/shard_map/ppermute | solution.py:34
  114.5 5.1 %collective-permute-start.43 = (bf16[8,2560]{1,0:T(8,128)(2,1)S(1)}, bf16[8,2560]{1,0:T(8,128)(2,1)S(1)}, u32[]{:S(2)}, u32[]{:S(2)}) collective-permute-start(bf16[8,2560]{1,0:T(8,128)(2,1)S(1)} %get-tuple-element.36), channel_id=1, source_target_pairs={{0,4},{1,5},{2,6},{3,7},{4,0},{5,1},{6,2},{7,3},{8,12},{9,13},{10,... | collective-permute-start | bytes 122888 | tf_op jit(solution)/shard_map/ppermute | solution.py:34
  115.6 4.4 %collective-permute-start.42 = (bf16[8,2560]{1,0:T(8,128)(2,1)S(1)}, bf16[8,2560]{1,0:T(8,128)(2,1)S(1)}, u32[]{:S(2)}, u32[]{:S(2)}) collective-permute-start(bf16[8,2560]{1,0:T(8,128)(2,1)S(1)} %get-tuple-element.36), channel_id=1, source_target_pairs={{0,2},{1,3},{2,0},{3,1},{4,6},{5,7},{6,4},{7,5},{8,10},{9,11},{10,... | collective-permute-start | bytes 122888 | tf_op jit(solution)/shard_map/ppermute | solution.py:34
  120.1 4.8 %collective-permute-start.45 = (bf16[8,2560]{1,0:T(8,128)(2,1)S(1)}, bf16[8,2560]{1,0:T(8,128)(2,1)S(1)}, u32[]{:S(2)}, u32[]{:S(2)}) collective-permute-start(bf16[8,2560]{1,0:T(8,128)(2,1)S(1)} %add_convert_fusion.2.refs_0_), channel_id=1, source_target_pairs={{0,1},{1,0},{2,3},{3,2},{4,5},{5,4},{6,7},{7,6},{8,9},{9,8},{10,11... | collective-permute-start | bytes 122888 | tf_op jit(solution)/shard_map/ppermute | solution.py:19
  124.9 5.6 %collective-permute-start.48 = (bf16[8,640]{1,0:T(8,128)(2,1)S(1)}, bf16[8,640]{1,0:T(8,128)(2,1)S(1)}, u32[]{:S(2)}, u32[]{:S(2)}) collective-permute-start(bf16[8,640]{1,0:T(8,128)(2,1)S(1)} %sep_rows.23), channel_id=1, source_target_pairs={{0,6},{1,7},{2,4},{3,5},{4,2},{5,3},{6,0},{7,1},{8,14},{9,15},{10,... | collective-permute-start | bytes 30728 | tf_op jit(solution)/shard_map/ppermute | solution.py:34
  126.5 4.7 %collective-permute-start.47 = (bf16[8,640]{1,0:T(8,128)(2,1)S(1)}, bf16[8,640]{1,0:T(8,128)(2,1)S(1)}, u32[]{:S(2)}, u32[]{:S(2)}) collective-permute-start(bf16[8,640]{1,0:T(8,128)(2,1)S(1)} %sep_rows.23), channel_id=1, source_target_pairs={{0,4},{1,5},{2,6},{3,7},{4,0},{5,1},{6,2},{7,3},{8,12},{9,13},{10,... | collective-permute-start | bytes 30728 | tf_op jit(solution)/shard_map/ppermute | solution.py:34
  127.1 4.1 %collective-permute-start.46 = (bf16[8,640]{1,0:T(8,128)(2,1)S(1)}, bf16[8,640]{1,0:T(8,128)(2,1)S(1)}, u32[]{:S(2)}, u32[]{:S(2)}) collective-permute-start(bf16[8,640]{1,0:T(8,128)(2,1)S(1)} %sep_rows.23), channel_id=1, source_target_pairs={{0,2},{1,3},{2,0},{3,1},{4,6},{5,7},{6,4},{7,5},{8,10},{9,11},{10,... | collective-permute-start | bytes 30728 | tf_op jit(solution)/shard_map/ppermute | solution.py:34
  132.4 7.8 %collective-permute-start.50 = (bf16[8,256]{1,0:T(8,128)(2,1)S(1)}, bf16[8,256]{1,0:T(8,128)(2,1)S(1)}, u32[]{:S(2)}, u32[]{:S(2)}) collective-permute-start(bf16[8,256]{1,0:T(8,128)(2,1)S(1)} %get-tuple-element.43), channel_id=1, source_target_pairs={{0,24},{8,16},{16,8},{24,0},{1,25},{9,17},{17,9},{25,1},{2,26},{10... | collective-permute-start | bytes 12296 | tf_op jit(solution)/shard_map/ppermute | solution.py:336
  140.3 6.0 %collective-permute-start.53 = (bf16[8,2560]{1,0:T(8,128)(2,1)S(1)}, bf16[8,2560]{1,0:T(8,128)(2,1)S(1)}, u32[]{:S(2)}, u32[]{:S(2)}) collective-permute-start(bf16[8,2560]{1,0:T(8,128)(2,1)S(1)} %get-tuple-element.38), channel_id=1, source_target_pairs={{0,6},{1,7},{2,4},{3,5},{4,2},{5,3},{6,0},{7,1},{8,14},{9,15},{10,... | collective-permute-start | bytes 122888 | tf_op jit(solution)/shard_map/ppermute | solution.py:34
  142.5 5.0 %collective-permute-start.52 = (bf16[8,2560]{1,0:T(8,128)(2,1)S(1)}, bf16[8,2560]{1,0:T(8,128)(2,1)S(1)}, u32[]{:S(2)}, u32[]{:S(2)}) collective-permute-start(bf16[8,2560]{1,0:T(8,128)(2,1)S(1)} %get-tuple-element.38), channel_id=1, source_target_pairs={{0,4},{1,5},{2,6},{3,7},{4,0},{5,1},{6,2},{7,3},{8,12},{9,13},{10,... | collective-permute-start | bytes 122888 | tf_op jit(solution)/shard_map/ppermute | solution.py:34
  143.7 4.3 %collective-permute-start.51 = (bf16[8,2560]{1,0:T(8,128)(2,1)S(1)}, bf16[8,2560]{1,0:T(8,128)(2,1)S(1)}, u32[]{:S(2)}, u32[]{:S(2)}) collective-permute-start(bf16[8,2560]{1,0:T(8,128)(2,1)S(1)} %get-tuple-element.38), channel_id=1, source_target_pairs={{0,2},{1,3},{2,0},{3,1},{4,6},{5,7},{6,4},{7,5},{8,10},{9,11},{10,... | collective-permute-start | bytes 122888 | tf_op jit(solution)/shard_map/ppermute | solution.py:34
  149.3 5.5 %collective-permute-start.57 = (bf16[8,640]{1,0:T(8,128)(2,1)S(1)}, bf16[8,640]{1,0:T(8,128)(2,1)S(1)}, u32[]{:S(2)}, u32[]{:S(2)}) collective-permute-start(bf16[8,640]{1,0:T(8,128)(2,1)S(1)} %sep_rows.25), channel_id=1, source_target_pairs={{0,6},{1,7},{2,4},{3,5},{4,2},{5,3},{6,0},{7,1},{8,14},{9,15},{10,... | collective-permute-start | bytes 30728 | tf_op jit(solution)/shard_map/ppermute | solution.py:34
  150.9 4.6 %collective-permute-start.56 = (bf16[8,640]{1,0:T(8,128)(2,1)S(1)}, bf16[8,640]{1,0:T(8,128)(2,1)S(1)}, u32[]{:S(2)}, u32[]{:S(2)}) collective-permute-start(bf16[8,640]{1,0:T(8,128)(2,1)S(1)} %sep_rows.25), channel_id=1, source_target_pairs={{0,4},{1,5},{2,6},{3,7},{4,0},{5,1},{6,2},{7,3},{8,12},{9,13},{10,... | collective-permute-start | bytes 30728 | tf_op jit(solution)/shard_map/ppermute | solution.py:34
  156.7 6.9 %collective-permute-start.59 = (bf16[8,256]{1,0:T(8,128)(2,1)S(1)}, bf16[8,256]{1,0:T(8,128)(2,1)S(1)}, u32[]{:S(2)}, u32[]{:S(2)}) collective-permute-start(bf16[8,256]{1,0:T(8,128)(2,1)S(1)} %get-tuple-element.41), channel_id=1, source_target_pairs={{0,8},{8,0},{16,24},{24,16},{1,9},{9,1},{17,25},{25,17},{2,10},{10... | collective-permute-start | bytes 12296 | tf_op jit(solution)/shard_map/ppermute | solution.py:336
  164.4 5.8 %collective-permute-start.62 = (bf16[8,2560]{1,0:T(8,128)(2,1)S(1)}, bf16[8,2560]{1,0:T(8,128)(2,1)S(1)}, u32[]{:S(2)}, u32[]{:S(2)}) collective-permute-start(bf16[8,2560]{1,0:T(8,128)(2,1)S(1)} %get-tuple-element.40), channel_id=1, source_target_pairs={{0,6},{1,7},{2,4},{3,5},{4,2},{5,3},{6,0},{7,1},{8,14},{9,15},{10,... | collective-permute-start | bytes 122888 | tf_op jit(solution)/shard_map/ppermute | solution.py:34
  166.6 5.1 %collective-permute-start.61 = (bf16[8,2560]{1,0:T(8,128)(2,1)S(1)}, bf16[8,2560]{1,0:T(8,128)(2,1)S(1)}, u32[]{:S(2)}, u32[]{:S(2)}) collective-permute-start(bf16[8,2560]{1,0:T(8,128)(2,1)S(1)} %get-tuple-element.40), channel_id=1, source_target_pairs={{0,4},{1,5},{2,6},{3,7},{4,0},{5,1},{6,2},{7,3},{8,12},{9,13},{10,... | collective-permute-start | bytes 122888 | tf_op jit(solution)/shard_map/ppermute | solution.py:34
  167.7 4.4 %collective-permute-start.60 = (bf16[8,2560]{1,0:T(8,128)(2,1)S(1)}, bf16[8,2560]{1,0:T(8,128)(2,1)S(1)}, u32[]{:S(2)}, u32[]{:S(2)}) collective-permute-start(bf16[8,2560]{1,0:T(8,128)(2,1)S(1)} %get-tuple-element.40), channel_id=1, source_target_pairs={{0,2},{1,3},{2,0},{3,1},{4,6},{5,7},{6,4},{7,5},{8,10},{9,11},{10,... | collective-permute-start | bytes 122888 | tf_op jit(solution)/shard_map/ppermute | solution.py:34
  174.4 5.5 %collective-permute-start.66 = (bf16[8,640]{1,0:T(8,128)(2,1)S(1)}, bf16[8,640]{1,0:T(8,128)(2,1)S(1)}, u32[]{:S(2)}, u32[]{:S(2)}) collective-permute-start(bf16[8,640]{1,0:T(8,128)(2,1)S(1)} %sep_rows.27), channel_id=1, source_target_pairs={{0,6},{1,7},{2,4},{3,5},{4,2},{5,3},{6,0},{7,1},{8,14},{9,15},{10,... | collective-permute-start | bytes 30728 | tf_op jit(solution)/shard_map/ppermute | solution.py:34
  176.0 4.6 %collective-permute-start.65 = (bf16[8,640]{1,0:T(8,128)(2,1)S(1)}, bf16[8,640]{1,0:T(8,128)(2,1)S(1)}, u32[]{:S(2)}, u32[]{:S(2)}) collective-permute-start(bf16[8,640]{1,0:T(8,128)(2,1)S(1)} %sep_rows.27), channel_id=1, source_target_pairs={{0,4},{1,5},{2,6},{3,7},{4,0},{5,1},{6,2},{7,3},{8,12},{9,13},{10,... | collective-permute-start | bytes 30728 | tf_op jit(solution)/shard_map/ppermute | solution.py:34
  176.6 4.0 %collective-permute-start.64 = (bf16[8,640]{1,0:T(8,128)(2,1)S(1)}, bf16[8,640]{1,0:T(8,128)(2,1)S(1)}, u32[]{:S(2)}, u32[]{:S(2)}) collective-permute-start(bf16[8,640]{1,0:T(8,128)(2,1)S(1)} %sep_rows.27), channel_id=1, source_target_pairs={{0,2},{1,3},{2,0},{3,1},{4,6},{5,7},{6,4},{7,5},{8,10},{9,11},{10,... | collective-permute-start | bytes 30728 | tf_op jit(solution)/shard_map/ppermute | solution.py:34
  (42 other events, 265.0 us)

commit v3 on v2

--- a/solution.py
+++ b/solution.py
@@ -268,6 +268,45 @@
         cost_estimate=cost(32 * spread.size, 2 * spread.size),
         name="spread_cells",
     )(stored, in_vmem(spread))
+
+
+def finish(level, leaf_values, part, theirs, before=None, subtract=False):
+    cells = part.shape[1] // 2
+    given = [leaf_values, part, theirs] + ([] if before is None else [before])
+
+    def kernel(*refs):
+        leaf_ref, part_ref, theirs_ref = refs[:3]
+        value_out, sent_out = refs[-2:]
+        here = lax.axis_index("layer") == level
+
+        @pl.when(here)
+        def _():
+            swapped = jnp.concatenate([theirs_ref[:, cells:], theirs_ref[:, :cells]], axis=1)
+            solved = leaf_ref[...] - (part_ref[...] + swapped)
+            if subtract:
+                solved = refs[3][...] - solved
+            value_out[...] = solved
+            sent_out[...] = solved.astype(BF16)
+
+        if before is not None:
+
+            @pl.when(jnp.logical_not(here))
+            def _():
+                value_out[...] = refs[3][...]
+                sent_out[...] = refs[3][...].astype(BF16)
+
+    return pl.pallas_call(
+        kernel,
+        in_specs=[VMEM] * len(given),
+        out_specs=[VMEM, VMEM],
+        out_shape=[
+            jax.ShapeDtypeStruct(part.shape, F32),
+            jax.ShapeDtypeStruct(part.shape, BF16),
+        ],
+        compiler_params=params(16),
+        cost_estimate=cost(4 * part.size, 16 * part.size),
+        name="finish",
+    )(*given)
 
 
 def local(
@@ -283,7 +322,6 @@
     depth = lax.axis_size("layer")
     slots = lax.axis_size("front")
     chips = slots // 2
-    layer = lax.axis_index("layer")
     place = lax.axis_index("front")
     core = place % 2
     cells = leaf_inverse.shape[2]
@@ -320,30 +358,25 @@
 
     sep = transpose_sep(sep_inverse[0])
 
-    def solve(level, **given):
+    def solve(level, before=None, subtract=False, **given):
         leaf_values, sums = leaf_and_gather(level, leaf, gather, **given)
         half_sums = sum_chips(sums).astype(BF16)
         other_sums = pair(half_sums)
         own_rows = sep_rows(level, half_sums, sep, False)
         own_rows = sep_rows(level, other_sums, sep, True, own_rows)
         part = spread_cells(level, gather_chips(own_rows), spread)
-        theirs = pair(part)
-        part = part + jnp.concatenate([theirs[:, cells:], theirs[:, :cells]], axis=1)
-        return leaf_values - part
-
-    def hop(value, source_layer, target_layer):
-        route = xor_route("layer", source_layer ^ target_layer)
-        return lax.ppermute(value.astype(BF16), "layer", route)
-
-    value = solve(0, sources=sources)
+        return finish(level, leaf_values, part, pair(part), before, subtract)
+
+    def hop(sent, source_layer, target_layer):
+        return lax.ppermute(sent, "layer", xor_route("layer", source_layer ^ target_layer))
+
+    value, sent = solve(0, sources=sources)
     for level in range(1, depth):
-        arrived = hop(value, level - 1, level)
-        solved = solve(level, sources=sources, couple=above, arrived=arrived)
-        value = jnp.where(layer == level, solved, value)
+        arrived = hop(sent, level - 1, level)
+        value, sent = solve(level, value, sources=sources, couple=above, arrived=arrived)
     for level in range(depth - 2, -1, -1):
-        arrived = hop(value, level + 1, level)
-        solved = solve(level, couple=below, arrived=arrived)
-        value = jnp.where(layer == level, value - solved, value)
+        arrived = hop(sent, level + 1, level)
+        value, sent = solve(level, value, True, couple=below, arrived=arrived)
     return value[:, :cells].reshape(1, 2, 4, cells)
 
 

time: 183 us -> 170 us (0.929)
  local copies, waits for them, and re-layouts: 19.8 us -> 6.16 us
  waiting for transfers between devices: 62.9 us -> 67.4 us
  starting transfers between devices: 81.6 us -> 77.4 us
    unnamed x44 -> x20, local copies, waits for them, and re-layouts: 18.5 us -> 4.29 us
    ppermute x20, waiting for transfers between devices: 12.3 us -> 16.7 us  [pair(): return lax.ppermute(block, 'front', xor_route('front', 1))]
    ppermute x6, starting transfers between devices: 15.9 us -> 12.9 us  [hop(): lax.ppermute(sent, 'layer', xor_route('layer', source_layer ^ target_layer))]
  transfers between devices with their start and end apart: 68 -> 68, of which waited for: 53 -> 54; matrix products, arithmetic and copies ran while one was open for 1% -> 1% of each run, Pallas kernels for 7% -> 8%
where the time goes in v3:
time: 170 us; the launch traced here: 169 us
  starting transfers between devices  77.4 us (46%)
  waiting for transfers between devices  67.4 us (40%)
  Pallas kernels  17.5 us (10%)
  local copies, waits for them, and re-layouts  6.16 us (4%)
    ppermute x42, starting transfers between devices, from_chips(): lax.ppermute(block, 'front', xor_route('front', 2 * step))  62.6 us
    ppermute x42, waiting for transfers between devices, from_chips(): lax.ppermute(block, 'front', xor_route('front', 2 * step))  36.2 us
    ppermute x20, waiting for transfers between devices, pair(): return lax.ppermute(block, 'front', xor_route('front', 1))  16.7 us
    ppermute x6, waiting for transfers between devices, hop(): lax.ppermute(sent, 'layer', xor_route('layer', source_layer ^ target_layer))  14.5 us
    ppermute x6, starting transfers between devices, hop(): lax.ppermute(sent, 'layer', xor_route('layer', source_layer ^ target_layer))  12.9 us
    pallas_call x1, Pallas kernels, transpose_sep(): pl.pallas_call(kernel, grid=(total // step,), in_specs=[pl.BlockSpec((2,...  4.87 us
    unnamed x20, local copies, waits for them, and re-layouts  4.29 us
    pallas_call x14, Pallas kernels, sep_rows(): pl.pallas_call(kernel, in_specs=[VMEM] * (len(given) + 1), out_specs=VMEM...  3.97 us
  transfers between devices with their start and end apart: 68, of which 54 were waited for; matrix products, arithmetic and copies ran while one was open for 1% of the time, Pallas kernels for 8%

profile of v3, /device:TPU:0, one launch (start us, length us, event | category | flops | bytes accessed | tf_op | source)
XLA Modules:
  0.0 169.4 jit_solution(8793028989126708807)
XLA Ops:
  0.0 1.9 %copy-done.3 = bf16[1,2,5120,128]{3,2,1,0:T(8,128)(2,1)S(1)} copy-done((bf16[1,2,5120,128]{3,2,1,0:T(8,128)(2,1)S(1)}, bf16[1,2,5120,128]{3,2,1,0:T(8,128)(2,1)}, u32[]{:S(2)}) %copy-start.3) | copy-done | bytes 2621464
  1.9 1.8 %transpose_gather.1 = (bf16[2,128,2560]{2,1,0:T(8,128)(2,1)S(1)}, bf16[2,128,2560]{2,1,0:T(8,128)(2,1)}) custom-call(bf16[2,5120,128]{2,1,0:T(8,128)(2,1)S(1)} %bitcast.24), custom_call_target="tpu_custom_call" | custom-call | bytes 5242880 | tf_op jit(solution)/shard_map/transpose_gather/pallas_call | solution.py:117
  6.7 2.0 %transpose_spread.1 = (bf16[2,2560,128]{2,1,0:T(8,128)(2,1)S(1)}, bf16[2,2560,128]{2,1,0:T(8,128)(2,1)S(1)}) custom-call(s32[8]{0:T(128)S(1)} %pad_add_fusion.order, bf16[2,128,5120]{2,1,0:T(8,128)(2,1)S(1)} %bitcast.14, bf16[2,128,5120]{2,1,0:T(8,128)(2,1)S(1)} %bitcast.15), custom_call_target="tpu_custom_call" | custom-call | bytes 5242880 | tf_op jit(solution)/shard_map/transpose_spread/pallas_call | solution.py:139
  9.4 2.4 %collective-permute-done = f32[8,128]{1,0:T(8,128)S(1)} collective-permute-done((f32[8,128]{1,0:T(8,128)S(1)}, f32[8,128]{1,0:T(8,128)S(1)}, u32[]{:S(2)}, u32[]{:S(2)}) %collective-permute-start) | collective-permute-done | bytes 4128 | tf_op jit(solution)/shard_map/ppermute | solution.py:19
  13.2 1.5 join.2.refs_3_.refs_6_.refs_5_
  15.3 4.8 %collective-permute-start.5 = (bf16[8,2560]{1,0:T(8,128)(2,1)S(1)}, bf16[8,2560]{1,0:T(8,128)(2,1)S(1)}, u32[]{:S(2)}, u32[]{:S(2)}) collective-permute-start(bf16[8,2560]{1,0:T(8,128)(2,1)S(1)} %get-tuple-element.39), channel_id=1, source_target_pairs={{0,6},{1,7},{2,4},{3,5},{4,2},{5,3},{6,0},{7,1},{8,14},{9,15},{10,... | collective-permute-start | bytes 122888 | tf_op jit(solution)/shard_map/ppermute | solution.py:34
  20.7 1.6 collective-permute-done.5
  22.2 2.7 %collective-permute-done.4 = bf16[8,2560]{1,0:T(8,128)(2,1)S(1)} collective-permute-done((bf16[8,2560]{1,0:T(8,128)(2,1)S(1)}, bf16[8,2560]{1,0:T(8,128)(2,1)S(1)}, u32[]{:S(2)}, u32[]{:S(2)}) %collective-permute-start.4) | collective-permute-done | bytes 40992 | tf_op jit(solution)/shard_map/ppermute | solution.py:34
  25.1 4.9 %transpose_sep.1.refs_1_.refs_2_ = bf16[2,5120,640]{2,1,0:T(8,128)(2,1)S(1)} custom-call(bf16[2,640,5120]{2,1,0:T(8,128)(2,1)S(1)} %bitcast.13), custom_call_target="tpu_custom_call" | custom-call | bytes 26214400 | tf_op jit(solution)/shard_map/transpose_sep/pallas_call | solution.py:91
  31.9 1.9 %collective-permute-start.9 = (bf16[8,640]{1,0:T(8,128)(2,1)S(1)}, bf16[8,640]{1,0:T(8,128)(2,1)S(1)}, u32[]{:S(2)}, u32[]{:S(2)}) collective-permute-start(bf16[8,640]{1,0:T(8,128)(2,1)S(1)} %sep_rows.15), channel_id=1, source_target_pairs={{0,6},{1,7},{2,4},{3,5},{4,2},{5,3},{6,0},{7,1},{8,14},{9,15},{10,... | collective-permute-start | bytes 30728 | tf_op jit(solution)/shard_map/ppermute | solution.py:34
  34.2 2.2 %collective-permute-start.7 = (bf16[8,640]{1,0:T(8,128)(2,1)S(1)}, bf16[8,640]{1,0:T(8,128)(2,1)S(1)}, u32[]{:S(2)}, u32[]{:S(2)}) collective-permute-start(bf16[8,640]{1,0:T(8,128)(2,1)S(1)} %sep_rows.15), channel_id=1, source_target_pairs={{0,2},{1,3},{2,0},{3,1},{4,6},{5,7},{6,4},{7,5},{8,10},{9,11},{10,... | collective-permute-start | bytes 30728 | tf_op jit(solution)/shard_map/ppermute | solution.py:34
  40.0 3.6 %collective-permute-done.12.refs_0_ = bf16[8,256]{1,0:T(8,128)(2,1)S(1)} collective-permute-done((bf16[8,256]{1,0:T(8,128)(2,1)S(1)}, bf16[8,256]{1,0:T(8,128)(2,1)S(1)}, u32[]{:S(2)}, u32[]{:S(2)}) %collective-permute-start.12) | collective-permute-done | bytes 4128 | tf_op jit(solution)/shard_map/ppermute | solution.py:371
  43.6 2.2 %collective-permute-start.16 = (bf16[8,2560]{1,0:T(8,128)(2,1)S(1)}, bf16[8,2560]{1,0:T(8,128)(2,1)S(1)}, u32[]{:S(2)}, u32[]{:S(2)}) collective-permute-start(bf16[8,2560]{1,0:T(8,128)(2,1)S(1)} %get-tuple-element.44), channel_id=1, source_target_pairs={{0,6},{1,7},{2,4},{3,5},{4,2},{5,3},{6,0},{7,1},{8,14},{9,15},{10,... | collective-permute-start | bytes 122888 | tf_op jit(solution)/shard_map/ppermute | solution.py:34
  48.0 1.6 collective-permute-done.16
  49.6 1.5 collective-permute-done.15
  52.5 1.6 collective-permute-start.20
  54.8 2.1 %collective-permute-start.18 = (bf16[8,640]{1,0:T(8,128)(2,1)S(1)}, bf16[8,640]{1,0:T(8,128)(2,1)S(1)}, u32[]{:S(2)}, u32[]{:S(2)}) collective-permute-start(bf16[8,640]{1,0:T(8,128)(2,1)S(1)} %sep_rows.17), channel_id=1, source_target_pairs={{0,2},{1,3},{2,0},{3,1},{4,6},{5,7},{6,4},{7,5},{8,10},{9,11},{10,... | collective-permute-start | bytes 30728 | tf_op jit(solution)/shard_map/ppermute | solution.py:34
  60.0 4.5 %collective-permute-done.22.refs_0_ = bf16[8,256]{1,0:T(8,128)(2,1)S(1)} collective-permute-done((bf16[8,256]{1,0:T(8,128)(2,1)S(1)}, bf16[8,256]{1,0:T(8,128)(2,1)S(1)}, u32[]{:S(2)}, u32[]{:S(2)}) %collective-permute-start.22) | collective-permute-done | bytes 4128 | tf_op jit(solution)/shard_map/ppermute | solution.py:371
  64.5 2.1 %collective-permute-start.25 = (bf16[8,2560]{1,0:T(8,128)(2,1)S(1)}, bf16[8,2560]{1,0:T(8,128)(2,1)S(1)}, u32[]{:S(2)}, u32[]{:S(2)}) collective-permute-start(bf16[8,2560]{1,0:T(8,128)(2,1)S(1)} %get-tuple-element.48), channel_id=1, source_target_pairs={{0,6},{1,7},{2,4},{3,5},{4,2},{5,3},{6,0},{7,1},{8,14},{9,15},{10,... | collective-permute-start | bytes 122888 | tf_op jit(solution)/shard_map/ppermute | solution.py:34
  68.9 1.7 collective-permute-done.25
  73.5 1.6 collective-permute-start.29
  75.7 2.1 %collective-permute-start.27 = (bf16[8,640]{1,0:T(8,128)(2,1)S(1)}, bf16[8,640]{1,0:T(8,128)(2,1)S(1)}, u32[]{:S(2)}, u32[]{:S(2)}) collective-permute-start(bf16[8,640]{1,0:T(8,128)(2,1)S(1)} %sep_rows.19), channel_id=1, source_target_pairs={{0,2},{1,3},{2,0},{3,1},{4,6},{5,7},{6,4},{7,5},{8,10},{9,11},{10,... | collective-permute-start | bytes 30728 | tf_op jit(solution)/shard_map/ppermute | solution.py:34
  80.9 2.2 %collective-permute-start.31 = (bf16[8,256]{1,0:T(8,128)(2,1)S(1)}, bf16[8,256]{1,0:T(8,128)(2,1)S(1)}, u32[]{:S(2)}, u32[]{:S(2)}) collective-permute-start(bf16[8,256]{1,0:T(8,128)(2,1)S(1)} %get-tuple-element.50), channel_id=1, source_target_pairs={{0,8},{8,0},{16,24},{24,16},{1,9},{9,1},{17,25},{25,17},{2,10},{10... | collective-permute-start | bytes 12296 | tf_op jit(solution)/shard_map/ppermute | solution.py:371
  83.1 1.6 collective-permute-done.31.refs_0_
  84.7 2.2 %collective-permute-start.34 = (bf16[8,2560]{1,0:T(8,128)(2,1)S(1)}, bf16[8,2560]{1,0:T(8,128)(2,1)S(1)}, u32[]{:S(2)}, u32[]{:S(2)}) collective-permute-start(bf16[8,2560]{1,0:T(8,128)(2,1)S(1)} %get-tuple-element.52), channel_id=1, source_target_pairs={{0,6},{1,7},{2,4},{3,5},{4,2},{5,3},{6,0},{7,1},{8,14},{9,15},{10,... | collective-permute-start | bytes 122888 | tf_op jit(solution)/shard_map/ppermute | solution.py:34
  89.1 1.5 collective-permute-done.34
  93.7 1.6 collective-permute-start.38
  95.9 2.2 %collective-permute-start.36 = (bf16[8,640]{1,0:T(8,128)(2,1)S(1)}, bf16[8,640]{1,0:T(8,128)(2,1)S(1)}, u32[]{:S(2)}, u32[]{:S(2)}) collective-permute-start(bf16[8,640]{1,0:T(8,128)(2,1)S(1)} %sep_rows.21), channel_id=1, source_target_pairs={{0,2},{1,3},{2,0},{3,1},{4,6},{5,7},{6,4},{7,5},{8,10},{9,11},{10,... | collective-permute-start | bytes 30728 | tf_op jit(solution)/shard_map/ppermute | solution.py:34
  101.2 1.9 %collective-permute-start.40 = (bf16[8,256]{1,0:T(8,128)(2,1)S(1)}, bf16[8,256]{1,0:T(8,128)(2,1)S(1)}, u32[]{:S(2)}, u32[]{:S(2)}) collective-permute-start(bf16[8,256]{1,0:T(8,128)(2,1)S(1)} %get-tuple-element.54), channel_id=1, source_target_pairs={{0,8},{8,0},{16,24},{24,16},{1,9},{9,1},{17,25},{25,17},{2,10},{10... | collective-permute-start | bytes 12296 | tf_op jit(solution)/shard_map/ppermute | solution.py:371
  103.1 1.7 collective-permute-done.40.refs_0_
  104.8 2.2 %collective-permute-start.44 = (bf16[8,2560]{1,0:T(8,128)(2,1)S(1)}, bf16[8,2560]{1,0:T(8,128)(2,1)S(1)}, u32[]{:S(2)}, u32[]{:S(2)}) collective-permute-start(bf16[8,2560]{1,0:T(8,128)(2,1)S(1)} %get-tuple-element.56), channel_id=1, source_target_pairs={{0,6},{1,7},{2,4},{3,5},{4,2},{5,3},{6,0},{7,1},{8,14},{9,15},{10,... | collective-permute-start | bytes 122888 | tf_op jit(solution)/shard_map/ppermute | solution.py:34
  109.2 1.5 collective-permute-done.44
  113.8 1.5 collective-permute-start.48
  115.9 2.2 %collective-permute-start.46 = (bf16[8,640]{1,0:T(8,128)(2,1)S(1)}, bf16[8,640]{1,0:T(8,128)(2,1)S(1)}, u32[]{:S(2)}, u32[]{:S(2)}) collective-permute-start(bf16[8,640]{1,0:T(8,128)(2,1)S(1)} %sep_rows.23), channel_id=1, source_target_pairs={{0,2},{1,3},{2,0},{3,1},{4,6},{5,7},{6,4},{7,5},{8,10},{9,11},{10,... | collective-permute-start | bytes 30728 | tf_op jit(solution)/shard_map/ppermute | solution.py:34
  121.2 4.3 %collective-permute-start.50 = (bf16[8,256]{1,0:T(8,128)(2,1)S(1)}, bf16[8,256]{1,0:T(8,128)(2,1)S(1)}, u32[]{:S(2)}, u32[]{:S(2)}) collective-permute-start(bf16[8,256]{1,0:T(8,128)(2,1)S(1)} %get-tuple-element.58), channel_id=1, source_target_pairs={{0,24},{8,16},{16,8},{24,0},{1,25},{9,17},{17,9},{25,1},{2,26},{10... | collective-permute-start | bytes 12296 | tf_op jit(solution)/shard_map/ppermute | solution.py:371
  125.6 1.6 collective-permute-done.50.refs_0_
  127.1 2.3 %collective-permute-start.53 = (bf16[8,2560]{1,0:T(8,128)(2,1)S(1)}, bf16[8,2560]{1,0:T(8,128)(2,1)S(1)}, u32[]{:S(2)}, u32[]{:S(2)}) collective-permute-start(bf16[8,2560]{1,0:T(8,128)(2,1)S(1)} %get-tuple-element.60), channel_id=1, source_target_pairs={{0,6},{1,7},{2,4},{3,5},{4,2},{5,3},{6,0},{7,1},{8,14},{9,15},{10,... | collective-permute-start | bytes 122888 | tf_op jit(solution)/shard_map/ppermute | solution.py:34
  131.5 1.5 collective-permute-done.53
  133.0 1.4 collective-permute-done.52
  136.2 1.5 collective-permute-start.57
  138.3 2.3 %collective-permute-start.55 = (bf16[8,640]{1,0:T(8,128)(2,1)S(1)}, bf16[8,640]{1,0:T(8,128)(2,1)S(1)}, u32[]{:S(2)}, u32[]{:S(2)}) collective-permute-start(bf16[8,640]{1,0:T(8,128)(2,1)S(1)} %sep_rows.25), channel_id=1, source_target_pairs={{0,2},{1,3},{2,0},{3,1},{4,6},{5,7},{6,4},{7,5},{8,10},{9,11},{10,... | collective-permute-start | bytes 30728 | tf_op jit(solution)/shard_map/ppermute | solution.py:34
  143.6 4.3 %collective-permute-start.59 = (bf16[8,256]{1,0:T(8,128)(2,1)S(1)}, bf16[8,256]{1,0:T(8,128)(2,1)S(1)}, u32[]{:S(2)}, u32[]{:S(2)}) collective-permute-start(bf16[8,256]{1,0:T(8,128)(2,1)S(1)} %get-tuple-element.62), channel_id=1, source_target_pairs={{0,8},{8,0},{16,24},{24,16},{1,9},{9,1},{17,25},{25,17},{2,10},{10... | collective-permute-start | bytes 12296 | tf_op jit(solution)/shard_map/ppermute | solution.py:371
  148.0 1.6 collective-permute-done.59.refs_0_
  150.3 2.3 %collective-permute-start.62 = (bf16[8,2560]{1,0:T(8,128)(2,1)S(1)}, bf16[8,2560]{1,0:T(8,128)(2,1)S(1)}, u32[]{:S(2)}, u32[]{:S(2)}) collective-permute-start(bf16[8,2560]{1,0:T(8,128)(2,1)S(1)} %get-tuple-element.64), channel_id=1, source_target_pairs={{0,6},{1,7},{2,4},{3,5},{4,2},{5,3},{6,0},{7,1},{8,14},{9,15},{10,... | collective-permute-start | bytes 122888 | tf_op jit(solution)/shard_map/ppermute | solution.py:34
  154.7 1.4 collective-permute-done.62
  156.1 1.5 collective-permute-done.61
  160.3 1.6 collective-permute-start.66
  162.5 2.3 %collective-permute-start.64 = (bf16[8,640]{1,0:T(8,128)(2,1)S(1)}, bf16[8,640]{1,0:T(8,128)(2,1)S(1)}, u32[]{:S(2)}, u32[]{:S(2)}) collective-permute-start(bf16[8,640]{1,0:T(8,128)(2,1)S(1)} %sep_rows.27), channel_id=1, source_target_pairs={{0,2},{1,3},{2,0},{3,1},{4,6},{5,7},{6,4},{7,5},{8,10},{9,11},{10,... | collective-permute-start | bytes 30728 | tf_op jit(solution)/shard_map/ppermute | solution.py:34
  (171 shorter events, 64.4 us)
Async XLA Ops:
  4.7 7.1 %collective-permute-start.2 = (bf16[2,128,2560]{2,1,0:T(8,128)(2,1)}, bf16[2,128,2560]{2,1,0:T(8,128)(2,1)}, u32[]{:S(2)}, u32[]{:S(2)}) collective-permute-start(bf16[2,128,2560]{2,1,0:T(8,128)(2,1)} %get-tuple-element.37), channel_id=1, source_target_pairs={{0,1},{1,0},{2,3},{3,2},{4,5},{5,4},{6,7},{7,6},{8,9},{9,8},{10,11... | collective-permute-start | bytes 3932168 | tf_op jit(solution)/shard_map/ppermute | solution.py:19
  8.7 27.6 %collective-permute-start.10 = (bf16[2,2560,128]{2,1,0:T(8,128)(2,1)S(1)}, bf16[2,2560,128]{2,1,0:T(8,128)(2,1)S(1)}, u32[]{:S(2)}, u32[]{:S(2)}) collective-permute-start(bf16[2,2560,128]{2,1,0:T(8,128)(2,1)S(1)} %get-tuple-element.41), channel_id=1, source_target_pairs={{0,1},{1,0},{2,3},{3,2},{4,5},{5,4},{6,7},{7,6},{8,9},{9,8},{10,11... | collective-permute-start | bytes 3932168 | tf_op jit(solution)/shard_map/ppermute | solution.py:19
  9.3 5.3 %collective-permute-start.1 = (bf16[2,128,128]{2,1,0:T(8,128)(2,1)S(1)}, bf16[2,128,128]{2,1,0:T(8,128)(2,1)S(1)}, u32[]{:S(2)}, u32[]{:S(2)}) collective-permute-start(bf16[2,128,128]{2,1,0:T(8,128)(2,1)S(1)} %bitcast.16), channel_id=1, source_target_pairs={{0,1},{1,0},{2,3},{3,2},{4,5},{5,4},{6,7},{7,6},{8,9},{9,8},{10,11... | collective-permute-start | bytes 196616 | tf_op jit(solution)/shard_map/ppermute | solution.py:19
  15.3 7.0 %collective-permute-start.5 = (bf16[8,2560]{1,0:T(8,128)(2,1)S(1)}, bf16[8,2560]{1,0:T(8,128)(2,1)S(1)}, u32[]{:S(2)}, u32[]{:S(2)}) collective-permute-start(bf16[8,2560]{1,0:T(8,128)(2,1)S(1)} %get-tuple-element.39), channel_id=1, source_target_pairs={{0,6},{1,7},{2,4},{3,5},{4,2},{5,3},{6,0},{7,1},{8,14},{9,15},{10,... | collective-permute-start | bytes 122888 | tf_op jit(solution)/shard_map/ppermute | solution.py:34
  20.0 4.9 %collective-permute-start.4 = (bf16[8,2560]{1,0:T(8,128)(2,1)S(1)}, bf16[8,2560]{1,0:T(8,128)(2,1)S(1)}, u32[]{:S(2)}, u32[]{:S(2)}) collective-permute-start(bf16[8,2560]{1,0:T(8,128)(2,1)S(1)} %get-tuple-element.39), channel_id=1, source_target_pairs={{0,4},{1,5},{2,6},{3,7},{4,0},{5,1},{6,2},{7,3},{8,12},{9,13},{10,... | collective-permute-start | bytes 122888 | tf_op jit(solution)/shard_map/ppermute | solution.py:34
  20.0 4.9 %collective-permute-start.3 = (bf16[8,2560]{1,0:T(8,128)(2,1)S(1)}, bf16[8,2560]{1,0:T(8,128)(2,1)S(1)}, u32[]{:S(2)}, u32[]{:S(2)}) collective-permute-start(bf16[8,2560]{1,0:T(8,128)(2,1)S(1)} %get-tuple-element.39), channel_id=1, source_target_pairs={{0,2},{1,3},{2,0},{3,1},{4,6},{5,7},{6,4},{7,5},{8,10},{9,11},{10,... | collective-permute-start | bytes 122888 | tf_op jit(solution)/shard_map/ppermute | solution.py:34
  25.0 5.9 %collective-permute-start.6 = (bf16[8,2560]{1,0:T(8,128)(2,1)S(1)}, bf16[8,2560]{1,0:T(8,128)(2,1)S(1)}, u32[]{:S(2)}, u32[]{:S(2)}) collective-permute-start(bf16[8,2560]{1,0:T(8,128)(2,1)S(1)} %add_convert_fusion.6.refs_0_), channel_id=1, source_target_pairs={{0,1},{1,0},{2,3},{3,2},{4,5},{5,4},{6,7},{7,6},{8,9},{9,8},{10,11... | collective-permute-start | bytes 122888 | tf_op jit(solution)/shard_map/ppermute | solution.py:19
  31.9 5.5 %collective-permute-start.9 = (bf16[8,640]{1,0:T(8,128)(2,1)S(1)}, bf16[8,640]{1,0:T(8,128)(2,1)S(1)}, u32[]{:S(2)}, u32[]{:S(2)}) collective-permute-start(bf16[8,640]{1,0:T(8,128)(2,1)S(1)} %sep_rows.15), channel_id=1, source_target_pairs={{0,6},{1,7},{2,4},{3,5},{4,2},{5,3},{6,0},{7,1},{8,14},{9,15},{10,... | collective-permute-start | bytes 30728 | tf_op jit(solution)/shard_map/ppermute | solution.py:34
  33.8 4.6 %collective-permute-start.8 = (bf16[8,640]{1,0:T(8,128)(2,1)S(1)}, bf16[8,640]{1,0:T(8,128)(2,1)S(1)}, u32[]{:S(2)}, u32[]{:S(2)}) collective-permute-start(bf16[8,640]{1,0:T(8,128)(2,1)S(1)} %sep_rows.15), channel_id=1, source_target_pairs={{0,4},{1,5},{2,6},{3,7},{4,0},{5,1},{6,2},{7,3},{8,12},{9,13},{10,... | collective-permute-start | bytes 30728 | tf_op jit(solution)/shard_map/ppermute | solution.py:34
  34.2 4.2 %collective-permute-start.7 = (bf16[8,640]{1,0:T(8,128)(2,1)S(1)}, bf16[8,640]{1,0:T(8,128)(2,1)S(1)}, u32[]{:S(2)}, u32[]{:S(2)}) collective-permute-start(bf16[8,640]{1,0:T(8,128)(2,1)S(1)} %sep_rows.15), channel_id=1, source_target_pairs={{0,2},{1,3},{2,0},{3,1},{4,6},{5,7},{6,4},{7,5},{8,10},{9,11},{10,... | collective-permute-start | bytes 30728 | tf_op jit(solution)/shard_map/ppermute | solution.py:34
  43.6 6.0 %collective-permute-start.16 = (bf16[8,2560]{1,0:T(8,128)(2,1)S(1)}, bf16[8,2560]{1,0:T(8,128)(2,1)S(1)}, u32[]{:S(2)}, u32[]{:S(2)}) collective-permute-start(bf16[8,2560]{1,0:T(8,128)(2,1)S(1)} %get-tuple-element.44), channel_id=1, source_target_pairs={{0,6},{1,7},{2,4},{3,5},{4,2},{5,3},{6,0},{7,1},{8,14},{9,15},{10,... | collective-permute-start | bytes 122888 | tf_op jit(solution)/shard_map/ppermute | solution.py:34
  45.8 5.3 %collective-permute-start.15 = (bf16[8,2560]{1,0:T(8,128)(2,1)S(1)}, bf16[8,2560]{1,0:T(8,128)(2,1)S(1)}, u32[]{:S(2)}, u32[]{:S(2)}) collective-permute-start(bf16[8,2560]{1,0:T(8,128)(2,1)S(1)} %get-tuple-element.44), channel_id=1, source_target_pairs={{0,4},{1,5},{2,6},{3,7},{4,0},{5,1},{6,2},{7,3},{8,12},{9,13},{10,... | collective-permute-start | bytes 122888 | tf_op jit(solution)/shard_map/ppermute | solution.py:34
  46.7 4.4 %collective-permute-start.14 = (bf16[8,2560]{1,0:T(8,128)(2,1)S(1)}, bf16[8,2560]{1,0:T(8,128)(2,1)S(1)}, u32[]{:S(2)}, u32[]{:S(2)}) collective-permute-start(bf16[8,2560]{1,0:T(8,128)(2,1)S(1)} %get-tuple-element.44), channel_id=1, source_target_pairs={{0,2},{1,3},{2,0},{3,1},{4,6},{5,7},{6,4},{7,5},{8,10},{9,11},{10,... | collective-permute-start | bytes 122888 | tf_op jit(solution)/shard_map/ppermute | solution.py:34
  52.5 5.5 %collective-permute-start.20 = (bf16[8,640]{1,0:T(8,128)(2,1)S(1)}, bf16[8,640]{1,0:T(8,128)(2,1)S(1)}, u32[]{:S(2)}, u32[]{:S(2)}) collective-permute-start(bf16[8,640]{1,0:T(8,128)(2,1)S(1)} %sep_rows.17), channel_id=1, source_target_pairs={{0,6},{1,7},{2,4},{3,5},{4,2},{5,3},{6,0},{7,1},{8,14},{9,15},{10,... | collective-permute-start | bytes 30728 | tf_op jit(solution)/shard_map/ppermute | solution.py:34
  54.1 4.6 %collective-permute-start.19 = (bf16[8,640]{1,0:T(8,128)(2,1)S(1)}, bf16[8,640]{1,0:T(8,128)(2,1)S(1)}, u32[]{:S(2)}, u32[]{:S(2)}) collective-permute-start(bf16[8,640]{1,0:T(8,128)(2,1)S(1)} %sep_rows.17), channel_id=1, source_target_pairs={{0,4},{1,5},{2,6},{3,7},{4,0},{5,1},{6,2},{7,3},{8,12},{9,13},{10,... | collective-permute-start | bytes 30728 | tf_op jit(solution)/shard_map/ppermute | solution.py:34
  60.0 4.5 %collective-permute-start.22 = (bf16[8,256]{1,0:T(8,128)(2,1)S(1)}, bf16[8,256]{1,0:T(8,128)(2,1)S(1)}, u32[]{:S(2)}, u32[]{:S(2)}) collective-permute-start(bf16[8,256]{1,0:T(8,128)(2,1)S(1)} %get-tuple-element.46), channel_id=1, source_target_pairs={{0,24},{8,16},{16,8},{24,0},{1,25},{9,17},{17,9},{25,1},{2,26},{10... | collective-permute-start | bytes 12296 | tf_op jit(solution)/shard_map/ppermute | solution.py:371
  64.5 6.1 %collective-permute-start.25 = (bf16[8,2560]{1,0:T(8,128)(2,1)S(1)}, bf16[8,2560]{1,0:T(8,128)(2,1)S(1)}, u32[]{:S(2)}, u32[]{:S(2)}) collective-permute-start(bf16[8,2560]{1,0:T(8,128)(2,1)S(1)} %get-tuple-element.48), channel_id=1, source_target_pairs={{0,6},{1,7},{2,4},{3,5},{4,2},{5,3},{6,0},{7,1},{8,14},{9,15},{10,... | collective-permute-start | bytes 122888 | tf_op jit(solution)/shard_map/ppermute | solution.py:34
  66.7 5.2 %collective-permute-start.24 = (bf16[8,2560]{1,0:T(8,128)(2,1)S(1)}, bf16[8,2560]{1,0:T(8,128)(2,1)S(1)}, u32[]{:S(2)}, u32[]{:S(2)}) collective-permute-start(bf16[8,2560]{1,0:T(8,128)(2,1)S(1)} %get-tuple-element.48), channel_id=1, source_target_pairs={{0,4},{1,5},{2,6},{3,7},{4,0},{5,1},{6,2},{7,3},{8,12},{9,13},{10,... | collective-permute-start | bytes 122888 | tf_op jit(solution)/shard_map/ppermute | solution.py:34
  67.7 4.4 %collective-permute-start.23 = (bf16[8,2560]{1,0:T(8,128)(2,1)S(1)}, bf16[8,2560]{1,0:T(8,128)(2,1)S(1)}, u32[]{:S(2)}, u32[]{:S(2)}) collective-permute-start(bf16[8,2560]{1,0:T(8,128)(2,1)S(1)} %get-tuple-element.48), channel_id=1, source_target_pairs={{0,2},{1,3},{2,0},{3,1},{4,6},{5,7},{6,4},{7,5},{8,10},{9,11},{10,... | collective-permute-start | bytes 122888 | tf_op jit(solution)/shard_map/ppermute | solution.py:34
  73.5 5.5 %collective-permute-start.29 = (bf16[8,640]{1,0:T(8,128)(2,1)S(1)}, bf16[8,640]{1,0:T(8,128)(2,1)S(1)}, u32[]{:S(2)}, u32[]{:S(2)}) collective-permute-start(bf16[8,640]{1,0:T(8,128)(2,1)S(1)} %sep_rows.19), channel_id=1, source_target_pairs={{0,6},{1,7},{2,4},{3,5},{4,2},{5,3},{6,0},{7,1},{8,14},{9,15},{10,... | collective-permute-start | bytes 30728 | tf_op jit(solution)/shard_map/ppermute | solution.py:34
  75.0 4.6 %collective-permute-start.28 = (bf16[8,640]{1,0:T(8,128)(2,1)S(1)}, bf16[8,640]{1,0:T(8,128)(2,1)S(1)}, u32[]{:S(2)}, u32[]{:S(2)}) collective-permute-start(bf16[8,640]{1,0:T(8,128)(2,1)S(1)} %sep_rows.19), channel_id=1, source_target_pairs={{0,4},{1,5},{2,6},{3,7},{4,0},{5,1},{6,2},{7,3},{8,12},{9,13},{10,... | collective-permute-start | bytes 30728 | tf_op jit(solution)/shard_map/ppermute | solution.py:34
  84.7 5.9 %collective-permute-start.34 = (bf16[8,2560]{1,0:T(8,128)(2,1)S(1)}, bf16[8,2560]{1,0:T(8,128)(2,1)S(1)}, u32[]{:S(2)}, u32[]{:S(2)}) collective-permute-start(bf16[8,2560]{1,0:T(8,128)(2,1)S(1)} %get-tuple-element.52), channel_id=1, source_target_pairs={{0,6},{1,7},{2,4},{3,5},{4,2},{5,3},{6,0},{7,1},{8,14},{9,15},{10,... | collective-permute-start | bytes 122888 | tf_op jit(solution)/shard_map/ppermute | solution.py:34
  87.0 5.1 %collective-permute-start.33 = (bf16[8,2560]{1,0:T(8,128)(2,1)S(1)}, bf16[8,2560]{1,0:T(8,128)(2,1)S(1)}, u32[]{:S(2)}, u32[]{:S(2)}) collective-permute-start(bf16[8,2560]{1,0:T(8,128)(2,1)S(1)} %get-tuple-element.52), channel_id=1, source_target_pairs={{0,4},{1,5},{2,6},{3,7},{4,0},{5,1},{6,2},{7,3},{8,12},{9,13},{10,... | collective-permute-start | bytes 122888 | tf_op jit(solution)/shard_map/ppermute | solution.py:34
  88.0 4.4 %collective-permute-start.32 = (bf16[8,2560]{1,0:T(8,128)(2,1)S(1)}, bf16[8,2560]{1,0:T(8,128)(2,1)S(1)}, u32[]{:S(2)}, u32[]{:S(2)}) collective-permute-start(bf16[8,2560]{1,0:T(8,128)(2,1)S(1)} %get-tuple-element.52), channel_id=1, source_target_pairs={{0,2},{1,3},{2,0},{3,1},{4,6},{5,7},{6,4},{7,5},{8,10},{9,11},{10,... | collective-permute-start | bytes 122888 | tf_op jit(solution)/shard_map/ppermute | solution.py:34
  93.7 5.5 %collective-permute-start.38 = (bf16[8,640]{1,0:T(8,128)(2,1)S(1)}, bf16[8,640]{1,0:T(8,128)(2,1)S(1)}, u32[]{:S(2)}, u32[]{:S(2)}) collective-permute-start(bf16[8,640]{1,0:T(8,128)(2,1)S(1)} %sep_rows.21), channel_id=1, source_target_pairs={{0,6},{1,7},{2,4},{3,5},{4,2},{5,3},{6,0},{7,1},{8,14},{9,15},{10,... | collective-permute-start | bytes 30728 | tf_op jit(solution)/shard_map/ppermute | solution.py:34
  95.3 4.6 %collective-permute-start.37 = (bf16[8,640]{1,0:T(8,128)(2,1)S(1)}, bf16[8,640]{1,0:T(8,128)(2,1)S(1)}, u32[]{:S(2)}, u32[]{:S(2)}) collective-permute-start(bf16[8,640]{1,0:T(8,128)(2,1)S(1)} %sep_rows.21), channel_id=1, source_target_pairs={{0,4},{1,5},{2,6},{3,7},{4,0},{5,1},{6,2},{7,3},{8,12},{9,13},{10,... | collective-permute-start | bytes 30728 | tf_op jit(solution)/shard_map/ppermute | solution.py:34
  95.9 4.0 %collective-permute-start.36 = (bf16[8,640]{1,0:T(8,128)(2,1)S(1)}, bf16[8,640]{1,0:T(8,128)(2,1)S(1)}, u32[]{:S(2)}, u32[]{:S(2)}) collective-permute-start(bf16[8,640]{1,0:T(8,128)(2,1)S(1)} %sep_rows.21), channel_id=1, source_target_pairs={{0,2},{1,3},{2,0},{3,1},{4,6},{5,7},{6,4},{7,5},{8,10},{9,11},{10,... | collective-permute-start | bytes 30728 | tf_op jit(solution)/shard_map/ppermute | solution.py:34
  98.1 5.0 %collective-permute-start.41 = (bf16[2,128,128]{2,1,0:T(8,128)(2,1)S(1)}, bf16[2,128,128]{2,1,0:T(8,128)(2,1)S(1)}, u32[]{:S(2)}, u32[]{:S(2)}) collective-permute-start(bf16[2,128,128]{2,1,0:T(8,128)(2,1)S(1)} %bitcast.29), channel_id=1, source_target_pairs={{0,1},{1,0},{2,3},{3,2},{4,5},{5,4},{6,7},{7,6},{8,9},{9,8},{10,11... | collective-permute-start | bytes 196616 | tf_op jit(solution)/shard_map/ppermute | solution.py:19
  104.8 5.9 %collective-permute-start.44 = (bf16[8,2560]{1,0:T(8,128)(2,1)S(1)}, bf16[8,2560]{1,0:T(8,128)(2,1)S(1)}, u32[]{:S(2)}, u32[]{:S(2)}) collective-permute-start(bf16[8,2560]{1,0:T(8,128)(2,1)S(1)} %get-tuple-element.56), channel_id=1, source_target_pairs={{0,6},{1,7},{2,4},{3,5},{4,2},{5,3},{6,0},{7,1},{8,14},{9,15},{10,... | collective-permute-start | bytes 122888 | tf_op jit(solution)/shard_map/ppermute | solution.py:34
  107.0 5.1 %collective-permute-start.43 = (bf16[8,2560]{1,0:T(8,128)(2,1)S(1)}, bf16[8,2560]{1,0:T(8,128)(2,1)S(1)}, u32[]{:S(2)}, u32[]{:S(2)}) collective-permute-start(bf16[8,2560]{1,0:T(8,128)(2,1)S(1)} %get-tuple-element.56), channel_id=1, source_target_pairs={{0,4},{1,5},{2,6},{3,7},{4,0},{5,1},{6,2},{7,3},{8,12},{9,13},{10,... | collective-permute-start | bytes 122888 | tf_op jit(solution)/shard_map/ppermute | solution.py:34
  108.0 4.4 %collective-permute-start.42 = (bf16[8,2560]{1,0:T(8,128)(2,1)S(1)}, bf16[8,2560]{1,0:T(8,128)(2,1)S(1)}, u32[]{:S(2)}, u32[]{:S(2)}) collective-permute-start(bf16[8,2560]{1,0:T(8,128)(2,1)S(1)} %get-tuple-element.56), channel_id=1, source_target_pairs={{0,2},{1,3},{2,0},{3,1},{4,6},{5,7},{6,4},{7,5},{8,10},{9,11},{10,... | collective-permute-start | bytes 122888 | tf_op jit(solution)/shard_map/ppermute | solution.py:34
  113.8 5.5 %collective-permute-start.48 = (bf16[8,640]{1,0:T(8,128)(2,1)S(1)}, bf16[8,640]{1,0:T(8,128)(2,1)S(1)}, u32[]{:S(2)}, u32[]{:S(2)}) collective-permute-start(bf16[8,640]{1,0:T(8,128)(2,1)S(1)} %sep_rows.23), channel_id=1, source_target_pairs={{0,6},{1,7},{2,4},{3,5},{4,2},{5,3},{6,0},{7,1},{8,14},{9,15},{10,... | collective-permute-start | bytes 30728 | tf_op jit(solution)/shard_map/ppermute | solution.py:34
  115.3 4.6 %collective-permute-start.47 = (bf16[8,640]{1,0:T(8,128)(2,1)S(1)}, bf16[8,640]{1,0:T(8,128)(2,1)S(1)}, u32[]{:S(2)}, u32[]{:S(2)}) collective-permute-start(bf16[8,640]{1,0:T(8,128)(2,1)S(1)} %sep_rows.23), channel_id=1, source_target_pairs={{0,4},{1,5},{2,6},{3,7},{4,0},{5,1},{6,2},{7,3},{8,12},{9,13},{10,... | collective-permute-start | bytes 30728 | tf_op jit(solution)/shard_map/ppermute | solution.py:34
  115.9 4.0 %collective-permute-start.46 = (bf16[8,640]{1,0:T(8,128)(2,1)S(1)}, bf16[8,640]{1,0:T(8,128)(2,1)S(1)}, u32[]{:S(2)}, u32[]{:S(2)}) collective-permute-start(bf16[8,640]{1,0:T(8,128)(2,1)S(1)} %sep_rows.23), channel_id=1, source_target_pairs={{0,2},{1,3},{2,0},{3,1},{4,6},{5,7},{6,4},{7,5},{8,10},{9,11},{10,... | collective-permute-start | bytes 30728 | tf_op jit(solution)/shard_map/ppermute | solution.py:34
  121.2 5.9 %collective-permute-start.50 = (bf16[8,256]{1,0:T(8,128)(2,1)S(1)}, bf16[8,256]{1,0:T(8,128)(2,1)S(1)}, u32[]{:S(2)}, u32[]{:S(2)}) collective-permute-start(bf16[8,256]{1,0:T(8,128)(2,1)S(1)} %get-tuple-element.58), channel_id=1, source_target_pairs={{0,24},{8,16},{16,8},{24,0},{1,25},{9,17},{17,9},{25,1},{2,26},{10... | collective-permute-start | bytes 12296 | tf_op jit(solution)/shard_map/ppermute | solution.py:371
  127.1 5.9 %collective-permute-start.53 = (bf16[8,2560]{1,0:T(8,128)(2,1)S(1)}, bf16[8,2560]{1,0:T(8,128)(2,1)S(1)}, u32[]{:S(2)}, u32[]{:S(2)}) collective-permute-start(bf16[8,2560]{1,0:T(8,128)(2,1)S(1)} %get-tuple-element.60), channel_id=1, source_target_pairs={{0,6},{1,7},{2,4},{3,5},{4,2},{5,3},{6,0},{7,1},{8,14},{9,15},{10,... | collective-permute-start | bytes 122888 | tf_op jit(solution)/shard_map/ppermute | solution.py:34
  129.4 5.1 %collective-permute-start.52 = (bf16[8,2560]{1,0:T(8,128)(2,1)S(1)}, bf16[8,2560]{1,0:T(8,128)(2,1)S(1)}, u32[]{:S(2)}, u32[]{:S(2)}) collective-permute-start(bf16[8,2560]{1,0:T(8,128)(2,1)S(1)} %get-tuple-element.60), channel_id=1, source_target_pairs={{0,4},{1,5},{2,6},{3,7},{4,0},{5,1},{6,2},{7,3},{8,12},{9,13},{10,... | collective-permute-start | bytes 122888 | tf_op jit(solution)/shard_map/ppermute | solution.py:34
  130.5 4.4 %collective-permute-start.51 = (bf16[8,2560]{1,0:T(8,128)(2,1)S(1)}, bf16[8,2560]{1,0:T(8,128)(2,1)S(1)}, u32[]{:S(2)}, u32[]{:S(2)}) collective-permute-start(bf16[8,2560]{1,0:T(8,128)(2,1)S(1)} %get-tuple-element.60), channel_id=1, source_target_pairs={{0,2},{1,3},{2,0},{3,1},{4,6},{5,7},{6,4},{7,5},{8,10},{9,11},{10,... | collective-permute-start | bytes 122888 | tf_op jit(solution)/shard_map/ppermute | solution.py:34
  136.2 5.5 %collective-permute-start.57 = (bf16[8,640]{1,0:T(8,128)(2,1)S(1)}, bf16[8,640]{1,0:T(8,128)(2,1)S(1)}, u32[]{:S(2)}, u32[]{:S(2)}) collective-permute-start(bf16[8,640]{1,0:T(8,128)(2,1)S(1)} %sep_rows.25), channel_id=1, source_target_pairs={{0,6},{1,7},{2,4},{3,5},{4,2},{5,3},{6,0},{7,1},{8,14},{9,15},{10,... | collective-permute-start | bytes 30728 | tf_op jit(solution)/shard_map/ppermute | solution.py:34
  137.7 4.6 %collective-permute-start.56 = (bf16[8,640]{1,0:T(8,128)(2,1)S(1)}, bf16[8,640]{1,0:T(8,128)(2,1)S(1)}, u32[]{:S(2)}, u32[]{:S(2)}) collective-permute-start(bf16[8,640]{1,0:T(8,128)(2,1)S(1)} %sep_rows.25), channel_id=1, source_target_pairs={{0,4},{1,5},{2,6},{3,7},{4,0},{5,1},{6,2},{7,3},{8,12},{9,13},{10,... | collective-permute-start | bytes 30728 | tf_op jit(solution)/shard_map/ppermute | solution.py:34
  138.3 4.0 %collective-permute-start.55 = (bf16[8,640]{1,0:T(8,128)(2,1)S(1)}, bf16[8,640]{1,0:T(8,128)(2,1)S(1)}, u32[]{:S(2)}, u32[]{:S(2)}) collective-permute-start(bf16[8,640]{1,0:T(8,128)(2,1)S(1)} %sep_rows.25), channel_id=1, source_target_pairs={{0,2},{1,3},{2,0},{3,1},{4,6},{5,7},{6,4},{7,5},{8,10},{9,11},{10,... | collective-permute-start | bytes 30728 | tf_op jit(solution)/shard_map/ppermute | solution.py:34
  143.6 5.9 %collective-permute-start.59 = (bf16[8,256]{1,0:T(8,128)(2,1)S(1)}, bf16[8,256]{1,0:T(8,128)(2,1)S(1)}, u32[]{:S(2)}, u32[]{:S(2)}) collective-permute-start(bf16[8,256]{1,0:T(8,128)(2,1)S(1)} %get-tuple-element.62), channel_id=1, source_target_pairs={{0,8},{8,0},{16,24},{24,16},{1,9},{9,1},{17,25},{25,17},{2,10},{10... | collective-permute-start | bytes 12296 | tf_op jit(solution)/shard_map/ppermute | solution.py:371
  150.3 5.8 %collective-permute-start.62 = (bf16[8,2560]{1,0:T(8,128)(2,1)S(1)}, bf16[8,2560]{1,0:T(8,128)(2,1)S(1)}, u32[]{:S(2)}, u32[]{:S(2)}) collective-permute-start(bf16[8,2560]{1,0:T(8,128)(2,1)S(1)} %get-tuple-element.64), channel_id=1, source_target_pairs={{0,6},{1,7},{2,4},{3,5},{4,2},{5,3},{6,0},{7,1},{8,14},{9,15},{10,... | collective-permute-start | bytes 122888 | tf_op jit(solution)/shard_map/ppermute | solution.py:34
  152.6 5.1 %collective-permute-start.61 = (bf16[8,2560]{1,0:T(8,128)(2,1)S(1)}, bf16[8,2560]{1,0:T(8,128)(2,1)S(1)}, u32[]{:S(2)}, u32[]{:S(2)}) collective-permute-start(bf16[8,2560]{1,0:T(8,128)(2,1)S(1)} %get-tuple-element.64), channel_id=1, source_target_pairs={{0,4},{1,5},{2,6},{3,7},{4,0},{5,1},{6,2},{7,3},{8,12},{9,13},{10,... | collective-permute-start | bytes 122888 | tf_op jit(solution)/shard_map/ppermute | solution.py:34
  153.7 4.4 %collective-permute-start.60 = (bf16[8,2560]{1,0:T(8,128)(2,1)S(1)}, bf16[8,2560]{1,0:T(8,128)(2,1)S(1)}, u32[]{:S(2)}, u32[]{:S(2)}) collective-permute-start(bf16[8,2560]{1,0:T(8,128)(2,1)S(1)} %get-tuple-element.64), channel_id=1, source_target_pairs={{0,2},{1,3},{2,0},{3,1},{4,6},{5,7},{6,4},{7,5},{8,10},{9,11},{10,... | collective-permute-start | bytes 122888 | tf_op jit(solution)/shard_map/ppermute | solution.py:34
  160.3 5.5 %collective-permute-start.66 = (bf16[8,640]{1,0:T(8,128)(2,1)S(1)}, bf16[8,640]{1,0:T(8,128)(2,1)S(1)}, u32[]{:S(2)}, u32[]{:S(2)}) collective-permute-start(bf16[8,640]{1,0:T(8,128)(2,1)S(1)} %sep_rows.27), channel_id=1, source_target_pairs={{0,6},{1,7},{2,4},{3,5},{4,2},{5,3},{6,0},{7,1},{8,14},{9,15},{10,... | collective-permute-start | bytes 30728 | tf_op jit(solution)/shard_map/ppermute | solution.py:34
  161.9 4.6 %collective-permute-start.65 = (bf16[8,640]{1,0:T(8,128)(2,1)S(1)}, bf16[8,640]{1,0:T(8,128)(2,1)S(1)}, u32[]{:S(2)}, u32[]{:S(2)}) collective-permute-start(bf16[8,640]{1,0:T(8,128)(2,1)S(1)} %sep_rows.27), channel_id=1, source_target_pairs={{0,4},{1,5},{2,6},{3,7},{4,0},{5,1},{6,2},{7,3},{8,12},{9,13},{10,... | collective-permute-start | bytes 30728 | tf_op jit(solution)/shard_map/ppermute | solution.py:34
  162.5 4.0 %collective-permute-start.64 = (bf16[8,640]{1,0:T(8,128)(2,1)S(1)}, bf16[8,640]{1,0:T(8,128)(2,1)S(1)}, u32[]{:S(2)}, u32[]{:S(2)}) collective-permute-start(bf16[8,640]{1,0:T(8,128)(2,1)S(1)} %sep_rows.27), channel_id=1, source_target_pairs={{0,2},{1,3},{2,0},{3,1},{4,6},{5,7},{6,4},{7,5},{8,10},{9,11},{10,... | collective-permute-start | bytes 30728 | tf_op jit(solution)/shard_map/ppermute | solution.py:34
  (30 other events, 91.7 us)

commit v4 on v3

v4 whole, which is shorter than its diff:
```python
import jax
import jax.numpy as jnp
from jax import lax
from jax.experimental import pallas as pl
from jax.experimental.pallas import tpu as pltpu
from jax.sharding import PartitionSpec as P

FEW_CHIPS = 8
BF16, F32 = jnp.bfloat16, jnp.float32
VMEM = pl.BlockSpec(memory_space=pltpu.VMEM)
SMEM = pl.BlockSpec(memory_space=pltpu.SMEM)
ANY = pl.BlockSpec(memory_space=pl.ANY)
MIB = 2**20


def xor_route(axis, distance):
    return [(i, i ^ distance) for i in range(lax.axis_size(axis))]


def pair(block):
    return lax.ppermute(block, "front", xor_route("front", 1))


def same_core_groups():
    slots = lax.axis_size("front")
    return [list(range(core, slots, 2)) for core in range(2)]


def arrival_order(chip, chips):
    steps = jnp.arange(chips, dtype=jnp.int32)
    return chip ^ ((chips - steps) % chips) if chips <= FEW_CHIPS else steps


def from_chips(block, chips):
    return [block] + [
        lax.ppermute(block, "front", xor_route("front", 2 * (chips - step)))
        for step in range(1, chips)
    ]


def gather_chips(block):
    chips = lax.axis_size("front") // 2
    if chips > FEW_CHIPS:
        groups = same_core_groups()
        return lax.all_gather(block, "front", axis=1, tiled=True, axis_index_groups=groups)
    return jnp.concatenate(from_chips(block, chips), axis=1)


def sum_chips(block, after=None):
    chips = lax.axis_size("front") // 2
    if chips > FEW_CHIPS:
        groups = same_core_groups()
        return lax.psum(block.astype(F32), "front", axis_index_groups=groups).astype(BF16)
    parts = from_chips(block, chips)
    if after is None:
        return sum(part.astype(F32) for part in parts).astype(BF16)
    return add_parts(parts, after)


def in_vmem(block):
    return pltpu.with_memory_space_constraint(block, pltpu.VMEM)


def in_hbm(block):
    return pltpu.with_memory_space_constraint(block, pltpu.HBM)


def params(mib):
    return pltpu.CompilerParams(vmem_limit_bytes=mib * MIB)


def cost(flops, nbytes):
    return pl.CostEstimate(flops=flops, bytes_accessed=nbytes, transcendentals=0)


def turned(vector):
    count = vector.shape[0] // 2
    return jnp.concatenate([-vector[count:], vector[:count]], axis=0)


def operands(vector):
    return vector.astype(BF16), turned(vector).astype(BF16)


def times(vector, real_matrix, imag_matrix, contract):
    straight, cross = operands(vector)
    dims = (((1,), (contract,)), ((), ()))
    return lax.dot_general(
        straight, real_matrix, dims, preferred_element_type=F32
    ) + lax.dot_general(cross, imag_matrix, dims, preferred_element_type=F32)


def transpose_sep(sep, after):
    _, rows, total = sep.shape
    step = 128 if rows % 128 == 0 else rows
    chunks = [(part, at) for part in range(2) for at in range(0, rows, step)]

    def kernel(sep_ref, _, out, stored, done):
        copies = []
        for index, (part, at) in enumerate(chunks):
            piece = (part, pl.ds(at, step))
            copy = pltpu.make_async_copy(sep_ref.at[piece], stored.at[piece], done.at[index])
            copy.start()
            copies.append(copy)
        for copy, (part, at) in zip(copies, chunks):
            copy.wait()
            out[part, :, pl.ds(at, step)] = stored[part, pl.ds(at, step), :].T

    return pl.pallas_call(
        kernel,
        in_specs=[ANY, ANY],
        out_specs=VMEM,
        out_shape=pltpu.VMEM((2, total, rows), BF16),
        scratch_shapes=[pltpu.VMEM(sep.shape, BF16), pltpu.SemaphoreType.DMA((len(chunks),))],
        compiler_params=params(18),
        cost_estimate=cost(0, 4 * sep.size),
        name="transpose_sep",
    )(in_hbm(sep), after)


def hold(blocks, after):
    def kernel(*refs):
        del refs

    return pl.pallas_call(
        kernel,
        in_specs=[VMEM] * len(blocks) + [ANY],
        out_specs=[VMEM] * len(blocks),
        out_shape=[pltpu.VMEM(block.shape, block.dtype) for block in blocks],
        input_output_aliases={index: index for index in range(len(blocks))},
        compiler_params=params(1),
        name="hold",
    )(*[in_vmem(block) for block in blocks], after)


def transpose_gather(own, theirs, after):
    _, total, cells = own.shape
    half = total // 2
    step = 512

    def kernel(own_ref, theirs_ref, _, out):
        start = (lax.axis_index("front") % 2) * half
        for side, block in enumerate((own_ref, theirs_ref)):
            for part in range(2):
                for at in range(0, half, step):
                    rows = pl.ds(pl.multiple_of(start + at, step), step)
                    out[part, pl.ds(side * cells, cells), pl.ds(at, step)] = block[part, rows, :].T

    return pl.pallas_call(
        kernel,
        in_specs=[VMEM, VMEM, ANY],
        out_specs=VMEM,
        out_shape=pltpu.VMEM((2, 2 * cells, half), BF16),
        compiler_params=params(16),
        cost_estimate=cost(0, 4 * own.size),
        name="transpose_gather",
    )(in_vmem(own), in_vmem(theirs), after)


def panel_columns(owner_ref, step, rows):
    slots = owner_ref.shape[0]
    place = lax.axis_index("front")
    chips = slots // 2
    chip = place // 2 ^ ((chips - step) % chips) if chips <= FEW_CHIPS else step
    panel = jnp.int32(0)
    for at in range(1, slots):
        panel = jnp.where(owner_ref[at] == 2 * chip + place % 2, at, panel)
    return pl.ds(pl.multiple_of(panel * rows, 128), rows)


def transpose_spread(own, theirs, owner, rows, after):
    _, cells, total = own.shape
    chips = owner.shape[0] // 2

    def kernel(owner_ref, own_ref, theirs_ref, _, out):
        for step in range(chips):
            columns = panel_columns(owner_ref, step, rows)
            for side, block in enumerate((own_ref, theirs_ref)):
                for part in range(2):
                    out[part, pl.ds(step * rows, rows), pl.ds(side * cells, cells)] = block[
                        part, :, columns
                    ].T

    return pl.pallas_call(
        kernel,
        in_specs=[SMEM, VMEM, VMEM, ANY],
        out_specs=VMEM,
        out_shape=pltpu.VMEM((2, total // 2, 2 * cells), BF16),
        compiler_params=params(16),
        cost_estimate=cost(0, 4 * own.size),
        name="transpose_spread",
    )(owner, in_vmem(own), in_vmem(theirs), after)


def take_spread(own, theirs, owner, rows):
    _, cells, total = own.shape
    slots = owner.shape[0]
    place = lax.axis_index("front")
    slot_ids = jnp.arange(slots, dtype=jnp.int32)
    panel_of = jnp.sum(jnp.where(owner[None, :] == slot_ids[:, None], slot_ids[None, :], 0), axis=1)
    wanted = panel_of[2 * arrival_order(place // 2, slots // 2) + place % 2]

    def columns(spread):
        chosen = jnp.take(spread.reshape(2, cells, slots, rows), wanted, axis=2)
        return jnp.swapaxes(chosen.reshape(2, cells, total // 2), 1, 2)

    return jnp.concatenate([columns(own), columns(theirs)], axis=2)


def first_spread_cells(stored, own, theirs, owner, rows):
    _, cells, _ = own.shape
    chips = owner.shape[0] // 2

    def kernel(owner_ref, stored_ref, own_ref, theirs_ref, out):
        @pl.when(lax.axis_index("layer") == 0)
        def _():
            for side, block in enumerate((own_ref, theirs_ref)):
                value = jnp.zeros((8, cells), F32)
                for step in range(chips):
                    columns = panel_columns(owner_ref, step, rows)
                    vector = stored_ref[:, pl.ds(step * rows, rows)].astype(F32)
                    value += times(vector, block[0, :, columns], block[1, :, columns], 1)
                out[:, pl.ds(side * cells, cells)] = value

    return pl.pallas_call(
        kernel,
        in_specs=[SMEM, VMEM, VMEM, VMEM],
        out_specs=VMEM,
        out_shape=jax.ShapeDtypeStruct((8, 2 * cells), F32),
        compiler_params=params(16),
        cost_estimate=cost(16 * own.size, 2 * own.size),
        name="first_spread_cells",
    )(owner, stored, in_vmem(own), in_vmem(theirs))


def add_parts(parts, after):
    def kernel(*refs):
        out = refs[-1]
        total = refs[0][...].astype(F32)
        for part in refs[1 : len(parts)]:
            total = total + part[...].astype(F32)
        out[...] = total.astype(BF16)

    return pl.pallas_call(
        kernel,
        in_specs=[VMEM] * len(parts) + [ANY],
        out_specs=VMEM,
        out_shape=jax.ShapeDtypeStruct(parts[0].shape, BF16),
        compiler_params=params(16),
        cost_estimate=cost(4 * parts[0].size, 10 * parts[0].size),
        name="add_parts",
    )(*parts, in_vmem(after))


def first_leaf_and_gather(sources, leaf, gather, spread):
    cells = leaf.shape[1]
    half = gather.shape[1] // 2

    def kernel(*refs):
        sources_hbm, leaf_hbm, gather_hbm, spread_hbm, leaf_out, keep, give = refs[:7]
        gather_ref, spread_ref, sources_ref, leaf_ref, done = refs[7:]
        core = lax.axis_index("front") % 2
        layer = lax.axis_index("layer")
        sides = [pl.ds(pl.multiple_of(side * half, half), half) for side in (1 - core, core)]
        copies = [
            pltpu.make_async_copy(sources_hbm, sources_ref, done.at[0]),
            pltpu.make_async_copy(leaf_hbm, leaf_ref, done.at[1]),
        ]
        for rows in sides:
            for part in range(2):
                copies.append(
                    pltpu.make_async_copy(
                        gather_hbm.at[part, rows], gather_ref.at[part, rows], done.at[len(copies)]
                    )
                )
        copies.append(pltpu.make_async_copy(spread_hbm, spread_ref, done.at[len(copies)]))
        for copy in copies:
            copy.start()
        copies[0].wait()
        copies[1].wait()

        @pl.when(layer == 0)
        def _():
            source = jnp.concatenate([sources_ref[0], sources_ref[1]], axis=0)
            leaf_out[...] = times(source, leaf_ref[0], leaf_ref[1], 1)

        for index, (out, rows) in enumerate(zip((give, keep), sides)):
            copies[2 + 2 * index].wait()
            copies[3 + 2 * index].wait()

            @pl.when(layer == 0)
            def _(out=out, rows=rows):
                value = times(leaf_out[...], gather_ref[0, rows, :], gather_ref[1, rows, :], 1)
                out[...] = value.astype(out.dtype)

        copies[-1].wait()

    return pl.pallas_call(
        kernel,
        in_specs=[ANY] * 4,
        out_specs=[VMEM] * 5,
        out_shape=[
            jax.ShapeDtypeStruct((8, cells), F32),
            jax.ShapeDtypeStruct((8, half), F32),
            jax.ShapeDtypeStruct((8, half), BF16),
            pltpu.VMEM(gather.shape, BF16),
            pltpu.VMEM(spread.shape, BF16),
        ],
        scratch_shapes=[
            pltpu.VMEM(sources.shape, F32),
            pltpu.VMEM(leaf.shape, BF16),
            pltpu.SemaphoreType.DMA((7,)),
        ],
        compiler_params=params(16),
        cost_estimate=cost(16 * gather.size, 2 * gather.size),
        name="first_leaf_and_gather",
    )(in_hbm(sources), in_hbm(leaf), in_hbm(gather), in_hbm(spread))


def leaf_and_gather(level, leaf, gather, couple, arrived, sources=None):
    cells = leaf[0].shape[1]
    width = gather.shape[2]
    given = [arrived] if sources is None else [arrived, sources]
    mats = list(couple) + list(leaf)

    def kernel(*refs):
        vectors = list(refs[: len(given)])
        matrices = list(refs[len(given) : len(given) + len(mats)])
        gather_ref, leaf_out, sums_out = refs[-3:]

        def blocks(vector, pair_of):
            return jnp.concatenate(
                [
                    times(vector[:, i * cells : (i + 1) * cells], pair_of[i][0], pair_of[i][1], 1)
                    for i in range(2)
                ],
                axis=1,
            )

        @pl.when(lax.axis_index("layer") == level)
        def _():
            source = blocks(vectors[0][...].astype(F32), matrices[:2])
            if sources is not None:
                source = vectors[1][...] - source
            leaf_values = blocks(source, matrices[-2:])
            leaf_out[...] = leaf_values
            sums_out[...] = times(leaf_values, gather_ref[0], gather_ref[1], 0).astype(BF16)

    return pl.pallas_call(
        kernel,
        in_specs=[VMEM] * (len(given) + len(mats) + 1),
        out_specs=[VMEM, VMEM],
        out_shape=[
            jax.ShapeDtypeStruct((8, 2 * cells), F32),
            jax.ShapeDtypeStruct((8, width), BF16),
        ],
        compiler_params=params(16),
        cost_estimate=cost(32 * gather.size, 2 * gather.size),
        name="leaf_and_gather",
    )(*given, *mats, in_vmem(gather))


def sep_rows(level, sums, sep, other, before=None):
    half = sums.shape[1]
    rows = sep.shape[2]
    given = [sums] if before is None else [sums, before]

    def kernel(*refs):
        sums_ref, sep_ref, out = refs[0], refs[-2], refs[-1]

        @pl.when(lax.axis_index("layer") == level)
        def _():
            core = lax.axis_index("front") % 2
            side = 1 - core if other else core
            at = pl.ds(pl.multiple_of(side * half, half), half)
            value = times(sums_ref[...].astype(F32), sep_ref[0, at, :], sep_ref[1, at, :], 0)
            if before is not None:
                value = value + refs[1][...]
            out[...] = value.astype(out.dtype)

    return pl.pallas_call(
        kernel,
        in_specs=[VMEM] * (len(given) + 1),
        out_specs=VMEM,
        out_shape=jax.ShapeDtypeStruct((8, rows), F32 if before is None else BF16),
        compiler_params=params(16),
        cost_estimate=cost(16 * sep.size, sep.size),
        name="sep_rows",
    )(*given, in_vmem(sep))


def spread_cells(level, stored, spread):
    def kernel(stored_ref, spread_ref, out):
        @pl.when(lax.axis_index("layer") == level)
        def _():
            out[...] = times(stored_ref[...].astype(F32), spread_ref[0], spread_ref[1], 0)

    return pl.pallas_call(
        kernel,
        in_specs=[VMEM, VMEM],
        out_specs=VMEM,
        out_shape=jax.ShapeDtypeStruct((8, spread.shape[2]), F32),
        compiler_params=params(16),
        cost_estimate=cost(32 * spread.size, 2 * spread.size),
        name="spread_cells",
    )(stored, in_vmem(spread))


def finish(level, leaf_values, part, theirs, before=None, subtract=False, last=False):
    cells = part.shape[1] // 2
    given = [leaf_values, part, theirs] + ([] if before is None else [before])

    def kernel(*refs):
        leaf_ref, part_ref, theirs_ref = refs[:3]
        here = lax.axis_index("layer") == level

        def store(value):
            if last:
                refs[-1][0, 0] = value[:4, :cells]
                refs[-1][0, 1] = value[4:, :cells]
            else:
                refs[-2][...] = value
                refs[-1][...] = value.astype(BF16)

        @pl.when(here)
        def _():
            swapped = jnp.concatenate([theirs_ref[:, cells:], theirs_ref[:, :cells]], axis=1)
            solved = leaf_ref[...] - (part_ref[...] + swapped)
            if subtract:
                solved = refs[3][...] - solved
            store(solved)

        if before is not None:

            @pl.when(jnp.logical_not(here))
            def _():
                store(refs[3][...])

    if last:
        out_shape = jax.ShapeDtypeStruct((1, 2, 4, cells), F32)
    else:
        out_shape = [jax.ShapeDtypeStruct(part.shape, dtype) for dtype in (F32, BF16)]
    return pl.pallas_call(
        kernel,
        in_specs=[VMEM] * len(given),
        out_specs=VMEM if last else [VMEM, VMEM],
        out_shape=out_shape,
        compiler_params=params(16),
        cost_estimate=cost(4 * part.size, 16 * part.size),
        name="finish",
    )(*given)


def local(
    right_sides,
    leaf_inverse,
    couple_above,
    couple_below,
    sep_gather,
    sep_inverse,
    sep_spread,
    panel_owner,
):
    depth = lax.axis_size("layer")
    cells = leaf_inverse.shape[2]
    rows = sep_inverse.shape[2]
    own_leaf, own_sources = leaf_inverse[0], right_sides[0]

    def with_partner(block):
        return [block, pair(block)]

    own_values, keep_sums, give_sums, own_gather, own_spread = first_leaf_and_gather(
        own_sources, own_leaf, sep_gather[0], sep_spread[0]
    )
    first_sums = (keep_sums + pair(give_sums).astype(F32)).astype(BF16)
    first_values = jnp.concatenate(with_partner(own_values), axis=1)

    leaf = with_partner(own_leaf)
    above = with_partner(couple_above[0])
    below = with_partner(couple_below[0])
    sources = jnp.concatenate(with_partner(own_sources.reshape(8, cells)), axis=1)

    own_gather, own_spread = hold([own_gather, own_spread], first_sums)
    their_gather, their_spread = pair(own_gather), pair(own_spread)
    sep = transpose_sep(sep_inverse[0], first_sums)

    def own_rows_of(level, half_sums):
        other_sums = pair(half_sums)
        own_rows = sep_rows(level, half_sums, sep, False)
        return sep_rows(level, other_sums, sep, True, own_rows)

    def solve(level, before, subtract=False, last=False, **given):
        leaf_values, sums = leaf_and_gather(level, leaf, gather, **given)
        stored = gather_chips(own_rows_of(level, sum_chips(sums)))
        part = spread_cells(level, stored, spread)
        return finish(level, leaf_values, part, pair(part), before, subtract, last)

    def hop(sent, source_layer, target_layer):
        return lax.ppermute(sent, "layer", xor_route("layer", source_layer ^ target_layer))

    stored = gather_chips(own_rows_of(0, sum_chips(first_sums, sep)))
    spreads = own_spread, their_spread, panel_owner[0], rows
    if rows % 128 == 0:
        part = first_spread_cells(stored, *spreads)
    else:
        spread = take_spread(*spreads)
        part = spread_cells(0, stored, spread)
    value, sent = finish(0, first_values, part, pair(part))
    arrived = hop(sent, 0, 1)
    gather = transpose_gather(own_gather, their_gather, sent)
    if rows % 128 == 0:
        spread = transpose_spread(*spreads, sent)

    for level in range(1, depth):
        if level > 1:
            arrived = hop(sent, level - 1, level)
        value, sent = solve(level, value, sources=sources, couple=above, arrived=arrived)
    for level in range(depth - 2, 0, -1):
        arrived = hop(sent, level + 1, level)
        value, sent = solve(level, value, True, couple=below, arrived=arrived)
    return solve(0, value, True, True, couple=below, arrived=hop(sent, 1, 0))


def solution(mesh):
    return jax.shard_map(
        local,
        mesh=mesh,
        in_specs=(
            P("layer", None, None, "front"),
            P("layer", None, "front", None),
            P("layer", None, "front", None),
            P("layer", None, "front", None),
            P("layer", None, None, "front"),
            P("layer", None, "front", None),
            P("layer", None, "front", None),
            P("layer", None),
        ),
        out_specs=P("layer", None, None, "front"),
        check_vma=False,
    )
```

time: 170 us -> 159 us (0.935)
  waiting for transfers between devices: 67.4 us -> 60.8 us
  local copies, waits for them, and re-layouts: 6.16 us -> 0.03 us
  starting transfers between devices: 77.4 us -> 79.4 us
    unnamed x20 -> x10, local copies, waits for them, and re-layouts: 4.29 us -> 0.03 us
    ppermute x42, waiting for transfers between devices: 36.2 us -> 32.6 us  [from_chips(): lax.ppermute(block, 'front', xor_route('front', 2 * (chips - step)))]
    ppermute x20 -> x22, waiting for transfers between devices: 16.7 us -> 15 us  [pair(): return lax.ppermute(block, 'front', xor_route('front', 1))]
    pallas_call x12 -> x14, Pallas kernels: 11.2 us -> 12.1 us  [the longest x1 5.35 us: transpose_sep(): pl.pallas_call(kernel, in_specs=[ANY, ANY], out_specs=VMEM, out_shape=plt...]
  transfers between devices with their start and end apart: 68 -> 70, of which waited for: 54 -> 49; matrix products, arithmetic and copies ran while one was open for 1% -> 0% of each run, Pallas kernels for 8% -> 7%
where the time goes in v4:
time: 159 us
  starting transfers between devices  79.4 us (50%)
  waiting for transfers between devices  60.8 us (38%)
  Pallas kernels  17.8 us (11%)
    ppermute x42, starting transfers between devices, from_chips(): lax.ppermute(block, 'front', xor_route('front', 2 * (chips - step)))  62.7 us
    ppermute x42, waiting for transfers between devices, from_chips(): lax.ppermute(block, 'front', xor_route('front', 2 * (chips - step)))  32.6 us
    ppermute x22, waiting for transfers between devices, pair(): return lax.ppermute(block, 'front', xor_route('front', 1))  15 us
    ppermute x6, starting transfers between devices, hop(): lax.ppermute(sent, 'layer', xor_route('layer', source_layer ^ target_layer))  13.6 us
    ppermute x6, waiting for transfers between devices, hop(): lax.ppermute(sent, 'layer', xor_route('layer', source_layer ^ target_layer))  13.2 us
    pallas_call x1, Pallas kernels, transpose_sep(): pl.pallas_call(kernel, in_specs=[ANY, ANY], out_specs=VMEM, out_shape=plt...  5.35 us
    pallas_call x14, Pallas kernels, sep_rows(): pl.pallas_call(kernel, in_specs=[VMEM] * (len(given) + 1), out_specs=VMEM...  3.95 us
  transfers between devices with their start and end apart: 70, of which 49 were waited for; matrix products, arithmetic and copies ran while one was open for 0% of the time, Pallas kernels for 7%

profile of v4, /device:TPU:0, one launch (start us, length us, event | category | flops | bytes accessed | tf_op | source)
XLA Modules:
  0.0 158.6 jit_solution(8609565461424346878)
XLA Ops:
  0.0 2.6 %first_leaf_and_gather.1 = (f32[8,128]{1,0:T(8,128)S(1)}, f32[8,2560]{1,0:T(8,128)S(1)}, bf16[8,2560]{1,0:T(8,128)(2,1)S(1)}, bf16[2,5120,128]{2,1,0:T(8,128)(2,1)S(1)}, bf16[2,128,5120]{2,1,0:T(8,128)(2,1)S(1)}) custom-call(f32[2,4,128]{2,1,0:T(4,128)} %bitcast.30, bf16[2,128,128]{2,1,0:T(8,128)(2,1)} %bitcast.9, bf16[2,5120,128]{2,1,0:T(8,128)(2,1)} %bitcast.28, ...), custom_call_target="tpu_custom_call" | custom-call | flops 20971520 | bytes 2621440 | tf_op jit(solution)/shard_map/first_leaf_and_gather/pallas_call | solution.py:298
  4.6 4.9 %collective-permute-start.2 = (bf16[8,2560]{1,0:T(8,128)(2,1)S(1)}, bf16[8,2560]{1,0:T(8,128)(2,1)S(1)}, u32[]{:S(2)}, u32[]{:S(2)}) collective-permute-start(bf16[8,2560]{1,0:T(8,128)(2,1)S(1)} %add_convert_fusion.6._.refs_0_.refs_2_), channel_id=1, source_target_pairs={{0,6},{1,7},{2,4},{3,5},{4,2},{5,3},{6,0},{7,1},{8,14},{9,15},{10,... | collective-permute-start | bytes 122888 | tf_op jit(solution)/shard_map/ppermute | solution.py:36
  10.2 5.3 %transpose_sep.1.refs_4_.refs_1_.refs_2_ = bf16[2,5120,640]{2,1,0:T(8,128)(2,1)S(1)} custom-call(bf16[2,640,5120]{2,1,0:T(8,128)(2,1)} %bitcast.27, bf16[8,2560]{1,0:T(8,128)(2,1)S(1)} %add_convert_fusion.6._.refs_0_.refs_2_), custom_call_target="tpu_custom_call" | custom-call | bytes 26214400 | tf_op jit(solution)/shard_map/transpose_sep/pallas_call | solution.py:109
  17.8 3.9 %collective-permute-start.6 = (bf16[8,640]{1,0:T(8,128)(2,1)S(1)}, bf16[8,640]{1,0:T(8,128)(2,1)S(1)}, u32[]{:S(2)}, u32[]{:S(2)}) collective-permute-start(bf16[8,640]{1,0:T(8,128)(2,1)S(1)} %sep_rows.15), channel_id=1, source_target_pairs={{0,6},{1,7},{2,4},{3,5},{4,2},{5,3},{6,0},{7,1},{8,14},{9,15},{10,... | collective-permute-start | bytes 30728 | tf_op jit(solution)/shard_map/ppermute | solution.py:36
  23.4 2.9 %collective-permute-done.7 = bf16[8,640]{1,0:T(8,128)(2,1)S(1)} collective-permute-done((bf16[8,640]{1,0:T(8,128)(2,1)S(1)}, bf16[8,640]{1,0:T(8,128)(2,1)S(1)}, u32[]{:S(2)}, u32[]{:S(2)}) %collective-permute-start.7) | collective-permute-done | bytes 10272 | tf_op jit(solution)/shard_map/ppermute | solution.py:36
  27.0 1.5 first_spread_cells.1.refs_1_
  30.5 2.8 %collective-permute-done.11.refs_0_ = bf16[8,256]{1,0:T(8,128)(2,1)S(1)} collective-permute-done((bf16[8,256]{1,0:T(8,128)(2,1)S(1)}, bf16[8,256]{1,0:T(8,128)(2,1)S(1)}, u32[]{:S(2)}, u32[]{:S(2)}) %collective-permute-start.11) | collective-permute-done | bytes 4128 | tf_op jit(solution)/shard_map/ppermute | solution.py:499
  35.2 2.5 %collective-permute-start.18 = (bf16[8,2560]{1,0:T(8,128)(2,1)S(1)}, bf16[8,2560]{1,0:T(8,128)(2,1)S(1)}, u32[]{:S(2)}, u32[]{:S(2)}) collective-permute-start(bf16[8,2560]{1,0:T(8,128)(2,1)S(1)} %get-tuple-element.45), channel_id=1, source_target_pairs={{0,2},{1,3},{2,0},{3,1},{4,6},{5,7},{6,4},{7,5},{8,10},{9,11},{10,... | collective-permute-start | bytes 122888 | tf_op jit(solution)/shard_map/ppermute | solution.py:36
  37.7 1.4 collective-permute-done.16
  41.3 2.5 %collective-permute-start.20 = (bf16[8,640]{1,0:T(8,128)(2,1)S(1)}, bf16[8,640]{1,0:T(8,128)(2,1)S(1)}, u32[]{:S(2)}, u32[]{:S(2)}) collective-permute-start(bf16[8,640]{1,0:T(8,128)(2,1)S(1)} %sep_rows.17), channel_id=1, source_target_pairs={{0,6},{1,7},{2,4},{3,5},{4,2},{5,3},{6,0},{7,1},{8,14},{9,15},{10,... | collective-permute-start | bytes 30728 | tf_op jit(solution)/shard_map/ppermute | solution.py:36
  47.0 1.4 collective-permute-done.21
  50.4 3.9 %collective-permute-done.24.refs_0_ = bf16[8,256]{1,0:T(8,128)(2,1)S(1)} collective-permute-done((bf16[8,256]{1,0:T(8,128)(2,1)S(1)}, bf16[8,256]{1,0:T(8,128)(2,1)S(1)}, u32[]{:S(2)}, u32[]{:S(2)}) %collective-permute-start.24) | collective-permute-done | bytes 4128 | tf_op jit(solution)/shard_map/ppermute | solution.py:499
  54.4 1.3 collective-permute-start.25
  56.6 2.2 %collective-permute-start.27 = (bf16[8,2560]{1,0:T(8,128)(2,1)S(1)}, bf16[8,2560]{1,0:T(8,128)(2,1)S(1)}, u32[]{:S(2)}, u32[]{:S(2)}) collective-permute-start(bf16[8,2560]{1,0:T(8,128)(2,1)S(1)} %get-tuple-element.49), channel_id=1, source_target_pairs={{0,2},{1,3},{2,0},{3,1},{4,6},{5,7},{6,4},{7,5},{8,10},{9,11},{10,... | collective-permute-start | bytes 122888 | tf_op jit(solution)/shard_map/ppermute | solution.py:36
  58.7 1.4 collective-permute-done.25
  62.4 2.4 %collective-permute-start.29 = (bf16[8,640]{1,0:T(8,128)(2,1)S(1)}, bf16[8,640]{1,0:T(8,128)(2,1)S(1)}, u32[]{:S(2)}, u32[]{:S(2)}) collective-permute-start(bf16[8,640]{1,0:T(8,128)(2,1)S(1)} %sep_rows.19), channel_id=1, source_target_pairs={{0,6},{1,7},{2,4},{3,5},{4,2},{5,3},{6,0},{7,1},{8,14},{9,15},{10,... | collective-permute-start | bytes 30728 | tf_op jit(solution)/shard_map/ppermute | solution.py:36
  67.8 1.5 collective-permute-done.30
  70.6 2.2 %collective-permute-start.33 = (bf16[8,256]{1,0:T(8,128)(2,1)S(1)}, bf16[8,256]{1,0:T(8,128)(2,1)S(1)}, u32[]{:S(2)}, u32[]{:S(2)}) collective-permute-start(bf16[8,256]{1,0:T(8,128)(2,1)S(1)} %get-tuple-element.51), channel_id=1, source_target_pairs={{0,8},{8,0},{16,24},{24,16},{1,9},{9,1},{17,25},{25,17},{2,10},{10... | collective-permute-start | bytes 12296 | tf_op jit(solution)/shard_map/ppermute | solution.py:499
  72.8 1.6 collective-permute-done.33.refs_0_
  74.4 1.5 collective-permute-start.34
  76.9 1.9 %collective-permute-start.36 = (bf16[8,2560]{1,0:T(8,128)(2,1)S(1)}, bf16[8,2560]{1,0:T(8,128)(2,1)S(1)}, u32[]{:S(2)}, u32[]{:S(2)}) collective-permute-start(bf16[8,2560]{1,0:T(8,128)(2,1)S(1)} %get-tuple-element.53), channel_id=1, source_target_pairs={{0,2},{1,3},{2,0},{3,1},{4,6},{5,7},{6,4},{7,5},{8,10},{9,11},{10,... | collective-permute-start | bytes 122888 | tf_op jit(solution)/shard_map/ppermute | solution.py:36
  78.8 1.6 %collective-permute-done.34 = bf16[8,2560]{1,0:T(8,128)(2,1)S(1)} collective-permute-done((bf16[8,2560]{1,0:T(8,128)(2,1)S(1)}, bf16[8,2560]{1,0:T(8,128)(2,1)S(1)}, u32[]{:S(2)}, u32[]{:S(2)}) %collective-permute-start.34) | collective-permute-done | bytes 40992 | tf_op jit(solution)/shard_map/ppermute | solution.py:36
  82.7 2.4 %collective-permute-start.38 = (bf16[8,640]{1,0:T(8,128)(2,1)S(1)}, bf16[8,640]{1,0:T(8,128)(2,1)S(1)}, u32[]{:S(2)}, u32[]{:S(2)}) collective-permute-start(bf16[8,640]{1,0:T(8,128)(2,1)S(1)} %sep_rows.21), channel_id=1, source_target_pairs={{0,6},{1,7},{2,4},{3,5},{4,2},{5,3},{6,0},{7,1},{8,14},{9,15},{10,... | collective-permute-start | bytes 30728 | tf_op jit(solution)/shard_map/ppermute | solution.py:36
  85.6 1.4 collective-permute-start.40
  88.1 1.5 collective-permute-done.39
  90.9 1.9 %collective-permute-start.42 = (bf16[8,256]{1,0:T(8,128)(2,1)S(1)}, bf16[8,256]{1,0:T(8,128)(2,1)S(1)}, u32[]{:S(2)}, u32[]{:S(2)}) collective-permute-start(bf16[8,256]{1,0:T(8,128)(2,1)S(1)} %get-tuple-element.55), channel_id=1, source_target_pairs={{0,8},{8,0},{16,24},{24,16},{1,9},{9,1},{17,25},{25,17},{2,10},{10... | collective-permute-start | bytes 12296 | tf_op jit(solution)/shard_map/ppermute | solution.py:499
  92.8 1.7 %collective-permute-done.42.refs_0_ = bf16[8,256]{1,0:T(8,128)(2,1)S(1)} collective-permute-done((bf16[8,256]{1,0:T(8,128)(2,1)S(1)}, bf16[8,256]{1,0:T(8,128)(2,1)S(1)}, u32[]{:S(2)}, u32[]{:S(2)}) %collective-permute-start.42) | collective-permute-done | bytes 4128 | tf_op jit(solution)/shard_map/ppermute | solution.py:499
  94.5 1.5 collective-permute-start.44
  97.0 1.9 %collective-permute-start.46 = (bf16[8,2560]{1,0:T(8,128)(2,1)S(1)}, bf16[8,2560]{1,0:T(8,128)(2,1)S(1)}, u32[]{:S(2)}, u32[]{:S(2)}) collective-permute-start(bf16[8,2560]{1,0:T(8,128)(2,1)S(1)} %get-tuple-element.57), channel_id=1, source_target_pairs={{0,2},{1,3},{2,0},{3,1},{4,6},{5,7},{6,4},{7,5},{8,10},{9,11},{10,... | collective-permute-start | bytes 122888 | tf_op jit(solution)/shard_map/ppermute | solution.py:36
  98.9 1.6 collective-permute-done.44
  102.6 2.3 %collective-permute-start.48 = (bf16[8,640]{1,0:T(8,128)(2,1)S(1)}, bf16[8,640]{1,0:T(8,128)(2,1)S(1)}, u32[]{:S(2)}, u32[]{:S(2)}) collective-permute-start(bf16[8,640]{1,0:T(8,128)(2,1)S(1)} %sep_rows.23), channel_id=1, source_target_pairs={{0,6},{1,7},{2,4},{3,5},{4,2},{5,3},{6,0},{7,1},{8,14},{9,15},{10,... | collective-permute-start | bytes 30728 | tf_op jit(solution)/shard_map/ppermute | solution.py:36
  105.6 1.4 collective-permute-start.50
  108.1 1.4 collective-permute-done.49
  110.8 4.5 %collective-permute-start.52 = (bf16[8,256]{1,0:T(8,128)(2,1)S(1)}, bf16[8,256]{1,0:T(8,128)(2,1)S(1)}, u32[]{:S(2)}, u32[]{:S(2)}) collective-permute-start(bf16[8,256]{1,0:T(8,128)(2,1)S(1)} %get-tuple-element.59), channel_id=1, source_target_pairs={{0,24},{8,16},{16,8},{24,0},{1,25},{9,17},{17,9},{25,1},{2,26},{10... | collective-permute-start | bytes 12296 | tf_op jit(solution)/shard_map/ppermute | solution.py:499
  115.4 1.6 collective-permute-done.52.refs_0_
  116.9 1.6 collective-permute-start.53
  119.4 2.0 %collective-permute-start.55 = (bf16[8,2560]{1,0:T(8,128)(2,1)S(1)}, bf16[8,2560]{1,0:T(8,128)(2,1)S(1)}, u32[]{:S(2)}, u32[]{:S(2)}) collective-permute-start(bf16[8,2560]{1,0:T(8,128)(2,1)S(1)} %get-tuple-element.61), channel_id=1, source_target_pairs={{0,2},{1,3},{2,0},{3,1},{4,6},{5,7},{6,4},{7,5},{8,10},{9,11},{10,... | collective-permute-start | bytes 122888 | tf_op jit(solution)/shard_map/ppermute | solution.py:36
  121.3 1.8 %collective-permute-done.53 = bf16[8,2560]{1,0:T(8,128)(2,1)S(1)} collective-permute-done((bf16[8,2560]{1,0:T(8,128)(2,1)S(1)}, bf16[8,2560]{1,0:T(8,128)(2,1)S(1)}, u32[]{:S(2)}, u32[]{:S(2)}) %collective-permute-start.53) | collective-permute-done | bytes 40992 | tf_op jit(solution)/shard_map/ppermute | solution.py:36
  125.3 2.3 %collective-permute-start.57 = (bf16[8,640]{1,0:T(8,128)(2,1)S(1)}, bf16[8,640]{1,0:T(8,128)(2,1)S(1)}, u32[]{:S(2)}, u32[]{:S(2)}) collective-permute-start(bf16[8,640]{1,0:T(8,128)(2,1)S(1)} %sep_rows.25), channel_id=1, source_target_pairs={{0,6},{1,7},{2,4},{3,5},{4,2},{5,3},{6,0},{7,1},{8,14},{9,15},{10,... | collective-permute-start | bytes 30728 | tf_op jit(solution)/shard_map/ppermute | solution.py:36
  128.1 1.5 collective-permute-start.59
  130.7 1.4 collective-permute-done.58
  133.6 4.3 %collective-permute-start.61 = (bf16[8,256]{1,0:T(8,128)(2,1)S(1)}, bf16[8,256]{1,0:T(8,128)(2,1)S(1)}, u32[]{:S(2)}, u32[]{:S(2)}) collective-permute-start(bf16[8,256]{1,0:T(8,128)(2,1)S(1)} %get-tuple-element.63), channel_id=1, source_target_pairs={{0,8},{8,0},{16,24},{24,16},{1,9},{9,1},{17,25},{25,17},{2,10},{10... | collective-permute-start | bytes 12296 | tf_op jit(solution)/shard_map/ppermute | solution.py:499
  137.9 1.6 collective-permute-done.61.refs_0_
  140.3 1.6 %collective-permute-start.62 = (bf16[8,2560]{1,0:T(8,128)(2,1)S(1)}, bf16[8,2560]{1,0:T(8,128)(2,1)S(1)}, u32[]{:S(2)}, u32[]{:S(2)}) collective-permute-start(bf16[8,2560]{1,0:T(8,128)(2,1)S(1)} %get-tuple-element.65), channel_id=1, source_target_pairs={{0,6},{1,7},{2,4},{3,5},{4,2},{5,3},{6,0},{7,1},{8,14},{9,15},{10,... | collective-permute-start | bytes 122888 | tf_op jit(solution)/shard_map/ppermute | solution.py:36
  142.7 1.9 %collective-permute-start.64 = (bf16[8,2560]{1,0:T(8,128)(2,1)S(1)}, bf16[8,2560]{1,0:T(8,128)(2,1)S(1)}, u32[]{:S(2)}, u32[]{:S(2)}) collective-permute-start(bf16[8,2560]{1,0:T(8,128)(2,1)S(1)} %get-tuple-element.65), channel_id=1, source_target_pairs={{0,2},{1,3},{2,0},{3,1},{4,6},{5,7},{6,4},{7,5},{8,10},{9,11},{10,... | collective-permute-start | bytes 122888 | tf_op jit(solution)/shard_map/ppermute | solution.py:36
  144.7 2.0 %collective-permute-done.62 = bf16[8,2560]{1,0:T(8,128)(2,1)S(1)} collective-permute-done((bf16[8,2560]{1,0:T(8,128)(2,1)S(1)}, bf16[8,2560]{1,0:T(8,128)(2,1)S(1)}, u32[]{:S(2)}, u32[]{:S(2)}) %collective-permute-start.62) | collective-permute-done | bytes 40992 | tf_op jit(solution)/shard_map/ppermute | solution.py:36
  149.6 2.2 %collective-permute-start.66 = (bf16[8,640]{1,0:T(8,128)(2,1)S(1)}, bf16[8,640]{1,0:T(8,128)(2,1)S(1)}, u32[]{:S(2)}, u32[]{:S(2)}) collective-permute-start(bf16[8,640]{1,0:T(8,128)(2,1)S(1)} %sep_rows.27), channel_id=1, source_target_pairs={{0,6},{1,7},{2,4},{3,5},{4,2},{5,3},{6,0},{7,1},{8,14},{9,15},{10,... | collective-permute-start | bytes 30728 | tf_op jit(solution)/shard_map/ppermute | solution.py:36
  152.5 1.6 collective-permute-start.68
  (158 shorter events, 53.8 us)
Async XLA Ops:
  4.1 22.7 %collective-permute-start.9 = (bf16[2,128,5120]{2,1,0:T(8,128)(2,1)S(1)}, bf16[2,128,5120]{2,1,0:T(8,128)(2,1)S(1)}, u32[]{:S(2)}, u32[]{:S(2)}) collective-permute-start(bf16[2,128,5120]{2,1,0:T(8,128)(2,1)S(1)} %get-tuple-element.41.own_ref), channel_id=1, source_target_pairs={{0,1},{1,0},{2,3},{3,2},{4,5},{5,4},{6,7},{7,6},{8,9},{9,8},{10,11... | collective-permute-start | bytes 7864328 | tf_op jit(solution)/shard_map/ppermute | solution.py:21
  4.5 25.3 %collective-permute-start.15 = (bf16[2,5120,128]{2,1,0:T(8,128)(2,1)S(1)}, bf16[2,5120,128]{2,1,0:T(8,128)(2,1)S(1)}, u32[]{:S(2)}, u32[]{:S(2)}) collective-permute-start(bf16[2,5120,128]{2,1,0:T(8,128)(2,1)S(1)} %get-tuple-element.43.own_ref), channel_id=1, source_target_pairs={{0,1},{1,0},{2,3},{3,2},{4,5},{5,4},{6,7},{7,6},{8,9},{9,8},{10,11... | collective-permute-start | bytes 7864328 | tf_op jit(solution)/shard_map/ppermute | solution.py:21
  4.6 10.9 %collective-permute-start.2 = (bf16[8,2560]{1,0:T(8,128)(2,1)S(1)}, bf16[8,2560]{1,0:T(8,128)(2,1)S(1)}, u32[]{:S(2)}, u32[]{:S(2)}) collective-permute-start(bf16[8,2560]{1,0:T(8,128)(2,1)S(1)} %add_convert_fusion.6._.refs_0_.refs_2_), channel_id=1, source_target_pairs={{0,6},{1,7},{2,4},{3,5},{4,2},{5,3},{6,0},{7,1},{8,14},{9,15},{10,... | collective-permute-start | bytes 122888 | tf_op jit(solution)/shard_map/ppermute | solution.py:36
  9.6 5.9 %collective-permute-start.3 = (bf16[8,2560]{1,0:T(8,128)(2,1)S(1)}, bf16[8,2560]{1,0:T(8,128)(2,1)S(1)}, u32[]{:S(2)}, u32[]{:S(2)}) collective-permute-start(bf16[8,2560]{1,0:T(8,128)(2,1)S(1)} %add_convert_fusion.6._.refs_0_.refs_2_), channel_id=1, source_target_pairs={{0,4},{1,5},{2,6},{3,7},{4,0},{5,1},{6,2},{7,3},{8,12},{9,13},{10,... | collective-permute-start | bytes 122888 | tf_op jit(solution)/shard_map/ppermute | solution.py:36
  9.6 5.9 %collective-permute-start.4 = (bf16[8,2560]{1,0:T(8,128)(2,1)S(1)}, bf16[8,2560]{1,0:T(8,128)(2,1)S(1)}, u32[]{:S(2)}, u32[]{:S(2)}) collective-permute-start(bf16[8,2560]{1,0:T(8,128)(2,1)S(1)} %add_convert_fusion.6._.refs_0_.refs_2_), channel_id=1, source_target_pairs={{0,2},{1,3},{2,0},{3,1},{4,6},{5,7},{6,4},{7,5},{8,10},{9,11},{10,... | collective-permute-start | bytes 122888 | tf_op jit(solution)/shard_map/ppermute | solution.py:36
  17.8 5.5 %collective-permute-start.6 = (bf16[8,640]{1,0:T(8,128)(2,1)S(1)}, bf16[8,640]{1,0:T(8,128)(2,1)S(1)}, u32[]{:S(2)}, u32[]{:S(2)}) collective-permute-start(bf16[8,640]{1,0:T(8,128)(2,1)S(1)} %sep_rows.15), channel_id=1, source_target_pairs={{0,6},{1,7},{2,4},{3,5},{4,2},{5,3},{6,0},{7,1},{8,14},{9,15},{10,... | collective-permute-start | bytes 30728 | tf_op jit(solution)/shard_map/ppermute | solution.py:36
  21.7 4.6 %collective-permute-start.7 = (bf16[8,640]{1,0:T(8,128)(2,1)S(1)}, bf16[8,640]{1,0:T(8,128)(2,1)S(1)}, u32[]{:S(2)}, u32[]{:S(2)}) collective-permute-start(bf16[8,640]{1,0:T(8,128)(2,1)S(1)} %sep_rows.15), channel_id=1, source_target_pairs={{0,4},{1,5},{2,6},{3,7},{4,0},{5,1},{6,2},{7,3},{8,12},{9,13},{10,... | collective-permute-start | bytes 30728 | tf_op jit(solution)/shard_map/ppermute | solution.py:36
  21.7 4.6 %collective-permute-start.8 = (bf16[8,640]{1,0:T(8,128)(2,1)S(1)}, bf16[8,640]{1,0:T(8,128)(2,1)S(1)}, u32[]{:S(2)}, u32[]{:S(2)}) collective-permute-start(bf16[8,640]{1,0:T(8,128)(2,1)S(1)} %sep_rows.15), channel_id=1, source_target_pairs={{0,2},{1,3},{2,0},{3,1},{4,6},{5,7},{6,4},{7,5},{8,10},{9,11},{10,... | collective-permute-start | bytes 30728 | tf_op jit(solution)/shard_map/ppermute | solution.py:36
  23.4 7.2 %collective-permute-start.14 = (bf16[2,128,128]{2,1,0:T(8,128)(2,1)S(1)}, bf16[2,128,128]{2,1,0:T(8,128)(2,1)S(1)}, u32[]{:S(2)}, u32[]{:S(2)}) collective-permute-start(bf16[2,128,128]{2,1,0:T(8,128)(2,1)S(1)} %bitcast.10), channel_id=1, source_target_pairs={{0,1},{1,0},{2,3},{3,2},{4,5},{5,4},{6,7},{7,6},{8,9},{9,8},{10,11... | collective-permute-start | bytes 196616 | tf_op jit(solution)/shard_map/ppermute | solution.py:21
  26.3 4.2 %collective-permute-start.13 = (bf16[2,128,128]{2,1,0:T(8,128)(2,1)S(1)}, bf16[2,128,128]{2,1,0:T(8,128)(2,1)S(1)}, u32[]{:S(2)}, u32[]{:S(2)}) collective-permute-start(bf16[2,128,128]{2,1,0:T(8,128)(2,1)S(1)} %bitcast.17), channel_id=1, source_target_pairs={{0,1},{1,0},{2,3},{3,2},{4,5},{5,4},{6,7},{7,6},{8,9},{9,8},{10,11... | collective-permute-start | bytes 196616 | tf_op jit(solution)/shard_map/ppermute | solution.py:21
  33.3 5.8 %collective-permute-start.16 = (bf16[8,2560]{1,0:T(8,128)(2,1)S(1)}, bf16[8,2560]{1,0:T(8,128)(2,1)S(1)}, u32[]{:S(2)}, u32[]{:S(2)}) collective-permute-start(bf16[8,2560]{1,0:T(8,128)(2,1)S(1)} %get-tuple-element.45), channel_id=1, source_target_pairs={{0,6},{1,7},{2,4},{3,5},{4,2},{5,3},{6,0},{7,1},{8,14},{9,15},{10,... | collective-permute-start | bytes 122888 | tf_op jit(solution)/shard_map/ppermute | solution.py:36
  34.6 5.0 %collective-permute-start.17 = (bf16[8,2560]{1,0:T(8,128)(2,1)S(1)}, bf16[8,2560]{1,0:T(8,128)(2,1)S(1)}, u32[]{:S(2)}, u32[]{:S(2)}) collective-permute-start(bf16[8,2560]{1,0:T(8,128)(2,1)S(1)} %get-tuple-element.45), channel_id=1, source_target_pairs={{0,4},{1,5},{2,6},{3,7},{4,0},{5,1},{6,2},{7,3},{8,12},{9,13},{10,... | collective-permute-start | bytes 122888 | tf_op jit(solution)/shard_map/ppermute | solution.py:36
  35.2 4.8 %collective-permute-start.18 = (bf16[8,2560]{1,0:T(8,128)(2,1)S(1)}, bf16[8,2560]{1,0:T(8,128)(2,1)S(1)}, u32[]{:S(2)}, u32[]{:S(2)}) collective-permute-start(bf16[8,2560]{1,0:T(8,128)(2,1)S(1)} %get-tuple-element.45), channel_id=1, source_target_pairs={{0,2},{1,3},{2,0},{3,1},{4,6},{5,7},{6,4},{7,5},{8,10},{9,11},{10,... | collective-permute-start | bytes 122888 | tf_op jit(solution)/shard_map/ppermute | solution.py:36
  41.3 5.7 %collective-permute-start.20 = (bf16[8,640]{1,0:T(8,128)(2,1)S(1)}, bf16[8,640]{1,0:T(8,128)(2,1)S(1)}, u32[]{:S(2)}, u32[]{:S(2)}) collective-permute-start(bf16[8,640]{1,0:T(8,128)(2,1)S(1)} %sep_rows.17), channel_id=1, source_target_pairs={{0,6},{1,7},{2,4},{3,5},{4,2},{5,3},{6,0},{7,1},{8,14},{9,15},{10,... | collective-permute-start | bytes 30728 | tf_op jit(solution)/shard_map/ppermute | solution.py:36
  43.8 4.6 %collective-permute-start.21 = (bf16[8,640]{1,0:T(8,128)(2,1)S(1)}, bf16[8,640]{1,0:T(8,128)(2,1)S(1)}, u32[]{:S(2)}, u32[]{:S(2)}) collective-permute-start(bf16[8,640]{1,0:T(8,128)(2,1)S(1)} %sep_rows.17), channel_id=1, source_target_pairs={{0,4},{1,5},{2,6},{3,7},{4,0},{5,1},{6,2},{7,3},{8,12},{9,13},{10,... | collective-permute-start | bytes 30728 | tf_op jit(solution)/shard_map/ppermute | solution.py:36
  44.5 3.9 %collective-permute-start.22 = (bf16[8,640]{1,0:T(8,128)(2,1)S(1)}, bf16[8,640]{1,0:T(8,128)(2,1)S(1)}, u32[]{:S(2)}, u32[]{:S(2)}) collective-permute-start(bf16[8,640]{1,0:T(8,128)(2,1)S(1)} %sep_rows.17), channel_id=1, source_target_pairs={{0,2},{1,3},{2,0},{3,1},{4,6},{5,7},{6,4},{7,5},{8,10},{9,11},{10,... | collective-permute-start | bytes 30728 | tf_op jit(solution)/shard_map/ppermute | solution.py:36
  49.9 4.5 %collective-permute-start.24 = (bf16[8,256]{1,0:T(8,128)(2,1)S(1)}, bf16[8,256]{1,0:T(8,128)(2,1)S(1)}, u32[]{:S(2)}, u32[]{:S(2)}) collective-permute-start(bf16[8,256]{1,0:T(8,128)(2,1)S(1)} %get-tuple-element.47), channel_id=1, source_target_pairs={{0,24},{8,16},{16,8},{24,0},{1,25},{9,17},{17,9},{25,1},{2,26},{10... | collective-permute-start | bytes 12296 | tf_op jit(solution)/shard_map/ppermute | solution.py:499
  54.4 5.8 %collective-permute-start.25 = (bf16[8,2560]{1,0:T(8,128)(2,1)S(1)}, bf16[8,2560]{1,0:T(8,128)(2,1)S(1)}, u32[]{:S(2)}, u32[]{:S(2)}) collective-permute-start(bf16[8,2560]{1,0:T(8,128)(2,1)S(1)} %get-tuple-element.49), channel_id=1, source_target_pairs={{0,6},{1,7},{2,4},{3,5},{4,2},{5,3},{6,0},{7,1},{8,14},{9,15},{10,... | collective-permute-start | bytes 122888 | tf_op jit(solution)/shard_map/ppermute | solution.py:36
  55.7 4.9 %collective-permute-start.26 = (bf16[8,2560]{1,0:T(8,128)(2,1)S(1)}, bf16[8,2560]{1,0:T(8,128)(2,1)S(1)}, u32[]{:S(2)}, u32[]{:S(2)}) collective-permute-start(bf16[8,2560]{1,0:T(8,128)(2,1)S(1)} %get-tuple-element.49), channel_id=1, source_target_pairs={{0,4},{1,5},{2,6},{3,7},{4,0},{5,1},{6,2},{7,3},{8,12},{9,13},{10,... | collective-permute-start | bytes 122888 | tf_op jit(solution)/shard_map/ppermute | solution.py:36
  56.6 4.5 %collective-permute-start.27 = (bf16[8,2560]{1,0:T(8,128)(2,1)S(1)}, bf16[8,2560]{1,0:T(8,128)(2,1)S(1)}, u32[]{:S(2)}, u32[]{:S(2)}) collective-permute-start(bf16[8,2560]{1,0:T(8,128)(2,1)S(1)} %get-tuple-element.49), channel_id=1, source_target_pairs={{0,2},{1,3},{2,0},{3,1},{4,6},{5,7},{6,4},{7,5},{8,10},{9,11},{10,... | collective-permute-start | bytes 122888 | tf_op jit(solution)/shard_map/ppermute | solution.py:36
  62.4 5.5 %collective-permute-start.29 = (bf16[8,640]{1,0:T(8,128)(2,1)S(1)}, bf16[8,640]{1,0:T(8,128)(2,1)S(1)}, u32[]{:S(2)}, u32[]{:S(2)}) collective-permute-start(bf16[8,640]{1,0:T(8,128)(2,1)S(1)} %sep_rows.19), channel_id=1, source_target_pairs={{0,6},{1,7},{2,4},{3,5},{4,2},{5,3},{6,0},{7,1},{8,14},{9,15},{10,... | collective-permute-start | bytes 30728 | tf_op jit(solution)/shard_map/ppermute | solution.py:36
  64.8 4.6 %collective-permute-start.30 = (bf16[8,640]{1,0:T(8,128)(2,1)S(1)}, bf16[8,640]{1,0:T(8,128)(2,1)S(1)}, u32[]{:S(2)}, u32[]{:S(2)}) collective-permute-start(bf16[8,640]{1,0:T(8,128)(2,1)S(1)} %sep_rows.19), channel_id=1, source_target_pairs={{0,4},{1,5},{2,6},{3,7},{4,0},{5,1},{6,2},{7,3},{8,12},{9,13},{10,... | collective-permute-start | bytes 30728 | tf_op jit(solution)/shard_map/ppermute | solution.py:36
  74.4 6.0 %collective-permute-start.34 = (bf16[8,2560]{1,0:T(8,128)(2,1)S(1)}, bf16[8,2560]{1,0:T(8,128)(2,1)S(1)}, u32[]{:S(2)}, u32[]{:S(2)}) collective-permute-start(bf16[8,2560]{1,0:T(8,128)(2,1)S(1)} %get-tuple-element.53), channel_id=1, source_target_pairs={{0,6},{1,7},{2,4},{3,5},{4,2},{5,3},{6,0},{7,1},{8,14},{9,15},{10,... | collective-permute-start | bytes 122888 | tf_op jit(solution)/shard_map/ppermute | solution.py:36
  75.9 5.4 %collective-permute-start.35 = (bf16[8,2560]{1,0:T(8,128)(2,1)S(1)}, bf16[8,2560]{1,0:T(8,128)(2,1)S(1)}, u32[]{:S(2)}, u32[]{:S(2)}) collective-permute-start(bf16[8,2560]{1,0:T(8,128)(2,1)S(1)} %get-tuple-element.53), channel_id=1, source_target_pairs={{0,4},{1,5},{2,6},{3,7},{4,0},{5,1},{6,2},{7,3},{8,12},{9,13},{10,... | collective-permute-start | bytes 122888 | tf_op jit(solution)/shard_map/ppermute | solution.py:36
  76.9 4.5 %collective-permute-start.36 = (bf16[8,2560]{1,0:T(8,128)(2,1)S(1)}, bf16[8,2560]{1,0:T(8,128)(2,1)S(1)}, u32[]{:S(2)}, u32[]{:S(2)}) collective-permute-start(bf16[8,2560]{1,0:T(8,128)(2,1)S(1)} %get-tuple-element.53), channel_id=1, source_target_pairs={{0,2},{1,3},{2,0},{3,1},{4,6},{5,7},{6,4},{7,5},{8,10},{9,11},{10,... | collective-permute-start | bytes 122888 | tf_op jit(solution)/shard_map/ppermute | solution.py:36
  82.7 5.5 %collective-permute-start.38 = (bf16[8,640]{1,0:T(8,128)(2,1)S(1)}, bf16[8,640]{1,0:T(8,128)(2,1)S(1)}, u32[]{:S(2)}, u32[]{:S(2)}) collective-permute-start(bf16[8,640]{1,0:T(8,128)(2,1)S(1)} %sep_rows.21), channel_id=1, source_target_pairs={{0,6},{1,7},{2,4},{3,5},{4,2},{5,3},{6,0},{7,1},{8,14},{9,15},{10,... | collective-permute-start | bytes 30728 | tf_op jit(solution)/shard_map/ppermute | solution.py:36
  85.0 4.6 %collective-permute-start.39 = (bf16[8,640]{1,0:T(8,128)(2,1)S(1)}, bf16[8,640]{1,0:T(8,128)(2,1)S(1)}, u32[]{:S(2)}, u32[]{:S(2)}) collective-permute-start(bf16[8,640]{1,0:T(8,128)(2,1)S(1)} %sep_rows.21), channel_id=1, source_target_pairs={{0,4},{1,5},{2,6},{3,7},{4,0},{5,1},{6,2},{7,3},{8,12},{9,13},{10,... | collective-permute-start | bytes 30728 | tf_op jit(solution)/shard_map/ppermute | solution.py:36
  85.6 4.0 %collective-permute-start.40 = (bf16[8,640]{1,0:T(8,128)(2,1)S(1)}, bf16[8,640]{1,0:T(8,128)(2,1)S(1)}, u32[]{:S(2)}, u32[]{:S(2)}) collective-permute-start(bf16[8,640]{1,0:T(8,128)(2,1)S(1)} %sep_rows.21), channel_id=1, source_target_pairs={{0,2},{1,3},{2,0},{3,1},{4,6},{5,7},{6,4},{7,5},{8,10},{9,11},{10,... | collective-permute-start | bytes 30728 | tf_op jit(solution)/shard_map/ppermute | solution.py:36
  87.0 5.7 %collective-permute-start.43 = (bf16[2,128,128]{2,1,0:T(8,128)(2,1)S(1)}, bf16[2,128,128]{2,1,0:T(8,128)(2,1)S(1)}, u32[]{:S(2)}, u32[]{:S(2)}) collective-permute-start(bf16[2,128,128]{2,1,0:T(8,128)(2,1)S(1)} %bitcast.21), channel_id=1, source_target_pairs={{0,1},{1,0},{2,3},{3,2},{4,5},{5,4},{6,7},{7,6},{8,9},{9,8},{10,11... | collective-permute-start | bytes 196616 | tf_op jit(solution)/shard_map/ppermute | solution.py:21
  94.5 6.0 %collective-permute-start.44 = (bf16[8,2560]{1,0:T(8,128)(2,1)S(1)}, bf16[8,2560]{1,0:T(8,128)(2,1)S(1)}, u32[]{:S(2)}, u32[]{:S(2)}) collective-permute-start(bf16[8,2560]{1,0:T(8,128)(2,1)S(1)} %get-tuple-element.57), channel_id=1, source_target_pairs={{0,6},{1,7},{2,4},{3,5},{4,2},{5,3},{6,0},{7,1},{8,14},{9,15},{10,... | collective-permute-start | bytes 122888 | tf_op jit(solution)/shard_map/ppermute | solution.py:36
  96.0 4.9 %collective-permute-start.45 = (bf16[8,2560]{1,0:T(8,128)(2,1)S(1)}, bf16[8,2560]{1,0:T(8,128)(2,1)S(1)}, u32[]{:S(2)}, u32[]{:S(2)}) collective-permute-start(bf16[8,2560]{1,0:T(8,128)(2,1)S(1)} %get-tuple-element.57), channel_id=1, source_target_pairs={{0,4},{1,5},{2,6},{3,7},{4,0},{5,1},{6,2},{7,3},{8,12},{9,13},{10,... | collective-permute-start | bytes 122888 | tf_op jit(solution)/shard_map/ppermute | solution.py:36
  97.0 4.4 %collective-permute-start.46 = (bf16[8,2560]{1,0:T(8,128)(2,1)S(1)}, bf16[8,2560]{1,0:T(8,128)(2,1)S(1)}, u32[]{:S(2)}, u32[]{:S(2)}) collective-permute-start(bf16[8,2560]{1,0:T(8,128)(2,1)S(1)} %get-tuple-element.57), channel_id=1, source_target_pairs={{0,2},{1,3},{2,0},{3,1},{4,6},{5,7},{6,4},{7,5},{8,10},{9,11},{10,... | collective-permute-start | bytes 122888 | tf_op jit(solution)/shard_map/ppermute | solution.py:36
  102.6 5.5 %collective-permute-start.48 = (bf16[8,640]{1,0:T(8,128)(2,1)S(1)}, bf16[8,640]{1,0:T(8,128)(2,1)S(1)}, u32[]{:S(2)}, u32[]{:S(2)}) collective-permute-start(bf16[8,640]{1,0:T(8,128)(2,1)S(1)} %sep_rows.23), channel_id=1, source_target_pairs={{0,6},{1,7},{2,4},{3,5},{4,2},{5,3},{6,0},{7,1},{8,14},{9,15},{10,... | collective-permute-start | bytes 30728 | tf_op jit(solution)/shard_map/ppermute | solution.py:36
  105.0 4.6 %collective-permute-start.49 = (bf16[8,640]{1,0:T(8,128)(2,1)S(1)}, bf16[8,640]{1,0:T(8,128)(2,1)S(1)}, u32[]{:S(2)}, u32[]{:S(2)}) collective-permute-start(bf16[8,640]{1,0:T(8,128)(2,1)S(1)} %sep_rows.23), channel_id=1, source_target_pairs={{0,4},{1,5},{2,6},{3,7},{4,0},{5,1},{6,2},{7,3},{8,12},{9,13},{10,... | collective-permute-start | bytes 30728 | tf_op jit(solution)/shard_map/ppermute | solution.py:36
  105.6 3.9 %collective-permute-start.50 = (bf16[8,640]{1,0:T(8,128)(2,1)S(1)}, bf16[8,640]{1,0:T(8,128)(2,1)S(1)}, u32[]{:S(2)}, u32[]{:S(2)}) collective-permute-start(bf16[8,640]{1,0:T(8,128)(2,1)S(1)} %sep_rows.23), channel_id=1, source_target_pairs={{0,2},{1,3},{2,0},{3,1},{4,6},{5,7},{6,4},{7,5},{8,10},{9,11},{10,... | collective-permute-start | bytes 30728 | tf_op jit(solution)/shard_map/ppermute | solution.py:36
  110.8 6.1 %collective-permute-start.52 = (bf16[8,256]{1,0:T(8,128)(2,1)S(1)}, bf16[8,256]{1,0:T(8,128)(2,1)S(1)}, u32[]{:S(2)}, u32[]{:S(2)}) collective-permute-start(bf16[8,256]{1,0:T(8,128)(2,1)S(1)} %get-tuple-element.59), channel_id=1, source_target_pairs={{0,24},{8,16},{16,8},{24,0},{1,25},{9,17},{17,9},{25,1},{2,26},{10... | collective-permute-start | bytes 12296 | tf_op jit(solution)/shard_map/ppermute | solution.py:499
  116.9 6.2 %collective-permute-start.53 = (bf16[8,2560]{1,0:T(8,128)(2,1)S(1)}, bf16[8,2560]{1,0:T(8,128)(2,1)S(1)}, u32[]{:S(2)}, u32[]{:S(2)}) collective-permute-start(bf16[8,2560]{1,0:T(8,128)(2,1)S(1)} %get-tuple-element.61), channel_id=1, source_target_pairs={{0,6},{1,7},{2,4},{3,5},{4,2},{5,3},{6,0},{7,1},{8,14},{9,15},{10,... | collective-permute-start | bytes 122888 | tf_op jit(solution)/shard_map/ppermute | solution.py:36
  118.5 5.4 %collective-permute-start.54 = (bf16[8,2560]{1,0:T(8,128)(2,1)S(1)}, bf16[8,2560]{1,0:T(8,128)(2,1)S(1)}, u32[]{:S(2)}, u32[]{:S(2)}) collective-permute-start(bf16[8,2560]{1,0:T(8,128)(2,1)S(1)} %get-tuple-element.61), channel_id=1, source_target_pairs={{0,4},{1,5},{2,6},{3,7},{4,0},{5,1},{6,2},{7,3},{8,12},{9,13},{10,... | collective-permute-start | bytes 122888 | tf_op jit(solution)/shard_map/ppermute | solution.py:36
  119.4 4.6 %collective-permute-start.55 = (bf16[8,2560]{1,0:T(8,128)(2,1)S(1)}, bf16[8,2560]{1,0:T(8,128)(2,1)S(1)}, u32[]{:S(2)}, u32[]{:S(2)}) collective-permute-start(bf16[8,2560]{1,0:T(8,128)(2,1)S(1)} %get-tuple-element.61), channel_id=1, source_target_pairs={{0,2},{1,3},{2,0},{3,1},{4,6},{5,7},{6,4},{7,5},{8,10},{9,11},{10,... | collective-permute-start | bytes 122888 | tf_op jit(solution)/shard_map/ppermute | solution.py:36
  125.3 5.5 %collective-permute-start.57 = (bf16[8,640]{1,0:T(8,128)(2,1)S(1)}, bf16[8,640]{1,0:T(8,128)(2,1)S(1)}, u32[]{:S(2)}, u32[]{:S(2)}) collective-permute-start(bf16[8,640]{1,0:T(8,128)(2,1)S(1)} %sep_rows.25), channel_id=1, source_target_pairs={{0,6},{1,7},{2,4},{3,5},{4,2},{5,3},{6,0},{7,1},{8,14},{9,15},{10,... | collective-permute-start | bytes 30728 | tf_op jit(solution)/shard_map/ppermute | solution.py:36
  127.5 4.6 %collective-permute-start.58 = (bf16[8,640]{1,0:T(8,128)(2,1)S(1)}, bf16[8,640]{1,0:T(8,128)(2,1)S(1)}, u32[]{:S(2)}, u32[]{:S(2)}) collective-permute-start(bf16[8,640]{1,0:T(8,128)(2,1)S(1)} %sep_rows.25), channel_id=1, source_target_pairs={{0,4},{1,5},{2,6},{3,7},{4,0},{5,1},{6,2},{7,3},{8,12},{9,13},{10,... | collective-permute-start | bytes 30728 | tf_op jit(solution)/shard_map/ppermute | solution.py:36
  128.1 4.0 %collective-permute-start.59 = (bf16[8,640]{1,0:T(8,128)(2,1)S(1)}, bf16[8,640]{1,0:T(8,128)(2,1)S(1)}, u32[]{:S(2)}, u32[]{:S(2)}) collective-permute-start(bf16[8,640]{1,0:T(8,128)(2,1)S(1)} %sep_rows.25), channel_id=1, source_target_pairs={{0,2},{1,3},{2,0},{3,1},{4,6},{5,7},{6,4},{7,5},{8,10},{9,11},{10,... | collective-permute-start | bytes 30728 | tf_op jit(solution)/shard_map/ppermute | solution.py:36
  133.6 5.9 %collective-permute-start.61 = (bf16[8,256]{1,0:T(8,128)(2,1)S(1)}, bf16[8,256]{1,0:T(8,128)(2,1)S(1)}, u32[]{:S(2)}, u32[]{:S(2)}) collective-permute-start(bf16[8,256]{1,0:T(8,128)(2,1)S(1)} %get-tuple-element.63), channel_id=1, source_target_pairs={{0,8},{8,0},{16,24},{24,16},{1,9},{9,1},{17,25},{25,17},{2,10},{10... | collective-permute-start | bytes 12296 | tf_op jit(solution)/shard_map/ppermute | solution.py:499
  140.3 6.4 %collective-permute-start.62 = (bf16[8,2560]{1,0:T(8,128)(2,1)S(1)}, bf16[8,2560]{1,0:T(8,128)(2,1)S(1)}, u32[]{:S(2)}, u32[]{:S(2)}) collective-permute-start(bf16[8,2560]{1,0:T(8,128)(2,1)S(1)} %get-tuple-element.65), channel_id=1, source_target_pairs={{0,6},{1,7},{2,4},{3,5},{4,2},{5,3},{6,0},{7,1},{8,14},{9,15},{10,... | collective-permute-start | bytes 122888 | tf_op jit(solution)/shard_map/ppermute | solution.py:36
  141.9 5.4 %collective-permute-start.63 = (bf16[8,2560]{1,0:T(8,128)(2,1)S(1)}, bf16[8,2560]{1,0:T(8,128)(2,1)S(1)}, u32[]{:S(2)}, u32[]{:S(2)}) collective-permute-start(bf16[8,2560]{1,0:T(8,128)(2,1)S(1)} %get-tuple-element.65), channel_id=1, source_target_pairs={{0,4},{1,5},{2,6},{3,7},{4,0},{5,1},{6,2},{7,3},{8,12},{9,13},{10,... | collective-permute-start | bytes 122888 | tf_op jit(solution)/shard_map/ppermute | solution.py:36
  142.7 4.6 %collective-permute-start.64 = (bf16[8,2560]{1,0:T(8,128)(2,1)S(1)}, bf16[8,2560]{1,0:T(8,128)(2,1)S(1)}, u32[]{:S(2)}, u32[]{:S(2)}) collective-permute-start(bf16[8,2560]{1,0:T(8,128)(2,1)S(1)} %get-tuple-element.65), channel_id=1, source_target_pairs={{0,2},{1,3},{2,0},{3,1},{4,6},{5,7},{6,4},{7,5},{8,10},{9,11},{10,... | collective-permute-start | bytes 122888 | tf_op jit(solution)/shard_map/ppermute | solution.py:36
  149.6 5.5 %collective-permute-start.66 = (bf16[8,640]{1,0:T(8,128)(2,1)S(1)}, bf16[8,640]{1,0:T(8,128)(2,1)S(1)}, u32[]{:S(2)}, u32[]{:S(2)}) collective-permute-start(bf16[8,640]{1,0:T(8,128)(2,1)S(1)} %sep_rows.27), channel_id=1, source_target_pairs={{0,6},{1,7},{2,4},{3,5},{4,2},{5,3},{6,0},{7,1},{8,14},{9,15},{10,... | collective-permute-start | bytes 30728 | tf_op jit(solution)/shard_map/ppermute | solution.py:36
  151.8 4.6 %collective-permute-start.67 = (bf16[8,640]{1,0:T(8,128)(2,1)S(1)}, bf16[8,640]{1,0:T(8,128)(2,1)S(1)}, u32[]{:S(2)}, u32[]{:S(2)}) collective-permute-start(bf16[8,640]{1,0:T(8,128)(2,1)S(1)} %sep_rows.27), channel_id=1, source_target_pairs={{0,4},{1,5},{2,6},{3,7},{4,0},{5,1},{6,2},{7,3},{8,12},{9,13},{10,... | collective-permute-start | bytes 30728 | tf_op jit(solution)/shard_map/ppermute | solution.py:36
  (27 other events, 85.3 us)

commit v5 on v4

--- a/solution.py
+++ b/solution.py
@@ -44,6 +44,21 @@
         groups = same_core_groups()
         return lax.all_gather(block, "front", axis=1, tiled=True, axis_index_groups=groups)
     return jnp.concatenate(from_chips(block, chips), axis=1)
+
+
+def hop(block, source_layer, target_layer):
+    slots = lax.axis_size("front")
+    others = [i for i in range(lax.axis_size("layer")) if i not in (source_layer, target_layer)]
+    order = [source_layer, target_layer] + others
+    target = dict(zip(order, order[1:] + order[:1]))
+    return [
+        lax.ppermute(
+            block,
+            ("layer", "front"),
+            [(i * slots + j, target[i] * slots + (j ^ cross)) for i in target for j in range(slots)],
+        )
+        for cross in range(2)
+    ]
 
 
 def sum_chips(block, after=None):
@@ -207,11 +222,11 @@
     return jnp.concatenate([columns(own), columns(theirs)], axis=2)
 
 
-def first_spread_cells(stored, own, theirs, owner, rows):
+def first_spread_cells(stored, leaf_values, own, theirs, owner, rows):
     _, cells, _ = own.shape
     chips = owner.shape[0] // 2
 
-    def kernel(owner_ref, stored_ref, own_ref, theirs_ref, out):
+    def kernel(owner_ref, stored_ref, leaf_ref, own_ref, theirs_ref, part_out, share_out):
         @pl.when(lax.axis_index("layer") == 0)
         def _():
             for side, block in enumerate((own_ref, theirs_ref)):
@@ -220,17 +235,18 @@
                     columns = panel_columns(owner_ref, step, rows)
                     vector = stored_ref[:, pl.ds(step * rows, rows)].astype(F32)
                     value += times(vector, block[0, :, columns], block[1, :, columns], 1)
-                out[:, pl.ds(side * cells, cells)] = value
-
-    return pl.pallas_call(
-        kernel,
-        in_specs=[SMEM, VMEM, VMEM, VMEM],
-        out_specs=VMEM,
-        out_shape=jax.ShapeDtypeStruct((8, 2 * cells), F32),
+                part_out[:, pl.ds(side * cells, cells)] = value
+            share_out[...] = share_of_value(part_out[...], leaf_ref[...], None, False)
+
+    return pl.pallas_call(
+        kernel,
+        in_specs=[SMEM] + [VMEM] * 4,
+        out_specs=[VMEM, VMEM],
+        out_shape=[jax.ShapeDtypeStruct((8, 2 * cells), F32)] * 2,
         compiler_params=params(16),
         cost_estimate=cost(16 * own.size, 2 * own.size),
         name="first_spread_cells",
-    )(owner, stored, in_vmem(own), in_vmem(theirs))
+    )(owner, stored, leaf_values, in_vmem(own), in_vmem(theirs))
 
 
 def add_parts(parts, after):
@@ -320,7 +336,7 @@
 def leaf_and_gather(level, leaf, gather, couple, arrived, sources=None):
     cells = leaf[0].shape[1]
     width = gather.shape[2]
-    given = [arrived] if sources is None else [arrived, sources]
+    given = list(arrived) if sources is None else [*arrived, sources]
     mats = list(couple) + list(leaf)
 
     def kernel(*refs):
@@ -339,9 +355,10 @@
 
         @pl.when(lax.axis_index("layer") == level)
         def _():
-            source = blocks(vectors[0][...].astype(F32), matrices[:2])
+            crossed = jnp.concatenate([vectors[1][:, cells:], vectors[1][:, :cells]], axis=1)
+            source = blocks(vectors[0][...] + crossed, matrices[:2])
             if sources is not None:
-                source = vectors[1][...] - source
+                source = vectors[2][...] - source
             leaf_values = blocks(source, matrices[-2:])
             leaf_out[...] = leaf_values
             sums_out[...] = times(leaf_values, gather_ref[0], gather_ref[1], 0).astype(BF16)
@@ -389,21 +406,36 @@
     )(*given, in_vmem(sep))
 
 
-def spread_cells(level, stored, spread):
-    def kernel(stored_ref, spread_ref, out):
+def share_of_value(part, leaf_values, before, subtract):
+    first = jnp.where(lax.axis_index("front") % 2 == 0, 1.0, 0.0)
+    if subtract:
+        return first * (before - leaf_values) + part
+    return first * leaf_values - part
+
+
+def spread_cells(level, stored, spread, leaf_values, before=None, subtract=False):
+    given = [stored, leaf_values] + ([before] if subtract else [])
+
+    def kernel(*refs):
+        stored_ref, leaf_ref = refs[:2]
+        spread_ref, part_out, share_out = refs[-3:]
+
         @pl.when(lax.axis_index("layer") == level)
         def _():
-            out[...] = times(stored_ref[...].astype(F32), spread_ref[0], spread_ref[1], 0)
-
-    return pl.pallas_call(
-        kernel,
-        in_specs=[VMEM, VMEM],
-        out_specs=VMEM,
-        out_shape=jax.ShapeDtypeStruct((8, spread.shape[2]), F32),
+            part = times(stored_ref[...].astype(F32), spread_ref[0], spread_ref[1], 0)
+            part_out[...] = part
+            held = refs[2][...] if subtract else None
+            share_out[...] = share_of_value(part, leaf_ref[...], held, subtract)
+
+    return pl.pallas_call(
+        kernel,
+        in_specs=[VMEM] * (len(given) + 1),
+        out_specs=[VMEM, VMEM],
+        out_shape=[jax.ShapeDtypeStruct((8, spread.shape[2]), F32)] * 2,
         compiler_params=params(16),
         cost_estimate=cost(32 * spread.size, 2 * spread.size),
         name="spread_cells",
-    )(stored, in_vmem(spread))
+    )(*given, in_vmem(spread))
 
 
 def finish(level, leaf_values, part, theirs, before=None, subtract=False, last=False):
@@ -419,8 +451,7 @@
                 refs[-1][0, 0] = value[:4, :cells]
                 refs[-1][0, 1] = value[4:, :cells]
             else:
-                refs[-2][...] = value
-                refs[-1][...] = value.astype(BF16)
+                refs[-1][...] = value
 
         @pl.when(here)
         def _():
@@ -436,15 +467,11 @@
             def _():
                 store(refs[3][...])
 
-    if last:
-        out_shape = jax.ShapeDtypeStruct((1, 2, 4, cells), F32)
-    else:
-        out_shape = [jax.ShapeDtypeStruct(part.shape, dtype) for dtype in (F32, BF16)]
     return pl.pallas_call(
         kernel,
         in_specs=[VMEM] * len(given),
-        out_specs=VMEM if last else [VMEM, VMEM],
-        out_shape=out_shape,
+        out_specs=VMEM,
+        out_shape=jax.ShapeDtypeStruct((1, 2, 4, cells) if last else part.shape, F32),
         compiler_params=params(16),
         cost_estimate=cost(4 * part.size, 16 * part.size),
         name="finish",
@@ -492,33 +519,30 @@
     def solve(level, before, subtract=False, last=False, **given):
         leaf_values, sums = leaf_and_gather(level, leaf, gather, **given)
         stored = gather_chips(own_rows_of(level, sum_chips(sums)))
-        part = spread_cells(level, stored, spread)
-        return finish(level, leaf_values, part, pair(part), before, subtract, last)
-
-    def hop(sent, source_layer, target_layer):
-        return lax.ppermute(sent, "layer", xor_route("layer", source_layer ^ target_layer))
+        part, share = spread_cells(level, stored, spread, leaf_values, before, subtract)
+        return finish(level, leaf_values, part, pair(part), before, subtract, last), share
 
     stored = gather_chips(own_rows_of(0, sum_chips(first_sums, sep)))
     spreads = own_spread, their_spread, panel_owner[0], rows
     if rows % 128 == 0:
-        part = first_spread_cells(stored, *spreads)
+        part, share = first_spread_cells(stored, first_values, *spreads)
     else:
         spread = take_spread(*spreads)
-        part = spread_cells(0, stored, spread)
-    value, sent = finish(0, first_values, part, pair(part))
-    arrived = hop(sent, 0, 1)
-    gather = transpose_gather(own_gather, their_gather, sent)
+        part, share = spread_cells(0, stored, spread, first_values)
+    arrived = hop(share, 0, 1)
+    value = finish(0, first_values, part, pair(part))
+    gather = transpose_gather(own_gather, their_gather, share)
     if rows % 128 == 0:
-        spread = transpose_spread(*spreads, sent)
+        spread = transpose_spread(*spreads, share)
 
     for level in range(1, depth):
         if level > 1:
-            arrived = hop(sent, level - 1, level)
-        value, sent = solve(level, value, sources=sources, couple=above, arrived=arrived)
-    for level in range(depth - 2, 0, -1):
-        arrived = hop(sent, level + 1, level)
-        value, sent = solve(level, value, True, couple=below, arrived=arrived)
-    return solve(0, value, True, True, couple=below, arrived=hop(sent, 1, 0))
+            arrived = hop(share, level - 1, level)
+        value, share = solve(level, value, sources=sources, couple=above, arrived=arrived)
+    for level in range(depth - 2, -1, -1):
+        arrived = hop(share, level + 1, level)
+        value, share = solve(level, value, True, level == 0, couple=below, arrived=arrived)
+    return value
 
 
 def solution(mesh):

time: 159 us -> 156 us (0.981)
  waiting for transfers between devices: 60.8 us -> 56.4 us
    ppermute x22, waiting for transfers between devices: 15 us -> 10.8 us  [pair(): return lax.ppermute(block, 'front', xor_route('front', 1))]
    ppermute x42, waiting for transfers between devices: 32.6 us -> 30.1 us  [from_chips(): lax.ppermute(block, 'front', xor_route('front', 2 * (chips - step)))]
    ppermute x6 -> x12, waiting for transfers between devices: 13.2 us -> 15.5 us  [hop(): lax.ppermute(block, ('layer', 'front'), [(i * slots + j, target[i] * slot...]
    ppermute x6 -> x12, starting transfers between devices: 13.6 us -> 14.2 us  [hop(): lax.ppermute(block, ('layer', 'front'), [(i * slots + j, target[i] * slot...]
  transfers between devices with their start and end apart: 70 -> 76, of which waited for: 49 -> 43; matrix products, arithmetic and copies ran while one was open for 0% -> 0% of each run, Pallas kernels for 7% -> 8%
where the time goes in v5:
time: 156 us
  starting transfers between devices  80.8 us (52%)
  waiting for transfers between devices  56.4 us (36%)
  Pallas kernels  18.1 us (12%)
    ppermute x42, starting transfers between devices, from_chips(): lax.ppermute(block, 'front', xor_route('front', 2 * (chips - step)))  62.7 us
    ppermute x42, waiting for transfers between devices, from_chips(): lax.ppermute(block, 'front', xor_route('front', 2 * (chips - step)))  30.1 us
    ppermute x12, waiting for transfers between devices, hop(): lax.ppermute(block, ('layer', 'front'), [(i * slots + j, target[i] * slot...  15.5 us
    ppermute x12, starting transfers between devices, hop(): lax.ppermute(block, ('layer', 'front'), [(i * slots + j, target[i] * slot...  14.2 us
    ppermute x22, waiting for transfers between devices, pair(): return lax.ppermute(block, 'front', xor_route('front', 1))  10.8 us
    pallas_call x1, Pallas kernels, transpose_sep(): pl.pallas_call(kernel, in_specs=[ANY, ANY], out_specs=VMEM, out_shape=plt...  5.35 us
    pallas_call x14, Pallas kernels, sep_rows(): pl.pallas_call(kernel, in_specs=[VMEM] * (len(given) + 1), out_specs=VMEM...  3.9 us
    ppermute x22, starting transfers between devices, pair(): return lax.ppermute(block, 'front', xor_route('front', 1))  3.85 us
  transfers between devices with their start and end apart: 76, of which 43 were waited for; matrix products, arithmetic and copies ran while one was open for 0% of the time, Pallas kernels for 8%

profile of v5, /device:TPU:0, one launch (start us, length us, event | category | flops | bytes accessed | tf_op | source)
XLA Modules:
  0.0 155.9 jit_solution(296610815771761212)
XLA Ops:
  0.0 2.6 %first_leaf_and_gather.1 = (f32[8,128]{1,0:T(8,128)S(1)}, f32[8,2560]{1,0:T(8,128)S(1)}, bf16[8,2560]{1,0:T(8,128)(2,1)S(1)}, bf16[2,5120,128]{2,1,0:T(8,128)(2,1)S(1)}, bf16[2,128,5120]{2,1,0:T(8,128)(2,1)S(1)}) custom-call(f32[2,4,128]{2,1,0:T(4,128)} %bitcast.30, bf16[2,128,128]{2,1,0:T(8,128)(2,1)} %bitcast.9, bf16[2,5120,128]{2,1,0:T(8,128)(2,1)} %bitcast.28, ...), custom_call_target="tpu_custom_call" | custom-call | flops 20971520 | bytes 2621440 | tf_op jit(solution)/shard_map/first_leaf_and_gather/pallas_call | solution.py:314
  4.6 4.9 %collective-permute-start.1 = (bf16[8,2560]{1,0:T(8,128)(2,1)S(1)}, bf16[8,2560]{1,0:T(8,128)(2,1)S(1)}, u32[]{:S(2)}, u32[]{:S(2)}) collective-permute-start(bf16[8,2560]{1,0:T(8,128)(2,1)S(1)} %add_convert_fusion.6._.refs_0_.refs_2_), channel_id=1, source_target_pairs={{0,6},{1,7},{2,4},{3,5},{4,2},{5,3},{6,0},{7,1},{8,14},{9,15},{10,... | collective-permute-start | bytes 122888 | tf_op jit(solution)/shard_map/ppermute | solution.py:36
  10.2 5.3 %transpose_sep.1.refs_4_.refs_1_.refs_2_ = bf16[2,5120,640]{2,1,0:T(8,128)(2,1)S(1)} custom-call(bf16[2,640,5120]{2,1,0:T(8,128)(2,1)} %bitcast.27, bf16[8,2560]{1,0:T(8,128)(2,1)S(1)} %add_convert_fusion.6._.refs_0_.refs_2_), custom_call_target="tpu_custom_call" | custom-call | bytes 26214400 | tf_op jit(solution)/shard_map/transpose_sep/pallas_call | solution.py:124
  18.2 3.9 %collective-permute-start.5 = (bf16[8,640]{1,0:T(8,128)(2,1)S(1)}, bf16[8,640]{1,0:T(8,128)(2,1)S(1)}, u32[]{:S(2)}, u32[]{:S(2)}) collective-permute-start(bf16[8,640]{1,0:T(8,128)(2,1)S(1)} %sep_rows.15), channel_id=1, source_target_pairs={{0,6},{1,7},{2,4},{3,5},{4,2},{5,3},{6,0},{7,1},{8,14},{9,15},{10,... | collective-permute-start | bytes 30728 | tf_op jit(solution)/shard_map/ppermute | solution.py:36
  23.7 2.9 %collective-permute-done.6 = bf16[8,640]{1,0:T(8,128)(2,1)S(1)} collective-permute-done((bf16[8,640]{1,0:T(8,128)(2,1)S(1)}, bf16[8,640]{1,0:T(8,128)(2,1)S(1)}, u32[]{:S(2)}, u32[]{:S(2)}) %collective-permute-start.6) | collective-permute-done | bytes 10272 | tf_op jit(solution)/shard_map/ppermute | solution.py:36
  27.2 1.5 first_spread_cells.1
  29.8 3.5 %collective-permute-done.10.refs_0_ = f32[8,256]{1,0:T(8,128)S(1)} collective-permute-done((f32[8,256]{1,0:T(8,128)S(1)}, f32[8,256]{1,0:T(8,128)S(1)}, u32[]{:S(2)}, u32[]{:S(2)}) %collective-permute-start.10) | collective-permute-done | bytes 8224 | tf_op jit(solution)/shard_map/ppermute | solution.py:55
  34.8 2.8 %collective-permute-start.18 = (bf16[8,2560]{1,0:T(8,128)(2,1)S(1)}, bf16[8,2560]{1,0:T(8,128)(2,1)S(1)}, u32[]{:S(2)}, u32[]{:S(2)}) collective-permute-start(bf16[8,2560]{1,0:T(8,128)(2,1)S(1)} %get-tuple-element.45), channel_id=1, source_target_pairs={{0,2},{1,3},{2,0},{3,1},{4,6},{5,7},{6,4},{7,5},{8,10},{9,11},{10,... | collective-permute-start | bytes 122888 | tf_op jit(solution)/shard_map/ppermute | solution.py:36
  37.6 1.8 %collective-permute-done.16 = bf16[8,2560]{1,0:T(8,128)(2,1)S(1)} collective-permute-done((bf16[8,2560]{1,0:T(8,128)(2,1)S(1)}, bf16[8,2560]{1,0:T(8,128)(2,1)S(1)}, u32[]{:S(2)}, u32[]{:S(2)}) %collective-permute-start.16) | collective-permute-done | bytes 40992 | tf_op jit(solution)/shard_map/ppermute | solution.py:36
  41.5 2.1 %collective-permute-start.20 = (bf16[8,640]{1,0:T(8,128)(2,1)S(1)}, bf16[8,640]{1,0:T(8,128)(2,1)S(1)}, u32[]{:S(2)}, u32[]{:S(2)}) collective-permute-start(bf16[8,640]{1,0:T(8,128)(2,1)S(1)} %sep_rows.17), channel_id=1, source_target_pairs={{0,6},{1,7},{2,4},{3,5},{4,2},{5,3},{6,0},{7,1},{8,14},{9,15},{10,... | collective-permute-start | bytes 30728 | tf_op jit(solution)/shard_map/ppermute | solution.py:36
  44.4 1.5 collective-permute-start.22
  48.4 1.6 %collective-permute-start.23 = (f32[8,256]{1,0:T(8,128)S(1)}, f32[8,256]{1,0:T(8,128)S(1)}, u32[]{:S(2)}, u32[]{:S(2)}) collective-permute-start(f32[8,256]{1,0:T(8,128)S(1)} %get-tuple-element.47), channel_id=1, source_target_pairs={{8,16},{9,17},{10,18},{11,19},{12,20},{13,21},{14,22},{15,23},{16,... | collective-permute-start | bytes 24584 | tf_op jit(solution)/shard_map/ppermute | solution.py:55
  50.0 2.1 %collective-permute-done.23.refs_0_ = f32[8,256]{1,0:T(8,128)S(1)} collective-permute-done((f32[8,256]{1,0:T(8,128)S(1)}, f32[8,256]{1,0:T(8,128)S(1)}, u32[]{:S(2)}, u32[]{:S(2)}) %collective-permute-start.23) | collective-permute-done | bytes 8224 | tf_op jit(solution)/shard_map/ppermute | solution.py:55
  53.0 1.8 %collective-permute-start.25 = (bf16[8,2560]{1,0:T(8,128)(2,1)S(1)}, bf16[8,2560]{1,0:T(8,128)(2,1)S(1)}, u32[]{:S(2)}, u32[]{:S(2)}) collective-permute-start(bf16[8,2560]{1,0:T(8,128)(2,1)S(1)} %get-tuple-element.48), channel_id=1, source_target_pairs={{0,6},{1,7},{2,4},{3,5},{4,2},{5,3},{6,0},{7,1},{8,14},{9,15},{10,... | collective-permute-start | bytes 122888 | tf_op jit(solution)/shard_map/ppermute | solution.py:36
  55.7 1.8 %collective-permute-start.27 = (bf16[8,2560]{1,0:T(8,128)(2,1)S(1)}, bf16[8,2560]{1,0:T(8,128)(2,1)S(1)}, u32[]{:S(2)}, u32[]{:S(2)}) collective-permute-start(bf16[8,2560]{1,0:T(8,128)(2,1)S(1)} %get-tuple-element.48), channel_id=1, source_target_pairs={{0,2},{1,3},{2,0},{3,1},{4,6},{5,7},{6,4},{7,5},{8,10},{9,11},{10,... | collective-permute-start | bytes 122888 | tf_op jit(solution)/shard_map/ppermute | solution.py:36
  57.4 1.6 collective-permute-done.25
  61.4 2.0 %collective-permute-start.29 = (bf16[8,640]{1,0:T(8,128)(2,1)S(1)}, bf16[8,640]{1,0:T(8,128)(2,1)S(1)}, u32[]{:S(2)}, u32[]{:S(2)}) collective-permute-start(bf16[8,640]{1,0:T(8,128)(2,1)S(1)} %sep_rows.19), channel_id=1, source_target_pairs={{0,6},{1,7},{2,4},{3,5},{4,2},{5,3},{6,0},{7,1},{8,14},{9,15},{10,... | collective-permute-start | bytes 30728 | tf_op jit(solution)/shard_map/ppermute | solution.py:36
  64.2 1.6 %collective-permute-start.31 = (bf16[8,640]{1,0:T(8,128)(2,1)S(1)}, bf16[8,640]{1,0:T(8,128)(2,1)S(1)}, u32[]{:S(2)}, u32[]{:S(2)}) collective-permute-start(bf16[8,640]{1,0:T(8,128)(2,1)S(1)} %sep_rows.19), channel_id=1, source_target_pairs={{0,2},{1,3},{2,0},{3,1},{4,6},{5,7},{6,4},{7,5},{8,10},{9,11},{10,... | collective-permute-start | bytes 30728 | tf_op jit(solution)/shard_map/ppermute | solution.py:36
  69.3 2.2 %collective-permute-start.33 = (f32[8,256]{1,0:T(8,128)S(1)}, f32[8,256]{1,0:T(8,128)S(1)}, u32[]{:S(2)}, u32[]{:S(2)}) collective-permute-start(f32[8,256]{1,0:T(8,128)S(1)} %get-tuple-element.50), channel_id=1, source_target_pairs={{16,25},{17,24},{18,27},{19,26},{20,29},{21,28},{22,31},{23,30},{2... | collective-permute-start | bytes 24584 | tf_op jit(solution)/shard_map/ppermute | solution.py:55
  73.2 1.6 %collective-permute-start.34 = (bf16[8,2560]{1,0:T(8,128)(2,1)S(1)}, bf16[8,2560]{1,0:T(8,128)(2,1)S(1)}, u32[]{:S(2)}, u32[]{:S(2)}) collective-permute-start(bf16[8,2560]{1,0:T(8,128)(2,1)S(1)} %get-tuple-element.51), channel_id=1, source_target_pairs={{0,6},{1,7},{2,4},{3,5},{4,2},{5,3},{6,0},{7,1},{8,14},{9,15},{10,... | collective-permute-start | bytes 122888 | tf_op jit(solution)/shard_map/ppermute | solution.py:36
  75.9 1.7 %collective-permute-start.36 = (bf16[8,2560]{1,0:T(8,128)(2,1)S(1)}, bf16[8,2560]{1,0:T(8,128)(2,1)S(1)}, u32[]{:S(2)}, u32[]{:S(2)}) collective-permute-start(bf16[8,2560]{1,0:T(8,128)(2,1)S(1)} %get-tuple-element.51), channel_id=1, source_target_pairs={{0,2},{1,3},{2,0},{3,1},{4,6},{5,7},{6,4},{7,5},{8,10},{9,11},{10,... | collective-permute-start | bytes 122888 | tf_op jit(solution)/shard_map/ppermute | solution.py:36
  77.6 1.8 %collective-permute-done.34 = bf16[8,2560]{1,0:T(8,128)(2,1)S(1)} collective-permute-done((bf16[8,2560]{1,0:T(8,128)(2,1)S(1)}, bf16[8,2560]{1,0:T(8,128)(2,1)S(1)}, u32[]{:S(2)}, u32[]{:S(2)}) %collective-permute-start.34) | collective-permute-done | bytes 40992 | tf_op jit(solution)/shard_map/ppermute | solution.py:36
  79.5 1.6 %collective-permute-done.35 = bf16[8,2560]{1,0:T(8,128)(2,1)S(1)} collective-permute-done((bf16[8,2560]{1,0:T(8,128)(2,1)S(1)}, bf16[8,2560]{1,0:T(8,128)(2,1)S(1)}, u32[]{:S(2)}, u32[]{:S(2)}) %collective-permute-start.35) | collective-permute-done | bytes 40992 | tf_op jit(solution)/shard_map/ppermute | solution.py:36
  82.4 2.0 %collective-permute-start.38 = (bf16[8,640]{1,0:T(8,128)(2,1)S(1)}, bf16[8,640]{1,0:T(8,128)(2,1)S(1)}, u32[]{:S(2)}, u32[]{:S(2)}) collective-permute-start(bf16[8,640]{1,0:T(8,128)(2,1)S(1)} %sep_rows.21), channel_id=1, source_target_pairs={{0,6},{1,7},{2,4},{3,5},{4,2},{5,3},{6,0},{7,1},{8,14},{9,15},{10,... | collective-permute-start | bytes 30728 | tf_op jit(solution)/shard_map/ppermute | solution.py:36
  84.4 2.4 %collective-permute-start.40 = (bf16[8,640]{1,0:T(8,128)(2,1)S(1)}, bf16[8,640]{1,0:T(8,128)(2,1)S(1)}, u32[]{:S(2)}, u32[]{:S(2)}) collective-permute-start(bf16[8,640]{1,0:T(8,128)(2,1)S(1)} %sep_rows.21), channel_id=1, source_target_pairs={{0,2},{1,3},{2,0},{3,1},{4,6},{5,7},{6,4},{7,5},{8,10},{9,11},{10,... | collective-permute-start | bytes 30728 | tf_op jit(solution)/shard_map/ppermute | solution.py:36
  89.0 2.6 %collective-permute-start.41 = (f32[8,256]{1,0:T(8,128)S(1)}, f32[8,256]{1,0:T(8,128)S(1)}, u32[]{:S(2)}, u32[]{:S(2)}) collective-permute-start(f32[8,256]{1,0:T(8,128)S(1)} %get-tuple-element.53), channel_id=1, source_target_pairs={{24,16},{25,17},{26,18},{27,19},{28,20},{29,21},{30,22},{31,23},{1... | collective-permute-start | bytes 24584 | tf_op jit(solution)/shard_map/ppermute | solution.py:55
  91.6 1.8 %collective-permute-done.41.refs_0_ = f32[8,256]{1,0:T(8,128)S(1)} collective-permute-done((f32[8,256]{1,0:T(8,128)S(1)}, f32[8,256]{1,0:T(8,128)S(1)}, u32[]{:S(2)}, u32[]{:S(2)}) %collective-permute-start.41) | collective-permute-done | bytes 8224 | tf_op jit(solution)/shard_map/ppermute | solution.py:55
  94.7 1.6 %collective-permute-start.44 = (bf16[8,2560]{1,0:T(8,128)(2,1)S(1)}, bf16[8,2560]{1,0:T(8,128)(2,1)S(1)}, u32[]{:S(2)}, u32[]{:S(2)}) collective-permute-start(bf16[8,2560]{1,0:T(8,128)(2,1)S(1)} %get-tuple-element.54), channel_id=1, source_target_pairs={{0,6},{1,7},{2,4},{3,5},{4,2},{5,3},{6,0},{7,1},{8,14},{9,15},{10,... | collective-permute-start | bytes 122888 | tf_op jit(solution)/shard_map/ppermute | solution.py:36
  97.3 1.7 %collective-permute-start.46 = (bf16[8,2560]{1,0:T(8,128)(2,1)S(1)}, bf16[8,2560]{1,0:T(8,128)(2,1)S(1)}, u32[]{:S(2)}, u32[]{:S(2)}) collective-permute-start(bf16[8,2560]{1,0:T(8,128)(2,1)S(1)} %get-tuple-element.54), channel_id=1, source_target_pairs={{0,2},{1,3},{2,0},{3,1},{4,6},{5,7},{6,4},{7,5},{8,10},{9,11},{10,... | collective-permute-start | bytes 122888 | tf_op jit(solution)/shard_map/ppermute | solution.py:36
  99.0 1.7 %collective-permute-done.44 = bf16[8,2560]{1,0:T(8,128)(2,1)S(1)} collective-permute-done((bf16[8,2560]{1,0:T(8,128)(2,1)S(1)}, bf16[8,2560]{1,0:T(8,128)(2,1)S(1)}, u32[]{:S(2)}, u32[]{:S(2)}) %collective-permute-start.44) | collective-permute-done | bytes 40992 | tf_op jit(solution)/shard_map/ppermute | solution.py:36
  102.9 2.3 %collective-permute-start.48 = (bf16[8,640]{1,0:T(8,128)(2,1)S(1)}, bf16[8,640]{1,0:T(8,128)(2,1)S(1)}, u32[]{:S(2)}, u32[]{:S(2)}) collective-permute-start(bf16[8,640]{1,0:T(8,128)(2,1)S(1)} %sep_rows.23), channel_id=1, source_target_pairs={{0,6},{1,7},{2,4},{3,5},{4,2},{5,3},{6,0},{7,1},{8,14},{9,15},{10,... | collective-permute-start | bytes 30728 | tf_op jit(solution)/shard_map/ppermute | solution.py:36
  105.8 1.5 collective-permute-start.50
  109.9 1.7 %collective-permute-start.55 = (f32[8,256]{1,0:T(8,128)S(1)}, f32[8,256]{1,0:T(8,128)S(1)}, u32[]{:S(2)}, u32[]{:S(2)}) collective-permute-start(f32[8,256]{1,0:T(8,128)S(1)} %get-tuple-element.60), channel_id=1, source_target_pairs={{16,8},{17,9},{18,10},{19,11},{20,12},{21,13},{22,14},{23,15},{8,0... | collective-permute-start | bytes 24584 | tf_op jit(solution)/shard_map/ppermute | solution.py:55
  111.6 2.1 %collective-permute-start.56 = (f32[8,256]{1,0:T(8,128)S(1)}, f32[8,256]{1,0:T(8,128)S(1)}, u32[]{:S(2)}, u32[]{:S(2)}) collective-permute-start(f32[8,256]{1,0:T(8,128)S(1)} %get-tuple-element.60), channel_id=1, source_target_pairs={{16,9},{17,8},{18,11},{19,10},{20,13},{21,12},{22,15},{23,14},{8,1... | collective-permute-start | bytes 24584 | tf_op jit(solution)/shard_map/ppermute | solution.py:55
  113.7 1.4 collective-permute-done.56.refs_1_
  115.1 2.0 %collective-permute-start.57 = (bf16[8,2560]{1,0:T(8,128)(2,1)S(1)}, bf16[8,2560]{1,0:T(8,128)(2,1)S(1)}, u32[]{:S(2)}, u32[]{:S(2)}) collective-permute-start(bf16[8,2560]{1,0:T(8,128)(2,1)S(1)} %get-tuple-element.61), channel_id=1, source_target_pairs={{0,6},{1,7},{2,4},{3,5},{4,2},{5,3},{6,0},{7,1},{8,14},{9,15},{10,... | collective-permute-start | bytes 122888 | tf_op jit(solution)/shard_map/ppermute | solution.py:36
  117.6 1.8 %collective-permute-start.59 = (bf16[8,2560]{1,0:T(8,128)(2,1)S(1)}, bf16[8,2560]{1,0:T(8,128)(2,1)S(1)}, u32[]{:S(2)}, u32[]{:S(2)}) collective-permute-start(bf16[8,2560]{1,0:T(8,128)(2,1)S(1)} %get-tuple-element.61), channel_id=1, source_target_pairs={{0,2},{1,3},{2,0},{3,1},{4,6},{5,7},{6,4},{7,5},{8,10},{9,11},{10,... | collective-permute-start | bytes 122888 | tf_op jit(solution)/shard_map/ppermute | solution.py:36
  119.5 1.7 %collective-permute-done.57 = bf16[8,2560]{1,0:T(8,128)(2,1)S(1)} collective-permute-done((bf16[8,2560]{1,0:T(8,128)(2,1)S(1)}, bf16[8,2560]{1,0:T(8,128)(2,1)S(1)}, u32[]{:S(2)}, u32[]{:S(2)}) %collective-permute-start.57) | collective-permute-done | bytes 40992 | tf_op jit(solution)/shard_map/ppermute | solution.py:36
  121.2 1.6 %collective-permute-done.58 = bf16[8,2560]{1,0:T(8,128)(2,1)S(1)} collective-permute-done((bf16[8,2560]{1,0:T(8,128)(2,1)S(1)}, bf16[8,2560]{1,0:T(8,128)(2,1)S(1)}, u32[]{:S(2)}, u32[]{:S(2)}) %collective-permute-start.58) | collective-permute-done | bytes 40992 | tf_op jit(solution)/shard_map/ppermute | solution.py:36
  124.2 1.8 %collective-permute-start.61 = (bf16[8,640]{1,0:T(8,128)(2,1)S(1)}, bf16[8,640]{1,0:T(8,128)(2,1)S(1)}, u32[]{:S(2)}, u32[]{:S(2)}) collective-permute-start(bf16[8,640]{1,0:T(8,128)(2,1)S(1)} %sep_rows.25), channel_id=1, source_target_pairs={{0,6},{1,7},{2,4},{3,5},{4,2},{5,3},{6,0},{7,1},{8,14},{9,15},{10,... | collective-permute-start | bytes 30728 | tf_op jit(solution)/shard_map/ppermute | solution.py:36
  126.3 2.3 %collective-permute-start.63 = (bf16[8,640]{1,0:T(8,128)(2,1)S(1)}, bf16[8,640]{1,0:T(8,128)(2,1)S(1)}, u32[]{:S(2)}, u32[]{:S(2)}) collective-permute-start(bf16[8,640]{1,0:T(8,128)(2,1)S(1)} %sep_rows.25), channel_id=1, source_target_pairs={{0,2},{1,3},{2,0},{3,1},{4,6},{5,7},{6,4},{7,5},{8,10},{9,11},{10,... | collective-permute-start | bytes 30728 | tf_op jit(solution)/shard_map/ppermute | solution.py:36
  130.6 2.0 %collective-permute-start.65 = (f32[8,256]{1,0:T(8,128)S(1)}, f32[8,256]{1,0:T(8,128)S(1)}, u32[]{:S(2)}, u32[]{:S(2)}) collective-permute-start(f32[8,256]{1,0:T(8,128)S(1)} %get-tuple-element.64), channel_id=1, source_target_pairs={{8,0},{9,1},{10,2},{11,3},{12,4},{13,5},{14,6},{15,7},{0,16},{1,17... | collective-permute-start | bytes 24584 | tf_op jit(solution)/shard_map/ppermute | solution.py:55
  133.1 2.8 %collective-permute-done.65.refs_0_ = f32[8,256]{1,0:T(8,128)S(1)} collective-permute-done((f32[8,256]{1,0:T(8,128)S(1)}, f32[8,256]{1,0:T(8,128)S(1)}, u32[]{:S(2)}, u32[]{:S(2)}) %collective-permute-start.65) | collective-permute-done | bytes 8224 | tf_op jit(solution)/shard_map/ppermute | solution.py:55
  136.6 1.8 %collective-permute-start.67 = (bf16[8,2560]{1,0:T(8,128)(2,1)S(1)}, bf16[8,2560]{1,0:T(8,128)(2,1)S(1)}, u32[]{:S(2)}, u32[]{:S(2)}) collective-permute-start(bf16[8,2560]{1,0:T(8,128)(2,1)S(1)} %get-tuple-element.66), channel_id=1, source_target_pairs={{0,6},{1,7},{2,4},{3,5},{4,2},{5,3},{6,0},{7,1},{8,14},{9,15},{10,... | collective-permute-start | bytes 122888 | tf_op jit(solution)/shard_map/ppermute | solution.py:36
  139.5 1.5 collective-permute-start.69
  141.0 1.8 %collective-permute-done.67 = bf16[8,2560]{1,0:T(8,128)(2,1)S(1)} collective-permute-done((bf16[8,2560]{1,0:T(8,128)(2,1)S(1)}, bf16[8,2560]{1,0:T(8,128)(2,1)S(1)}, u32[]{:S(2)}, u32[]{:S(2)}) %collective-permute-start.67) | collective-permute-done | bytes 40992 | tf_op jit(solution)/shard_map/ppermute | solution.py:36
  146.4 2.0 %collective-permute-start.71 = (bf16[8,640]{1,0:T(8,128)(2,1)S(1)}, bf16[8,640]{1,0:T(8,128)(2,1)S(1)}, u32[]{:S(2)}, u32[]{:S(2)}) collective-permute-start(bf16[8,640]{1,0:T(8,128)(2,1)S(1)} %sep_rows.27), channel_id=1, source_target_pairs={{0,6},{1,7},{2,4},{3,5},{4,2},{5,3},{6,0},{7,1},{8,14},{9,15},{10,... | collective-permute-start | bytes 30728 | tf_op jit(solution)/shard_map/ppermute | solution.py:36
  148.8 2.1 %collective-permute-start.73 = (bf16[8,640]{1,0:T(8,128)(2,1)S(1)}, bf16[8,640]{1,0:T(8,128)(2,1)S(1)}, u32[]{:S(2)}, u32[]{:S(2)}) collective-permute-start(bf16[8,640]{1,0:T(8,128)(2,1)S(1)} %sep_rows.27), channel_id=1, source_target_pairs={{0,2},{1,3},{2,0},{3,1},{4,6},{5,7},{6,4},{7,5},{8,10},{9,11},{10,... | collective-permute-start | bytes 30728 | tf_op jit(solution)/shard_map/ppermute | solution.py:36
  (171 shorter events, 52.9 us)
Async XLA Ops:
  4.1 23.1 %collective-permute-start.9 = (bf16[2,128,5120]{2,1,0:T(8,128)(2,1)S(1)}, bf16[2,128,5120]{2,1,0:T(8,128)(2,1)S(1)}, u32[]{:S(2)}, u32[]{:S(2)}) collective-permute-start(bf16[2,128,5120]{2,1,0:T(8,128)(2,1)S(1)} %get-tuple-element.42.own_ref), channel_id=1, source_target_pairs={{0,1},{1,0},{2,3},{3,2},{4,5},{5,4},{6,7},{7,6},{8,9},{9,8},{10,11... | collective-permute-start | bytes 7864328 | tf_op jit(solution)/shard_map/ppermute | solution.py:21
  4.5 24.5 %collective-permute-start.15 = (bf16[2,5120,128]{2,1,0:T(8,128)(2,1)S(1)}, bf16[2,5120,128]{2,1,0:T(8,128)(2,1)S(1)}, u32[]{:S(2)}, u32[]{:S(2)}) collective-permute-start(bf16[2,5120,128]{2,1,0:T(8,128)(2,1)S(1)} %get-tuple-element.44.own_ref), channel_id=1, source_target_pairs={{0,1},{1,0},{2,3},{3,2},{4,5},{5,4},{6,7},{7,6},{8,9},{9,8},{10,11... | collective-permute-start | bytes 7864328 | tf_op jit(solution)/shard_map/ppermute | solution.py:21
  4.6 10.9 %collective-permute-start.1 = (bf16[8,2560]{1,0:T(8,128)(2,1)S(1)}, bf16[8,2560]{1,0:T(8,128)(2,1)S(1)}, u32[]{:S(2)}, u32[]{:S(2)}) collective-permute-start(bf16[8,2560]{1,0:T(8,128)(2,1)S(1)} %add_convert_fusion.6._.refs_0_.refs_2_), channel_id=1, source_target_pairs={{0,6},{1,7},{2,4},{3,5},{4,2},{5,3},{6,0},{7,1},{8,14},{9,15},{10,... | collective-permute-start | bytes 122888 | tf_op jit(solution)/shard_map/ppermute | solution.py:36
  9.6 6.0 %collective-permute-start.2 = (bf16[8,2560]{1,0:T(8,128)(2,1)S(1)}, bf16[8,2560]{1,0:T(8,128)(2,1)S(1)}, u32[]{:S(2)}, u32[]{:S(2)}) collective-permute-start(bf16[8,2560]{1,0:T(8,128)(2,1)S(1)} %add_convert_fusion.6._.refs_0_.refs_2_), channel_id=1, source_target_pairs={{0,4},{1,5},{2,6},{3,7},{4,0},{5,1},{6,2},{7,3},{8,12},{9,13},{10,... | collective-permute-start | bytes 122888 | tf_op jit(solution)/shard_map/ppermute | solution.py:36
  9.6 6.0 %collective-permute-start.3 = (bf16[8,2560]{1,0:T(8,128)(2,1)S(1)}, bf16[8,2560]{1,0:T(8,128)(2,1)S(1)}, u32[]{:S(2)}, u32[]{:S(2)}) collective-permute-start(bf16[8,2560]{1,0:T(8,128)(2,1)S(1)} %add_convert_fusion.6._.refs_0_.refs_2_), channel_id=1, source_target_pairs={{0,2},{1,3},{2,0},{3,1},{4,6},{5,7},{6,4},{7,5},{8,10},{9,11},{10,... | collective-permute-start | bytes 122888 | tf_op jit(solution)/shard_map/ppermute | solution.py:36
  15.5 6.5 %collective-permute-start.8 = (f32[8,128]{1,0:T(8,128)S(1)}, f32[8,128]{1,0:T(8,128)S(1)}, u32[]{:S(2)}, u32[]{:S(2)}) collective-permute-start(f32[8,128]{1,0:T(8,128)S(1)} %get-tuple-element.39), channel_id=1, source_target_pairs={{0,1},{1,0},{2,3},{3,2},{4,5},{5,4},{6,7},{7,6},{8,9},{9,8},{10,11... | collective-permute-start | bytes 12296 | tf_op jit(solution)/shard_map/ppermute | solution.py:21
  18.2 5.5 %collective-permute-start.5 = (bf16[8,640]{1,0:T(8,128)(2,1)S(1)}, bf16[8,640]{1,0:T(8,128)(2,1)S(1)}, u32[]{:S(2)}, u32[]{:S(2)}) collective-permute-start(bf16[8,640]{1,0:T(8,128)(2,1)S(1)} %sep_rows.15), channel_id=1, source_target_pairs={{0,6},{1,7},{2,4},{3,5},{4,2},{5,3},{6,0},{7,1},{8,14},{9,15},{10,... | collective-permute-start | bytes 30728 | tf_op jit(solution)/shard_map/ppermute | solution.py:36
  22.1 4.6 %collective-permute-start.6 = (bf16[8,640]{1,0:T(8,128)(2,1)S(1)}, bf16[8,640]{1,0:T(8,128)(2,1)S(1)}, u32[]{:S(2)}, u32[]{:S(2)}) collective-permute-start(bf16[8,640]{1,0:T(8,128)(2,1)S(1)} %sep_rows.15), channel_id=1, source_target_pairs={{0,4},{1,5},{2,6},{3,7},{4,0},{5,1},{6,2},{7,3},{8,12},{9,13},{10,... | collective-permute-start | bytes 30728 | tf_op jit(solution)/shard_map/ppermute | solution.py:36
  22.1 4.6 %collective-permute-start.7 = (bf16[8,640]{1,0:T(8,128)(2,1)S(1)}, bf16[8,640]{1,0:T(8,128)(2,1)S(1)}, u32[]{:S(2)}, u32[]{:S(2)}) collective-permute-start(bf16[8,640]{1,0:T(8,128)(2,1)S(1)} %sep_rows.15), channel_id=1, source_target_pairs={{0,2},{1,3},{2,0},{3,1},{4,6},{5,7},{6,4},{7,5},{8,10},{9,11},{10,... | collective-permute-start | bytes 30728 | tf_op jit(solution)/shard_map/ppermute | solution.py:36
  23.7 6.0 %collective-permute-start.14 = (bf16[2,128,128]{2,1,0:T(8,128)(2,1)S(1)}, bf16[2,128,128]{2,1,0:T(8,128)(2,1)S(1)}, u32[]{:S(2)}, u32[]{:S(2)}) collective-permute-start(bf16[2,128,128]{2,1,0:T(8,128)(2,1)S(1)} %bitcast.10), channel_id=1, source_target_pairs={{0,1},{1,0},{2,3},{3,2},{4,5},{5,4},{6,7},{7,6},{8,9},{9,8},{10,11... | collective-permute-start | bytes 196616 | tf_op jit(solution)/shard_map/ppermute | solution.py:21
  28.7 4.6 %collective-permute-start.10 = (f32[8,256]{1,0:T(8,128)S(1)}, f32[8,256]{1,0:T(8,128)S(1)}, u32[]{:S(2)}, u32[]{:S(2)}) collective-permute-start(f32[8,256]{1,0:T(8,128)S(1)} %get-tuple-element.43._), channel_id=1, source_target_pairs={{0,8},{1,9},{2,10},{3,11},{4,12},{5,13},{6,14},{7,15},{8,16},{9,17... | collective-permute-start | bytes 24584 | tf_op jit(solution)/shard_map/ppermute | solution.py:55
  28.7 4.5 %collective-permute-start.11 = (f32[8,256]{1,0:T(8,128)S(1)}, f32[8,256]{1,0:T(8,128)S(1)}, u32[]{:S(2)}, u32[]{:S(2)}) collective-permute-start(f32[8,256]{1,0:T(8,128)S(1)} %get-tuple-element.43._), channel_id=1, source_target_pairs={{0,9},{1,8},{2,11},{3,10},{4,13},{5,12},{6,15},{7,14},{8,17},{9,16... | collective-permute-start | bytes 24584 | tf_op jit(solution)/shard_map/ppermute | solution.py:55
  33.2 6.2 %collective-permute-start.16 = (bf16[8,2560]{1,0:T(8,128)(2,1)S(1)}, bf16[8,2560]{1,0:T(8,128)(2,1)S(1)}, u32[]{:S(2)}, u32[]{:S(2)}) collective-permute-start(bf16[8,2560]{1,0:T(8,128)(2,1)S(1)} %get-tuple-element.45), channel_id=1, source_target_pairs={{0,6},{1,7},{2,4},{3,5},{4,2},{5,3},{6,0},{7,1},{8,14},{9,15},{10,... | collective-permute-start | bytes 122888 | tf_op jit(solution)/shard_map/ppermute | solution.py:36
  34.2 6.0 %collective-permute-start.17 = (bf16[8,2560]{1,0:T(8,128)(2,1)S(1)}, bf16[8,2560]{1,0:T(8,128)(2,1)S(1)}, u32[]{:S(2)}, u32[]{:S(2)}) collective-permute-start(bf16[8,2560]{1,0:T(8,128)(2,1)S(1)} %get-tuple-element.45), channel_id=1, source_target_pairs={{0,4},{1,5},{2,6},{3,7},{4,0},{5,1},{6,2},{7,3},{8,12},{9,13},{10,... | collective-permute-start | bytes 122888 | tf_op jit(solution)/shard_map/ppermute | solution.py:36
  34.8 5.4 %collective-permute-start.18 = (bf16[8,2560]{1,0:T(8,128)(2,1)S(1)}, bf16[8,2560]{1,0:T(8,128)(2,1)S(1)}, u32[]{:S(2)}, u32[]{:S(2)}) collective-permute-start(bf16[8,2560]{1,0:T(8,128)(2,1)S(1)} %get-tuple-element.45), channel_id=1, source_target_pairs={{0,2},{1,3},{2,0},{3,1},{4,6},{5,7},{6,4},{7,5},{8,10},{9,11},{10,... | collective-permute-start | bytes 122888 | tf_op jit(solution)/shard_map/ppermute | solution.py:36
  41.5 5.7 %collective-permute-start.20 = (bf16[8,640]{1,0:T(8,128)(2,1)S(1)}, bf16[8,640]{1,0:T(8,128)(2,1)S(1)}, u32[]{:S(2)}, u32[]{:S(2)}) collective-permute-start(bf16[8,640]{1,0:T(8,128)(2,1)S(1)} %sep_rows.17), channel_id=1, source_target_pairs={{0,6},{1,7},{2,4},{3,5},{4,2},{5,3},{6,0},{7,1},{8,14},{9,15},{10,... | collective-permute-start | bytes 30728 | tf_op jit(solution)/shard_map/ppermute | solution.py:36
  43.6 4.6 %collective-permute-start.21 = (bf16[8,640]{1,0:T(8,128)(2,1)S(1)}, bf16[8,640]{1,0:T(8,128)(2,1)S(1)}, u32[]{:S(2)}, u32[]{:S(2)}) collective-permute-start(bf16[8,640]{1,0:T(8,128)(2,1)S(1)} %sep_rows.17), channel_id=1, source_target_pairs={{0,4},{1,5},{2,6},{3,7},{4,0},{5,1},{6,2},{7,3},{8,12},{9,13},{10,... | collective-permute-start | bytes 30728 | tf_op jit(solution)/shard_map/ppermute | solution.py:36
  53.0 5.9 %collective-permute-start.25 = (bf16[8,2560]{1,0:T(8,128)(2,1)S(1)}, bf16[8,2560]{1,0:T(8,128)(2,1)S(1)}, u32[]{:S(2)}, u32[]{:S(2)}) collective-permute-start(bf16[8,2560]{1,0:T(8,128)(2,1)S(1)} %get-tuple-element.48), channel_id=1, source_target_pairs={{0,6},{1,7},{2,4},{3,5},{4,2},{5,3},{6,0},{7,1},{8,14},{9,15},{10,... | collective-permute-start | bytes 122888 | tf_op jit(solution)/shard_map/ppermute | solution.py:36
  54.8 5.3 %collective-permute-start.26 = (bf16[8,2560]{1,0:T(8,128)(2,1)S(1)}, bf16[8,2560]{1,0:T(8,128)(2,1)S(1)}, u32[]{:S(2)}, u32[]{:S(2)}) collective-permute-start(bf16[8,2560]{1,0:T(8,128)(2,1)S(1)} %get-tuple-element.48), channel_id=1, source_target_pairs={{0,4},{1,5},{2,6},{3,7},{4,0},{5,1},{6,2},{7,3},{8,12},{9,13},{10,... | collective-permute-start | bytes 122888 | tf_op jit(solution)/shard_map/ppermute | solution.py:36
  55.7 4.5 %collective-permute-start.27 = (bf16[8,2560]{1,0:T(8,128)(2,1)S(1)}, bf16[8,2560]{1,0:T(8,128)(2,1)S(1)}, u32[]{:S(2)}, u32[]{:S(2)}) collective-permute-start(bf16[8,2560]{1,0:T(8,128)(2,1)S(1)} %get-tuple-element.48), channel_id=1, source_target_pairs={{0,2},{1,3},{2,0},{3,1},{4,6},{5,7},{6,4},{7,5},{8,10},{9,11},{10,... | collective-permute-start | bytes 122888 | tf_op jit(solution)/shard_map/ppermute | solution.py:36
  61.4 5.5 %collective-permute-start.29 = (bf16[8,640]{1,0:T(8,128)(2,1)S(1)}, bf16[8,640]{1,0:T(8,128)(2,1)S(1)}, u32[]{:S(2)}, u32[]{:S(2)}) collective-permute-start(bf16[8,640]{1,0:T(8,128)(2,1)S(1)} %sep_rows.19), channel_id=1, source_target_pairs={{0,6},{1,7},{2,4},{3,5},{4,2},{5,3},{6,0},{7,1},{8,14},{9,15},{10,... | collective-permute-start | bytes 30728 | tf_op jit(solution)/shard_map/ppermute | solution.py:36
  63.4 4.6 %collective-permute-start.30 = (bf16[8,640]{1,0:T(8,128)(2,1)S(1)}, bf16[8,640]{1,0:T(8,128)(2,1)S(1)}, u32[]{:S(2)}, u32[]{:S(2)}) collective-permute-start(bf16[8,640]{1,0:T(8,128)(2,1)S(1)} %sep_rows.19), channel_id=1, source_target_pairs={{0,4},{1,5},{2,6},{3,7},{4,0},{5,1},{6,2},{7,3},{8,12},{9,13},{10,... | collective-permute-start | bytes 30728 | tf_op jit(solution)/shard_map/ppermute | solution.py:36
  68.1 4.6 %collective-permute-start.32 = (f32[8,256]{1,0:T(8,128)S(1)}, f32[8,256]{1,0:T(8,128)S(1)}, u32[]{:S(2)}, u32[]{:S(2)}) collective-permute-start(f32[8,256]{1,0:T(8,128)S(1)} %get-tuple-element.50), channel_id=1, source_target_pairs={{16,24},{17,25},{18,26},{19,27},{20,28},{21,29},{22,30},{23,31},{2... | collective-permute-start | bytes 24584 | tf_op jit(solution)/shard_map/ppermute | solution.py:55
  73.2 6.2 %collective-permute-start.34 = (bf16[8,2560]{1,0:T(8,128)(2,1)S(1)}, bf16[8,2560]{1,0:T(8,128)(2,1)S(1)}, u32[]{:S(2)}, u32[]{:S(2)}) collective-permute-start(bf16[8,2560]{1,0:T(8,128)(2,1)S(1)} %get-tuple-element.51), channel_id=1, source_target_pairs={{0,6},{1,7},{2,4},{3,5},{4,2},{5,3},{6,0},{7,1},{8,14},{9,15},{10,... | collective-permute-start | bytes 122888 | tf_op jit(solution)/shard_map/ppermute | solution.py:36
  74.9 6.2 %collective-permute-start.35 = (bf16[8,2560]{1,0:T(8,128)(2,1)S(1)}, bf16[8,2560]{1,0:T(8,128)(2,1)S(1)}, u32[]{:S(2)}, u32[]{:S(2)}) collective-permute-start(bf16[8,2560]{1,0:T(8,128)(2,1)S(1)} %get-tuple-element.51), channel_id=1, source_target_pairs={{0,4},{1,5},{2,6},{3,7},{4,0},{5,1},{6,2},{7,3},{8,12},{9,13},{10,... | collective-permute-start | bytes 122888 | tf_op jit(solution)/shard_map/ppermute | solution.py:36
  75.9 5.2 %collective-permute-start.36 = (bf16[8,2560]{1,0:T(8,128)(2,1)S(1)}, bf16[8,2560]{1,0:T(8,128)(2,1)S(1)}, u32[]{:S(2)}, u32[]{:S(2)}) collective-permute-start(bf16[8,2560]{1,0:T(8,128)(2,1)S(1)} %get-tuple-element.51), channel_id=1, source_target_pairs={{0,2},{1,3},{2,0},{3,1},{4,6},{5,7},{6,4},{7,5},{8,10},{9,11},{10,... | collective-permute-start | bytes 122888 | tf_op jit(solution)/shard_map/ppermute | solution.py:36
  82.4 5.5 %collective-permute-start.38 = (bf16[8,640]{1,0:T(8,128)(2,1)S(1)}, bf16[8,640]{1,0:T(8,128)(2,1)S(1)}, u32[]{:S(2)}, u32[]{:S(2)}) collective-permute-start(bf16[8,640]{1,0:T(8,128)(2,1)S(1)} %sep_rows.21), channel_id=1, source_target_pairs={{0,6},{1,7},{2,4},{3,5},{4,2},{5,3},{6,0},{7,1},{8,14},{9,15},{10,... | collective-permute-start | bytes 30728 | tf_op jit(solution)/shard_map/ppermute | solution.py:36
  84.4 4.6 %collective-permute-start.39 = (bf16[8,640]{1,0:T(8,128)(2,1)S(1)}, bf16[8,640]{1,0:T(8,128)(2,1)S(1)}, u32[]{:S(2)}, u32[]{:S(2)}) collective-permute-start(bf16[8,640]{1,0:T(8,128)(2,1)S(1)} %sep_rows.21), channel_id=1, source_target_pairs={{0,4},{1,5},{2,6},{3,7},{4,0},{5,1},{6,2},{7,3},{8,12},{9,13},{10,... | collective-permute-start | bytes 30728 | tf_op jit(solution)/shard_map/ppermute | solution.py:36
  84.4 4.6 %collective-permute-start.40 = (bf16[8,640]{1,0:T(8,128)(2,1)S(1)}, bf16[8,640]{1,0:T(8,128)(2,1)S(1)}, u32[]{:S(2)}, u32[]{:S(2)}) collective-permute-start(bf16[8,640]{1,0:T(8,128)(2,1)S(1)} %sep_rows.21), channel_id=1, source_target_pairs={{0,2},{1,3},{2,0},{3,1},{4,6},{5,7},{6,4},{7,5},{8,10},{9,11},{10,... | collective-permute-start | bytes 30728 | tf_op jit(solution)/shard_map/ppermute | solution.py:36
  86.8 4.8 %collective-permute-start.43 = (bf16[2,128,128]{2,1,0:T(8,128)(2,1)S(1)}, bf16[2,128,128]{2,1,0:T(8,128)(2,1)S(1)}, u32[]{:S(2)}, u32[]{:S(2)}) collective-permute-start(bf16[2,128,128]{2,1,0:T(8,128)(2,1)S(1)} %bitcast.21), channel_id=1, source_target_pairs={{0,1},{1,0},{2,3},{3,2},{4,5},{5,4},{6,7},{7,6},{8,9},{9,8},{10,11... | collective-permute-start | bytes 196616 | tf_op jit(solution)/shard_map/ppermute | solution.py:21
  89.0 4.4 %collective-permute-start.41 = (f32[8,256]{1,0:T(8,128)S(1)}, f32[8,256]{1,0:T(8,128)S(1)}, u32[]{:S(2)}, u32[]{:S(2)}) collective-permute-start(f32[8,256]{1,0:T(8,128)S(1)} %get-tuple-element.53), channel_id=1, source_target_pairs={{24,16},{25,17},{26,18},{27,19},{28,20},{29,21},{30,22},{31,23},{1... | collective-permute-start | bytes 24584 | tf_op jit(solution)/shard_map/ppermute | solution.py:55
  94.7 6.1 %collective-permute-start.44 = (bf16[8,2560]{1,0:T(8,128)(2,1)S(1)}, bf16[8,2560]{1,0:T(8,128)(2,1)S(1)}, u32[]{:S(2)}, u32[]{:S(2)}) collective-permute-start(bf16[8,2560]{1,0:T(8,128)(2,1)S(1)} %get-tuple-element.54), channel_id=1, source_target_pairs={{0,6},{1,7},{2,4},{3,5},{4,2},{5,3},{6,0},{7,1},{8,14},{9,15},{10,... | collective-permute-start | bytes 122888 | tf_op jit(solution)/shard_map/ppermute | solution.py:36
  96.3 5.3 %collective-permute-start.45 = (bf16[8,2560]{1,0:T(8,128)(2,1)S(1)}, bf16[8,2560]{1,0:T(8,128)(2,1)S(1)}, u32[]{:S(2)}, u32[]{:S(2)}) collective-permute-start(bf16[8,2560]{1,0:T(8,128)(2,1)S(1)} %get-tuple-element.54), channel_id=1, source_target_pairs={{0,4},{1,5},{2,6},{3,7},{4,0},{5,1},{6,2},{7,3},{8,12},{9,13},{10,... | collective-permute-start | bytes 122888 | tf_op jit(solution)/shard_map/ppermute | solution.py:36
  101.7 5.6 %collective-permute-start.54 = (f32[8,256]{1,0:T(8,128)S(1)}, f32[8,256]{1,0:T(8,128)S(1)}, u32[]{:S(2)}, u32[]{:S(2)}) collective-permute-start(f32[8,256]{1,0:T(8,128)S(1)} %get-tuple-element.59.refs_1_), channel_id=1, source_target_pairs={{0,1},{1,0},{2,3},{3,2},{4,5},{5,4},{6,7},{7,6},{8,9},{9,8},{10,11... | collective-permute-start | bytes 24584 | tf_op jit(solution)/shard_map/ppermute | solution.py:21
  102.2 5.1 %collective-permute-start.53 = (f32[8,256]{1,0:T(8,128)S(1)}, f32[8,256]{1,0:T(8,128)S(1)}, u32[]{:S(2)}, u32[]{:S(2)}) collective-permute-start(f32[8,256]{1,0:T(8,128)S(1)} %get-tuple-element.58.refs_1_), channel_id=1, source_target_pairs={{0,1},{1,0},{2,3},{3,2},{4,5},{5,4},{6,7},{7,6},{8,9},{9,8},{10,11... | collective-permute-start | bytes 24584 | tf_op jit(solution)/shard_map/ppermute | solution.py:21
  102.9 5.7 %collective-permute-start.48 = (bf16[8,640]{1,0:T(8,128)(2,1)S(1)}, bf16[8,640]{1,0:T(8,128)(2,1)S(1)}, u32[]{:S(2)}, u32[]{:S(2)}) collective-permute-start(bf16[8,640]{1,0:T(8,128)(2,1)S(1)} %sep_rows.23), channel_id=1, source_target_pairs={{0,6},{1,7},{2,4},{3,5},{4,2},{5,3},{6,0},{7,1},{8,14},{9,15},{10,... | collective-permute-start | bytes 30728 | tf_op jit(solution)/shard_map/ppermute | solution.py:36
  105.3 4.6 %collective-permute-start.49 = (bf16[8,640]{1,0:T(8,128)(2,1)S(1)}, bf16[8,640]{1,0:T(8,128)(2,1)S(1)}, u32[]{:S(2)}, u32[]{:S(2)}) collective-permute-start(bf16[8,640]{1,0:T(8,128)(2,1)S(1)} %sep_rows.23), channel_id=1, source_target_pairs={{0,4},{1,5},{2,6},{3,7},{4,0},{5,1},{6,2},{7,3},{8,12},{9,13},{10,... | collective-permute-start | bytes 30728 | tf_op jit(solution)/shard_map/ppermute | solution.py:36
  115.1 6.1 %collective-permute-start.57 = (bf16[8,2560]{1,0:T(8,128)(2,1)S(1)}, bf16[8,2560]{1,0:T(8,128)(2,1)S(1)}, u32[]{:S(2)}, u32[]{:S(2)}) collective-permute-start(bf16[8,2560]{1,0:T(8,128)(2,1)S(1)} %get-tuple-element.61), channel_id=1, source_target_pairs={{0,6},{1,7},{2,4},{3,5},{4,2},{5,3},{6,0},{7,1},{8,14},{9,15},{10,... | collective-permute-start | bytes 122888 | tf_op jit(solution)/shard_map/ppermute | solution.py:36
  117.1 5.7 %collective-permute-start.58 = (bf16[8,2560]{1,0:T(8,128)(2,1)S(1)}, bf16[8,2560]{1,0:T(8,128)(2,1)S(1)}, u32[]{:S(2)}, u32[]{:S(2)}) collective-permute-start(bf16[8,2560]{1,0:T(8,128)(2,1)S(1)} %get-tuple-element.61), channel_id=1, source_target_pairs={{0,4},{1,5},{2,6},{3,7},{4,0},{5,1},{6,2},{7,3},{8,12},{9,13},{10,... | collective-permute-start | bytes 122888 | tf_op jit(solution)/shard_map/ppermute | solution.py:36
  117.6 5.2 %collective-permute-start.59 = (bf16[8,2560]{1,0:T(8,128)(2,1)S(1)}, bf16[8,2560]{1,0:T(8,128)(2,1)S(1)}, u32[]{:S(2)}, u32[]{:S(2)}) collective-permute-start(bf16[8,2560]{1,0:T(8,128)(2,1)S(1)} %get-tuple-element.61), channel_id=1, source_target_pairs={{0,2},{1,3},{2,0},{3,1},{4,6},{5,7},{6,4},{7,5},{8,10},{9,11},{10,... | collective-permute-start | bytes 122888 | tf_op jit(solution)/shard_map/ppermute | solution.py:36
  124.2 5.6 %collective-permute-start.61 = (bf16[8,640]{1,0:T(8,128)(2,1)S(1)}, bf16[8,640]{1,0:T(8,128)(2,1)S(1)}, u32[]{:S(2)}, u32[]{:S(2)}) collective-permute-start(bf16[8,640]{1,0:T(8,128)(2,1)S(1)} %sep_rows.25), channel_id=1, source_target_pairs={{0,6},{1,7},{2,4},{3,5},{4,2},{5,3},{6,0},{7,1},{8,14},{9,15},{10,... | collective-permute-start | bytes 30728 | tf_op jit(solution)/shard_map/ppermute | solution.py:36
  126.0 4.6 %collective-permute-start.62 = (bf16[8,640]{1,0:T(8,128)(2,1)S(1)}, bf16[8,640]{1,0:T(8,128)(2,1)S(1)}, u32[]{:S(2)}, u32[]{:S(2)}) collective-permute-start(bf16[8,640]{1,0:T(8,128)(2,1)S(1)} %sep_rows.25), channel_id=1, source_target_pairs={{0,4},{1,5},{2,6},{3,7},{4,0},{5,1},{6,2},{7,3},{8,12},{9,13},{10,... | collective-permute-start | bytes 30728 | tf_op jit(solution)/shard_map/ppermute | solution.py:36
  130.6 5.2 %collective-permute-start.65 = (f32[8,256]{1,0:T(8,128)S(1)}, f32[8,256]{1,0:T(8,128)S(1)}, u32[]{:S(2)}, u32[]{:S(2)}) collective-permute-start(f32[8,256]{1,0:T(8,128)S(1)} %get-tuple-element.64), channel_id=1, source_target_pairs={{8,0},{9,1},{10,2},{11,3},{12,4},{13,5},{14,6},{15,7},{0,16},{1,17... | collective-permute-start | bytes 24584 | tf_op jit(solution)/shard_map/ppermute | solution.py:55
  136.6 6.2 %collective-permute-start.67 = (bf16[8,2560]{1,0:T(8,128)(2,1)S(1)}, bf16[8,2560]{1,0:T(8,128)(2,1)S(1)}, u32[]{:S(2)}, u32[]{:S(2)}) collective-permute-start(bf16[8,2560]{1,0:T(8,128)(2,1)S(1)} %get-tuple-element.66), channel_id=1, source_target_pairs={{0,6},{1,7},{2,4},{3,5},{4,2},{5,3},{6,0},{7,1},{8,14},{9,15},{10,... | collective-permute-start | bytes 122888 | tf_op jit(solution)/shard_map/ppermute | solution.py:36
  138.4 5.7 %collective-permute-start.68 = (bf16[8,2560]{1,0:T(8,128)(2,1)S(1)}, bf16[8,2560]{1,0:T(8,128)(2,1)S(1)}, u32[]{:S(2)}, u32[]{:S(2)}) collective-permute-start(bf16[8,2560]{1,0:T(8,128)(2,1)S(1)} %get-tuple-element.66), channel_id=1, source_target_pairs={{0,4},{1,5},{2,6},{3,7},{4,0},{5,1},{6,2},{7,3},{8,12},{9,13},{10,... | collective-permute-start | bytes 122888 | tf_op jit(solution)/shard_map/ppermute | solution.py:36
  139.5 4.6 %collective-permute-start.69 = (bf16[8,2560]{1,0:T(8,128)(2,1)S(1)}, bf16[8,2560]{1,0:T(8,128)(2,1)S(1)}, u32[]{:S(2)}, u32[]{:S(2)}) collective-permute-start(bf16[8,2560]{1,0:T(8,128)(2,1)S(1)} %get-tuple-element.66), channel_id=1, source_target_pairs={{0,2},{1,3},{2,0},{3,1},{4,6},{5,7},{6,4},{7,5},{8,10},{9,11},{10,... | collective-permute-start | bytes 122888 | tf_op jit(solution)/shard_map/ppermute | solution.py:36
  146.4 5.6 %collective-permute-start.71 = (bf16[8,640]{1,0:T(8,128)(2,1)S(1)}, bf16[8,640]{1,0:T(8,128)(2,1)S(1)}, u32[]{:S(2)}, u32[]{:S(2)}) collective-permute-start(bf16[8,640]{1,0:T(8,128)(2,1)S(1)} %sep_rows.27), channel_id=1, source_target_pairs={{0,6},{1,7},{2,4},{3,5},{4,2},{5,3},{6,0},{7,1},{8,14},{9,15},{10,... | collective-permute-start | bytes 30728 | tf_op jit(solution)/shard_map/ppermute | solution.py:36
  148.4 4.6 %collective-permute-start.72 = (bf16[8,640]{1,0:T(8,128)(2,1)S(1)}, bf16[8,640]{1,0:T(8,128)(2,1)S(1)}, u32[]{:S(2)}, u32[]{:S(2)}) collective-permute-start(bf16[8,640]{1,0:T(8,128)(2,1)S(1)} %sep_rows.27), channel_id=1, source_target_pairs={{0,4},{1,5},{2,6},{3,7},{4,0},{5,1},{6,2},{7,3},{8,12},{9,13},{10,... | collective-permute-start | bytes 30728 | tf_op jit(solution)/shard_map/ppermute | solution.py:36
  (33 other events, 111.7 us)

commit v6 on v5

--- a/solution.py
+++ b/solution.py
@@ -38,12 +38,15 @@
     ]
 
 
-def gather_chips(block):
+def gather_chips(block, after=None):
     chips = lax.axis_size("front") // 2
     if chips > FEW_CHIPS:
         groups = same_core_groups()
         return lax.all_gather(block, "front", axis=1, tiled=True, axis_index_groups=groups)
-    return jnp.concatenate(from_chips(block, chips), axis=1)
+    parts = from_chips(block, chips)
+    if after is None:
+        return jnp.concatenate(parts, axis=1)
+    return join_parts(parts, after)
 
 
 def hop(block, source_layer, target_layer):
@@ -139,13 +142,13 @@
 
     return pl.pallas_call(
         kernel,
-        in_specs=[VMEM] * len(blocks) + [ANY],
-        out_specs=[VMEM] * len(blocks),
-        out_shape=[pltpu.VMEM(block.shape, block.dtype) for block in blocks],
+        in_specs=[ANY] * (len(blocks) + 1),
+        out_specs=[ANY] * len(blocks),
+        out_shape=[jax.ShapeDtypeStruct(block.shape, block.dtype) for block in blocks],
         input_output_aliases={index: index for index in range(len(blocks))},
         compiler_params=params(1),
         name="hold",
-    )(*[in_vmem(block) for block in blocks], after)
+    )(*blocks, after)
 
 
 def transpose_gather(own, theirs, after):
@@ -183,11 +186,12 @@
     return pl.ds(pl.multiple_of(panel * rows, 128), rows)
 
 
-def transpose_spread(own, theirs, owner, rows, after):
-    _, cells, total = own.shape
-    chips = owner.shape[0] // 2
-
-    def kernel(owner_ref, own_ref, theirs_ref, _, out):
+def transpose_maps(own, theirs, owner, rows, after):
+    _, cells, width = own.shape
+    slots = owner.shape[0]
+    chips = slots // 2
+
+    def kernel(owner_ref, own_ref, theirs_ref, _, out, blocks_out):
         for step in range(chips):
             columns = panel_columns(owner_ref, step, rows)
             for side, block in enumerate((own_ref, theirs_ref)):
@@ -195,58 +199,44 @@
                     out[part, pl.ds(step * rows, rows), pl.ds(side * cells, cells)] = block[
                         part, :, columns
                     ].T
+        for side, block in enumerate((own_ref, theirs_ref)):
+            for kind in range(3):
+                columns = pl.ds(slots * rows + kind * cells, cells)
+                for part in range(2):
+                    blocks_out[side, kind, part] = block[part, :, columns]
 
     return pl.pallas_call(
         kernel,
         in_specs=[SMEM, VMEM, VMEM, ANY],
-        out_specs=VMEM,
-        out_shape=pltpu.VMEM((2, total // 2, 2 * cells), BF16),
+        out_specs=[VMEM, VMEM],
+        out_shape=[
+            pltpu.VMEM((2, chips * rows, 2 * cells), BF16),
+            jax.ShapeDtypeStruct((2, 3, 2, cells, cells), BF16),
+        ],
         compiler_params=params(16),
         cost_estimate=cost(0, 4 * own.size),
-        name="transpose_spread",
+        name="transpose_maps",
     )(owner, in_vmem(own), in_vmem(theirs), after)
 
 
-def take_spread(own, theirs, owner, rows):
-    _, cells, total = own.shape
+def take_maps(own, theirs, owner, rows):
+    _, cells, width = own.shape
     slots = owner.shape[0]
+    total = slots * rows
     place = lax.axis_index("front")
     slot_ids = jnp.arange(slots, dtype=jnp.int32)
     panel_of = jnp.sum(jnp.where(owner[None, :] == slot_ids[:, None], slot_ids[None, :], 0), axis=1)
     wanted = panel_of[2 * arrival_order(place // 2, slots // 2) + place % 2]
 
-    def columns(spread):
-        chosen = jnp.take(spread.reshape(2, cells, slots, rows), wanted, axis=2)
+    def columns(maps):
+        chosen = jnp.take(maps[:, :, :total].reshape(2, cells, slots, rows), wanted, axis=2)
         return jnp.swapaxes(chosen.reshape(2, cells, total // 2), 1, 2)
 
-    return jnp.concatenate([columns(own), columns(theirs)], axis=2)
-
-
-def first_spread_cells(stored, leaf_values, own, theirs, owner, rows):
-    _, cells, _ = own.shape
-    chips = owner.shape[0] // 2
-
-    def kernel(owner_ref, stored_ref, leaf_ref, own_ref, theirs_ref, part_out, share_out):
-        @pl.when(lax.axis_index("layer") == 0)
-        def _():
-            for side, block in enumerate((own_ref, theirs_ref)):
-                value = jnp.zeros((8, cells), F32)
-                for step in range(chips):
-                    columns = panel_columns(owner_ref, step, rows)
-                    vector = stored_ref[:, pl.ds(step * rows, rows)].astype(F32)
-                    value += times(vector, block[0, :, columns], block[1, :, columns], 1)
-                part_out[:, pl.ds(side * cells, cells)] = value
-            share_out[...] = share_of_value(part_out[...], leaf_ref[...], None, False)
-
-    return pl.pallas_call(
-        kernel,
-        in_specs=[SMEM] + [VMEM] * 4,
-        out_specs=[VMEM, VMEM],
-        out_shape=[jax.ShapeDtypeStruct((8, 2 * cells), F32)] * 2,
-        compiler_params=params(16),
-        cost_estimate=cost(16 * own.size, 2 * own.size),
-        name="first_spread_cells",
-    )(owner, stored, leaf_values, in_vmem(own), in_vmem(theirs))
+    def blocks(maps):
+        return jnp.moveaxis(maps[:, :, total:].reshape(2, cells, 3, cells), 2, 0)
+
+    spread = jnp.concatenate([columns(own), columns(theirs)], axis=2)
+    return spread, jnp.stack([blocks(own), blocks(theirs)])
 
 
 def add_parts(parts, after):
@@ -268,37 +258,63 @@
     )(*parts, in_vmem(after))
 
 
-def first_leaf_and_gather(sources, leaf, gather, spread):
-    cells = leaf.shape[1]
+def join_parts(parts, after):
+    width = parts[0].shape[1]
+
+    def kernel(*refs):
+        out = refs[-1]
+        for index, part in enumerate(refs[: len(parts)]):
+            out[:, pl.ds(index * width, width)] = part[...]
+
+    return pl.pallas_call(
+        kernel,
+        in_specs=[VMEM] * len(parts) + [ANY],
+        out_specs=VMEM,
+        out_shape=jax.ShapeDtypeStruct((8, len(parts) * width), BF16),
+        compiler_params=params(16),
+        cost_estimate=cost(0, 8 * parts[0].size),
+        name="join_parts",
+    )(*parts, in_vmem(after))
+
+
+def first_leaf_and_gather(sources, gather, maps):
+    cells = gather.shape[2]
     half = gather.shape[1] // 2
-
-    def kernel(*refs):
-        sources_hbm, leaf_hbm, gather_hbm, spread_hbm, leaf_out, keep, give = refs[:7]
-        gather_ref, spread_ref, sources_ref, leaf_ref, done = refs[7:]
+    starts = [sum(block.shape[2] for block in maps[:index]) for index in range(len(maps))]
+    width = sum(block.shape[2] for block in maps)
+
+    def kernel(*refs):
+        sources_hbm, gather_hbm, *maps_hbm = refs[: 2 + len(maps)]
+        keep, give, gather_ref, maps_ref, sources_ref, done = refs[2 + len(maps) :]
         core = lax.axis_index("front") % 2
         layer = lax.axis_index("layer")
         sides = [pl.ds(pl.multiple_of(side * half, half), half) for side in (1 - core, core)]
-        copies = [
-            pltpu.make_async_copy(sources_hbm, sources_ref, done.at[0]),
-            pltpu.make_async_copy(leaf_hbm, leaf_ref, done.at[1]),
-        ]
+        leaf_at = pl.ds(starts[1], cells)
+        values_at, sources_at = pl.ds(half, cells), pl.ds(half + cells, cells)
+        pieces = [(sources_hbm, sources_ref), (maps_hbm[1], maps_ref.at[:, :, leaf_at])]
         for rows in sides:
             for part in range(2):
-                copies.append(
-                    pltpu.make_async_copy(
-                        gather_hbm.at[part, rows], gather_ref.at[part, rows], done.at[len(copies)]
-                    )
-                )
-        copies.append(pltpu.make_async_copy(spread_hbm, spread_ref, done.at[len(copies)]))
+                pieces.append((gather_hbm.at[part, rows], gather_ref.at[part, rows]))
+        for index in (0, 2, 3):
+            columns = pl.ds(starts[index], maps[index].shape[2])
+            pieces.append((maps_hbm[index], maps_ref.at[:, :, columns]))
+        copies = [
+            pltpu.make_async_copy(source, target, done.at[index])
+            for index, (source, target) in enumerate(pieces)
+        ]
         for copy in copies:
             copy.start()
         copies[0].wait()
         copies[1].wait()
+        source = jnp.concatenate([sources_ref[0], sources_ref[1]], axis=0)
+        for out in (give, keep):
+            out[:, sources_at] = source
 
         @pl.when(layer == 0)
         def _():
-            source = jnp.concatenate([sources_ref[0], sources_ref[1]], axis=0)
-            leaf_out[...] = times(source, leaf_ref[0], leaf_ref[1], 1)
+            leaf_values = times(source, maps_ref[0, :, leaf_at], maps_ref[1, :, leaf_at], 1)
+            for out in (give, keep):
+                out[:, values_at] = leaf_values
 
         for index, (out, rows) in enumerate(zip((give, keep), sides)):
             copies[2 + 2 * index].wait()
@@ -306,66 +322,66 @@
 
             @pl.when(layer == 0)
             def _(out=out, rows=rows):
-                value = times(leaf_out[...], gather_ref[0, rows, :], gather_ref[1, rows, :], 1)
-                out[...] = value.astype(out.dtype)
-
-        copies[-1].wait()
-
-    return pl.pallas_call(
-        kernel,
-        in_specs=[ANY] * 4,
-        out_specs=[VMEM] * 5,
+                leaf_values = out[:, values_at]
+                out[:, pl.ds(0, half)] = times(
+                    leaf_values, gather_ref[0, rows, :], gather_ref[1, rows, :], 1
+                )
+
+        for copy in copies[6:]:
+            copy.wait()
+
+    return pl.pallas_call(
+        kernel,
+        in_specs=[ANY] * (2 + len(maps)),
+        out_specs=[VMEM] * 4,
         out_shape=[
-            jax.ShapeDtypeStruct((8, cells), F32),
-            jax.ShapeDtypeStruct((8, half), F32),
-            jax.ShapeDtypeStruct((8, half), BF16),
+            jax.ShapeDtypeStruct((8, half + 2 * cells), F32),
+            jax.ShapeDtypeStruct((8, half + 2 * cells), F32),
             pltpu.VMEM(gather.shape, BF16),
-            pltpu.VMEM(spread.shape, BF16),
+            pltpu.VMEM((2, cells, width), BF16),
         ],
-        scratch_shapes=[
-            pltpu.VMEM(sources.shape, F32),
-            pltpu.VMEM(leaf.shape, BF16),
-            pltpu.SemaphoreType.DMA((7,)),
-        ],
+        scratch_shapes=[pltpu.VMEM(sources.shape, F32), pltpu.SemaphoreType.DMA((9,))],
         compiler_params=params(16),
         cost_estimate=cost(16 * gather.size, 2 * gather.size),
         name="first_leaf_and_gather",
-    )(in_hbm(sources), in_hbm(leaf), in_hbm(gather), in_hbm(spread))
-
-
-def leaf_and_gather(level, leaf, gather, couple, arrived, sources=None):
-    cells = leaf[0].shape[1]
+    )(in_hbm(sources), in_hbm(gather), *[in_hbm(block) for block in maps])
+
+
+def leaf_and_gather(level, blocks, gather, arrived, sources=None):
+    cells = blocks.shape[3]
     width = gather.shape[2]
     given = list(arrived) if sources is None else [*arrived, sources]
-    mats = list(couple) + list(leaf)
-
-    def kernel(*refs):
-        vectors = list(refs[: len(given)])
-        matrices = list(refs[len(given) : len(given) + len(mats)])
-        gather_ref, leaf_out, sums_out = refs[-3:]
-
-        def blocks(vector, pair_of):
+
+    def kernel(*refs):
+        blocks_ref, gather_ref, leaf_out, sums_out = refs[-4:]
+
+        def apply(vector, kind):
             return jnp.concatenate(
                 [
-                    times(vector[:, i * cells : (i + 1) * cells], pair_of[i][0], pair_of[i][1], 1)
-                    for i in range(2)
+                    times(
+                        vector[:, side * cells : (side + 1) * cells],
+                        blocks_ref[side, kind, 0],
+                        blocks_ref[side, kind, 1],
+                        1,
+                    )
+                    for side in range(2)
                 ],
                 axis=1,
             )
 
         @pl.when(lax.axis_index("layer") == level)
         def _():
-            crossed = jnp.concatenate([vectors[1][:, cells:], vectors[1][:, :cells]], axis=1)
-            source = blocks(vectors[0][...] + crossed, matrices[:2])
+            crossed = jnp.concatenate([refs[1][:, cells:], refs[1][:, :cells]], axis=1)
+            source = apply(refs[0][...] + crossed, 2 if sources is None else 1)
             if sources is not None:
-                source = vectors[2][...] - source
-            leaf_values = blocks(source, matrices[-2:])
+                source = refs[2][...] - source
+            leaf_values = apply(source, 0)
             leaf_out[...] = leaf_values
             sums_out[...] = times(leaf_values, gather_ref[0], gather_ref[1], 0).astype(BF16)
 
     return pl.pallas_call(
         kernel,
-        in_specs=[VMEM] * (len(given) + len(mats) + 1),
+        in_specs=[VMEM] * (len(given) + 2),
         out_specs=[VMEM, VMEM],
         out_shape=[
             jax.ShapeDtypeStruct((8, 2 * cells), F32),
@@ -374,7 +390,7 @@
         compiler_params=params(16),
         cost_estimate=cost(32 * gather.size, 2 * gather.size),
         name="leaf_and_gather",
-    )(*given, *mats, in_vmem(gather))
+    )(*given, blocks, in_vmem(gather))
 
 
 def sep_rows(level, sums, sep, other, before=None):
@@ -491,24 +507,19 @@
     depth = lax.axis_size("layer")
     cells = leaf_inverse.shape[2]
     rows = sep_inverse.shape[2]
-    own_leaf, own_sources = leaf_inverse[0], right_sides[0]
-
-    def with_partner(block):
-        return [block, pair(block)]
-
-    own_values, keep_sums, give_sums, own_gather, own_spread = first_leaf_and_gather(
-        own_sources, own_leaf, sep_gather[0], sep_spread[0]
+
+    maps = [sep_spread[0], leaf_inverse[0], couple_above[0], couple_below[0]]
+    keep, give, own_gather, own_maps = first_leaf_and_gather(right_sides[0], sep_gather[0], maps)
+    got = pair(give)
+    half = sep_gather.shape[2] // 2
+    first_sums = (keep[:, :half] + got[:, :half]).astype(BF16)
+    first_values, sources = (
+        jnp.concatenate([block[:, at : at + cells] for block in (keep, got)], axis=1)
+        for at in (half, half + cells)
     )
-    first_sums = (keep_sums + pair(give_sums).astype(F32)).astype(BF16)
-    first_values = jnp.concatenate(with_partner(own_values), axis=1)
-
-    leaf = with_partner(own_leaf)
-    above = with_partner(couple_above[0])
-    below = with_partner(couple_below[0])
-    sources = jnp.concatenate(with_partner(own_sources.reshape(8, cells)), axis=1)
-
-    own_gather, own_spread = hold([own_gather, own_spread], first_sums)
-    their_gather, their_spread = pair(own_gather), pair(own_spread)
+
+    own_gather, own_maps = hold([own_gather, own_maps], first_sums)
+    their_gather, their_maps = pair(own_gather), pair(own_maps)
     sep = transpose_sep(sep_inverse[0], first_sums)
 
     def own_rows_of(level, half_sums):
@@ -517,31 +528,28 @@
         return sep_rows(level, other_sums, sep, True, own_rows)
 
     def solve(level, before, subtract=False, last=False, **given):
-        leaf_values, sums = leaf_and_gather(level, leaf, gather, **given)
+        leaf_values, sums = leaf_and_gather(level, blocks, gather, **given)
         stored = gather_chips(own_rows_of(level, sum_chips(sums)))
         part, share = spread_cells(level, stored, spread, leaf_values, before, subtract)
         return finish(level, leaf_values, part, pair(part), before, subtract, last), share
 
-    stored = gather_chips(own_rows_of(0, sum_chips(first_sums, sep)))
-    spreads = own_spread, their_spread, panel_owner[0], rows
+    own_rows = own_rows_of(0, sum_chips(first_sums, sep))
     if rows % 128 == 0:
-        part, share = first_spread_cells(stored, first_values, *spreads)
+        spread, blocks = transpose_maps(own_maps, their_maps, panel_owner[0], rows, own_rows)
     else:
-        spread = take_spread(*spreads)
-        part, share = spread_cells(0, stored, spread, first_values)
+        spread, blocks = take_maps(own_maps, their_maps, panel_owner[0], rows)
+    part, share = spread_cells(0, gather_chips(own_rows, spread), spread, first_values)
     arrived = hop(share, 0, 1)
     value = finish(0, first_values, part, pair(part))
     gather = transpose_gather(own_gather, their_gather, share)
-    if rows % 128 == 0:
-        spread = transpose_spread(*spreads, share)
 
     for level in range(1, depth):
         if level > 1:
             arrived = hop(share, level - 1, level)
-        value, share = solve(level, value, sources=sources, couple=above, arrived=arrived)
+        value, share = solve(level, value, sources=sources, arrived=arrived)
     for level in range(depth - 2, -1, -1):
         arrived = hop(share, level + 1, level)
-        value, share = solve(level, value, True, level == 0, couple=below, arrived=arrived)
+        value, share = solve(level, value, True, level == 0, arrived=arrived)
     return value
 
 

time: 156 us -> 155 us (level)
  starting transfers between devices: 80.8 us -> 79.1 us
    ppermute x22 -> x17, starting transfers between devices: 3.85 us -> 2.76 us  [pair(): return lax.ppermute(block, 'front', xor_route('front', 1))]
    ppermute x22 -> x17, waiting for transfers between devices: 10.8 us -> 11 us  [pair(): return lax.ppermute(block, 'front', xor_route('front', 1))]
  transfers between devices with their start and end apart: 76 -> 71, of which waited for: 43 -> 46; matrix products, arithmetic and copies ran while one was open for 0% -> 0% of each run, Pallas kernels for 8% -> 7%
where the time goes in v6:
time: 155 us; the launch traced here: 154 us
  starting transfers between devices  79.1 us (51%)
  waiting for transfers between devices  57.5 us (37%)
  Pallas kernels  17.2 us (11%)
    ppermute x42, starting transfers between devices, from_chips(): lax.ppermute(block, 'front', xor_route('front', 2 * (chips - step)))  62.8 us
    ppermute x42, waiting for transfers between devices, from_chips(): lax.ppermute(block, 'front', xor_route('front', 2 * (chips - step)))  31 us
    ppermute x12, waiting for transfers between devices, hop(): lax.ppermute(block, ('layer', 'front'), [(i * slots + j, target[i] * slot...  15.5 us
    ppermute x12, starting transfers between devices, hop(): lax.ppermute(block, ('layer', 'front'), [(i * slots + j, target[i] * slot...  13.6 us
    ppermute x17, waiting for transfers between devices, pair(): return lax.ppermute(block, 'front', xor_route('front', 1))  11 us
    pallas_call x1, Pallas kernels, transpose_sep(): pl.pallas_call(kernel, in_specs=[ANY, ANY], out_specs=VMEM, out_shape=plt...  5.35 us
    pallas_call x14, Pallas kernels, sep_rows(): pl.pallas_call(kernel, in_specs=[VMEM] * (len(given) + 1), out_specs=VMEM...  3.9 us
  transfers between devices with their start and end apart: 71, of which 46 were waited for; matrix products, arithmetic and copies ran while one was open for 0% of the time, Pallas kernels for 7%

profile of v6, /device:TPU:0, one launch (start us, length us, event | category | flops | bytes accessed | tf_op | source)
XLA Modules:
  0.0 154.4 jit_solution(538029263655388483)
XLA Ops:
  0.0 2.7 %first_leaf_and_gather.1 = (f32[8,2816]{1,0:T(8,128)S(1)}, f32[8,2816]{1,0:T(8,128)S(1)}, bf16[2,5120,128]{2,1,0:T(8,128)(2,1)S(1)}, bf16[2,128,5504]{2,1,0:T(8,128)(2,1)S(1)}) custom-call(f32[2,4,128]{2,1,0:T(4,128)} %bitcast.15, bf16[2,5120,128]{2,1,0:T(8,128)(2,1)} %bitcast.10, bf16[2,128,5120]{2,1,0:T(8,128)(2,1)} %bitcast.11, ...), custom_call_target="tpu_custom_call" | custom-call | flops 20971520 | bytes 2621440 | tf_op jit(solution)/shard_map/first_leaf_and_gather/pallas_call | solution.py:333
  4.7 5.0 %collective-permute-start.1 = (bf16[8,2560]{1,0:T(8,128)(2,1)S(1)}, bf16[8,2560]{1,0:T(8,128)(2,1)S(1)}, u32[]{:S(2)}, u32[]{:S(2)}) collective-permute-start(bf16[8,2560]{1,0:T(8,128)(2,1)S(1)} %fusion._.refs_0_.refs_2_), channel_id=1, source_target_pairs={{0,6},{1,7},{2,4},{3,5},{4,2},{5,3},{6,0},{7,1},{8,14},{9,15},{10,... | collective-permute-start | bytes 122888 | tf_op jit(solution)/shard_map/ppermute | solution.py:36
  10.3 5.3 %transpose_sep.1.refs_4_.refs_1_.refs_2_ = bf16[2,5120,640]{2,1,0:T(8,128)(2,1)S(1)} custom-call(bf16[2,640,5120]{2,1,0:T(8,128)(2,1)} %bitcast.9, bf16[8,2560]{1,0:T(8,128)(2,1)S(1)} %fusion._.refs_0_.refs_2_), custom_call_target="tpu_custom_call" | custom-call | bytes 26214400 | tf_op jit(solution)/shard_map/transpose_sep/pallas_call | solution.py:127
  17.9 3.9 %collective-permute-start.5 = (bf16[8,640]{1,0:T(8,128)(2,1)S(1)}, bf16[8,640]{1,0:T(8,128)(2,1)S(1)}, u32[]{:S(2)}, u32[]{:S(2)}) collective-permute-start(bf16[8,640]{1,0:T(8,128)(2,1)S(1)} %sep_rows.15._.refs_0_), channel_id=1, source_target_pairs={{0,6},{1,7},{2,4},{3,5},{4,2},{5,3},{6,0},{7,1},{8,14},{9,15},{10,... | collective-permute-start | bytes 30728 | tf_op jit(solution)/shard_map/ppermute | solution.py:36
  23.8 2.6 %collective-permute-done.6.refs_2_ = bf16[8,640]{1,0:T(8,128)(2,1)S(1)} collective-permute-done((bf16[8,640]{1,0:T(8,128)(2,1)S(1)}, bf16[8,640]{1,0:T(8,128)(2,1)S(1)}, u32[]{:S(2)}, u32[]{:S(2)}) %collective-permute-start.6) | collective-permute-done | bytes 10272 | tf_op jit(solution)/shard_map/ppermute | solution.py:36
  27.7 3.1 %collective-permute-done.10.refs_1_ = f32[8,256]{1,0:T(8,128)S(1)} collective-permute-done((f32[8,256]{1,0:T(8,128)S(1)}, f32[8,256]{1,0:T(8,128)S(1)}, u32[]{:S(2)}, u32[]{:S(2)}) %collective-permute-start.10) | collective-permute-done | bytes 8224 | tf_op jit(solution)/shard_map/ppermute | solution.py:58
  31.4 1.4 collective-permute-start.12
  33.4 2.4 %collective-permute-start.14 = (bf16[8,2560]{1,0:T(8,128)(2,1)S(1)}, bf16[8,2560]{1,0:T(8,128)(2,1)S(1)}, u32[]{:S(2)}, u32[]{:S(2)}) collective-permute-start(bf16[8,2560]{1,0:T(8,128)(2,1)S(1)} %get-tuple-element.47), channel_id=1, source_target_pairs={{0,2},{1,3},{2,0},{3,1},{4,6},{5,7},{6,4},{7,5},{8,10},{9,11},{10,... | collective-permute-start | bytes 122888 | tf_op jit(solution)/shard_map/ppermute | solution.py:36
  35.8 1.9 %collective-permute-done.12 = bf16[8,2560]{1,0:T(8,128)(2,1)S(1)} collective-permute-done((bf16[8,2560]{1,0:T(8,128)(2,1)S(1)}, bf16[8,2560]{1,0:T(8,128)(2,1)S(1)}, u32[]{:S(2)}, u32[]{:S(2)}) %collective-permute-start.12) | collective-permute-done | bytes 40992 | tf_op jit(solution)/shard_map/ppermute | solution.py:36
  39.7 2.2 %collective-permute-start.16 = (bf16[8,640]{1,0:T(8,128)(2,1)S(1)}, bf16[8,640]{1,0:T(8,128)(2,1)S(1)}, u32[]{:S(2)}, u32[]{:S(2)}) collective-permute-start(bf16[8,640]{1,0:T(8,128)(2,1)S(1)} %sep_rows.17), channel_id=1, source_target_pairs={{0,6},{1,7},{2,4},{3,5},{4,2},{5,3},{6,0},{7,1},{8,14},{9,15},{10,... | collective-permute-start | bytes 30728 | tf_op jit(solution)/shard_map/ppermute | solution.py:36
  42.6 1.5 collective-permute-start.18
  48.1 2.2 %collective-permute-done.19.refs_0_ = f32[8,256]{1,0:T(8,128)S(1)} collective-permute-done((f32[8,256]{1,0:T(8,128)S(1)}, f32[8,256]{1,0:T(8,128)S(1)}, u32[]{:S(2)}, u32[]{:S(2)}) %collective-permute-start.19) | collective-permute-done | bytes 8224 | tf_op jit(solution)/shard_map/ppermute | solution.py:58
  50.5 1.8 %collective-permute-start.21 = (bf16[8,2560]{1,0:T(8,128)(2,1)S(1)}, bf16[8,2560]{1,0:T(8,128)(2,1)S(1)}, u32[]{:S(2)}, u32[]{:S(2)}) collective-permute-start(bf16[8,2560]{1,0:T(8,128)(2,1)S(1)} %get-tuple-element.50), channel_id=1, source_target_pairs={{0,6},{1,7},{2,4},{3,5},{4,2},{5,3},{6,0},{7,1},{8,14},{9,15},{10,... | collective-permute-start | bytes 122888 | tf_op jit(solution)/shard_map/ppermute | solution.py:36
  53.3 1.5 collective-permute-start.23
  54.9 1.7 %collective-permute-done.21 = bf16[8,2560]{1,0:T(8,128)(2,1)S(1)} collective-permute-done((bf16[8,2560]{1,0:T(8,128)(2,1)S(1)}, bf16[8,2560]{1,0:T(8,128)(2,1)S(1)}, u32[]{:S(2)}, u32[]{:S(2)}) %collective-permute-start.21) | collective-permute-done | bytes 40992 | tf_op jit(solution)/shard_map/ppermute | solution.py:36
  56.5 1.4 collective-permute-done.22
  59.3 2.1 %collective-permute-start.25 = (bf16[8,640]{1,0:T(8,128)(2,1)S(1)}, bf16[8,640]{1,0:T(8,128)(2,1)S(1)}, u32[]{:S(2)}, u32[]{:S(2)}) collective-permute-start(bf16[8,640]{1,0:T(8,128)(2,1)S(1)} %sep_rows.19), channel_id=1, source_target_pairs={{0,6},{1,7},{2,4},{3,5},{4,2},{5,3},{6,0},{7,1},{8,14},{9,15},{10,... | collective-permute-start | bytes 30728 | tf_op jit(solution)/shard_map/ppermute | solution.py:36
  61.6 2.0 %collective-permute-start.27 = (bf16[8,640]{1,0:T(8,128)(2,1)S(1)}, bf16[8,640]{1,0:T(8,128)(2,1)S(1)}, u32[]{:S(2)}, u32[]{:S(2)}) collective-permute-start(bf16[8,640]{1,0:T(8,128)(2,1)S(1)} %sep_rows.19), channel_id=1, source_target_pairs={{0,2},{1,3},{2,0},{3,1},{4,6},{5,7},{6,4},{7,5},{8,10},{9,11},{10,... | collective-permute-start | bytes 30728 | tf_op jit(solution)/shard_map/ppermute | solution.py:36
  66.0 1.5 %collective-permute-start.28 = (f32[8,256]{1,0:T(8,128)S(1)}, f32[8,256]{1,0:T(8,128)S(1)}, u32[]{:S(2)}, u32[]{:S(2)}) collective-permute-start(f32[8,256]{1,0:T(8,128)S(1)} %get-tuple-element.52), channel_id=1, source_target_pairs={{16,24},{17,25},{18,26},{19,27},{20,28},{21,29},{22,30},{23,31},{2... | collective-permute-start | bytes 24584 | tf_op jit(solution)/shard_map/ppermute | solution.py:58
  67.6 2.1 %collective-permute-start.29 = (f32[8,256]{1,0:T(8,128)S(1)}, f32[8,256]{1,0:T(8,128)S(1)}, u32[]{:S(2)}, u32[]{:S(2)}) collective-permute-start(f32[8,256]{1,0:T(8,128)S(1)} %get-tuple-element.52), channel_id=1, source_target_pairs={{16,25},{17,24},{18,27},{19,26},{20,29},{21,28},{22,31},{23,30},{2... | collective-permute-start | bytes 24584 | tf_op jit(solution)/shard_map/ppermute | solution.py:58
  71.5 1.6 %collective-permute-start.30 = (bf16[8,2560]{1,0:T(8,128)(2,1)S(1)}, bf16[8,2560]{1,0:T(8,128)(2,1)S(1)}, u32[]{:S(2)}, u32[]{:S(2)}) collective-permute-start(bf16[8,2560]{1,0:T(8,128)(2,1)S(1)} %get-tuple-element.53), channel_id=1, source_target_pairs={{0,6},{1,7},{2,4},{3,5},{4,2},{5,3},{6,0},{7,1},{8,14},{9,15},{10,... | collective-permute-start | bytes 122888 | tf_op jit(solution)/shard_map/ppermute | solution.py:36
  74.2 1.7 %collective-permute-start.32 = (bf16[8,2560]{1,0:T(8,128)(2,1)S(1)}, bf16[8,2560]{1,0:T(8,128)(2,1)S(1)}, u32[]{:S(2)}, u32[]{:S(2)}) collective-permute-start(bf16[8,2560]{1,0:T(8,128)(2,1)S(1)} %get-tuple-element.53), channel_id=1, source_target_pairs={{0,2},{1,3},{2,0},{3,1},{4,6},{5,7},{6,4},{7,5},{8,10},{9,11},{10,... | collective-permute-start | bytes 122888 | tf_op jit(solution)/shard_map/ppermute | solution.py:36
  75.9 1.9 %collective-permute-done.30 = bf16[8,2560]{1,0:T(8,128)(2,1)S(1)} collective-permute-done((bf16[8,2560]{1,0:T(8,128)(2,1)S(1)}, bf16[8,2560]{1,0:T(8,128)(2,1)S(1)}, u32[]{:S(2)}, u32[]{:S(2)}) %collective-permute-start.30) | collective-permute-done | bytes 40992 | tf_op jit(solution)/shard_map/ppermute | solution.py:36
  77.8 1.6 %collective-permute-done.31 = bf16[8,2560]{1,0:T(8,128)(2,1)S(1)} collective-permute-done((bf16[8,2560]{1,0:T(8,128)(2,1)S(1)}, bf16[8,2560]{1,0:T(8,128)(2,1)S(1)}, u32[]{:S(2)}, u32[]{:S(2)}) %collective-permute-start.31) | collective-permute-done | bytes 40992 | tf_op jit(solution)/shard_map/ppermute | solution.py:36
  80.8 2.0 %collective-permute-start.34 = (bf16[8,640]{1,0:T(8,128)(2,1)S(1)}, bf16[8,640]{1,0:T(8,128)(2,1)S(1)}, u32[]{:S(2)}, u32[]{:S(2)}) collective-permute-start(bf16[8,640]{1,0:T(8,128)(2,1)S(1)} %sep_rows.21), channel_id=1, source_target_pairs={{0,6},{1,7},{2,4},{3,5},{4,2},{5,3},{6,0},{7,1},{8,14},{9,15},{10,... | collective-permute-start | bytes 30728 | tf_op jit(solution)/shard_map/ppermute | solution.py:36
  82.7 2.4 %collective-permute-start.36 = (bf16[8,640]{1,0:T(8,128)(2,1)S(1)}, bf16[8,640]{1,0:T(8,128)(2,1)S(1)}, u32[]{:S(2)}, u32[]{:S(2)}) collective-permute-start(bf16[8,640]{1,0:T(8,128)(2,1)S(1)} %sep_rows.21), channel_id=1, source_target_pairs={{0,2},{1,3},{2,0},{3,1},{4,6},{5,7},{6,4},{7,5},{8,10},{9,11},{10,... | collective-permute-start | bytes 30728 | tf_op jit(solution)/shard_map/ppermute | solution.py:36
  87.3 2.5 %collective-permute-start.37 = (f32[8,256]{1,0:T(8,128)S(1)}, f32[8,256]{1,0:T(8,128)S(1)}, u32[]{:S(2)}, u32[]{:S(2)}) collective-permute-start(f32[8,256]{1,0:T(8,128)S(1)} %get-tuple-element.55), channel_id=1, source_target_pairs={{24,16},{25,17},{26,18},{27,19},{28,20},{29,21},{30,22},{31,23},{1... | collective-permute-start | bytes 24584 | tf_op jit(solution)/shard_map/ppermute | solution.py:58
  89.9 1.8 %collective-permute-done.37.refs_0_ = f32[8,256]{1,0:T(8,128)S(1)} collective-permute-done((f32[8,256]{1,0:T(8,128)S(1)}, f32[8,256]{1,0:T(8,128)S(1)}, u32[]{:S(2)}, u32[]{:S(2)}) %collective-permute-start.37) | collective-permute-done | bytes 8224 | tf_op jit(solution)/shard_map/ppermute | solution.py:58
  93.0 1.6 %collective-permute-start.39 = (bf16[8,2560]{1,0:T(8,128)(2,1)S(1)}, bf16[8,2560]{1,0:T(8,128)(2,1)S(1)}, u32[]{:S(2)}, u32[]{:S(2)}) collective-permute-start(bf16[8,2560]{1,0:T(8,128)(2,1)S(1)} %get-tuple-element.56), channel_id=1, source_target_pairs={{0,6},{1,7},{2,4},{3,5},{4,2},{5,3},{6,0},{7,1},{8,14},{9,15},{10,... | collective-permute-start | bytes 122888 | tf_op jit(solution)/shard_map/ppermute | solution.py:36
  95.4 1.9 %collective-permute-start.41 = (bf16[8,2560]{1,0:T(8,128)(2,1)S(1)}, bf16[8,2560]{1,0:T(8,128)(2,1)S(1)}, u32[]{:S(2)}, u32[]{:S(2)}) collective-permute-start(bf16[8,2560]{1,0:T(8,128)(2,1)S(1)} %get-tuple-element.56), channel_id=1, source_target_pairs={{0,2},{1,3},{2,0},{3,1},{4,6},{5,7},{6,4},{7,5},{8,10},{9,11},{10,... | collective-permute-start | bytes 122888 | tf_op jit(solution)/shard_map/ppermute | solution.py:36
  97.4 1.9 %collective-permute-done.39 = bf16[8,2560]{1,0:T(8,128)(2,1)S(1)} collective-permute-done((bf16[8,2560]{1,0:T(8,128)(2,1)S(1)}, bf16[8,2560]{1,0:T(8,128)(2,1)S(1)}, u32[]{:S(2)}, u32[]{:S(2)}) %collective-permute-start.39) | collective-permute-done | bytes 40992 | tf_op jit(solution)/shard_map/ppermute | solution.py:36
  101.3 2.3 %collective-permute-start.43 = (bf16[8,640]{1,0:T(8,128)(2,1)S(1)}, bf16[8,640]{1,0:T(8,128)(2,1)S(1)}, u32[]{:S(2)}, u32[]{:S(2)}) collective-permute-start(bf16[8,640]{1,0:T(8,128)(2,1)S(1)} %sep_rows.23), channel_id=1, source_target_pairs={{0,6},{1,7},{2,4},{3,5},{4,2},{5,3},{6,0},{7,1},{8,14},{9,15},{10,... | collective-permute-start | bytes 30728 | tf_op jit(solution)/shard_map/ppermute | solution.py:36
  104.1 1.5 %collective-permute-start.45 = (bf16[8,640]{1,0:T(8,128)(2,1)S(1)}, bf16[8,640]{1,0:T(8,128)(2,1)S(1)}, u32[]{:S(2)}, u32[]{:S(2)}) collective-permute-start(bf16[8,640]{1,0:T(8,128)(2,1)S(1)} %sep_rows.23), channel_id=1, source_target_pairs={{0,2},{1,3},{2,0},{3,1},{4,6},{5,7},{6,4},{7,5},{8,10},{9,11},{10,... | collective-permute-start | bytes 30728 | tf_op jit(solution)/shard_map/ppermute | solution.py:36
  108.2 1.8 %collective-permute-start.50 = (f32[8,256]{1,0:T(8,128)S(1)}, f32[8,256]{1,0:T(8,128)S(1)}, u32[]{:S(2)}, u32[]{:S(2)}) collective-permute-start(f32[8,256]{1,0:T(8,128)S(1)} %get-tuple-element.62), channel_id=1, source_target_pairs={{16,8},{17,9},{18,10},{19,11},{20,12},{21,13},{22,14},{23,15},{8,0... | collective-permute-start | bytes 24584 | tf_op jit(solution)/shard_map/ppermute | solution.py:58
  110.0 1.8 %collective-permute-start.51 = (f32[8,256]{1,0:T(8,128)S(1)}, f32[8,256]{1,0:T(8,128)S(1)}, u32[]{:S(2)}, u32[]{:S(2)}) collective-permute-start(f32[8,256]{1,0:T(8,128)S(1)} %get-tuple-element.62), channel_id=1, source_target_pairs={{16,9},{17,8},{18,11},{19,10},{20,13},{21,12},{22,15},{23,14},{8,1... | collective-permute-start | bytes 24584 | tf_op jit(solution)/shard_map/ppermute | solution.py:58
  113.2 2.3 %collective-permute-start.52 = (bf16[8,2560]{1,0:T(8,128)(2,1)S(1)}, bf16[8,2560]{1,0:T(8,128)(2,1)S(1)}, u32[]{:S(2)}, u32[]{:S(2)}) collective-permute-start(bf16[8,2560]{1,0:T(8,128)(2,1)S(1)} %get-tuple-element.63), channel_id=1, source_target_pairs={{0,6},{1,7},{2,4},{3,5},{4,2},{5,3},{6,0},{7,1},{8,14},{9,15},{10,... | collective-permute-start | bytes 122888 | tf_op jit(solution)/shard_map/ppermute | solution.py:36
  115.9 1.7 %collective-permute-start.54 = (bf16[8,2560]{1,0:T(8,128)(2,1)S(1)}, bf16[8,2560]{1,0:T(8,128)(2,1)S(1)}, u32[]{:S(2)}, u32[]{:S(2)}) collective-permute-start(bf16[8,2560]{1,0:T(8,128)(2,1)S(1)} %get-tuple-element.63), channel_id=1, source_target_pairs={{0,2},{1,3},{2,0},{3,1},{4,6},{5,7},{6,4},{7,5},{8,10},{9,11},{10,... | collective-permute-start | bytes 122888 | tf_op jit(solution)/shard_map/ppermute | solution.py:36
  117.5 2.0 %collective-permute-done.52 = bf16[8,2560]{1,0:T(8,128)(2,1)S(1)} collective-permute-done((bf16[8,2560]{1,0:T(8,128)(2,1)S(1)}, bf16[8,2560]{1,0:T(8,128)(2,1)S(1)}, u32[]{:S(2)}, u32[]{:S(2)}) %collective-permute-start.52) | collective-permute-done | bytes 40992 | tf_op jit(solution)/shard_map/ppermute | solution.py:36
  119.5 1.6 %collective-permute-done.53 = bf16[8,2560]{1,0:T(8,128)(2,1)S(1)} collective-permute-done((bf16[8,2560]{1,0:T(8,128)(2,1)S(1)}, bf16[8,2560]{1,0:T(8,128)(2,1)S(1)}, u32[]{:S(2)}, u32[]{:S(2)}) %collective-permute-start.53) | collective-permute-done | bytes 40992 | tf_op jit(solution)/shard_map/ppermute | solution.py:36
  122.5 1.9 %collective-permute-start.56 = (bf16[8,640]{1,0:T(8,128)(2,1)S(1)}, bf16[8,640]{1,0:T(8,128)(2,1)S(1)}, u32[]{:S(2)}, u32[]{:S(2)}) collective-permute-start(bf16[8,640]{1,0:T(8,128)(2,1)S(1)} %sep_rows.25), channel_id=1, source_target_pairs={{0,6},{1,7},{2,4},{3,5},{4,2},{5,3},{6,0},{7,1},{8,14},{9,15},{10,... | collective-permute-start | bytes 30728 | tf_op jit(solution)/shard_map/ppermute | solution.py:36
  124.4 2.4 %collective-permute-start.58 = (bf16[8,640]{1,0:T(8,128)(2,1)S(1)}, bf16[8,640]{1,0:T(8,128)(2,1)S(1)}, u32[]{:S(2)}, u32[]{:S(2)}) collective-permute-start(bf16[8,640]{1,0:T(8,128)(2,1)S(1)} %sep_rows.25), channel_id=1, source_target_pairs={{0,2},{1,3},{2,0},{3,1},{4,6},{5,7},{6,4},{7,5},{8,10},{9,11},{10,... | collective-permute-start | bytes 30728 | tf_op jit(solution)/shard_map/ppermute | solution.py:36
  129.2 1.9 %collective-permute-start.60 = (f32[8,256]{1,0:T(8,128)S(1)}, f32[8,256]{1,0:T(8,128)S(1)}, u32[]{:S(2)}, u32[]{:S(2)}) collective-permute-start(f32[8,256]{1,0:T(8,128)S(1)} %get-tuple-element.66), channel_id=1, source_target_pairs={{8,0},{9,1},{10,2},{11,3},{12,4},{13,5},{14,6},{15,7},{0,16},{1,17... | collective-permute-start | bytes 24584 | tf_op jit(solution)/shard_map/ppermute | solution.py:58
  131.4 3.0 %collective-permute-done.60.refs_0_ = f32[8,256]{1,0:T(8,128)S(1)} collective-permute-done((f32[8,256]{1,0:T(8,128)S(1)}, f32[8,256]{1,0:T(8,128)S(1)}, u32[]{:S(2)}, u32[]{:S(2)}) %collective-permute-start.60) | collective-permute-done | bytes 8224 | tf_op jit(solution)/shard_map/ppermute | solution.py:58
  135.1 1.6 %collective-permute-start.62 = (bf16[8,2560]{1,0:T(8,128)(2,1)S(1)}, bf16[8,2560]{1,0:T(8,128)(2,1)S(1)}, u32[]{:S(2)}, u32[]{:S(2)}) collective-permute-start(bf16[8,2560]{1,0:T(8,128)(2,1)S(1)} %get-tuple-element.68), channel_id=1, source_target_pairs={{0,6},{1,7},{2,4},{3,5},{4,2},{5,3},{6,0},{7,1},{8,14},{9,15},{10,... | collective-permute-start | bytes 122888 | tf_op jit(solution)/shard_map/ppermute | solution.py:36
  137.6 2.0 %collective-permute-start.64 = (bf16[8,2560]{1,0:T(8,128)(2,1)S(1)}, bf16[8,2560]{1,0:T(8,128)(2,1)S(1)}, u32[]{:S(2)}, u32[]{:S(2)}) collective-permute-start(bf16[8,2560]{1,0:T(8,128)(2,1)S(1)} %get-tuple-element.68), channel_id=1, source_target_pairs={{0,2},{1,3},{2,0},{3,1},{4,6},{5,7},{6,4},{7,5},{8,10},{9,11},{10,... | collective-permute-start | bytes 122888 | tf_op jit(solution)/shard_map/ppermute | solution.py:36
  139.5 1.6 %collective-permute-done.62 = bf16[8,2560]{1,0:T(8,128)(2,1)S(1)} collective-permute-done((bf16[8,2560]{1,0:T(8,128)(2,1)S(1)}, bf16[8,2560]{1,0:T(8,128)(2,1)S(1)}, u32[]{:S(2)}, u32[]{:S(2)}) %collective-permute-start.62) | collective-permute-done | bytes 40992 | tf_op jit(solution)/shard_map/ppermute | solution.py:36
  144.6 2.4 %collective-permute-start.66 = (bf16[8,640]{1,0:T(8,128)(2,1)S(1)}, bf16[8,640]{1,0:T(8,128)(2,1)S(1)}, u32[]{:S(2)}, u32[]{:S(2)}) collective-permute-start(bf16[8,640]{1,0:T(8,128)(2,1)S(1)} %sep_rows.27), channel_id=1, source_target_pairs={{0,6},{1,7},{2,4},{3,5},{4,2},{5,3},{6,0},{7,1},{8,14},{9,15},{10,... | collective-permute-start | bytes 30728 | tf_op jit(solution)/shard_map/ppermute | solution.py:36
  147.3 1.7 %collective-permute-start.68 = (bf16[8,640]{1,0:T(8,128)(2,1)S(1)}, bf16[8,640]{1,0:T(8,128)(2,1)S(1)}, u32[]{:S(2)}, u32[]{:S(2)}) collective-permute-start(bf16[8,640]{1,0:T(8,128)(2,1)S(1)} %sep_rows.27), channel_id=1, source_target_pairs={{0,2},{1,3},{2,0},{3,1},{4,6},{5,7},{6,4},{7,5},{8,10},{9,11},{10,... | collective-permute-start | bytes 30728 | tf_op jit(solution)/shard_map/ppermute | solution.py:36
  (154 shorter events, 51.2 us)
Async XLA Ops:
  4.2 18.3 %collective-permute-start.8 = (bf16[2,128,5504]{2,1,0:T(8,128)(2,1)S(1)}, bf16[2,128,5504]{2,1,0:T(8,128)(2,1)S(1)}, u32[]{:S(2)}, u32[]{:S(2)}) collective-permute-start(bf16[2,128,5504]{2,1,0:T(8,128)(2,1)S(1)} %get-tuple-element.42.own_ref), channel_id=1, source_target_pairs={{0,1},{1,0},{2,3},{3,2},{4,5},{5,4},{6,7},{7,6},{8,9},{9,8},{10,11... | collective-permute-start | bytes 8454152 | tf_op jit(solution)/shard_map/ppermute | solution.py:21
  4.6 22.4 %collective-permute-start.11 = (bf16[2,5120,128]{2,1,0:T(8,128)(2,1)S(1)}, bf16[2,5120,128]{2,1,0:T(8,128)(2,1)S(1)}, u32[]{:S(2)}, u32[]{:S(2)}) collective-permute-start(bf16[2,5120,128]{2,1,0:T(8,128)(2,1)S(1)} %get-tuple-element.46.own_ref), channel_id=1, source_target_pairs={{0,1},{1,0},{2,3},{3,2},{4,5},{5,4},{6,7},{7,6},{8,9},{9,8},{10,11... | collective-permute-start | bytes 7864328 | tf_op jit(solution)/shard_map/ppermute | solution.py:21
  4.7 10.9 %collective-permute-start.1 = (bf16[8,2560]{1,0:T(8,128)(2,1)S(1)}, bf16[8,2560]{1,0:T(8,128)(2,1)S(1)}, u32[]{:S(2)}, u32[]{:S(2)}) collective-permute-start(bf16[8,2560]{1,0:T(8,128)(2,1)S(1)} %fusion._.refs_0_.refs_2_), channel_id=1, source_target_pairs={{0,6},{1,7},{2,4},{3,5},{4,2},{5,3},{6,0},{7,1},{8,14},{9,15},{10,... | collective-permute-start | bytes 122888 | tf_op jit(solution)/shard_map/ppermute | solution.py:36
  9.7 5.9 %collective-permute-start.2 = (bf16[8,2560]{1,0:T(8,128)(2,1)S(1)}, bf16[8,2560]{1,0:T(8,128)(2,1)S(1)}, u32[]{:S(2)}, u32[]{:S(2)}) collective-permute-start(bf16[8,2560]{1,0:T(8,128)(2,1)S(1)} %fusion._.refs_0_.refs_2_), channel_id=1, source_target_pairs={{0,4},{1,5},{2,6},{3,7},{4,0},{5,1},{6,2},{7,3},{8,12},{9,13},{10,... | collective-permute-start | bytes 122888 | tf_op jit(solution)/shard_map/ppermute | solution.py:36
  9.7 5.9 %collective-permute-start.3 = (bf16[8,2560]{1,0:T(8,128)(2,1)S(1)}, bf16[8,2560]{1,0:T(8,128)(2,1)S(1)}, u32[]{:S(2)}, u32[]{:S(2)}) collective-permute-start(bf16[8,2560]{1,0:T(8,128)(2,1)S(1)} %fusion._.refs_0_.refs_2_), channel_id=1, source_target_pairs={{0,2},{1,3},{2,0},{3,1},{4,6},{5,7},{6,4},{7,5},{8,10},{9,11},{10,... | collective-permute-start | bytes 122888 | tf_op jit(solution)/shard_map/ppermute | solution.py:36
  17.9 5.9 %collective-permute-start.5 = (bf16[8,640]{1,0:T(8,128)(2,1)S(1)}, bf16[8,640]{1,0:T(8,128)(2,1)S(1)}, u32[]{:S(2)}, u32[]{:S(2)}) collective-permute-start(bf16[8,640]{1,0:T(8,128)(2,1)S(1)} %sep_rows.15._.refs_0_), channel_id=1, source_target_pairs={{0,6},{1,7},{2,4},{3,5},{4,2},{5,3},{6,0},{7,1},{8,14},{9,15},{10,... | collective-permute-start | bytes 30728 | tf_op jit(solution)/shard_map/ppermute | solution.py:36
  21.8 4.6 %collective-permute-start.6 = (bf16[8,640]{1,0:T(8,128)(2,1)S(1)}, bf16[8,640]{1,0:T(8,128)(2,1)S(1)}, u32[]{:S(2)}, u32[]{:S(2)}) collective-permute-start(bf16[8,640]{1,0:T(8,128)(2,1)S(1)} %sep_rows.15._.refs_0_), channel_id=1, source_target_pairs={{0,4},{1,5},{2,6},{3,7},{4,0},{5,1},{6,2},{7,3},{8,12},{9,13},{10,... | collective-permute-start | bytes 30728 | tf_op jit(solution)/shard_map/ppermute | solution.py:36
  21.8 4.6 %collective-permute-start.7 = (bf16[8,640]{1,0:T(8,128)(2,1)S(1)}, bf16[8,640]{1,0:T(8,128)(2,1)S(1)}, u32[]{:S(2)}, u32[]{:S(2)}) collective-permute-start(bf16[8,640]{1,0:T(8,128)(2,1)S(1)} %sep_rows.15._.refs_0_), channel_id=1, source_target_pairs={{0,2},{1,3},{2,0},{3,1},{4,6},{5,7},{6,4},{7,5},{8,10},{9,11},{10,... | collective-permute-start | bytes 30728 | tf_op jit(solution)/shard_map/ppermute | solution.py:36
  26.8 4.6 %collective-permute-start.9 = (f32[8,256]{1,0:T(8,128)S(1)}, f32[8,256]{1,0:T(8,128)S(1)}, u32[]{:S(2)}, u32[]{:S(2)}) collective-permute-start(f32[8,256]{1,0:T(8,128)S(1)} %get-tuple-element.44._), channel_id=1, source_target_pairs={{0,8},{1,9},{2,10},{3,11},{4,12},{5,13},{6,14},{7,15},{8,16},{9,17... | collective-permute-start | bytes 24584 | tf_op jit(solution)/shard_map/ppermute | solution.py:58
  31.4 6.3 %collective-permute-start.12 = (bf16[8,2560]{1,0:T(8,128)(2,1)S(1)}, bf16[8,2560]{1,0:T(8,128)(2,1)S(1)}, u32[]{:S(2)}, u32[]{:S(2)}) collective-permute-start(bf16[8,2560]{1,0:T(8,128)(2,1)S(1)} %get-tuple-element.47), channel_id=1, source_target_pairs={{0,6},{1,7},{2,4},{3,5},{4,2},{5,3},{6,0},{7,1},{8,14},{9,15},{10,... | collective-permute-start | bytes 122888 | tf_op jit(solution)/shard_map/ppermute | solution.py:36
  32.9 5.5 %collective-permute-start.13 = (bf16[8,2560]{1,0:T(8,128)(2,1)S(1)}, bf16[8,2560]{1,0:T(8,128)(2,1)S(1)}, u32[]{:S(2)}, u32[]{:S(2)}) collective-permute-start(bf16[8,2560]{1,0:T(8,128)(2,1)S(1)} %get-tuple-element.47), channel_id=1, source_target_pairs={{0,4},{1,5},{2,6},{3,7},{4,0},{5,1},{6,2},{7,3},{8,12},{9,13},{10,... | collective-permute-start | bytes 122888 | tf_op jit(solution)/shard_map/ppermute | solution.py:36
  33.4 4.9 %collective-permute-start.14 = (bf16[8,2560]{1,0:T(8,128)(2,1)S(1)}, bf16[8,2560]{1,0:T(8,128)(2,1)S(1)}, u32[]{:S(2)}, u32[]{:S(2)}) collective-permute-start(bf16[8,2560]{1,0:T(8,128)(2,1)S(1)} %get-tuple-element.47), channel_id=1, source_target_pairs={{0,2},{1,3},{2,0},{3,1},{4,6},{5,7},{6,4},{7,5},{8,10},{9,11},{10,... | collective-permute-start | bytes 122888 | tf_op jit(solution)/shard_map/ppermute | solution.py:36
  39.7 5.5 %collective-permute-start.16 = (bf16[8,640]{1,0:T(8,128)(2,1)S(1)}, bf16[8,640]{1,0:T(8,128)(2,1)S(1)}, u32[]{:S(2)}, u32[]{:S(2)}) collective-permute-start(bf16[8,640]{1,0:T(8,128)(2,1)S(1)} %sep_rows.17), channel_id=1, source_target_pairs={{0,6},{1,7},{2,4},{3,5},{4,2},{5,3},{6,0},{7,1},{8,14},{9,15},{10,... | collective-permute-start | bytes 30728 | tf_op jit(solution)/shard_map/ppermute | solution.py:36
  41.9 4.6 %collective-permute-start.17 = (bf16[8,640]{1,0:T(8,128)(2,1)S(1)}, bf16[8,640]{1,0:T(8,128)(2,1)S(1)}, u32[]{:S(2)}, u32[]{:S(2)}) collective-permute-start(bf16[8,640]{1,0:T(8,128)(2,1)S(1)} %sep_rows.17), channel_id=1, source_target_pairs={{0,4},{1,5},{2,6},{3,7},{4,0},{5,1},{6,2},{7,3},{8,12},{9,13},{10,... | collective-permute-start | bytes 30728 | tf_op jit(solution)/shard_map/ppermute | solution.py:36
  50.5 6.1 %collective-permute-start.21 = (bf16[8,2560]{1,0:T(8,128)(2,1)S(1)}, bf16[8,2560]{1,0:T(8,128)(2,1)S(1)}, u32[]{:S(2)}, u32[]{:S(2)}) collective-permute-start(bf16[8,2560]{1,0:T(8,128)(2,1)S(1)} %get-tuple-element.50), channel_id=1, source_target_pairs={{0,6},{1,7},{2,4},{3,5},{4,2},{5,3},{6,0},{7,1},{8,14},{9,15},{10,... | collective-permute-start | bytes 122888 | tf_op jit(solution)/shard_map/ppermute | solution.py:36
  52.3 5.7 %collective-permute-start.22 = (bf16[8,2560]{1,0:T(8,128)(2,1)S(1)}, bf16[8,2560]{1,0:T(8,128)(2,1)S(1)}, u32[]{:S(2)}, u32[]{:S(2)}) collective-permute-start(bf16[8,2560]{1,0:T(8,128)(2,1)S(1)} %get-tuple-element.50), channel_id=1, source_target_pairs={{0,4},{1,5},{2,6},{3,7},{4,0},{5,1},{6,2},{7,3},{8,12},{9,13},{10,... | collective-permute-start | bytes 122888 | tf_op jit(solution)/shard_map/ppermute | solution.py:36
  53.3 4.6 %collective-permute-start.23 = (bf16[8,2560]{1,0:T(8,128)(2,1)S(1)}, bf16[8,2560]{1,0:T(8,128)(2,1)S(1)}, u32[]{:S(2)}, u32[]{:S(2)}) collective-permute-start(bf16[8,2560]{1,0:T(8,128)(2,1)S(1)} %get-tuple-element.50), channel_id=1, source_target_pairs={{0,2},{1,3},{2,0},{3,1},{4,6},{5,7},{6,4},{7,5},{8,10},{9,11},{10,... | collective-permute-start | bytes 122888 | tf_op jit(solution)/shard_map/ppermute | solution.py:36
  59.3 5.5 %collective-permute-start.25 = (bf16[8,640]{1,0:T(8,128)(2,1)S(1)}, bf16[8,640]{1,0:T(8,128)(2,1)S(1)}, u32[]{:S(2)}, u32[]{:S(2)}) collective-permute-start(bf16[8,640]{1,0:T(8,128)(2,1)S(1)} %sep_rows.19), channel_id=1, source_target_pairs={{0,6},{1,7},{2,4},{3,5},{4,2},{5,3},{6,0},{7,1},{8,14},{9,15},{10,... | collective-permute-start | bytes 30728 | tf_op jit(solution)/shard_map/ppermute | solution.py:36
  61.4 4.6 %collective-permute-start.26 = (bf16[8,640]{1,0:T(8,128)(2,1)S(1)}, bf16[8,640]{1,0:T(8,128)(2,1)S(1)}, u32[]{:S(2)}, u32[]{:S(2)}) collective-permute-start(bf16[8,640]{1,0:T(8,128)(2,1)S(1)} %sep_rows.19), channel_id=1, source_target_pairs={{0,4},{1,5},{2,6},{3,7},{4,0},{5,1},{6,2},{7,3},{8,12},{9,13},{10,... | collective-permute-start | bytes 30728 | tf_op jit(solution)/shard_map/ppermute | solution.py:36
  61.6 4.3 %collective-permute-start.27 = (bf16[8,640]{1,0:T(8,128)(2,1)S(1)}, bf16[8,640]{1,0:T(8,128)(2,1)S(1)}, u32[]{:S(2)}, u32[]{:S(2)}) collective-permute-start(bf16[8,640]{1,0:T(8,128)(2,1)S(1)} %sep_rows.19), channel_id=1, source_target_pairs={{0,2},{1,3},{2,0},{3,1},{4,6},{5,7},{6,4},{7,5},{8,10},{9,11},{10,... | collective-permute-start | bytes 30728 | tf_op jit(solution)/shard_map/ppermute | solution.py:36
  66.0 4.8 %collective-permute-start.28 = (f32[8,256]{1,0:T(8,128)S(1)}, f32[8,256]{1,0:T(8,128)S(1)}, u32[]{:S(2)}, u32[]{:S(2)}) collective-permute-start(f32[8,256]{1,0:T(8,128)S(1)} %get-tuple-element.52), channel_id=1, source_target_pairs={{16,24},{17,25},{18,26},{19,27},{20,28},{21,29},{22,30},{23,31},{2... | collective-permute-start | bytes 24584 | tf_op jit(solution)/shard_map/ppermute | solution.py:58
  71.5 6.3 %collective-permute-start.30 = (bf16[8,2560]{1,0:T(8,128)(2,1)S(1)}, bf16[8,2560]{1,0:T(8,128)(2,1)S(1)}, u32[]{:S(2)}, u32[]{:S(2)}) collective-permute-start(bf16[8,2560]{1,0:T(8,128)(2,1)S(1)} %get-tuple-element.53), channel_id=1, source_target_pairs={{0,6},{1,7},{2,4},{3,5},{4,2},{5,3},{6,0},{7,1},{8,14},{9,15},{10,... | collective-permute-start | bytes 122888 | tf_op jit(solution)/shard_map/ppermute | solution.py:36
  73.2 6.2 %collective-permute-start.31 = (bf16[8,2560]{1,0:T(8,128)(2,1)S(1)}, bf16[8,2560]{1,0:T(8,128)(2,1)S(1)}, u32[]{:S(2)}, u32[]{:S(2)}) collective-permute-start(bf16[8,2560]{1,0:T(8,128)(2,1)S(1)} %get-tuple-element.53), channel_id=1, source_target_pairs={{0,4},{1,5},{2,6},{3,7},{4,0},{5,1},{6,2},{7,3},{8,12},{9,13},{10,... | collective-permute-start | bytes 122888 | tf_op jit(solution)/shard_map/ppermute | solution.py:36
  74.2 5.2 %collective-permute-start.32 = (bf16[8,2560]{1,0:T(8,128)(2,1)S(1)}, bf16[8,2560]{1,0:T(8,128)(2,1)S(1)}, u32[]{:S(2)}, u32[]{:S(2)}) collective-permute-start(bf16[8,2560]{1,0:T(8,128)(2,1)S(1)} %get-tuple-element.53), channel_id=1, source_target_pairs={{0,2},{1,3},{2,0},{3,1},{4,6},{5,7},{6,4},{7,5},{8,10},{9,11},{10,... | collective-permute-start | bytes 122888 | tf_op jit(solution)/shard_map/ppermute | solution.py:36
  80.8 5.5 %collective-permute-start.34 = (bf16[8,640]{1,0:T(8,128)(2,1)S(1)}, bf16[8,640]{1,0:T(8,128)(2,1)S(1)}, u32[]{:S(2)}, u32[]{:S(2)}) collective-permute-start(bf16[8,640]{1,0:T(8,128)(2,1)S(1)} %sep_rows.21), channel_id=1, source_target_pairs={{0,6},{1,7},{2,4},{3,5},{4,2},{5,3},{6,0},{7,1},{8,14},{9,15},{10,... | collective-permute-start | bytes 30728 | tf_op jit(solution)/shard_map/ppermute | solution.py:36
  82.7 4.6 %collective-permute-start.35 = (bf16[8,640]{1,0:T(8,128)(2,1)S(1)}, bf16[8,640]{1,0:T(8,128)(2,1)S(1)}, u32[]{:S(2)}, u32[]{:S(2)}) collective-permute-start(bf16[8,640]{1,0:T(8,128)(2,1)S(1)} %sep_rows.21), channel_id=1, source_target_pairs={{0,4},{1,5},{2,6},{3,7},{4,0},{5,1},{6,2},{7,3},{8,12},{9,13},{10,... | collective-permute-start | bytes 30728 | tf_op jit(solution)/shard_map/ppermute | solution.py:36
  82.7 4.6 %collective-permute-start.36 = (bf16[8,640]{1,0:T(8,128)(2,1)S(1)}, bf16[8,640]{1,0:T(8,128)(2,1)S(1)}, u32[]{:S(2)}, u32[]{:S(2)}) collective-permute-start(bf16[8,640]{1,0:T(8,128)(2,1)S(1)} %sep_rows.21), channel_id=1, source_target_pairs={{0,2},{1,3},{2,0},{3,1},{4,6},{5,7},{6,4},{7,5},{8,10},{9,11},{10,... | collective-permute-start | bytes 30728 | tf_op jit(solution)/shard_map/ppermute | solution.py:36
  87.3 4.4 %collective-permute-start.37 = (f32[8,256]{1,0:T(8,128)S(1)}, f32[8,256]{1,0:T(8,128)S(1)}, u32[]{:S(2)}, u32[]{:S(2)}) collective-permute-start(f32[8,256]{1,0:T(8,128)S(1)} %get-tuple-element.55), channel_id=1, source_target_pairs={{24,16},{25,17},{26,18},{27,19},{28,20},{29,21},{30,22},{31,23},{1... | collective-permute-start | bytes 24584 | tf_op jit(solution)/shard_map/ppermute | solution.py:58
  93.0 6.3 %collective-permute-start.39 = (bf16[8,2560]{1,0:T(8,128)(2,1)S(1)}, bf16[8,2560]{1,0:T(8,128)(2,1)S(1)}, u32[]{:S(2)}, u32[]{:S(2)}) collective-permute-start(bf16[8,2560]{1,0:T(8,128)(2,1)S(1)} %get-tuple-element.56), channel_id=1, source_target_pairs={{0,6},{1,7},{2,4},{3,5},{4,2},{5,3},{6,0},{7,1},{8,14},{9,15},{10,... | collective-permute-start | bytes 122888 | tf_op jit(solution)/shard_map/ppermute | solution.py:36
  94.5 5.5 %collective-permute-start.40 = (bf16[8,2560]{1,0:T(8,128)(2,1)S(1)}, bf16[8,2560]{1,0:T(8,128)(2,1)S(1)}, u32[]{:S(2)}, u32[]{:S(2)}) collective-permute-start(bf16[8,2560]{1,0:T(8,128)(2,1)S(1)} %get-tuple-element.56), channel_id=1, source_target_pairs={{0,4},{1,5},{2,6},{3,7},{4,0},{5,1},{6,2},{7,3},{8,12},{9,13},{10,... | collective-permute-start | bytes 122888 | tf_op jit(solution)/shard_map/ppermute | solution.py:36
  95.4 4.6 %collective-permute-start.41 = (bf16[8,2560]{1,0:T(8,128)(2,1)S(1)}, bf16[8,2560]{1,0:T(8,128)(2,1)S(1)}, u32[]{:S(2)}, u32[]{:S(2)}) collective-permute-start(bf16[8,2560]{1,0:T(8,128)(2,1)S(1)} %get-tuple-element.56), channel_id=1, source_target_pairs={{0,2},{1,3},{2,0},{3,1},{4,6},{5,7},{6,4},{7,5},{8,10},{9,11},{10,... | collective-permute-start | bytes 122888 | tf_op jit(solution)/shard_map/ppermute | solution.py:36
  100.1 5.6 %collective-permute-start.49 = (f32[8,256]{1,0:T(8,128)S(1)}, f32[8,256]{1,0:T(8,128)S(1)}, u32[]{:S(2)}, u32[]{:S(2)}) collective-permute-start(f32[8,256]{1,0:T(8,128)S(1)} %get-tuple-element.61.refs_1_), channel_id=1, source_target_pairs={{0,1},{1,0},{2,3},{3,2},{4,5},{5,4},{6,7},{7,6},{8,9},{9,8},{10,11... | collective-permute-start | bytes 24584 | tf_op jit(solution)/shard_map/ppermute | solution.py:21
  100.6 5.1 %collective-permute-start.48 = (f32[8,256]{1,0:T(8,128)S(1)}, f32[8,256]{1,0:T(8,128)S(1)}, u32[]{:S(2)}, u32[]{:S(2)}) collective-permute-start(f32[8,256]{1,0:T(8,128)S(1)} %get-tuple-element.60.refs_1_), channel_id=1, source_target_pairs={{0,1},{1,0},{2,3},{3,2},{4,5},{5,4},{6,7},{7,6},{8,9},{9,8},{10,11... | collective-permute-start | bytes 24584 | tf_op jit(solution)/shard_map/ppermute | solution.py:21
  101.3 5.7 %collective-permute-start.43 = (bf16[8,640]{1,0:T(8,128)(2,1)S(1)}, bf16[8,640]{1,0:T(8,128)(2,1)S(1)}, u32[]{:S(2)}, u32[]{:S(2)}) collective-permute-start(bf16[8,640]{1,0:T(8,128)(2,1)S(1)} %sep_rows.23), channel_id=1, source_target_pairs={{0,6},{1,7},{2,4},{3,5},{4,2},{5,3},{6,0},{7,1},{8,14},{9,15},{10,... | collective-permute-start | bytes 30728 | tf_op jit(solution)/shard_map/ppermute | solution.py:36
  103.6 4.6 %collective-permute-start.44 = (bf16[8,640]{1,0:T(8,128)(2,1)S(1)}, bf16[8,640]{1,0:T(8,128)(2,1)S(1)}, u32[]{:S(2)}, u32[]{:S(2)}) collective-permute-start(bf16[8,640]{1,0:T(8,128)(2,1)S(1)} %sep_rows.23), channel_id=1, source_target_pairs={{0,4},{1,5},{2,6},{3,7},{4,0},{5,1},{6,2},{7,3},{8,12},{9,13},{10,... | collective-permute-start | bytes 30728 | tf_op jit(solution)/shard_map/ppermute | solution.py:36
  113.2 6.4 %collective-permute-start.52 = (bf16[8,2560]{1,0:T(8,128)(2,1)S(1)}, bf16[8,2560]{1,0:T(8,128)(2,1)S(1)}, u32[]{:S(2)}, u32[]{:S(2)}) collective-permute-start(bf16[8,2560]{1,0:T(8,128)(2,1)S(1)} %get-tuple-element.63), channel_id=1, source_target_pairs={{0,6},{1,7},{2,4},{3,5},{4,2},{5,3},{6,0},{7,1},{8,14},{9,15},{10,... | collective-permute-start | bytes 122888 | tf_op jit(solution)/shard_map/ppermute | solution.py:36
  115.4 5.7 %collective-permute-start.53 = (bf16[8,2560]{1,0:T(8,128)(2,1)S(1)}, bf16[8,2560]{1,0:T(8,128)(2,1)S(1)}, u32[]{:S(2)}, u32[]{:S(2)}) collective-permute-start(bf16[8,2560]{1,0:T(8,128)(2,1)S(1)} %get-tuple-element.63), channel_id=1, source_target_pairs={{0,4},{1,5},{2,6},{3,7},{4,0},{5,1},{6,2},{7,3},{8,12},{9,13},{10,... | collective-permute-start | bytes 122888 | tf_op jit(solution)/shard_map/ppermute | solution.py:36
  115.9 5.3 %collective-permute-start.54 = (bf16[8,2560]{1,0:T(8,128)(2,1)S(1)}, bf16[8,2560]{1,0:T(8,128)(2,1)S(1)}, u32[]{:S(2)}, u32[]{:S(2)}) collective-permute-start(bf16[8,2560]{1,0:T(8,128)(2,1)S(1)} %get-tuple-element.63), channel_id=1, source_target_pairs={{0,2},{1,3},{2,0},{3,1},{4,6},{5,7},{6,4},{7,5},{8,10},{9,11},{10,... | collective-permute-start | bytes 122888 | tf_op jit(solution)/shard_map/ppermute | solution.py:36
  122.5 5.6 %collective-permute-start.56 = (bf16[8,640]{1,0:T(8,128)(2,1)S(1)}, bf16[8,640]{1,0:T(8,128)(2,1)S(1)}, u32[]{:S(2)}, u32[]{:S(2)}) collective-permute-start(bf16[8,640]{1,0:T(8,128)(2,1)S(1)} %sep_rows.25), channel_id=1, source_target_pairs={{0,6},{1,7},{2,4},{3,5},{4,2},{5,3},{6,0},{7,1},{8,14},{9,15},{10,... | collective-permute-start | bytes 30728 | tf_op jit(solution)/shard_map/ppermute | solution.py:36
  124.4 4.6 %collective-permute-start.57 = (bf16[8,640]{1,0:T(8,128)(2,1)S(1)}, bf16[8,640]{1,0:T(8,128)(2,1)S(1)}, u32[]{:S(2)}, u32[]{:S(2)}) collective-permute-start(bf16[8,640]{1,0:T(8,128)(2,1)S(1)} %sep_rows.25), channel_id=1, source_target_pairs={{0,4},{1,5},{2,6},{3,7},{4,0},{5,1},{6,2},{7,3},{8,12},{9,13},{10,... | collective-permute-start | bytes 30728 | tf_op jit(solution)/shard_map/ppermute | solution.py:36
  124.4 4.6 %collective-permute-start.58 = (bf16[8,640]{1,0:T(8,128)(2,1)S(1)}, bf16[8,640]{1,0:T(8,128)(2,1)S(1)}, u32[]{:S(2)}, u32[]{:S(2)}) collective-permute-start(bf16[8,640]{1,0:T(8,128)(2,1)S(1)} %sep_rows.25), channel_id=1, source_target_pairs={{0,2},{1,3},{2,0},{3,1},{4,6},{5,7},{6,4},{7,5},{8,10},{9,11},{10,... | collective-permute-start | bytes 30728 | tf_op jit(solution)/shard_map/ppermute | solution.py:36
  129.2 5.1 %collective-permute-start.60 = (f32[8,256]{1,0:T(8,128)S(1)}, f32[8,256]{1,0:T(8,128)S(1)}, u32[]{:S(2)}, u32[]{:S(2)}) collective-permute-start(f32[8,256]{1,0:T(8,128)S(1)} %get-tuple-element.66), channel_id=1, source_target_pairs={{8,0},{9,1},{10,2},{11,3},{12,4},{13,5},{14,6},{15,7},{0,16},{1,17... | collective-permute-start | bytes 24584 | tf_op jit(solution)/shard_map/ppermute | solution.py:58
  135.1 6.0 %collective-permute-start.62 = (bf16[8,2560]{1,0:T(8,128)(2,1)S(1)}, bf16[8,2560]{1,0:T(8,128)(2,1)S(1)}, u32[]{:S(2)}, u32[]{:S(2)}) collective-permute-start(bf16[8,2560]{1,0:T(8,128)(2,1)S(1)} %get-tuple-element.68), channel_id=1, source_target_pairs={{0,6},{1,7},{2,4},{3,5},{4,2},{5,3},{6,0},{7,1},{8,14},{9,15},{10,... | collective-permute-start | bytes 122888 | tf_op jit(solution)/shard_map/ppermute | solution.py:36
  136.7 5.6 %collective-permute-start.63 = (bf16[8,2560]{1,0:T(8,128)(2,1)S(1)}, bf16[8,2560]{1,0:T(8,128)(2,1)S(1)}, u32[]{:S(2)}, u32[]{:S(2)}) collective-permute-start(bf16[8,2560]{1,0:T(8,128)(2,1)S(1)} %get-tuple-element.68), channel_id=1, source_target_pairs={{0,4},{1,5},{2,6},{3,7},{4,0},{5,1},{6,2},{7,3},{8,12},{9,13},{10,... | collective-permute-start | bytes 122888 | tf_op jit(solution)/shard_map/ppermute | solution.py:36
  137.6 4.7 %collective-permute-start.64 = (bf16[8,2560]{1,0:T(8,128)(2,1)S(1)}, bf16[8,2560]{1,0:T(8,128)(2,1)S(1)}, u32[]{:S(2)}, u32[]{:S(2)}) collective-permute-start(bf16[8,2560]{1,0:T(8,128)(2,1)S(1)} %get-tuple-element.68), channel_id=1, source_target_pairs={{0,2},{1,3},{2,0},{3,1},{4,6},{5,7},{6,4},{7,5},{8,10},{9,11},{10,... | collective-permute-start | bytes 122888 | tf_op jit(solution)/shard_map/ppermute | solution.py:36
  144.6 5.6 %collective-permute-start.66 = (bf16[8,640]{1,0:T(8,128)(2,1)S(1)}, bf16[8,640]{1,0:T(8,128)(2,1)S(1)}, u32[]{:S(2)}, u32[]{:S(2)}) collective-permute-start(bf16[8,640]{1,0:T(8,128)(2,1)S(1)} %sep_rows.27), channel_id=1, source_target_pairs={{0,6},{1,7},{2,4},{3,5},{4,2},{5,3},{6,0},{7,1},{8,14},{9,15},{10,... | collective-permute-start | bytes 30728 | tf_op jit(solution)/shard_map/ppermute | solution.py:36
  146.9 4.6 %collective-permute-start.67 = (bf16[8,640]{1,0:T(8,128)(2,1)S(1)}, bf16[8,640]{1,0:T(8,128)(2,1)S(1)}, u32[]{:S(2)}, u32[]{:S(2)}) collective-permute-start(bf16[8,640]{1,0:T(8,128)(2,1)S(1)} %sep_rows.27), channel_id=1, source_target_pairs={{0,4},{1,5},{2,6},{3,7},{4,0},{5,1},{6,2},{7,3},{8,12},{9,13},{10,... | collective-permute-start | bytes 30728 | tf_op jit(solution)/shard_map/ppermute | solution.py:36
  147.3 4.2 %collective-permute-start.68 = (bf16[8,640]{1,0:T(8,128)(2,1)S(1)}, bf16[8,640]{1,0:T(8,128)(2,1)S(1)}, u32[]{:S(2)}, u32[]{:S(2)}) collective-permute-start(bf16[8,640]{1,0:T(8,128)(2,1)S(1)} %sep_rows.27), channel_id=1, source_target_pairs={{0,2},{1,3},{2,0},{3,1},{4,6},{5,7},{6,4},{7,5},{8,10},{9,11},{10,... | collective-permute-start | bytes 30728 | tf_op jit(solution)/shard_map/ppermute | solution.py:36
  (24 other events, 58.0 us)

commit v7 on v6

--- a/solution.py
+++ b/solution.py
@@ -393,13 +393,142 @@
     )(*given, blocks, in_vmem(gather))
 
 
+def folded(blocks, gather, kind, layers, after):
+    cells = blocks.shape[3]
+
+    def kernel(blocks_ref, gather_ref, _, out):
+        layer = lax.axis_index("layer")
+
+        @pl.when(jnp.logical_and(layer >= layers[0], layer <= layers[-1]))
+        def _():
+            for side in range(2):
+                left = [blocks_ref[side, 0, part] for part in range(2)]
+                right = [blocks_ref[side, kind, part] for part in range(2)]
+
+                def product(i, j, left=left, right=right):
+                    return jnp.dot(left[i], right[j], preferred_element_type=F32)
+
+                real = (product(0, 0) - product(1, 1)).T
+                imag = (product(0, 1) + product(1, 0)).T
+                at = pl.ds(side * cells, cells)
+                maps = [gather_ref[part, at, :] for part in range(2)]
+
+                def applied(matrix, part, maps=maps):
+                    return jnp.dot(matrix.astype(BF16), maps[part], preferred_element_type=F32)
+
+                out[0, at, :] = (applied(real, 0) - applied(imag, 1)).astype(BF16)
+                out[1, at, :] = (applied(real, 1) + applied(imag, 0)).astype(BF16)
+
+    return pl.pallas_call(
+        kernel,
+        in_specs=[VMEM, VMEM, ANY],
+        out_specs=VMEM,
+        out_shape=pltpu.VMEM(gather.shape, BF16),
+        compiler_params=params(20),
+        cost_estimate=cost(8 * cells * gather.size, 4 * gather.size),
+        name="folded",
+    )(blocks, in_vmem(gather), after)
+
+
+def block_products(vector, blocks_ref, kind):
+    cells = blocks_ref.shape[3]
+    return jnp.concatenate(
+        [
+            times(
+                vector[:, side * cells : (side + 1) * cells],
+                blocks_ref[side, kind, 0],
+                blocks_ref[side, kind, 1],
+                1,
+            )
+            for side in range(2)
+        ],
+        axis=1,
+    )
+
+
+def source_sums(blocks, gather, sources, layers):
+    def kernel(blocks_ref, gather_ref, sources_ref, leaf_out, sums_out):
+        layer = lax.axis_index("layer")
+
+        @pl.when(jnp.logical_and(layer >= layers[0], layer <= layers[-1]))
+        def _():
+            leaf_values = block_products(sources_ref[...], blocks_ref, 0)
+            leaf_out[...] = leaf_values
+            sums_out[...] = times(leaf_values, gather_ref[0], gather_ref[1], 0)
+
+    return pl.pallas_call(
+        kernel,
+        in_specs=[VMEM] * 3,
+        out_specs=[VMEM] * 2,
+        out_shape=[
+            jax.ShapeDtypeStruct(sources.shape, F32),
+            jax.ShapeDtypeStruct((8, gather.shape[2]), F32),
+        ],
+        compiler_params=params(16),
+        cost_estimate=cost(32 * gather.size, 2 * gather.size),
+        name="source_sums",
+    )(blocks, in_vmem(gather), sources)
+
+
+def folded_sums(level, arrived, fold, own_sums=None):
+    given = [*arrived] if own_sums is None else [*arrived, own_sums]
+
+    def kernel(*refs):
+        fold_ref, out = refs[-2:]
+        cells = refs[0].shape[1] // 2
+
+        @pl.when(lax.axis_index("layer") == level)
+        def _():
+            crossed = jnp.concatenate([refs[1][:, cells:], refs[1][:, :cells]], axis=1)
+            sums = times(refs[0][...] + crossed, fold_ref[0], fold_ref[1], 0)
+            if own_sums is not None:
+                sums = refs[2][...] - sums
+            out[...] = sums.astype(BF16)
+
+    return pl.pallas_call(
+        kernel,
+        in_specs=[VMEM] * (len(given) + 1),
+        out_specs=VMEM,
+        out_shape=jax.ShapeDtypeStruct((8, fold.shape[2]), BF16),
+        compiler_params=params(16),
+        cost_estimate=cost(32 * fold.size, 2 * fold.size),
+        name="folded_sums",
+    )(*given, in_vmem(fold))
+
+
+def leaf_only(level, arrived, blocks, own_values=None):
+    given = [*arrived] if own_values is None else [*arrived, own_values]
+
+    def kernel(*refs):
+        blocks_ref, out = refs[-2:]
+        cells = blocks_ref.shape[3]
+
+        @pl.when(lax.axis_index("layer") == level)
+        def _():
+            crossed = jnp.concatenate([refs[1][:, cells:], refs[1][:, :cells]], axis=1)
+            kind = 2 if own_values is None else 1
+            coupled = block_products(refs[0][...] + crossed, blocks_ref, kind)
+            value = block_products(coupled, blocks_ref, 0)
+            out[...] = value if own_values is None else refs[2][...] - value
+
+    return pl.pallas_call(
+        kernel,
+        in_specs=[VMEM] * (len(given) + 1),
+        out_specs=VMEM,
+        out_shape=jax.ShapeDtypeStruct(arrived[0].shape, F32),
+        compiler_params=params(16),
+        cost_estimate=cost(16 * blocks.size, 2 * blocks.size),
+        name="leaf_only",
+    )(*given, blocks)
+
+
 def sep_rows(level, sums, sep, other, before=None):
     half = sums.shape[1]
     rows = sep.shape[2]
     given = [sums] if before is None else [sums, before]
 
     def kernel(*refs):
-        sums_ref, sep_ref, out = refs[0], refs[-2], refs[-1]
+        sums_ref, sep_ref, out = refs[0], refs[len(given)], refs[-1]
 
         @pl.when(lax.axis_index("layer") == level)
         def _():
@@ -429,25 +558,27 @@
     return first * leaf_values - part
 
 
-def spread_cells(level, stored, spread, leaf_values, before=None, subtract=False):
+def spread_cells(level, stored, spread, leaf_values, before=None, subtract=False, last=False):
     given = [stored, leaf_values] + ([before] if subtract else [])
+    outputs = 1 if last else 2
 
     def kernel(*refs):
         stored_ref, leaf_ref = refs[:2]
-        spread_ref, part_out, share_out = refs[-3:]
+        spread_ref, part_out = refs[-1 - outputs], refs[-outputs]
 
         @pl.when(lax.axis_index("layer") == level)
         def _():
             part = times(stored_ref[...].astype(F32), spread_ref[0], spread_ref[1], 0)
             part_out[...] = part
-            held = refs[2][...] if subtract else None
-            share_out[...] = share_of_value(part, leaf_ref[...], held, subtract)
+            if not last:
+                held = refs[2][...] if subtract else None
+                refs[-1][...] = share_of_value(part, leaf_ref[...], held, subtract)
 
     return pl.pallas_call(
         kernel,
         in_specs=[VMEM] * (len(given) + 1),
-        out_specs=[VMEM, VMEM],
-        out_shape=[jax.ShapeDtypeStruct((8, spread.shape[2]), F32)] * 2,
+        out_specs=[VMEM] * outputs,
+        out_shape=[jax.ShapeDtypeStruct((8, spread.shape[2]), F32)] * outputs,
         compiler_params=params(16),
         cost_estimate=cost(32 * spread.size, 2 * spread.size),
         name="spread_cells",
@@ -527,11 +658,18 @@
         own_rows = sep_rows(level, half_sums, sep, False)
         return sep_rows(level, other_sums, sep, True, own_rows)
 
-    def solve(level, before, subtract=False, last=False, **given):
-        leaf_values, sums = leaf_and_gather(level, blocks, gather, **given)
-        stored = gather_chips(own_rows_of(level, sum_chips(sums)))
-        part, share = spread_cells(level, stored, spread, leaf_values, before, subtract)
-        return finish(level, leaf_values, part, pair(part), before, subtract, last), share
+    def solve(level, before, subtract=False, last=False, arrived=None):
+        if subtract:
+            sums = folded_sums(level, arrived, fold_below)
+            leaf_values = leaf_only(level, arrived, blocks)
+        elif level > 1:
+            sums = folded_sums(level, arrived, fold_above, source_parts[1])
+            leaf_values = leaf_only(level, arrived, blocks, source_parts[0])
+        else:
+            leaf_values, sums = leaf_and_gather(level, blocks, gather, arrived, sources)
+        stored = gather_chips(own_rows_of(level, sum_chips(sums, leaf_values)))
+        part, *share = spread_cells(level, stored, spread, leaf_values, before, subtract, last)
+        return finish(level, leaf_values, part, pair(part), before, subtract, last), *share
 
     own_rows = own_rows_of(0, sum_chips(first_sums, sep))
     if rows % 128 == 0:
@@ -543,13 +681,18 @@
     value = finish(0, first_values, part, pair(part))
     gather = transpose_gather(own_gather, their_gather, share)
 
+    fold_above = folded(blocks, gather, 1, range(2, depth), share)
+    source_parts = source_sums(blocks, gather, sources, range(2, depth))
+
     for level in range(1, depth):
         if level > 1:
             arrived = hop(share, level - 1, level)
-        value, share = solve(level, value, sources=sources, arrived=arrived)
+        value, share = solve(level, value, arrived=arrived)
+        if level == depth - 2:
+            fold_below = folded(blocks, gather, 2, range(depth - 1), share)
     for level in range(depth - 2, -1, -1):
-        arrived = hop(share, level + 1, level)
-        value, share = solve(level, value, True, level == 0, arrived=arrived)
+        arrived = hop(share[0] if level < depth - 2 else share, level + 1, level)
+        value, *share = solve(level, value, True, level == 0, arrived=arrived)
     return value
 
 

time: 155 us -> 153 us (0.987)
  waiting for transfers between devices: 57.5 us -> 55.7 us
    pallas_call x0 -> x13, Pallas kernels: none -> 2.68 us  [the longest x2 1.94 us: folded(): pl.pallas_call(kernel, in_specs=[VMEM, VMEM, ANY], out_specs=VMEM, out_sh...]
    ppermute x12, waiting for transfers between devices: 15.5 us -> 13.7 us  [hop(): lax.ppermute(block, ('layer', 'front'), [(i * slots + j, target[i] * slot...]
  transfers between devices with their start and end apart: 71 -> 71, of which waited for: 46 -> 46; matrix products, arithmetic and copies ran while one was open for 0% -> 0% of each run, Pallas kernels for 7% -> 9%
where the time goes in v7:
time: 153 us
  starting transfers between devices  77.9 us (51%)
  waiting for transfers between devices  55.7 us (36%)
  Pallas kernels  18.7 us (12%)
    ppermute x42, starting transfers between devices, from_chips(): lax.ppermute(block, 'front', xor_route('front', 2 * (chips - step)))  62.8 us
    ppermute x42, waiting for transfers between devices, from_chips(): lax.ppermute(block, 'front', xor_route('front', 2 * (chips - step)))  30.9 us
    ppermute x12, waiting for transfers between devices, hop(): lax.ppermute(block, ('layer', 'front'), [(i * slots + j, target[i] * slot...  13.7 us
    ppermute x12, starting transfers between devices, hop(): lax.ppermute(block, ('layer', 'front'), [(i * slots + j, target[i] * slot...  12.4 us
    ppermute x17, waiting for transfers between devices, pair(): return lax.ppermute(block, 'front', xor_route('front', 1))  11.1 us
    pallas_call x1, Pallas kernels, transpose_sep(): pl.pallas_call(kernel, in_specs=[ANY, ANY], out_specs=VMEM, out_shape=plt...  5.35 us
    pallas_call x14, Pallas kernels, sep_rows(): pl.pallas_call(kernel, in_specs=[VMEM] * (len(given) + 1), out_specs=VMEM...  3.93 us
  transfers between devices with their start and end apart: 71, of which 46 were waited for; matrix products, arithmetic and copies ran while one was open for 0% of the time, Pallas kernels for 9%

profile of v7, /device:TPU:0, one launch (start us, length us, event | category | flops | bytes accessed | tf_op | source)
XLA Modules:
  0.0 152.7 jit_solution(5043960200920127866)
XLA Ops:
  0.0 2.7 %first_leaf_and_gather.1 = (f32[8,2816]{1,0:T(8,128)S(1)}, f32[8,2816]{1,0:T(8,128)S(1)}, bf16[2,5120,128]{2,1,0:T(8,128)(2,1)S(1)}, bf16[2,128,5504]{2,1,0:T(8,128)(2,1)S(1)}) custom-call(f32[2,4,128]{2,1,0:T(4,128)} %bitcast.15, bf16[2,5120,128]{2,1,0:T(8,128)(2,1)} %bitcast.10, bf16[2,128,5120]{2,1,0:T(8,128)(2,1)} %bitcast.11, ...), custom_call_target="tpu_custom_call" | custom-call | flops 20971520 | bytes 2621440 | tf_op jit(solution)/shard_map/first_leaf_and_gather/pallas_call | solution.py:333
  4.7 5.0 %collective-permute-start.1 = (bf16[8,2560]{1,0:T(8,128)(2,1)S(1)}, bf16[8,2560]{1,0:T(8,128)(2,1)S(1)}, u32[]{:S(2)}, u32[]{:S(2)}) collective-permute-start(bf16[8,2560]{1,0:T(8,128)(2,1)S(1)} %fusion._.refs_0_.refs_2_), channel_id=1, source_target_pairs={{0,6},{1,7},{2,4},{3,5},{4,2},{5,3},{6,0},{7,1},{8,14},{9,15},{10,... | collective-permute-start | bytes 122888 | tf_op jit(solution)/shard_map/ppermute | solution.py:36
  10.3 5.3 %transpose_sep.1.refs_4_.refs_1_.refs_2_ = bf16[2,5120,640]{2,1,0:T(8,128)(2,1)S(1)} custom-call(bf16[2,640,5120]{2,1,0:T(8,128)(2,1)} %bitcast.9, bf16[8,2560]{1,0:T(8,128)(2,1)S(1)} %fusion._.refs_0_.refs_2_), custom_call_target="tpu_custom_call" | custom-call | bytes 26214400 | tf_op jit(solution)/shard_map/transpose_sep/pallas_call | solution.py:127
  17.9 3.9 %collective-permute-start.5 = (bf16[8,640]{1,0:T(8,128)(2,1)S(1)}, bf16[8,640]{1,0:T(8,128)(2,1)S(1)}, u32[]{:S(2)}, u32[]{:S(2)}) collective-permute-start(bf16[8,640]{1,0:T(8,128)(2,1)S(1)} %sep_rows.15._.refs_0_), channel_id=1, source_target_pairs={{0,6},{1,7},{2,4},{3,5},{4,2},{5,3},{6,0},{7,1},{8,14},{9,15},{10,... | collective-permute-start | bytes 30728 | tf_op jit(solution)/shard_map/ppermute | solution.py:36
  23.8 2.6 %collective-permute-done.6.refs_2_ = bf16[8,640]{1,0:T(8,128)(2,1)S(1)} collective-permute-done((bf16[8,640]{1,0:T(8,128)(2,1)S(1)}, bf16[8,640]{1,0:T(8,128)(2,1)S(1)}, u32[]{:S(2)}, u32[]{:S(2)}) %collective-permute-start.6) | collective-permute-done | bytes 10272 | tf_op jit(solution)/shard_map/ppermute | solution.py:36
  27.7 3.1 %collective-permute-done.10.refs_1_ = f32[8,256]{1,0:T(8,128)S(1)} collective-permute-done((f32[8,256]{1,0:T(8,128)S(1)}, f32[8,256]{1,0:T(8,128)S(1)}, u32[]{:S(2)}, u32[]{:S(2)}) %collective-permute-start.10) | collective-permute-done | bytes 8224 | tf_op jit(solution)/shard_map/ppermute | solution.py:58
  31.4 1.4 collective-permute-start.12
  33.4 2.4 %collective-permute-start.14 = (bf16[8,2560]{1,0:T(8,128)(2,1)S(1)}, bf16[8,2560]{1,0:T(8,128)(2,1)S(1)}, u32[]{:S(2)}, u32[]{:S(2)}) collective-permute-start(bf16[8,2560]{1,0:T(8,128)(2,1)S(1)} %get-tuple-element.38.refs_0_), channel_id=1, source_target_pairs={{0,2},{1,3},{2,0},{3,1},{4,6},{5,7},{6,4},{7,5},{8,10},{9,11},{10,... | collective-permute-start | bytes 122888 | tf_op jit(solution)/shard_map/ppermute | solution.py:36
  35.8 1.9 %collective-permute-done.12.refs_1_ = bf16[8,2560]{1,0:T(8,128)(2,1)S(1)} collective-permute-done((bf16[8,2560]{1,0:T(8,128)(2,1)S(1)}, bf16[8,2560]{1,0:T(8,128)(2,1)S(1)}, u32[]{:S(2)}, u32[]{:S(2)}) %collective-permute-start.12) | collective-permute-done | bytes 40992 | tf_op jit(solution)/shard_map/ppermute | solution.py:36
  39.7 2.2 %collective-permute-start.16 = (bf16[8,640]{1,0:T(8,128)(2,1)S(1)}, bf16[8,640]{1,0:T(8,128)(2,1)S(1)}, u32[]{:S(2)}, u32[]{:S(2)}) collective-permute-start(bf16[8,640]{1,0:T(8,128)(2,1)S(1)} %sep_rows.17), channel_id=1, source_target_pairs={{0,6},{1,7},{2,4},{3,5},{4,2},{5,3},{6,0},{7,1},{8,14},{9,15},{10,... | collective-permute-start | bytes 30728 | tf_op jit(solution)/shard_map/ppermute | solution.py:36
  42.6 1.5 collective-permute-start.18
  48.1 2.2 %collective-permute-done.19.refs_0_ = f32[8,256]{1,0:T(8,128)S(1)} collective-permute-done((f32[8,256]{1,0:T(8,128)S(1)}, f32[8,256]{1,0:T(8,128)S(1)}, u32[]{:S(2)}, u32[]{:S(2)}) %collective-permute-start.19) | collective-permute-done | bytes 8224 | tf_op jit(solution)/shard_map/ppermute | solution.py:58
  50.5 1.8 %collective-permute-start.21 = (bf16[8,2560]{1,0:T(8,128)(2,1)S(1)}, bf16[8,2560]{1,0:T(8,128)(2,1)S(1)}, u32[]{:S(2)}, u32[]{:S(2)}) collective-permute-start(bf16[8,2560]{1,0:T(8,128)(2,1)S(1)} %folded_sums.5.refs_0_), channel_id=1, source_target_pairs={{0,6},{1,7},{2,4},{3,5},{4,2},{5,3},{6,0},{7,1},{8,14},{9,15},{10,... | collective-permute-start | bytes 122888 | tf_op jit(solution)/shard_map/ppermute | solution.py:36
  53.3 1.5 collective-permute-start.23
  54.9 1.7 %collective-permute-done.21.refs_1_ = bf16[8,2560]{1,0:T(8,128)(2,1)S(1)} collective-permute-done((bf16[8,2560]{1,0:T(8,128)(2,1)S(1)}, bf16[8,2560]{1,0:T(8,128)(2,1)S(1)}, u32[]{:S(2)}, u32[]{:S(2)}) %collective-permute-start.21) | collective-permute-done | bytes 40992 | tf_op jit(solution)/shard_map/ppermute | solution.py:36
  56.5 1.4 collective-permute-done.22.refs_2_
  59.3 2.1 %collective-permute-start.25 = (bf16[8,640]{1,0:T(8,128)(2,1)S(1)}, bf16[8,640]{1,0:T(8,128)(2,1)S(1)}, u32[]{:S(2)}, u32[]{:S(2)}) collective-permute-start(bf16[8,640]{1,0:T(8,128)(2,1)S(1)} %sep_rows.19), channel_id=1, source_target_pairs={{0,6},{1,7},{2,4},{3,5},{4,2},{5,3},{6,0},{7,1},{8,14},{9,15},{10,... | collective-permute-start | bytes 30728 | tf_op jit(solution)/shard_map/ppermute | solution.py:36
  61.6 2.0 %collective-permute-start.27 = (bf16[8,640]{1,0:T(8,128)(2,1)S(1)}, bf16[8,640]{1,0:T(8,128)(2,1)S(1)}, u32[]{:S(2)}, u32[]{:S(2)}) collective-permute-start(bf16[8,640]{1,0:T(8,128)(2,1)S(1)} %sep_rows.19), channel_id=1, source_target_pairs={{0,2},{1,3},{2,0},{3,1},{4,6},{5,7},{6,4},{7,5},{8,10},{9,11},{10,... | collective-permute-start | bytes 30728 | tf_op jit(solution)/shard_map/ppermute | solution.py:36
  66.0 1.5 %collective-permute-start.28 = (f32[8,256]{1,0:T(8,128)S(1)}, f32[8,256]{1,0:T(8,128)S(1)}, u32[]{:S(2)}, u32[]{:S(2)}) collective-permute-start(f32[8,256]{1,0:T(8,128)S(1)} %get-tuple-element.43._), channel_id=1, source_target_pairs={{16,24},{17,25},{18,26},{19,27},{20,28},{21,29},{22,30},{23,31},{2... | collective-permute-start | bytes 24584 | tf_op jit(solution)/shard_map/ppermute | solution.py:58
  67.6 1.7 %collective-permute-start.29 = (f32[8,256]{1,0:T(8,128)S(1)}, f32[8,256]{1,0:T(8,128)S(1)}, u32[]{:S(2)}, u32[]{:S(2)}) collective-permute-start(f32[8,256]{1,0:T(8,128)S(1)} %get-tuple-element.43._), channel_id=1, source_target_pairs={{16,25},{17,24},{18,27},{19,26},{20,29},{21,28},{22,31},{23,30},{2... | collective-permute-start | bytes 24584 | tf_op jit(solution)/shard_map/ppermute | solution.py:58
  69.3 1.6 %collective-permute-done.28.refs_0_ = f32[8,256]{1,0:T(8,128)S(1)} collective-permute-done((f32[8,256]{1,0:T(8,128)S(1)}, f32[8,256]{1,0:T(8,128)S(1)}, u32[]{:S(2)}, u32[]{:S(2)}) %collective-permute-start.28) | collective-permute-done | bytes 8224 | tf_op jit(solution)/shard_map/ppermute | solution.py:58
  71.5 1.6 %collective-permute-start.30 = (bf16[8,2560]{1,0:T(8,128)(2,1)S(1)}, bf16[8,2560]{1,0:T(8,128)(2,1)S(1)}, u32[]{:S(2)}, u32[]{:S(2)}) collective-permute-start(bf16[8,2560]{1,0:T(8,128)(2,1)S(1)} %folded_sums.6.refs_0_), channel_id=1, source_target_pairs={{0,6},{1,7},{2,4},{3,5},{4,2},{5,3},{6,0},{7,1},{8,14},{9,15},{10,... | collective-permute-start | bytes 122888 | tf_op jit(solution)/shard_map/ppermute | solution.py:36
  74.2 1.7 %collective-permute-start.32 = (bf16[8,2560]{1,0:T(8,128)(2,1)S(1)}, bf16[8,2560]{1,0:T(8,128)(2,1)S(1)}, u32[]{:S(2)}, u32[]{:S(2)}) collective-permute-start(bf16[8,2560]{1,0:T(8,128)(2,1)S(1)} %folded_sums.6.refs_0_), channel_id=1, source_target_pairs={{0,2},{1,3},{2,0},{3,1},{4,6},{5,7},{6,4},{7,5},{8,10},{9,11},{10,... | collective-permute-start | bytes 122888 | tf_op jit(solution)/shard_map/ppermute | solution.py:36
  75.9 1.6 %collective-permute-done.30.refs_1_ = bf16[8,2560]{1,0:T(8,128)(2,1)S(1)} collective-permute-done((bf16[8,2560]{1,0:T(8,128)(2,1)S(1)}, bf16[8,2560]{1,0:T(8,128)(2,1)S(1)}, u32[]{:S(2)}, u32[]{:S(2)}) %collective-permute-start.30) | collective-permute-done | bytes 40992 | tf_op jit(solution)/shard_map/ppermute | solution.py:36
  77.6 1.5 collective-permute-done.31.refs_2_
  80.4 2.2 %collective-permute-start.34 = (bf16[8,640]{1,0:T(8,128)(2,1)S(1)}, bf16[8,640]{1,0:T(8,128)(2,1)S(1)}, u32[]{:S(2)}, u32[]{:S(2)}) collective-permute-start(bf16[8,640]{1,0:T(8,128)(2,1)S(1)} %sep_rows.21), channel_id=1, source_target_pairs={{0,6},{1,7},{2,4},{3,5},{4,2},{5,3},{6,0},{7,1},{8,14},{9,15},{10,... | collective-permute-start | bytes 30728 | tf_op jit(solution)/shard_map/ppermute | solution.py:36
  82.7 2.1 %collective-permute-start.36 = (bf16[8,640]{1,0:T(8,128)(2,1)S(1)}, bf16[8,640]{1,0:T(8,128)(2,1)S(1)}, u32[]{:S(2)}, u32[]{:S(2)}) collective-permute-start(bf16[8,640]{1,0:T(8,128)(2,1)S(1)} %sep_rows.21), channel_id=1, source_target_pairs={{0,2},{1,3},{2,0},{3,1},{4,6},{5,7},{6,4},{7,5},{8,10},{9,11},{10,... | collective-permute-start | bytes 30728 | tf_op jit(solution)/shard_map/ppermute | solution.py:36
  87.2 2.4 %collective-permute-start.37 = (f32[8,256]{1,0:T(8,128)S(1)}, f32[8,256]{1,0:T(8,128)S(1)}, u32[]{:S(2)}, u32[]{:S(2)}) collective-permute-start(f32[8,256]{1,0:T(8,128)S(1)} %get-tuple-element.44), channel_id=1, source_target_pairs={{24,16},{25,17},{26,18},{27,19},{28,20},{29,21},{30,22},{31,23},{1... | collective-permute-start | bytes 24584 | tf_op jit(solution)/shard_map/ppermute | solution.py:58
  89.5 1.9 %folded.3.refs_2_ = bf16[2,256,2560]{2,1,0:T(8,128)(2,1)S(1)} custom-call(bf16[2,3,2,128,128]{4,3,2,1,0:T(8,128)(2,1)S(1)} %get-tuple-element.36.refs_3_.blocks_ref.refs_2_, bf16[2,256,2560]{2,1,0:T(8,128)(2,1)S(1)} %transpose_gather.1.refs_4_.gather_ref, f32[8,256]{1,0:T(8,128)S(1)} %get-tuple-element.43._), custom_call_target="tpu_custom_call" | custom-call | flops 1342177280 | bytes 5242880 | tf_op jit(solution)/shard_map/folded/pallas_call | solution.py:422
  92.6 1.6 %collective-permute-start.39 = (bf16[8,2560]{1,0:T(8,128)(2,1)S(1)}, bf16[8,2560]{1,0:T(8,128)(2,1)S(1)}, u32[]{:S(2)}, u32[]{:S(2)}) collective-permute-start(bf16[8,2560]{1,0:T(8,128)(2,1)S(1)} %folded_sums.7.refs_0_), channel_id=1, source_target_pairs={{0,6},{1,7},{2,4},{3,5},{4,2},{5,3},{6,0},{7,1},{8,14},{9,15},{10,... | collective-permute-start | bytes 122888 | tf_op jit(solution)/shard_map/ppermute | solution.py:36
  95.1 1.9 %collective-permute-start.41 = (bf16[8,2560]{1,0:T(8,128)(2,1)S(1)}, bf16[8,2560]{1,0:T(8,128)(2,1)S(1)}, u32[]{:S(2)}, u32[]{:S(2)}) collective-permute-start(bf16[8,2560]{1,0:T(8,128)(2,1)S(1)} %folded_sums.7.refs_0_), channel_id=1, source_target_pairs={{0,2},{1,3},{2,0},{3,1},{4,6},{5,7},{6,4},{7,5},{8,10},{9,11},{10,... | collective-permute-start | bytes 122888 | tf_op jit(solution)/shard_map/ppermute | solution.py:36
  97.0 1.6 %collective-permute-done.39.refs_1_ = bf16[8,2560]{1,0:T(8,128)(2,1)S(1)} collective-permute-done((bf16[8,2560]{1,0:T(8,128)(2,1)S(1)}, bf16[8,2560]{1,0:T(8,128)(2,1)S(1)}, u32[]{:S(2)}, u32[]{:S(2)}) %collective-permute-start.39) | collective-permute-done | bytes 40992 | tf_op jit(solution)/shard_map/ppermute | solution.py:36
  101.3 2.3 %collective-permute-start.43 = (bf16[8,640]{1,0:T(8,128)(2,1)S(1)}, bf16[8,640]{1,0:T(8,128)(2,1)S(1)}, u32[]{:S(2)}, u32[]{:S(2)}) collective-permute-start(bf16[8,640]{1,0:T(8,128)(2,1)S(1)} %sep_rows.23), channel_id=1, source_target_pairs={{0,6},{1,7},{2,4},{3,5},{4,2},{5,3},{6,0},{7,1},{8,14},{9,15},{10,... | collective-permute-start | bytes 30728 | tf_op jit(solution)/shard_map/ppermute | solution.py:36
  103.8 1.9 %collective-permute-start.45 = (bf16[8,640]{1,0:T(8,128)(2,1)S(1)}, bf16[8,640]{1,0:T(8,128)(2,1)S(1)}, u32[]{:S(2)}, u32[]{:S(2)}) collective-permute-start(bf16[8,640]{1,0:T(8,128)(2,1)S(1)} %sep_rows.23), channel_id=1, source_target_pairs={{0,2},{1,3},{2,0},{3,1},{4,6},{5,7},{6,4},{7,5},{8,10},{9,11},{10,... | collective-permute-start | bytes 30728 | tf_op jit(solution)/shard_map/ppermute | solution.py:36
  109.7 1.7 %collective-permute-start.51 = (f32[8,256]{1,0:T(8,128)S(1)}, f32[8,256]{1,0:T(8,128)S(1)}, u32[]{:S(2)}, u32[]{:S(2)}) collective-permute-start(f32[8,256]{1,0:T(8,128)S(1)} %get-tuple-element.49), channel_id=1, source_target_pairs={{16,9},{17,8},{18,11},{19,10},{20,13},{21,12},{22,15},{23,14},{8,1... | collective-permute-start | bytes 24584 | tf_op jit(solution)/shard_map/ppermute | solution.py:58
  112.8 2.3 %collective-permute-start.52 = (bf16[8,2560]{1,0:T(8,128)(2,1)S(1)}, bf16[8,2560]{1,0:T(8,128)(2,1)S(1)}, u32[]{:S(2)}, u32[]{:S(2)}) collective-permute-start(bf16[8,2560]{1,0:T(8,128)(2,1)S(1)} %folded_sums.8.refs_0_), channel_id=1, source_target_pairs={{0,6},{1,7},{2,4},{3,5},{4,2},{5,3},{6,0},{7,1},{8,14},{9,15},{10,... | collective-permute-start | bytes 122888 | tf_op jit(solution)/shard_map/ppermute | solution.py:36
  115.4 1.8 %collective-permute-start.54 = (bf16[8,2560]{1,0:T(8,128)(2,1)S(1)}, bf16[8,2560]{1,0:T(8,128)(2,1)S(1)}, u32[]{:S(2)}, u32[]{:S(2)}) collective-permute-start(bf16[8,2560]{1,0:T(8,128)(2,1)S(1)} %folded_sums.8.refs_0_), channel_id=1, source_target_pairs={{0,2},{1,3},{2,0},{3,1},{4,6},{5,7},{6,4},{7,5},{8,10},{9,11},{10,... | collective-permute-start | bytes 122888 | tf_op jit(solution)/shard_map/ppermute | solution.py:36
  117.2 1.9 %collective-permute-done.52.refs_1_ = bf16[8,2560]{1,0:T(8,128)(2,1)S(1)} collective-permute-done((bf16[8,2560]{1,0:T(8,128)(2,1)S(1)}, bf16[8,2560]{1,0:T(8,128)(2,1)S(1)}, u32[]{:S(2)}, u32[]{:S(2)}) %collective-permute-start.52) | collective-permute-done | bytes 40992 | tf_op jit(solution)/shard_map/ppermute | solution.py:36
  119.1 1.7 %collective-permute-done.53.refs_2_ = bf16[8,2560]{1,0:T(8,128)(2,1)S(1)} collective-permute-done((bf16[8,2560]{1,0:T(8,128)(2,1)S(1)}, bf16[8,2560]{1,0:T(8,128)(2,1)S(1)}, u32[]{:S(2)}, u32[]{:S(2)}) %collective-permute-start.53) | collective-permute-done | bytes 40992 | tf_op jit(solution)/shard_map/ppermute | solution.py:36
  122.1 1.9 %collective-permute-start.56 = (bf16[8,640]{1,0:T(8,128)(2,1)S(1)}, bf16[8,640]{1,0:T(8,128)(2,1)S(1)}, u32[]{:S(2)}, u32[]{:S(2)}) collective-permute-start(bf16[8,640]{1,0:T(8,128)(2,1)S(1)} %sep_rows.25), channel_id=1, source_target_pairs={{0,6},{1,7},{2,4},{3,5},{4,2},{5,3},{6,0},{7,1},{8,14},{9,15},{10,... | collective-permute-start | bytes 30728 | tf_op jit(solution)/shard_map/ppermute | solution.py:36
  124.0 2.5 %collective-permute-start.58 = (bf16[8,640]{1,0:T(8,128)(2,1)S(1)}, bf16[8,640]{1,0:T(8,128)(2,1)S(1)}, u32[]{:S(2)}, u32[]{:S(2)}) collective-permute-start(bf16[8,640]{1,0:T(8,128)(2,1)S(1)} %sep_rows.25), channel_id=1, source_target_pairs={{0,2},{1,3},{2,0},{3,1},{4,6},{5,7},{6,4},{7,5},{8,10},{9,11},{10,... | collective-permute-start | bytes 30728 | tf_op jit(solution)/shard_map/ppermute | solution.py:36
  128.6 1.9 %collective-permute-start.60 = (f32[8,256]{1,0:T(8,128)S(1)}, f32[8,256]{1,0:T(8,128)S(1)}, u32[]{:S(2)}, u32[]{:S(2)}) collective-permute-start(f32[8,256]{1,0:T(8,128)S(1)} %get-tuple-element.51), channel_id=1, source_target_pairs={{8,0},{9,1},{10,2},{11,3},{12,4},{13,5},{14,6},{15,7},{0,16},{1,17... | collective-permute-start | bytes 24584 | tf_op jit(solution)/shard_map/ppermute | solution.py:58
  130.8 2.7 %collective-permute-done.60.refs_0_ = f32[8,256]{1,0:T(8,128)S(1)} collective-permute-done((f32[8,256]{1,0:T(8,128)S(1)}, f32[8,256]{1,0:T(8,128)S(1)}, u32[]{:S(2)}, u32[]{:S(2)}) %collective-permute-start.60) | collective-permute-done | bytes 8224 | tf_op jit(solution)/shard_map/ppermute | solution.py:58
  134.0 1.6 %collective-permute-start.62 = (bf16[8,2560]{1,0:T(8,128)(2,1)S(1)}, bf16[8,2560]{1,0:T(8,128)(2,1)S(1)}, u32[]{:S(2)}, u32[]{:S(2)}) collective-permute-start(bf16[8,2560]{1,0:T(8,128)(2,1)S(1)} %folded_sums.9.refs_0_), channel_id=1, source_target_pairs={{0,6},{1,7},{2,4},{3,5},{4,2},{5,3},{6,0},{7,1},{8,14},{9,15},{10,... | collective-permute-start | bytes 122888 | tf_op jit(solution)/shard_map/ppermute | solution.py:36
  136.6 1.8 %collective-permute-start.64 = (bf16[8,2560]{1,0:T(8,128)(2,1)S(1)}, bf16[8,2560]{1,0:T(8,128)(2,1)S(1)}, u32[]{:S(2)}, u32[]{:S(2)}) collective-permute-start(bf16[8,2560]{1,0:T(8,128)(2,1)S(1)} %folded_sums.9.refs_0_), channel_id=1, source_target_pairs={{0,2},{1,3},{2,0},{3,1},{4,6},{5,7},{6,4},{7,5},{8,10},{9,11},{10,... | collective-permute-start | bytes 122888 | tf_op jit(solution)/shard_map/ppermute | solution.py:36
  138.8 1.6 %collective-permute-done.62.refs_1_ = bf16[8,2560]{1,0:T(8,128)(2,1)S(1)} collective-permute-done((bf16[8,2560]{1,0:T(8,128)(2,1)S(1)}, bf16[8,2560]{1,0:T(8,128)(2,1)S(1)}, u32[]{:S(2)}, u32[]{:S(2)}) %collective-permute-start.62) | collective-permute-done | bytes 40992 | tf_op jit(solution)/shard_map/ppermute | solution.py:36
  143.5 2.4 %collective-permute-start.66 = (bf16[8,640]{1,0:T(8,128)(2,1)S(1)}, bf16[8,640]{1,0:T(8,128)(2,1)S(1)}, u32[]{:S(2)}, u32[]{:S(2)}) collective-permute-start(bf16[8,640]{1,0:T(8,128)(2,1)S(1)} %sep_rows.27), channel_id=1, source_target_pairs={{0,6},{1,7},{2,4},{3,5},{4,2},{5,3},{6,0},{7,1},{8,14},{9,15},{10,... | collective-permute-start | bytes 30728 | tf_op jit(solution)/shard_map/ppermute | solution.py:36
  146.3 1.7 %collective-permute-start.68 = (bf16[8,640]{1,0:T(8,128)(2,1)S(1)}, bf16[8,640]{1,0:T(8,128)(2,1)S(1)}, u32[]{:S(2)}, u32[]{:S(2)}) collective-permute-start(bf16[8,640]{1,0:T(8,128)(2,1)S(1)} %sep_rows.27), channel_id=1, source_target_pairs={{0,2},{1,3},{2,0},{3,1},{4,6},{5,7},{6,4},{7,5},{8,10},{9,11},{10,... | collective-permute-start | bytes 30728 | tf_op jit(solution)/shard_map/ppermute | solution.py:36
  (162 shorter events, 51.2 us)
Async XLA Ops:
  4.2 18.3 %collective-permute-start.8 = (bf16[2,128,5504]{2,1,0:T(8,128)(2,1)S(1)}, bf16[2,128,5504]{2,1,0:T(8,128)(2,1)S(1)}, u32[]{:S(2)}, u32[]{:S(2)}) collective-permute-start(bf16[2,128,5504]{2,1,0:T(8,128)(2,1)S(1)} %get-tuple-element.33.own_ref), channel_id=1, source_target_pairs={{0,1},{1,0},{2,3},{3,2},{4,5},{5,4},{6,7},{7,6},{8,9},{9,8},{10,11... | collective-permute-start | bytes 8454152 | tf_op jit(solution)/shard_map/ppermute | solution.py:21
  4.6 22.4 %collective-permute-start.11 = (bf16[2,5120,128]{2,1,0:T(8,128)(2,1)S(1)}, bf16[2,5120,128]{2,1,0:T(8,128)(2,1)S(1)}, u32[]{:S(2)}, u32[]{:S(2)}) collective-permute-start(bf16[2,5120,128]{2,1,0:T(8,128)(2,1)S(1)} %get-tuple-element.37.own_ref), channel_id=1, source_target_pairs={{0,1},{1,0},{2,3},{3,2},{4,5},{5,4},{6,7},{7,6},{8,9},{9,8},{10,11... | collective-permute-start | bytes 7864328 | tf_op jit(solution)/shard_map/ppermute | solution.py:21
  4.7 10.9 %collective-permute-start.1 = (bf16[8,2560]{1,0:T(8,128)(2,1)S(1)}, bf16[8,2560]{1,0:T(8,128)(2,1)S(1)}, u32[]{:S(2)}, u32[]{:S(2)}) collective-permute-start(bf16[8,2560]{1,0:T(8,128)(2,1)S(1)} %fusion._.refs_0_.refs_2_), channel_id=1, source_target_pairs={{0,6},{1,7},{2,4},{3,5},{4,2},{5,3},{6,0},{7,1},{8,14},{9,15},{10,... | collective-permute-start | bytes 122888 | tf_op jit(solution)/shard_map/ppermute | solution.py:36
  9.7 5.9 %collective-permute-start.2 = (bf16[8,2560]{1,0:T(8,128)(2,1)S(1)}, bf16[8,2560]{1,0:T(8,128)(2,1)S(1)}, u32[]{:S(2)}, u32[]{:S(2)}) collective-permute-start(bf16[8,2560]{1,0:T(8,128)(2,1)S(1)} %fusion._.refs_0_.refs_2_), channel_id=1, source_target_pairs={{0,4},{1,5},{2,6},{3,7},{4,0},{5,1},{6,2},{7,3},{8,12},{9,13},{10,... | collective-permute-start | bytes 122888 | tf_op jit(solution)/shard_map/ppermute | solution.py:36
  9.7 5.9 %collective-permute-start.3 = (bf16[8,2560]{1,0:T(8,128)(2,1)S(1)}, bf16[8,2560]{1,0:T(8,128)(2,1)S(1)}, u32[]{:S(2)}, u32[]{:S(2)}) collective-permute-start(bf16[8,2560]{1,0:T(8,128)(2,1)S(1)} %fusion._.refs_0_.refs_2_), channel_id=1, source_target_pairs={{0,2},{1,3},{2,0},{3,1},{4,6},{5,7},{6,4},{7,5},{8,10},{9,11},{10,... | collective-permute-start | bytes 122888 | tf_op jit(solution)/shard_map/ppermute | solution.py:36
  17.9 5.8 %collective-permute-start.5 = (bf16[8,640]{1,0:T(8,128)(2,1)S(1)}, bf16[8,640]{1,0:T(8,128)(2,1)S(1)}, u32[]{:S(2)}, u32[]{:S(2)}) collective-permute-start(bf16[8,640]{1,0:T(8,128)(2,1)S(1)} %sep_rows.15._.refs_0_), channel_id=1, source_target_pairs={{0,6},{1,7},{2,4},{3,5},{4,2},{5,3},{6,0},{7,1},{8,14},{9,15},{10,... | collective-permute-start | bytes 30728 | tf_op jit(solution)/shard_map/ppermute | solution.py:36
  21.8 4.6 %collective-permute-start.6 = (bf16[8,640]{1,0:T(8,128)(2,1)S(1)}, bf16[8,640]{1,0:T(8,128)(2,1)S(1)}, u32[]{:S(2)}, u32[]{:S(2)}) collective-permute-start(bf16[8,640]{1,0:T(8,128)(2,1)S(1)} %sep_rows.15._.refs_0_), channel_id=1, source_target_pairs={{0,4},{1,5},{2,6},{3,7},{4,0},{5,1},{6,2},{7,3},{8,12},{9,13},{10,... | collective-permute-start | bytes 30728 | tf_op jit(solution)/shard_map/ppermute | solution.py:36
  21.8 4.6 %collective-permute-start.7 = (bf16[8,640]{1,0:T(8,128)(2,1)S(1)}, bf16[8,640]{1,0:T(8,128)(2,1)S(1)}, u32[]{:S(2)}, u32[]{:S(2)}) collective-permute-start(bf16[8,640]{1,0:T(8,128)(2,1)S(1)} %sep_rows.15._.refs_0_), channel_id=1, source_target_pairs={{0,2},{1,3},{2,0},{3,1},{4,6},{5,7},{6,4},{7,5},{8,10},{9,11},{10,... | collective-permute-start | bytes 30728 | tf_op jit(solution)/shard_map/ppermute | solution.py:36
  26.8 4.6 %collective-permute-start.9 = (f32[8,256]{1,0:T(8,128)S(1)}, f32[8,256]{1,0:T(8,128)S(1)}, u32[]{:S(2)}, u32[]{:S(2)}) collective-permute-start(f32[8,256]{1,0:T(8,128)S(1)} %get-tuple-element.35._), channel_id=1, source_target_pairs={{0,8},{1,9},{2,10},{3,11},{4,12},{5,13},{6,14},{7,15},{8,16},{9,17... | collective-permute-start | bytes 24584 | tf_op jit(solution)/shard_map/ppermute | solution.py:58
  31.4 6.3 %collective-permute-start.12 = (bf16[8,2560]{1,0:T(8,128)(2,1)S(1)}, bf16[8,2560]{1,0:T(8,128)(2,1)S(1)}, u32[]{:S(2)}, u32[]{:S(2)}) collective-permute-start(bf16[8,2560]{1,0:T(8,128)(2,1)S(1)} %get-tuple-element.38.refs_0_), channel_id=1, source_target_pairs={{0,6},{1,7},{2,4},{3,5},{4,2},{5,3},{6,0},{7,1},{8,14},{9,15},{10,... | collective-permute-start | bytes 122888 | tf_op jit(solution)/shard_map/ppermute | solution.py:36
  32.9 5.5 %collective-permute-start.13 = (bf16[8,2560]{1,0:T(8,128)(2,1)S(1)}, bf16[8,2560]{1,0:T(8,128)(2,1)S(1)}, u32[]{:S(2)}, u32[]{:S(2)}) collective-permute-start(bf16[8,2560]{1,0:T(8,128)(2,1)S(1)} %get-tuple-element.38.refs_0_), channel_id=1, source_target_pairs={{0,4},{1,5},{2,6},{3,7},{4,0},{5,1},{6,2},{7,3},{8,12},{9,13},{10,... | collective-permute-start | bytes 122888 | tf_op jit(solution)/shard_map/ppermute | solution.py:36
  33.4 4.9 %collective-permute-start.14 = (bf16[8,2560]{1,0:T(8,128)(2,1)S(1)}, bf16[8,2560]{1,0:T(8,128)(2,1)S(1)}, u32[]{:S(2)}, u32[]{:S(2)}) collective-permute-start(bf16[8,2560]{1,0:T(8,128)(2,1)S(1)} %get-tuple-element.38.refs_0_), channel_id=1, source_target_pairs={{0,2},{1,3},{2,0},{3,1},{4,6},{5,7},{6,4},{7,5},{8,10},{9,11},{10,... | collective-permute-start | bytes 122888 | tf_op jit(solution)/shard_map/ppermute | solution.py:36
  39.7 5.5 %collective-permute-start.16 = (bf16[8,640]{1,0:T(8,128)(2,1)S(1)}, bf16[8,640]{1,0:T(8,128)(2,1)S(1)}, u32[]{:S(2)}, u32[]{:S(2)}) collective-permute-start(bf16[8,640]{1,0:T(8,128)(2,1)S(1)} %sep_rows.17), channel_id=1, source_target_pairs={{0,6},{1,7},{2,4},{3,5},{4,2},{5,3},{6,0},{7,1},{8,14},{9,15},{10,... | collective-permute-start | bytes 30728 | tf_op jit(solution)/shard_map/ppermute | solution.py:36
  41.9 4.6 %collective-permute-start.17 = (bf16[8,640]{1,0:T(8,128)(2,1)S(1)}, bf16[8,640]{1,0:T(8,128)(2,1)S(1)}, u32[]{:S(2)}, u32[]{:S(2)}) collective-permute-start(bf16[8,640]{1,0:T(8,128)(2,1)S(1)} %sep_rows.17), channel_id=1, source_target_pairs={{0,4},{1,5},{2,6},{3,7},{4,0},{5,1},{6,2},{7,3},{8,12},{9,13},{10,... | collective-permute-start | bytes 30728 | tf_op jit(solution)/shard_map/ppermute | solution.py:36
  50.5 6.1 %collective-permute-start.21 = (bf16[8,2560]{1,0:T(8,128)(2,1)S(1)}, bf16[8,2560]{1,0:T(8,128)(2,1)S(1)}, u32[]{:S(2)}, u32[]{:S(2)}) collective-permute-start(bf16[8,2560]{1,0:T(8,128)(2,1)S(1)} %folded_sums.5.refs_0_), channel_id=1, source_target_pairs={{0,6},{1,7},{2,4},{3,5},{4,2},{5,3},{6,0},{7,1},{8,14},{9,15},{10,... | collective-permute-start | bytes 122888 | tf_op jit(solution)/shard_map/ppermute | solution.py:36
  52.3 5.7 %collective-permute-start.22 = (bf16[8,2560]{1,0:T(8,128)(2,1)S(1)}, bf16[8,2560]{1,0:T(8,128)(2,1)S(1)}, u32[]{:S(2)}, u32[]{:S(2)}) collective-permute-start(bf16[8,2560]{1,0:T(8,128)(2,1)S(1)} %folded_sums.5.refs_0_), channel_id=1, source_target_pairs={{0,4},{1,5},{2,6},{3,7},{4,0},{5,1},{6,2},{7,3},{8,12},{9,13},{10,... | collective-permute-start | bytes 122888 | tf_op jit(solution)/shard_map/ppermute | solution.py:36
  53.3 4.6 %collective-permute-start.23 = (bf16[8,2560]{1,0:T(8,128)(2,1)S(1)}, bf16[8,2560]{1,0:T(8,128)(2,1)S(1)}, u32[]{:S(2)}, u32[]{:S(2)}) collective-permute-start(bf16[8,2560]{1,0:T(8,128)(2,1)S(1)} %folded_sums.5.refs_0_), channel_id=1, source_target_pairs={{0,2},{1,3},{2,0},{3,1},{4,6},{5,7},{6,4},{7,5},{8,10},{9,11},{10,... | collective-permute-start | bytes 122888 | tf_op jit(solution)/shard_map/ppermute | solution.py:36
  59.3 5.5 %collective-permute-start.25 = (bf16[8,640]{1,0:T(8,128)(2,1)S(1)}, bf16[8,640]{1,0:T(8,128)(2,1)S(1)}, u32[]{:S(2)}, u32[]{:S(2)}) collective-permute-start(bf16[8,640]{1,0:T(8,128)(2,1)S(1)} %sep_rows.19), channel_id=1, source_target_pairs={{0,6},{1,7},{2,4},{3,5},{4,2},{5,3},{6,0},{7,1},{8,14},{9,15},{10,... | collective-permute-start | bytes 30728 | tf_op jit(solution)/shard_map/ppermute | solution.py:36
  61.4 4.6 %collective-permute-start.26 = (bf16[8,640]{1,0:T(8,128)(2,1)S(1)}, bf16[8,640]{1,0:T(8,128)(2,1)S(1)}, u32[]{:S(2)}, u32[]{:S(2)}) collective-permute-start(bf16[8,640]{1,0:T(8,128)(2,1)S(1)} %sep_rows.19), channel_id=1, source_target_pairs={{0,4},{1,5},{2,6},{3,7},{4,0},{5,1},{6,2},{7,3},{8,12},{9,13},{10,... | collective-permute-start | bytes 30728 | tf_op jit(solution)/shard_map/ppermute | solution.py:36
  61.6 4.3 %collective-permute-start.27 = (bf16[8,640]{1,0:T(8,128)(2,1)S(1)}, bf16[8,640]{1,0:T(8,128)(2,1)S(1)}, u32[]{:S(2)}, u32[]{:S(2)}) collective-permute-start(bf16[8,640]{1,0:T(8,128)(2,1)S(1)} %sep_rows.19), channel_id=1, source_target_pairs={{0,2},{1,3},{2,0},{3,1},{4,6},{5,7},{6,4},{7,5},{8,10},{9,11},{10,... | collective-permute-start | bytes 30728 | tf_op jit(solution)/shard_map/ppermute | solution.py:36
  66.0 4.8 %collective-permute-start.28 = (f32[8,256]{1,0:T(8,128)S(1)}, f32[8,256]{1,0:T(8,128)S(1)}, u32[]{:S(2)}, u32[]{:S(2)}) collective-permute-start(f32[8,256]{1,0:T(8,128)S(1)} %get-tuple-element.43._), channel_id=1, source_target_pairs={{16,24},{17,25},{18,26},{19,27},{20,28},{21,29},{22,30},{23,31},{2... | collective-permute-start | bytes 24584 | tf_op jit(solution)/shard_map/ppermute | solution.py:58
  71.5 6.0 %collective-permute-start.30 = (bf16[8,2560]{1,0:T(8,128)(2,1)S(1)}, bf16[8,2560]{1,0:T(8,128)(2,1)S(1)}, u32[]{:S(2)}, u32[]{:S(2)}) collective-permute-start(bf16[8,2560]{1,0:T(8,128)(2,1)S(1)} %folded_sums.6.refs_0_), channel_id=1, source_target_pairs={{0,6},{1,7},{2,4},{3,5},{4,2},{5,3},{6,0},{7,1},{8,14},{9,15},{10,... | collective-permute-start | bytes 122888 | tf_op jit(solution)/shard_map/ppermute | solution.py:36
  73.2 5.9 %collective-permute-start.31 = (bf16[8,2560]{1,0:T(8,128)(2,1)S(1)}, bf16[8,2560]{1,0:T(8,128)(2,1)S(1)}, u32[]{:S(2)}, u32[]{:S(2)}) collective-permute-start(bf16[8,2560]{1,0:T(8,128)(2,1)S(1)} %folded_sums.6.refs_0_), channel_id=1, source_target_pairs={{0,4},{1,5},{2,6},{3,7},{4,0},{5,1},{6,2},{7,3},{8,12},{9,13},{10,... | collective-permute-start | bytes 122888 | tf_op jit(solution)/shard_map/ppermute | solution.py:36
  74.2 4.8 %collective-permute-start.32 = (bf16[8,2560]{1,0:T(8,128)(2,1)S(1)}, bf16[8,2560]{1,0:T(8,128)(2,1)S(1)}, u32[]{:S(2)}, u32[]{:S(2)}) collective-permute-start(bf16[8,2560]{1,0:T(8,128)(2,1)S(1)} %folded_sums.6.refs_0_), channel_id=1, source_target_pairs={{0,2},{1,3},{2,0},{3,1},{4,6},{5,7},{6,4},{7,5},{8,10},{9,11},{10,... | collective-permute-start | bytes 122888 | tf_op jit(solution)/shard_map/ppermute | solution.py:36
  80.4 5.5 %collective-permute-start.34 = (bf16[8,640]{1,0:T(8,128)(2,1)S(1)}, bf16[8,640]{1,0:T(8,128)(2,1)S(1)}, u32[]{:S(2)}, u32[]{:S(2)}) collective-permute-start(bf16[8,640]{1,0:T(8,128)(2,1)S(1)} %sep_rows.21), channel_id=1, source_target_pairs={{0,6},{1,7},{2,4},{3,5},{4,2},{5,3},{6,0},{7,1},{8,14},{9,15},{10,... | collective-permute-start | bytes 30728 | tf_op jit(solution)/shard_map/ppermute | solution.py:36
  82.6 4.6 %collective-permute-start.35 = (bf16[8,640]{1,0:T(8,128)(2,1)S(1)}, bf16[8,640]{1,0:T(8,128)(2,1)S(1)}, u32[]{:S(2)}, u32[]{:S(2)}) collective-permute-start(bf16[8,640]{1,0:T(8,128)(2,1)S(1)} %sep_rows.21), channel_id=1, source_target_pairs={{0,4},{1,5},{2,6},{3,7},{4,0},{5,1},{6,2},{7,3},{8,12},{9,13},{10,... | collective-permute-start | bytes 30728 | tf_op jit(solution)/shard_map/ppermute | solution.py:36
  82.7 4.4 %collective-permute-start.36 = (bf16[8,640]{1,0:T(8,128)(2,1)S(1)}, bf16[8,640]{1,0:T(8,128)(2,1)S(1)}, u32[]{:S(2)}, u32[]{:S(2)}) collective-permute-start(bf16[8,640]{1,0:T(8,128)(2,1)S(1)} %sep_rows.21), channel_id=1, source_target_pairs={{0,2},{1,3},{2,0},{3,1},{4,6},{5,7},{6,4},{7,5},{8,10},{9,11},{10,... | collective-permute-start | bytes 30728 | tf_op jit(solution)/shard_map/ppermute | solution.py:36
  87.2 4.3 %collective-permute-start.37 = (f32[8,256]{1,0:T(8,128)S(1)}, f32[8,256]{1,0:T(8,128)S(1)}, u32[]{:S(2)}, u32[]{:S(2)}) collective-permute-start(f32[8,256]{1,0:T(8,128)S(1)} %get-tuple-element.44), channel_id=1, source_target_pairs={{24,16},{25,17},{26,18},{27,19},{28,20},{29,21},{30,22},{31,23},{1... | collective-permute-start | bytes 24584 | tf_op jit(solution)/shard_map/ppermute | solution.py:58
  92.6 6.0 %collective-permute-start.39 = (bf16[8,2560]{1,0:T(8,128)(2,1)S(1)}, bf16[8,2560]{1,0:T(8,128)(2,1)S(1)}, u32[]{:S(2)}, u32[]{:S(2)}) collective-permute-start(bf16[8,2560]{1,0:T(8,128)(2,1)S(1)} %folded_sums.7.refs_0_), channel_id=1, source_target_pairs={{0,6},{1,7},{2,4},{3,5},{4,2},{5,3},{6,0},{7,1},{8,14},{9,15},{10,... | collective-permute-start | bytes 122888 | tf_op jit(solution)/shard_map/ppermute | solution.py:36
  94.2 5.8 %collective-permute-start.40 = (bf16[8,2560]{1,0:T(8,128)(2,1)S(1)}, bf16[8,2560]{1,0:T(8,128)(2,1)S(1)}, u32[]{:S(2)}, u32[]{:S(2)}) collective-permute-start(bf16[8,2560]{1,0:T(8,128)(2,1)S(1)} %folded_sums.7.refs_0_), channel_id=1, source_target_pairs={{0,4},{1,5},{2,6},{3,7},{4,0},{5,1},{6,2},{7,3},{8,12},{9,13},{10,... | collective-permute-start | bytes 122888 | tf_op jit(solution)/shard_map/ppermute | solution.py:36
  95.1 4.9 %collective-permute-start.41 = (bf16[8,2560]{1,0:T(8,128)(2,1)S(1)}, bf16[8,2560]{1,0:T(8,128)(2,1)S(1)}, u32[]{:S(2)}, u32[]{:S(2)}) collective-permute-start(bf16[8,2560]{1,0:T(8,128)(2,1)S(1)} %folded_sums.7.refs_0_), channel_id=1, source_target_pairs={{0,2},{1,3},{2,0},{3,1},{4,6},{5,7},{6,4},{7,5},{8,10},{9,11},{10,... | collective-permute-start | bytes 122888 | tf_op jit(solution)/shard_map/ppermute | solution.py:36
  100.1 5.6 %collective-permute-start.49 = (f32[8,256]{1,0:T(8,128)S(1)}, f32[8,256]{1,0:T(8,128)S(1)}, u32[]{:S(2)}, u32[]{:S(2)}) collective-permute-start(f32[8,256]{1,0:T(8,128)S(1)} %get-tuple-element.48.refs_1_), channel_id=1, source_target_pairs={{0,1},{1,0},{2,3},{3,2},{4,5},{5,4},{6,7},{7,6},{8,9},{9,8},{10,11... | collective-permute-start | bytes 24584 | tf_op jit(solution)/shard_map/ppermute | solution.py:21
  100.6 5.1 %collective-permute-start.48 = (f32[8,256]{1,0:T(8,128)S(1)}, f32[8,256]{1,0:T(8,128)S(1)}, u32[]{:S(2)}, u32[]{:S(2)}) collective-permute-start(f32[8,256]{1,0:T(8,128)S(1)} %get-tuple-element.47.refs_1_), channel_id=1, source_target_pairs={{0,1},{1,0},{2,3},{3,2},{4,5},{5,4},{6,7},{7,6},{8,9},{9,8},{10,11... | collective-permute-start | bytes 24584 | tf_op jit(solution)/shard_map/ppermute | solution.py:21
  101.3 5.7 %collective-permute-start.43 = (bf16[8,640]{1,0:T(8,128)(2,1)S(1)}, bf16[8,640]{1,0:T(8,128)(2,1)S(1)}, u32[]{:S(2)}, u32[]{:S(2)}) collective-permute-start(bf16[8,640]{1,0:T(8,128)(2,1)S(1)} %sep_rows.23), channel_id=1, source_target_pairs={{0,6},{1,7},{2,4},{3,5},{4,2},{5,3},{6,0},{7,1},{8,14},{9,15},{10,... | collective-permute-start | bytes 30728 | tf_op jit(solution)/shard_map/ppermute | solution.py:36
  103.6 4.6 %collective-permute-start.44 = (bf16[8,640]{1,0:T(8,128)(2,1)S(1)}, bf16[8,640]{1,0:T(8,128)(2,1)S(1)}, u32[]{:S(2)}, u32[]{:S(2)}) collective-permute-start(bf16[8,640]{1,0:T(8,128)(2,1)S(1)} %sep_rows.23), channel_id=1, source_target_pairs={{0,4},{1,5},{2,6},{3,7},{4,0},{5,1},{6,2},{7,3},{8,12},{9,13},{10,... | collective-permute-start | bytes 30728 | tf_op jit(solution)/shard_map/ppermute | solution.py:36
  103.8 4.4 %collective-permute-start.45 = (bf16[8,640]{1,0:T(8,128)(2,1)S(1)}, bf16[8,640]{1,0:T(8,128)(2,1)S(1)}, u32[]{:S(2)}, u32[]{:S(2)}) collective-permute-start(bf16[8,640]{1,0:T(8,128)(2,1)S(1)} %sep_rows.23), channel_id=1, source_target_pairs={{0,2},{1,3},{2,0},{3,1},{4,6},{5,7},{6,4},{7,5},{8,10},{9,11},{10,... | collective-permute-start | bytes 30728 | tf_op jit(solution)/shard_map/ppermute | solution.py:36
  112.8 6.3 %collective-permute-start.52 = (bf16[8,2560]{1,0:T(8,128)(2,1)S(1)}, bf16[8,2560]{1,0:T(8,128)(2,1)S(1)}, u32[]{:S(2)}, u32[]{:S(2)}) collective-permute-start(bf16[8,2560]{1,0:T(8,128)(2,1)S(1)} %folded_sums.8.refs_0_), channel_id=1, source_target_pairs={{0,6},{1,7},{2,4},{3,5},{4,2},{5,3},{6,0},{7,1},{8,14},{9,15},{10,... | collective-permute-start | bytes 122888 | tf_op jit(solution)/shard_map/ppermute | solution.py:36
  115.1 5.7 %collective-permute-start.53 = (bf16[8,2560]{1,0:T(8,128)(2,1)S(1)}, bf16[8,2560]{1,0:T(8,128)(2,1)S(1)}, u32[]{:S(2)}, u32[]{:S(2)}) collective-permute-start(bf16[8,2560]{1,0:T(8,128)(2,1)S(1)} %folded_sums.8.refs_0_), channel_id=1, source_target_pairs={{0,4},{1,5},{2,6},{3,7},{4,0},{5,1},{6,2},{7,3},{8,12},{9,13},{10,... | collective-permute-start | bytes 122888 | tf_op jit(solution)/shard_map/ppermute | solution.py:36
  115.4 5.4 %collective-permute-start.54 = (bf16[8,2560]{1,0:T(8,128)(2,1)S(1)}, bf16[8,2560]{1,0:T(8,128)(2,1)S(1)}, u32[]{:S(2)}, u32[]{:S(2)}) collective-permute-start(bf16[8,2560]{1,0:T(8,128)(2,1)S(1)} %folded_sums.8.refs_0_), channel_id=1, source_target_pairs={{0,2},{1,3},{2,0},{3,1},{4,6},{5,7},{6,4},{7,5},{8,10},{9,11},{10,... | collective-permute-start | bytes 122888 | tf_op jit(solution)/shard_map/ppermute | solution.py:36
  122.1 5.6 %collective-permute-start.56 = (bf16[8,640]{1,0:T(8,128)(2,1)S(1)}, bf16[8,640]{1,0:T(8,128)(2,1)S(1)}, u32[]{:S(2)}, u32[]{:S(2)}) collective-permute-start(bf16[8,640]{1,0:T(8,128)(2,1)S(1)} %sep_rows.25), channel_id=1, source_target_pairs={{0,6},{1,7},{2,4},{3,5},{4,2},{5,3},{6,0},{7,1},{8,14},{9,15},{10,... | collective-permute-start | bytes 30728 | tf_op jit(solution)/shard_map/ppermute | solution.py:36
  124.0 4.6 %collective-permute-start.57 = (bf16[8,640]{1,0:T(8,128)(2,1)S(1)}, bf16[8,640]{1,0:T(8,128)(2,1)S(1)}, u32[]{:S(2)}, u32[]{:S(2)}) collective-permute-start(bf16[8,640]{1,0:T(8,128)(2,1)S(1)} %sep_rows.25), channel_id=1, source_target_pairs={{0,4},{1,5},{2,6},{3,7},{4,0},{5,1},{6,2},{7,3},{8,12},{9,13},{10,... | collective-permute-start | bytes 30728 | tf_op jit(solution)/shard_map/ppermute | solution.py:36
  124.0 4.6 %collective-permute-start.58 = (bf16[8,640]{1,0:T(8,128)(2,1)S(1)}, bf16[8,640]{1,0:T(8,128)(2,1)S(1)}, u32[]{:S(2)}, u32[]{:S(2)}) collective-permute-start(bf16[8,640]{1,0:T(8,128)(2,1)S(1)} %sep_rows.25), channel_id=1, source_target_pairs={{0,2},{1,3},{2,0},{3,1},{4,6},{5,7},{6,4},{7,5},{8,10},{9,11},{10,... | collective-permute-start | bytes 30728 | tf_op jit(solution)/shard_map/ppermute | solution.py:36
  128.6 4.9 %collective-permute-start.60 = (f32[8,256]{1,0:T(8,128)S(1)}, f32[8,256]{1,0:T(8,128)S(1)}, u32[]{:S(2)}, u32[]{:S(2)}) collective-permute-start(f32[8,256]{1,0:T(8,128)S(1)} %get-tuple-element.51), channel_id=1, source_target_pairs={{8,0},{9,1},{10,2},{11,3},{12,4},{13,5},{14,6},{15,7},{0,16},{1,17... | collective-permute-start | bytes 24584 | tf_op jit(solution)/shard_map/ppermute | solution.py:58
  134.0 6.3 %collective-permute-start.62 = (bf16[8,2560]{1,0:T(8,128)(2,1)S(1)}, bf16[8,2560]{1,0:T(8,128)(2,1)S(1)}, u32[]{:S(2)}, u32[]{:S(2)}) collective-permute-start(bf16[8,2560]{1,0:T(8,128)(2,1)S(1)} %folded_sums.9.refs_0_), channel_id=1, source_target_pairs={{0,6},{1,7},{2,4},{3,5},{4,2},{5,3},{6,0},{7,1},{8,14},{9,15},{10,... | collective-permute-start | bytes 122888 | tf_op jit(solution)/shard_map/ppermute | solution.py:36
  135.6 5.6 %collective-permute-start.63 = (bf16[8,2560]{1,0:T(8,128)(2,1)S(1)}, bf16[8,2560]{1,0:T(8,128)(2,1)S(1)}, u32[]{:S(2)}, u32[]{:S(2)}) collective-permute-start(bf16[8,2560]{1,0:T(8,128)(2,1)S(1)} %folded_sums.9.refs_0_), channel_id=1, source_target_pairs={{0,4},{1,5},{2,6},{3,7},{4,0},{5,1},{6,2},{7,3},{8,12},{9,13},{10,... | collective-permute-start | bytes 122888 | tf_op jit(solution)/shard_map/ppermute | solution.py:36
  136.6 4.6 %collective-permute-start.64 = (bf16[8,2560]{1,0:T(8,128)(2,1)S(1)}, bf16[8,2560]{1,0:T(8,128)(2,1)S(1)}, u32[]{:S(2)}, u32[]{:S(2)}) collective-permute-start(bf16[8,2560]{1,0:T(8,128)(2,1)S(1)} %folded_sums.9.refs_0_), channel_id=1, source_target_pairs={{0,2},{1,3},{2,0},{3,1},{4,6},{5,7},{6,4},{7,5},{8,10},{9,11},{10,... | collective-permute-start | bytes 122888 | tf_op jit(solution)/shard_map/ppermute | solution.py:36
  143.5 5.6 %collective-permute-start.66 = (bf16[8,640]{1,0:T(8,128)(2,1)S(1)}, bf16[8,640]{1,0:T(8,128)(2,1)S(1)}, u32[]{:S(2)}, u32[]{:S(2)}) collective-permute-start(bf16[8,640]{1,0:T(8,128)(2,1)S(1)} %sep_rows.27), channel_id=1, source_target_pairs={{0,6},{1,7},{2,4},{3,5},{4,2},{5,3},{6,0},{7,1},{8,14},{9,15},{10,... | collective-permute-start | bytes 30728 | tf_op jit(solution)/shard_map/ppermute | solution.py:36
  145.9 4.6 %collective-permute-start.67 = (bf16[8,640]{1,0:T(8,128)(2,1)S(1)}, bf16[8,640]{1,0:T(8,128)(2,1)S(1)}, u32[]{:S(2)}, u32[]{:S(2)}) collective-permute-start(bf16[8,640]{1,0:T(8,128)(2,1)S(1)} %sep_rows.27), channel_id=1, source_target_pairs={{0,4},{1,5},{2,6},{3,7},{4,0},{5,1},{6,2},{7,3},{8,12},{9,13},{10,... | collective-permute-start | bytes 30728 | tf_op jit(solution)/shard_map/ppermute | solution.py:36
  (24 other events, 58.1 us)

commit v8 on v7

--- a/solution.py
+++ b/solution.py
@@ -558,21 +558,31 @@
     return first * leaf_values - part
 
 
-def spread_cells(level, stored, spread, leaf_values, before=None, subtract=False, last=False):
-    given = [stored, leaf_values] + ([before] if subtract else [])
-    outputs = 1 if last else 2
+def spread_cells(level, stored, spread, leaf_values, held=(), before=None, last=False):
+    given = [stored, leaf_values, *held] + ([] if before is None else [before])
+    outputs = 2 if last else 3
 
     def kernel(*refs):
         stored_ref, leaf_ref = refs[:2]
-        spread_ref, part_out = refs[-1 - outputs], refs[-outputs]
-
-        @pl.when(lax.axis_index("layer") == level)
+        spread_ref = refs[len(given)]
+        part_out, leaf_out = refs[len(given) + 1 : len(given) + 3]
+        here = lax.axis_index("layer") == level
+
+        @pl.when(here)
         def _():
             part = times(stored_ref[...].astype(F32), spread_ref[0], spread_ref[1], 0)
             part_out[...] = part
+            leaf_out[...] = leaf_ref[...]
             if not last:
-                held = refs[2][...] if subtract else None
-                refs[-1][...] = share_of_value(part, leaf_ref[...], held, subtract)
+                value = None if before is None else refs[len(given) - 1][...]
+                refs[-1][...] = share_of_value(part, leaf_ref[...], value, before is not None)
+
+        if held:
+
+            @pl.when(jnp.logical_not(here))
+            def _():
+                part_out[...] = refs[2][...]
+                leaf_out[...] = refs[3][...]
 
     return pl.pallas_call(
         kernel,
@@ -585,40 +595,27 @@
     )(*given, in_vmem(spread))
 
 
-def finish(level, leaf_values, part, theirs, before=None, subtract=False, last=False):
+def finish(part, leaf_values, before=None, depth=0):
     cells = part.shape[1] // 2
-    given = [leaf_values, part, theirs] + ([] if before is None else [before])
+    given = [leaf_values, part, pair(part)] + ([] if before is None else [before])
 
     def kernel(*refs):
         leaf_ref, part_ref, theirs_ref = refs[:3]
-        here = lax.axis_index("layer") == level
-
-        def store(value):
-            if last:
-                refs[-1][0, 0] = value[:4, :cells]
-                refs[-1][0, 1] = value[4:, :cells]
-            else:
-                refs[-1][...] = value
-
-        @pl.when(here)
-        def _():
-            swapped = jnp.concatenate([theirs_ref[:, cells:], theirs_ref[:, :cells]], axis=1)
-            solved = leaf_ref[...] - (part_ref[...] + swapped)
-            if subtract:
-                solved = refs[3][...] - solved
-            store(solved)
-
-        if before is not None:
-
-            @pl.when(jnp.logical_not(here))
-            def _():
-                store(refs[3][...])
+        swapped = jnp.concatenate([theirs_ref[:, cells:], theirs_ref[:, :cells]], axis=1)
+        solved = leaf_ref[...] - (part_ref[...] + swapped)
+        if before is None:
+            refs[-1][...] = solved
+        else:
+            bottom = lax.axis_index("layer") == depth - 1
+            value = refs[3][...] - jnp.where(bottom, 0.0, solved)
+            refs[-1][0, 0] = value[:4, :cells]
+            refs[-1][0, 1] = value[4:, :cells]
 
     return pl.pallas_call(
         kernel,
         in_specs=[VMEM] * len(given),
         out_specs=VMEM,
-        out_shape=jax.ShapeDtypeStruct((1, 2, 4, cells) if last else part.shape, F32),
+        out_shape=jax.ShapeDtypeStruct(part.shape if before is None else (1, 2, 4, cells), F32),
         compiler_params=params(16),
         cost_estimate=cost(4 * part.size, 16 * part.size),
         name="finish",
@@ -658,8 +655,8 @@
         own_rows = sep_rows(level, half_sums, sep, False)
         return sep_rows(level, other_sums, sep, True, own_rows)
 
-    def solve(level, before, subtract=False, last=False, arrived=None):
-        if subtract:
+    def solve(level, arrived, held, before=None, last=False):
+        if before is not None:
             sums = folded_sums(level, arrived, fold_below)
             leaf_values = leaf_only(level, arrived, blocks)
         elif level > 1:
@@ -668,17 +665,15 @@
         else:
             leaf_values, sums = leaf_and_gather(level, blocks, gather, arrived, sources)
         stored = gather_chips(own_rows_of(level, sum_chips(sums, leaf_values)))
-        part, *share = spread_cells(level, stored, spread, leaf_values, before, subtract, last)
-        return finish(level, leaf_values, part, pair(part), before, subtract, last), *share
+        return spread_cells(level, stored, spread, leaf_values, held, before, last)
 
     own_rows = own_rows_of(0, sum_chips(first_sums, sep))
     if rows % 128 == 0:
         spread, blocks = transpose_maps(own_maps, their_maps, panel_owner[0], rows, own_rows)
     else:
         spread, blocks = take_maps(own_maps, their_maps, panel_owner[0], rows)
-    part, share = spread_cells(0, gather_chips(own_rows, spread), spread, first_values)
+    *held, share = spread_cells(0, gather_chips(own_rows, spread), spread, first_values)
     arrived = hop(share, 0, 1)
-    value = finish(0, first_values, part, pair(part))
     gather = transpose_gather(own_gather, their_gather, share)
 
     fold_above = folded(blocks, gather, 1, range(2, depth), share)
@@ -687,13 +682,15 @@
     for level in range(1, depth):
         if level > 1:
             arrived = hop(share, level - 1, level)
-        value, share = solve(level, value, arrived=arrived)
+        *held, share = solve(level, arrived, held)
         if level == depth - 2:
             fold_below = folded(blocks, gather, 2, range(depth - 1), share)
-    for level in range(depth - 2, -1, -1):
-        arrived = hop(share[0] if level < depth - 2 else share, level + 1, level)
-        value, *share = solve(level, value, True, level == 0, arrived=arrived)
-    return value
+    value = finish(*held)
+    for level in range(depth - 2, 0, -1):
+        arrived = hop(share, level + 1, level)
+        *held, share = solve(level, arrived, held, value)
+    held = solve(0, hop(share, 1, 0), held, value, last=True)
+    return finish(*held, value, depth)
 
 
 def solution(mesh):

time: 153 us -> 153 us (level)
  waiting for transfers between devices: 55.7 us -> 57.6 us
  starting transfers between devices: 77.9 us -> 76.1 us
    ppermute x42, waiting for transfers between devices: 30.9 us -> 33.4 us  [from_chips(): lax.ppermute(block, 'front', xor_route('front', 2 * (chips - step)))]
    ppermute x17 -> x12, waiting for transfers between devices: 11.1 us -> 9.64 us  [pair(): return lax.ppermute(block, 'front', xor_route('front', 1))]
  transfers between devices with their start and end apart: 71 -> 66, of which waited for: 46 -> 44; matrix products, arithmetic and copies ran while one was open for 0% -> 0% of each run, Pallas kernels for 9% -> 9%
where the time goes in v8:
time: 153 us
  starting transfers between devices  76.1 us (50%)
  waiting for transfers between devices  57.6 us (38%)
  Pallas kernels  18.5 us (12%)
    ppermute x42, starting transfers between devices, from_chips(): lax.ppermute(block, 'front', xor_route('front', 2 * (chips - step)))  62.8 us
    ppermute x42, waiting for transfers between devices, from_chips(): lax.ppermute(block, 'front', xor_route('front', 2 * (chips - step)))  33.4 us
    ppermute x12, waiting for transfers between devices, hop(): lax.ppermute(block, ('layer', 'front'), [(i * slots + j, target[i] * slot...  14.6 us
    ppermute x12, starting transfers between devices, hop(): lax.ppermute(block, ('layer', 'front'), [(i * slots + j, target[i] * slot...  11.7 us
    ppermute x12, waiting for transfers between devices, pair(): return lax.ppermute(block, 'front', xor_route('front', 1))  9.64 us
    pallas_call x1, Pallas kernels, transpose_sep(): pl.pallas_call(kernel, in_specs=[ANY, ANY], out_specs=VMEM, out_shape=plt...  5.35 us
    pallas_call x14, Pallas kernels, sep_rows(): pl.pallas_call(kernel, in_specs=[VMEM] * (len(given) + 1), out_specs=VMEM...  3.91 us
  transfers between devices with their start and end apart: 66, of which 44 were waited for; matrix products, arithmetic and copies ran while one was open for 0% of the time, Pallas kernels for 9%

profile of v8, /device:TPU:0, one launch (start us, length us, event | category | flops | bytes accessed | tf_op | source)
XLA Modules:
  0.0 152.6 jit_solution(14379636158755366788)
XLA Ops:
  0.0 2.7 %first_leaf_and_gather.1 = (f32[8,2816]{1,0:T(8,128)S(1)}, f32[8,2816]{1,0:T(8,128)S(1)}, bf16[2,5120,128]{2,1,0:T(8,128)(2,1)S(1)}, bf16[2,128,5504]{2,1,0:T(8,128)(2,1)S(1)}) custom-call(f32[2,4,128]{2,1,0:T(4,128)} %bitcast.15, bf16[2,5120,128]{2,1,0:T(8,128)(2,1)} %bitcast.10, bf16[2,128,5120]{2,1,0:T(8,128)(2,1)} %bitcast.11, ...), custom_call_target="tpu_custom_call" | custom-call | flops 20971520 | bytes 2621440 | tf_op jit(solution)/shard_map/first_leaf_and_gather/pallas_call | solution.py:333
  4.7 5.0 %collective-permute-start.1 = (bf16[8,2560]{1,0:T(8,128)(2,1)S(1)}, bf16[8,2560]{1,0:T(8,128)(2,1)S(1)}, u32[]{:S(2)}, u32[]{:S(2)}) collective-permute-start(bf16[8,2560]{1,0:T(8,128)(2,1)S(1)} %fusion._.refs_0_.refs_2_), channel_id=1, source_target_pairs={{0,6},{1,7},{2,4},{3,5},{4,2},{5,3},{6,0},{7,1},{8,14},{9,15},{10,... | collective-permute-start | bytes 122888 | tf_op jit(solution)/shard_map/ppermute | solution.py:36
  10.3 5.3 %transpose_sep.1.refs_4_.refs_1_.refs_2_ = bf16[2,5120,640]{2,1,0:T(8,128)(2,1)S(1)} custom-call(bf16[2,640,5120]{2,1,0:T(8,128)(2,1)} %bitcast.9, bf16[8,2560]{1,0:T(8,128)(2,1)S(1)} %fusion._.refs_0_.refs_2_), custom_call_target="tpu_custom_call" | custom-call | bytes 26214400 | tf_op jit(solution)/shard_map/transpose_sep/pallas_call | solution.py:127
  17.9 3.9 %collective-permute-start.5 = (bf16[8,640]{1,0:T(8,128)(2,1)S(1)}, bf16[8,640]{1,0:T(8,128)(2,1)S(1)}, u32[]{:S(2)}, u32[]{:S(2)}) collective-permute-start(bf16[8,640]{1,0:T(8,128)(2,1)S(1)} %sep_rows.15._.refs_0_), channel_id=1, source_target_pairs={{0,6},{1,7},{2,4},{3,5},{4,2},{5,3},{6,0},{7,1},{8,14},{9,15},{10,... | collective-permute-start | bytes 30728 | tf_op jit(solution)/shard_map/ppermute | solution.py:36
  23.8 2.6 %collective-permute-done.6.refs_2_ = bf16[8,640]{1,0:T(8,128)(2,1)S(1)} collective-permute-done((bf16[8,640]{1,0:T(8,128)(2,1)S(1)}, bf16[8,640]{1,0:T(8,128)(2,1)S(1)}, u32[]{:S(2)}, u32[]{:S(2)}) %collective-permute-start.6) | collective-permute-done | bytes 10272 | tf_op jit(solution)/shard_map/ppermute | solution.py:36
  27.7 3.1 %collective-permute-done.10.refs_1_ = f32[8,256]{1,0:T(8,128)S(1)} collective-permute-done((f32[8,256]{1,0:T(8,128)S(1)}, f32[8,256]{1,0:T(8,128)S(1)}, u32[]{:S(2)}, u32[]{:S(2)}) %collective-permute-start.10) | collective-permute-done | bytes 8224 | tf_op jit(solution)/shard_map/ppermute | solution.py:58
  31.4 1.4 collective-permute-start.12
  33.4 2.4 %collective-permute-start.14 = (bf16[8,2560]{1,0:T(8,128)(2,1)S(1)}, bf16[8,2560]{1,0:T(8,128)(2,1)S(1)}, u32[]{:S(2)}, u32[]{:S(2)}) collective-permute-start(bf16[8,2560]{1,0:T(8,128)(2,1)S(1)} %get-tuple-element.46.refs_0_), channel_id=1, source_target_pairs={{0,2},{1,3},{2,0},{3,1},{4,6},{5,7},{6,4},{7,5},{8,10},{9,11},{10,... | collective-permute-start | bytes 122888 | tf_op jit(solution)/shard_map/ppermute | solution.py:36
  35.8 1.9 %collective-permute-done.12.refs_1_ = bf16[8,2560]{1,0:T(8,128)(2,1)S(1)} collective-permute-done((bf16[8,2560]{1,0:T(8,128)(2,1)S(1)}, bf16[8,2560]{1,0:T(8,128)(2,1)S(1)}, u32[]{:S(2)}, u32[]{:S(2)}) %collective-permute-start.12) | collective-permute-done | bytes 40992 | tf_op jit(solution)/shard_map/ppermute | solution.py:36
  39.7 2.2 %collective-permute-start.16 = (bf16[8,640]{1,0:T(8,128)(2,1)S(1)}, bf16[8,640]{1,0:T(8,128)(2,1)S(1)}, u32[]{:S(2)}, u32[]{:S(2)}) collective-permute-start(bf16[8,640]{1,0:T(8,128)(2,1)S(1)} %sep_rows.17), channel_id=1, source_target_pairs={{0,6},{1,7},{2,4},{3,5},{4,2},{5,3},{6,0},{7,1},{8,14},{9,15},{10,... | collective-permute-start | bytes 30728 | tf_op jit(solution)/shard_map/ppermute | solution.py:36
  42.6 1.5 collective-permute-start.18
  48.1 2.2 %collective-permute-done.19.refs_0_ = f32[8,256]{1,0:T(8,128)S(1)} collective-permute-done((f32[8,256]{1,0:T(8,128)S(1)}, f32[8,256]{1,0:T(8,128)S(1)}, u32[]{:S(2)}, u32[]{:S(2)}) %collective-permute-start.19) | collective-permute-done | bytes 8224 | tf_op jit(solution)/shard_map/ppermute | solution.py:58
  50.5 1.8 %collective-permute-start.21 = (bf16[8,2560]{1,0:T(8,128)(2,1)S(1)}, bf16[8,2560]{1,0:T(8,128)(2,1)S(1)}, u32[]{:S(2)}, u32[]{:S(2)}) collective-permute-start(bf16[8,2560]{1,0:T(8,128)(2,1)S(1)} %folded_sums.5.refs_0_), channel_id=1, source_target_pairs={{0,6},{1,7},{2,4},{3,5},{4,2},{5,3},{6,0},{7,1},{8,14},{9,15},{10,... | collective-permute-start | bytes 122888 | tf_op jit(solution)/shard_map/ppermute | solution.py:36
  53.4 1.5 collective-permute-start.23
  54.9 1.7 %collective-permute-done.21.refs_1_ = bf16[8,2560]{1,0:T(8,128)(2,1)S(1)} collective-permute-done((bf16[8,2560]{1,0:T(8,128)(2,1)S(1)}, bf16[8,2560]{1,0:T(8,128)(2,1)S(1)}, u32[]{:S(2)}, u32[]{:S(2)}) %collective-permute-start.21) | collective-permute-done | bytes 40992 | tf_op jit(solution)/shard_map/ppermute | solution.py:36
  56.5 1.5 collective-permute-done.22.refs_2_
  59.3 2.0 %collective-permute-start.25 = (bf16[8,640]{1,0:T(8,128)(2,1)S(1)}, bf16[8,640]{1,0:T(8,128)(2,1)S(1)}, u32[]{:S(2)}, u32[]{:S(2)}) collective-permute-start(bf16[8,640]{1,0:T(8,128)(2,1)S(1)} %sep_rows.19), channel_id=1, source_target_pairs={{0,6},{1,7},{2,4},{3,5},{4,2},{5,3},{6,0},{7,1},{8,14},{9,15},{10,... | collective-permute-start | bytes 30728 | tf_op jit(solution)/shard_map/ppermute | solution.py:36
  61.6 2.1 %collective-permute-start.27 = (bf16[8,640]{1,0:T(8,128)(2,1)S(1)}, bf16[8,640]{1,0:T(8,128)(2,1)S(1)}, u32[]{:S(2)}, u32[]{:S(2)}) collective-permute-start(bf16[8,640]{1,0:T(8,128)(2,1)S(1)} %sep_rows.19), channel_id=1, source_target_pairs={{0,2},{1,3},{2,0},{3,1},{4,6},{5,7},{6,4},{7,5},{8,10},{9,11},{10,... | collective-permute-start | bytes 30728 | tf_op jit(solution)/shard_map/ppermute | solution.py:36
  66.0 1.6 %collective-permute-start.28 = (f32[8,256]{1,0:T(8,128)S(1)}, f32[8,256]{1,0:T(8,128)S(1)}, u32[]{:S(2)}, u32[]{:S(2)}) collective-permute-start(f32[8,256]{1,0:T(8,128)S(1)} %get-tuple-element.55._), channel_id=1, source_target_pairs={{16,24},{17,25},{18,26},{19,27},{20,28},{21,29},{22,30},{23,31},{2... | collective-permute-start | bytes 24584 | tf_op jit(solution)/shard_map/ppermute | solution.py:58
  67.6 1.8 %collective-permute-start.29 = (f32[8,256]{1,0:T(8,128)S(1)}, f32[8,256]{1,0:T(8,128)S(1)}, u32[]{:S(2)}, u32[]{:S(2)}) collective-permute-start(f32[8,256]{1,0:T(8,128)S(1)} %get-tuple-element.55._), channel_id=1, source_target_pairs={{16,25},{17,24},{18,27},{19,26},{20,29},{21,28},{22,31},{23,30},{2... | collective-permute-start | bytes 24584 | tf_op jit(solution)/shard_map/ppermute | solution.py:58
  69.4 1.4 collective-permute-done.28.refs_0_
  71.6 1.6 %collective-permute-start.30 = (bf16[8,2560]{1,0:T(8,128)(2,1)S(1)}, bf16[8,2560]{1,0:T(8,128)(2,1)S(1)}, u32[]{:S(2)}, u32[]{:S(2)}) collective-permute-start(bf16[8,2560]{1,0:T(8,128)(2,1)S(1)} %folded_sums.6.refs_0_), channel_id=1, source_target_pairs={{0,6},{1,7},{2,4},{3,5},{4,2},{5,3},{6,0},{7,1},{8,14},{9,15},{10,... | collective-permute-start | bytes 122888 | tf_op jit(solution)/shard_map/ppermute | solution.py:36
  74.3 1.6 %collective-permute-start.32 = (bf16[8,2560]{1,0:T(8,128)(2,1)S(1)}, bf16[8,2560]{1,0:T(8,128)(2,1)S(1)}, u32[]{:S(2)}, u32[]{:S(2)}) collective-permute-start(bf16[8,2560]{1,0:T(8,128)(2,1)S(1)} %folded_sums.6.refs_0_), channel_id=1, source_target_pairs={{0,2},{1,3},{2,0},{3,1},{4,6},{5,7},{6,4},{7,5},{8,10},{9,11},{10,... | collective-permute-start | bytes 122888 | tf_op jit(solution)/shard_map/ppermute | solution.py:36
  75.9 1.6 %collective-permute-done.30.refs_1_ = bf16[8,2560]{1,0:T(8,128)(2,1)S(1)} collective-permute-done((bf16[8,2560]{1,0:T(8,128)(2,1)S(1)}, bf16[8,2560]{1,0:T(8,128)(2,1)S(1)}, u32[]{:S(2)}, u32[]{:S(2)}) %collective-permute-start.30) | collective-permute-done | bytes 40992 | tf_op jit(solution)/shard_map/ppermute | solution.py:36
  77.6 1.6 %collective-permute-done.31.refs_2_ = bf16[8,2560]{1,0:T(8,128)(2,1)S(1)} collective-permute-done((bf16[8,2560]{1,0:T(8,128)(2,1)S(1)}, bf16[8,2560]{1,0:T(8,128)(2,1)S(1)}, u32[]{:S(2)}, u32[]{:S(2)}) %collective-permute-start.31) | collective-permute-done | bytes 40992 | tf_op jit(solution)/shard_map/ppermute | solution.py:36
  80.5 2.1 %collective-permute-start.34 = (bf16[8,640]{1,0:T(8,128)(2,1)S(1)}, bf16[8,640]{1,0:T(8,128)(2,1)S(1)}, u32[]{:S(2)}, u32[]{:S(2)}) collective-permute-start(bf16[8,640]{1,0:T(8,128)(2,1)S(1)} %sep_rows.21), channel_id=1, source_target_pairs={{0,6},{1,7},{2,4},{3,5},{4,2},{5,3},{6,0},{7,1},{8,14},{9,15},{10,... | collective-permute-start | bytes 30728 | tf_op jit(solution)/shard_map/ppermute | solution.py:36
  82.7 2.2 %collective-permute-start.36 = (bf16[8,640]{1,0:T(8,128)(2,1)S(1)}, bf16[8,640]{1,0:T(8,128)(2,1)S(1)}, u32[]{:S(2)}, u32[]{:S(2)}) collective-permute-start(bf16[8,640]{1,0:T(8,128)(2,1)S(1)} %sep_rows.21), channel_id=1, source_target_pairs={{0,2},{1,3},{2,0},{3,1},{4,6},{5,7},{6,4},{7,5},{8,10},{9,11},{10,... | collective-permute-start | bytes 30728 | tf_op jit(solution)/shard_map/ppermute | solution.py:36
  87.2 2.4 %collective-permute-start.37 = (f32[8,256]{1,0:T(8,128)S(1)}, f32[8,256]{1,0:T(8,128)S(1)}, u32[]{:S(2)}, u32[]{:S(2)}) collective-permute-start(f32[8,256]{1,0:T(8,128)S(1)} %get-tuple-element.58), channel_id=1, source_target_pairs={{24,16},{25,17},{26,18},{27,19},{28,20},{29,21},{30,22},{31,23},{1... | collective-permute-start | bytes 24584 | tf_op jit(solution)/shard_map/ppermute | solution.py:58
  89.6 2.0 %folded.3.refs_2_ = bf16[2,256,2560]{2,1,0:T(8,128)(2,1)S(1)} custom-call(bf16[2,3,2,128,128]{4,3,2,1,0:T(8,128)(2,1)S(1)} %get-tuple-element.44.refs_3_.blocks_ref.refs_2_, bf16[2,256,2560]{2,1,0:T(8,128)(2,1)S(1)} %transpose_gather.1.refs_4_.gather_ref, f32[8,256]{1,0:T(8,128)S(1)} %get-tuple-element.55._), custom_call_target="tpu_custom_call" | custom-call | flops 1342177280 | bytes 5242880 | tf_op jit(solution)/shard_map/folded/pallas_call | solution.py:422
  92.7 1.6 %collective-permute-start.39 = (bf16[8,2560]{1,0:T(8,128)(2,1)S(1)}, bf16[8,2560]{1,0:T(8,128)(2,1)S(1)}, u32[]{:S(2)}, u32[]{:S(2)}) collective-permute-start(bf16[8,2560]{1,0:T(8,128)(2,1)S(1)} %folded_sums.7.refs_0_), channel_id=1, source_target_pairs={{0,6},{1,7},{2,4},{3,5},{4,2},{5,3},{6,0},{7,1},{8,14},{9,15},{10,... | collective-permute-start | bytes 122888 | tf_op jit(solution)/shard_map/ppermute | solution.py:36
  95.2 1.9 %collective-permute-start.41 = (bf16[8,2560]{1,0:T(8,128)(2,1)S(1)}, bf16[8,2560]{1,0:T(8,128)(2,1)S(1)}, u32[]{:S(2)}, u32[]{:S(2)}) collective-permute-start(bf16[8,2560]{1,0:T(8,128)(2,1)S(1)} %folded_sums.7.refs_0_), channel_id=1, source_target_pairs={{0,2},{1,3},{2,0},{3,1},{4,6},{5,7},{6,4},{7,5},{8,10},{9,11},{10,... | collective-permute-start | bytes 122888 | tf_op jit(solution)/shard_map/ppermute | solution.py:36
  97.1 1.7 %collective-permute-done.39.refs_1_ = bf16[8,2560]{1,0:T(8,128)(2,1)S(1)} collective-permute-done((bf16[8,2560]{1,0:T(8,128)(2,1)S(1)}, bf16[8,2560]{1,0:T(8,128)(2,1)S(1)}, u32[]{:S(2)}, u32[]{:S(2)}) %collective-permute-start.39) | collective-permute-done | bytes 40992 | tf_op jit(solution)/shard_map/ppermute | solution.py:36
  101.3 2.4 %collective-permute-start.43 = (bf16[8,640]{1,0:T(8,128)(2,1)S(1)}, bf16[8,640]{1,0:T(8,128)(2,1)S(1)}, u32[]{:S(2)}, u32[]{:S(2)}) collective-permute-start(bf16[8,640]{1,0:T(8,128)(2,1)S(1)} %sep_rows.23), channel_id=1, source_target_pairs={{0,6},{1,7},{2,4},{3,5},{4,2},{5,3},{6,0},{7,1},{8,14},{9,15},{10,... | collective-permute-start | bytes 30728 | tf_op jit(solution)/shard_map/ppermute | solution.py:36
  103.8 1.9 %collective-permute-start.45 = (bf16[8,640]{1,0:T(8,128)(2,1)S(1)}, bf16[8,640]{1,0:T(8,128)(2,1)S(1)}, u32[]{:S(2)}, u32[]{:S(2)}) collective-permute-start(bf16[8,640]{1,0:T(8,128)(2,1)S(1)} %sep_rows.23), channel_id=1, source_target_pairs={{0,2},{1,3},{2,0},{3,1},{4,6},{5,7},{6,4},{7,5},{8,10},{9,11},{10,... | collective-permute-start | bytes 30728 | tf_op jit(solution)/shard_map/ppermute | solution.py:36
  112.7 1.7 %collective-permute-start.49 = (bf16[8,2560]{1,0:T(8,128)(2,1)S(1)}, bf16[8,2560]{1,0:T(8,128)(2,1)S(1)}, u32[]{:S(2)}, u32[]{:S(2)}) collective-permute-start(bf16[8,2560]{1,0:T(8,128)(2,1)S(1)} %folded_sums.8.refs_0_), channel_id=1, source_target_pairs={{0,6},{1,7},{2,4},{3,5},{4,2},{5,3},{6,0},{7,1},{8,14},{9,15},{10,... | collective-permute-start | bytes 122888 | tf_op jit(solution)/shard_map/ppermute | solution.py:36
  115.5 1.7 %collective-permute-start.51 = (bf16[8,2560]{1,0:T(8,128)(2,1)S(1)}, bf16[8,2560]{1,0:T(8,128)(2,1)S(1)}, u32[]{:S(2)}, u32[]{:S(2)}) collective-permute-start(bf16[8,2560]{1,0:T(8,128)(2,1)S(1)} %folded_sums.8.refs_0_), channel_id=1, source_target_pairs={{0,2},{1,3},{2,0},{3,1},{4,6},{5,7},{6,4},{7,5},{8,10},{9,11},{10,... | collective-permute-start | bytes 122888 | tf_op jit(solution)/shard_map/ppermute | solution.py:36
  117.1 1.7 %collective-permute-done.49.refs_1_ = bf16[8,2560]{1,0:T(8,128)(2,1)S(1)} collective-permute-done((bf16[8,2560]{1,0:T(8,128)(2,1)S(1)}, bf16[8,2560]{1,0:T(8,128)(2,1)S(1)}, u32[]{:S(2)}, u32[]{:S(2)}) %collective-permute-start.49) | collective-permute-done | bytes 40992 | tf_op jit(solution)/shard_map/ppermute | solution.py:36
  118.8 1.6 %collective-permute-done.50.refs_2_ = bf16[8,2560]{1,0:T(8,128)(2,1)S(1)} collective-permute-done((bf16[8,2560]{1,0:T(8,128)(2,1)S(1)}, bf16[8,2560]{1,0:T(8,128)(2,1)S(1)}, u32[]{:S(2)}, u32[]{:S(2)}) %collective-permute-start.50) | collective-permute-done | bytes 40992 | tf_op jit(solution)/shard_map/ppermute | solution.py:36
  121.7 2.1 %collective-permute-start.53 = (bf16[8,640]{1,0:T(8,128)(2,1)S(1)}, bf16[8,640]{1,0:T(8,128)(2,1)S(1)}, u32[]{:S(2)}, u32[]{:S(2)}) collective-permute-start(bf16[8,640]{1,0:T(8,128)(2,1)S(1)} %sep_rows.25), channel_id=1, source_target_pairs={{0,6},{1,7},{2,4},{3,5},{4,2},{5,3},{6,0},{7,1},{8,14},{9,15},{10,... | collective-permute-start | bytes 30728 | tf_op jit(solution)/shard_map/ppermute | solution.py:36
  123.9 2.2 %collective-permute-start.55 = (bf16[8,640]{1,0:T(8,128)(2,1)S(1)}, bf16[8,640]{1,0:T(8,128)(2,1)S(1)}, u32[]{:S(2)}, u32[]{:S(2)}) collective-permute-start(bf16[8,640]{1,0:T(8,128)(2,1)S(1)} %sep_rows.25), channel_id=1, source_target_pairs={{0,2},{1,3},{2,0},{3,1},{4,6},{5,7},{6,4},{7,5},{8,10},{9,11},{10,... | collective-permute-start | bytes 30728 | tf_op jit(solution)/shard_map/ppermute | solution.py:36
  128.4 1.8 %collective-permute-start.56 = (f32[8,256]{1,0:T(8,128)S(1)}, f32[8,256]{1,0:T(8,128)S(1)}, u32[]{:S(2)}, u32[]{:S(2)}) collective-permute-start(f32[8,256]{1,0:T(8,128)S(1)} %get-tuple-element.64), channel_id=1, source_target_pairs={{8,0},{9,1},{10,2},{11,3},{12,4},{13,5},{14,6},{15,7},{0,16},{1,17... | collective-permute-start | bytes 24584 | tf_op jit(solution)/shard_map/ppermute | solution.py:58
  130.3 3.1 %collective-permute-done.56.refs_0_ = f32[8,256]{1,0:T(8,128)S(1)} collective-permute-done((f32[8,256]{1,0:T(8,128)S(1)}, f32[8,256]{1,0:T(8,128)S(1)}, u32[]{:S(2)}, u32[]{:S(2)}) %collective-permute-start.56) | collective-permute-done | bytes 8224 | tf_op jit(solution)/shard_map/ppermute | solution.py:58
  133.9 1.5 collective-permute-start.58
  136.4 1.9 %collective-permute-start.60 = (bf16[8,2560]{1,0:T(8,128)(2,1)S(1)}, bf16[8,2560]{1,0:T(8,128)(2,1)S(1)}, u32[]{:S(2)}, u32[]{:S(2)}) collective-permute-start(bf16[8,2560]{1,0:T(8,128)(2,1)S(1)} %folded_sums.9.refs_0_), channel_id=1, source_target_pairs={{0,2},{1,3},{2,0},{3,1},{4,6},{5,7},{6,4},{7,5},{8,10},{9,11},{10,... | collective-permute-start | bytes 122888 | tf_op jit(solution)/shard_map/ppermute | solution.py:36
  138.6 1.6 %collective-permute-done.58.refs_1_ = bf16[8,2560]{1,0:T(8,128)(2,1)S(1)} collective-permute-done((bf16[8,2560]{1,0:T(8,128)(2,1)S(1)}, bf16[8,2560]{1,0:T(8,128)(2,1)S(1)}, u32[]{:S(2)}, u32[]{:S(2)}) %collective-permute-start.58) | collective-permute-done | bytes 40992 | tf_op jit(solution)/shard_map/ppermute | solution.py:36
  143.3 2.5 %collective-permute-start.62 = (bf16[8,640]{1,0:T(8,128)(2,1)S(1)}, bf16[8,640]{1,0:T(8,128)(2,1)S(1)}, u32[]{:S(2)}, u32[]{:S(2)}) collective-permute-start(bf16[8,640]{1,0:T(8,128)(2,1)S(1)} %sep_rows.27), channel_id=1, source_target_pairs={{0,6},{1,7},{2,4},{3,5},{4,2},{5,3},{6,0},{7,1},{8,14},{9,15},{10,... | collective-permute-start | bytes 30728 | tf_op jit(solution)/shard_map/ppermute | solution.py:36
  146.1 1.7 %collective-permute-start.64 = (bf16[8,640]{1,0:T(8,128)(2,1)S(1)}, bf16[8,640]{1,0:T(8,128)(2,1)S(1)}, u32[]{:S(2)}, u32[]{:S(2)}) collective-permute-start(bf16[8,640]{1,0:T(8,128)(2,1)S(1)} %sep_rows.27), channel_id=1, source_target_pairs={{0,2},{1,3},{2,0},{3,1},{4,6},{5,7},{6,4},{7,5},{8,10},{9,11},{10,... | collective-permute-start | bytes 30728 | tf_op jit(solution)/shard_map/ppermute | solution.py:36
  148.9 1.5 collective-permute-done.63
  (147 shorter events, 51.9 us)
Async XLA Ops:
  4.2 18.3 %collective-permute-start.8 = (bf16[2,128,5504]{2,1,0:T(8,128)(2,1)S(1)}, bf16[2,128,5504]{2,1,0:T(8,128)(2,1)S(1)}, u32[]{:S(2)}, u32[]{:S(2)}) collective-permute-start(bf16[2,128,5504]{2,1,0:T(8,128)(2,1)S(1)} %get-tuple-element.41.own_ref), channel_id=1, source_target_pairs={{0,1},{1,0},{2,3},{3,2},{4,5},{5,4},{6,7},{7,6},{8,9},{9,8},{10,11... | collective-permute-start | bytes 8454152 | tf_op jit(solution)/shard_map/ppermute | solution.py:21
  4.6 22.4 %collective-permute-start.11 = (bf16[2,5120,128]{2,1,0:T(8,128)(2,1)S(1)}, bf16[2,5120,128]{2,1,0:T(8,128)(2,1)S(1)}, u32[]{:S(2)}, u32[]{:S(2)}) collective-permute-start(bf16[2,5120,128]{2,1,0:T(8,128)(2,1)S(1)} %get-tuple-element.45.own_ref), channel_id=1, source_target_pairs={{0,1},{1,0},{2,3},{3,2},{4,5},{5,4},{6,7},{7,6},{8,9},{9,8},{10,11... | collective-permute-start | bytes 7864328 | tf_op jit(solution)/shard_map/ppermute | solution.py:21
  4.7 10.9 %collective-permute-start.1 = (bf16[8,2560]{1,0:T(8,128)(2,1)S(1)}, bf16[8,2560]{1,0:T(8,128)(2,1)S(1)}, u32[]{:S(2)}, u32[]{:S(2)}) collective-permute-start(bf16[8,2560]{1,0:T(8,128)(2,1)S(1)} %fusion._.refs_0_.refs_2_), channel_id=1, source_target_pairs={{0,6},{1,7},{2,4},{3,5},{4,2},{5,3},{6,0},{7,1},{8,14},{9,15},{10,... | collective-permute-start | bytes 122888 | tf_op jit(solution)/shard_map/ppermute | solution.py:36
  9.7 5.9 %collective-permute-start.2 = (bf16[8,2560]{1,0:T(8,128)(2,1)S(1)}, bf16[8,2560]{1,0:T(8,128)(2,1)S(1)}, u32[]{:S(2)}, u32[]{:S(2)}) collective-permute-start(bf16[8,2560]{1,0:T(8,128)(2,1)S(1)} %fusion._.refs_0_.refs_2_), channel_id=1, source_target_pairs={{0,4},{1,5},{2,6},{3,7},{4,0},{5,1},{6,2},{7,3},{8,12},{9,13},{10,... | collective-permute-start | bytes 122888 | tf_op jit(solution)/shard_map/ppermute | solution.py:36
  9.7 5.9 %collective-permute-start.3 = (bf16[8,2560]{1,0:T(8,128)(2,1)S(1)}, bf16[8,2560]{1,0:T(8,128)(2,1)S(1)}, u32[]{:S(2)}, u32[]{:S(2)}) collective-permute-start(bf16[8,2560]{1,0:T(8,128)(2,1)S(1)} %fusion._.refs_0_.refs_2_), channel_id=1, source_target_pairs={{0,2},{1,3},{2,0},{3,1},{4,6},{5,7},{6,4},{7,5},{8,10},{9,11},{10,... | collective-permute-start | bytes 122888 | tf_op jit(solution)/shard_map/ppermute | solution.py:36
  17.9 5.8 %collective-permute-start.5 = (bf16[8,640]{1,0:T(8,128)(2,1)S(1)}, bf16[8,640]{1,0:T(8,128)(2,1)S(1)}, u32[]{:S(2)}, u32[]{:S(2)}) collective-permute-start(bf16[8,640]{1,0:T(8,128)(2,1)S(1)} %sep_rows.15._.refs_0_), channel_id=1, source_target_pairs={{0,6},{1,7},{2,4},{3,5},{4,2},{5,3},{6,0},{7,1},{8,14},{9,15},{10,... | collective-permute-start | bytes 30728 | tf_op jit(solution)/shard_map/ppermute | solution.py:36
  21.8 4.6 %collective-permute-start.6 = (bf16[8,640]{1,0:T(8,128)(2,1)S(1)}, bf16[8,640]{1,0:T(8,128)(2,1)S(1)}, u32[]{:S(2)}, u32[]{:S(2)}) collective-permute-start(bf16[8,640]{1,0:T(8,128)(2,1)S(1)} %sep_rows.15._.refs_0_), channel_id=1, source_target_pairs={{0,4},{1,5},{2,6},{3,7},{4,0},{5,1},{6,2},{7,3},{8,12},{9,13},{10,... | collective-permute-start | bytes 30728 | tf_op jit(solution)/shard_map/ppermute | solution.py:36
  21.8 4.6 %collective-permute-start.7 = (bf16[8,640]{1,0:T(8,128)(2,1)S(1)}, bf16[8,640]{1,0:T(8,128)(2,1)S(1)}, u32[]{:S(2)}, u32[]{:S(2)}) collective-permute-start(bf16[8,640]{1,0:T(8,128)(2,1)S(1)} %sep_rows.15._.refs_0_), channel_id=1, source_target_pairs={{0,2},{1,3},{2,0},{3,1},{4,6},{5,7},{6,4},{7,5},{8,10},{9,11},{10,... | collective-permute-start | bytes 30728 | tf_op jit(solution)/shard_map/ppermute | solution.py:36
  26.8 4.0 %collective-permute-start.10 = (f32[8,256]{1,0:T(8,128)S(1)}, f32[8,256]{1,0:T(8,128)S(1)}, u32[]{:S(2)}, u32[]{:S(2)}) collective-permute-start(f32[8,256]{1,0:T(8,128)S(1)} %get-tuple-element.43._), channel_id=1, source_target_pairs={{0,9},{1,8},{2,11},{3,10},{4,13},{5,12},{6,15},{7,14},{8,17},{9,16... | collective-permute-start | bytes 24584 | tf_op jit(solution)/shard_map/ppermute | solution.py:58
  26.8 4.6 %collective-permute-start.9 = (f32[8,256]{1,0:T(8,128)S(1)}, f32[8,256]{1,0:T(8,128)S(1)}, u32[]{:S(2)}, u32[]{:S(2)}) collective-permute-start(f32[8,256]{1,0:T(8,128)S(1)} %get-tuple-element.43._), channel_id=1, source_target_pairs={{0,8},{1,9},{2,10},{3,11},{4,12},{5,13},{6,14},{7,15},{8,16},{9,17... | collective-permute-start | bytes 24584 | tf_op jit(solution)/shard_map/ppermute | solution.py:58
  31.4 6.3 %collective-permute-start.12 = (bf16[8,2560]{1,0:T(8,128)(2,1)S(1)}, bf16[8,2560]{1,0:T(8,128)(2,1)S(1)}, u32[]{:S(2)}, u32[]{:S(2)}) collective-permute-start(bf16[8,2560]{1,0:T(8,128)(2,1)S(1)} %get-tuple-element.46.refs_0_), channel_id=1, source_target_pairs={{0,6},{1,7},{2,4},{3,5},{4,2},{5,3},{6,0},{7,1},{8,14},{9,15},{10,... | collective-permute-start | bytes 122888 | tf_op jit(solution)/shard_map/ppermute | solution.py:36
  32.9 5.5 %collective-permute-start.13 = (bf16[8,2560]{1,0:T(8,128)(2,1)S(1)}, bf16[8,2560]{1,0:T(8,128)(2,1)S(1)}, u32[]{:S(2)}, u32[]{:S(2)}) collective-permute-start(bf16[8,2560]{1,0:T(8,128)(2,1)S(1)} %get-tuple-element.46.refs_0_), channel_id=1, source_target_pairs={{0,4},{1,5},{2,6},{3,7},{4,0},{5,1},{6,2},{7,3},{8,12},{9,13},{10,... | collective-permute-start | bytes 122888 | tf_op jit(solution)/shard_map/ppermute | solution.py:36
  33.4 4.9 %collective-permute-start.14 = (bf16[8,2560]{1,0:T(8,128)(2,1)S(1)}, bf16[8,2560]{1,0:T(8,128)(2,1)S(1)}, u32[]{:S(2)}, u32[]{:S(2)}) collective-permute-start(bf16[8,2560]{1,0:T(8,128)(2,1)S(1)} %get-tuple-element.46.refs_0_), channel_id=1, source_target_pairs={{0,2},{1,3},{2,0},{3,1},{4,6},{5,7},{6,4},{7,5},{8,10},{9,11},{10,... | collective-permute-start | bytes 122888 | tf_op jit(solution)/shard_map/ppermute | solution.py:36
  39.7 5.5 %collective-permute-start.16 = (bf16[8,640]{1,0:T(8,128)(2,1)S(1)}, bf16[8,640]{1,0:T(8,128)(2,1)S(1)}, u32[]{:S(2)}, u32[]{:S(2)}) collective-permute-start(bf16[8,640]{1,0:T(8,128)(2,1)S(1)} %sep_rows.17), channel_id=1, source_target_pairs={{0,6},{1,7},{2,4},{3,5},{4,2},{5,3},{6,0},{7,1},{8,14},{9,15},{10,... | collective-permute-start | bytes 30728 | tf_op jit(solution)/shard_map/ppermute | solution.py:36
  41.9 4.6 %collective-permute-start.17 = (bf16[8,640]{1,0:T(8,128)(2,1)S(1)}, bf16[8,640]{1,0:T(8,128)(2,1)S(1)}, u32[]{:S(2)}, u32[]{:S(2)}) collective-permute-start(bf16[8,640]{1,0:T(8,128)(2,1)S(1)} %sep_rows.17), channel_id=1, source_target_pairs={{0,4},{1,5},{2,6},{3,7},{4,0},{5,1},{6,2},{7,3},{8,12},{9,13},{10,... | collective-permute-start | bytes 30728 | tf_op jit(solution)/shard_map/ppermute | solution.py:36
  50.5 6.1 %collective-permute-start.21 = (bf16[8,2560]{1,0:T(8,128)(2,1)S(1)}, bf16[8,2560]{1,0:T(8,128)(2,1)S(1)}, u32[]{:S(2)}, u32[]{:S(2)}) collective-permute-start(bf16[8,2560]{1,0:T(8,128)(2,1)S(1)} %folded_sums.5.refs_0_), channel_id=1, source_target_pairs={{0,6},{1,7},{2,4},{3,5},{4,2},{5,3},{6,0},{7,1},{8,14},{9,15},{10,... | collective-permute-start | bytes 122888 | tf_op jit(solution)/shard_map/ppermute | solution.py:36
  52.3 5.7 %collective-permute-start.22 = (bf16[8,2560]{1,0:T(8,128)(2,1)S(1)}, bf16[8,2560]{1,0:T(8,128)(2,1)S(1)}, u32[]{:S(2)}, u32[]{:S(2)}) collective-permute-start(bf16[8,2560]{1,0:T(8,128)(2,1)S(1)} %folded_sums.5.refs_0_), channel_id=1, source_target_pairs={{0,4},{1,5},{2,6},{3,7},{4,0},{5,1},{6,2},{7,3},{8,12},{9,13},{10,... | collective-permute-start | bytes 122888 | tf_op jit(solution)/shard_map/ppermute | solution.py:36
  53.4 4.6 %collective-permute-start.23 = (bf16[8,2560]{1,0:T(8,128)(2,1)S(1)}, bf16[8,2560]{1,0:T(8,128)(2,1)S(1)}, u32[]{:S(2)}, u32[]{:S(2)}) collective-permute-start(bf16[8,2560]{1,0:T(8,128)(2,1)S(1)} %folded_sums.5.refs_0_), channel_id=1, source_target_pairs={{0,2},{1,3},{2,0},{3,1},{4,6},{5,7},{6,4},{7,5},{8,10},{9,11},{10,... | collective-permute-start | bytes 122888 | tf_op jit(solution)/shard_map/ppermute | solution.py:36
  59.3 5.5 %collective-permute-start.25 = (bf16[8,640]{1,0:T(8,128)(2,1)S(1)}, bf16[8,640]{1,0:T(8,128)(2,1)S(1)}, u32[]{:S(2)}, u32[]{:S(2)}) collective-permute-start(bf16[8,640]{1,0:T(8,128)(2,1)S(1)} %sep_rows.19), channel_id=1, source_target_pairs={{0,6},{1,7},{2,4},{3,5},{4,2},{5,3},{6,0},{7,1},{8,14},{9,15},{10,... | collective-permute-start | bytes 30728 | tf_op jit(solution)/shard_map/ppermute | solution.py:36
  61.4 4.6 %collective-permute-start.26 = (bf16[8,640]{1,0:T(8,128)(2,1)S(1)}, bf16[8,640]{1,0:T(8,128)(2,1)S(1)}, u32[]{:S(2)}, u32[]{:S(2)}) collective-permute-start(bf16[8,640]{1,0:T(8,128)(2,1)S(1)} %sep_rows.19), channel_id=1, source_target_pairs={{0,4},{1,5},{2,6},{3,7},{4,0},{5,1},{6,2},{7,3},{8,12},{9,13},{10,... | collective-permute-start | bytes 30728 | tf_op jit(solution)/shard_map/ppermute | solution.py:36
  61.6 4.3 %collective-permute-start.27 = (bf16[8,640]{1,0:T(8,128)(2,1)S(1)}, bf16[8,640]{1,0:T(8,128)(2,1)S(1)}, u32[]{:S(2)}, u32[]{:S(2)}) collective-permute-start(bf16[8,640]{1,0:T(8,128)(2,1)S(1)} %sep_rows.19), channel_id=1, source_target_pairs={{0,2},{1,3},{2,0},{3,1},{4,6},{5,7},{6,4},{7,5},{8,10},{9,11},{10,... | collective-permute-start | bytes 30728 | tf_op jit(solution)/shard_map/ppermute | solution.py:36
  66.0 4.8 %collective-permute-start.28 = (f32[8,256]{1,0:T(8,128)S(1)}, f32[8,256]{1,0:T(8,128)S(1)}, u32[]{:S(2)}, u32[]{:S(2)}) collective-permute-start(f32[8,256]{1,0:T(8,128)S(1)} %get-tuple-element.55._), channel_id=1, source_target_pairs={{16,24},{17,25},{18,26},{19,27},{20,28},{21,29},{22,30},{23,31},{2... | collective-permute-start | bytes 24584 | tf_op jit(solution)/shard_map/ppermute | solution.py:58
  71.6 6.0 %collective-permute-start.30 = (bf16[8,2560]{1,0:T(8,128)(2,1)S(1)}, bf16[8,2560]{1,0:T(8,128)(2,1)S(1)}, u32[]{:S(2)}, u32[]{:S(2)}) collective-permute-start(bf16[8,2560]{1,0:T(8,128)(2,1)S(1)} %folded_sums.6.refs_0_), channel_id=1, source_target_pairs={{0,6},{1,7},{2,4},{3,5},{4,2},{5,3},{6,0},{7,1},{8,14},{9,15},{10,... | collective-permute-start | bytes 122888 | tf_op jit(solution)/shard_map/ppermute | solution.py:36
  73.2 6.0 %collective-permute-start.31 = (bf16[8,2560]{1,0:T(8,128)(2,1)S(1)}, bf16[8,2560]{1,0:T(8,128)(2,1)S(1)}, u32[]{:S(2)}, u32[]{:S(2)}) collective-permute-start(bf16[8,2560]{1,0:T(8,128)(2,1)S(1)} %folded_sums.6.refs_0_), channel_id=1, source_target_pairs={{0,4},{1,5},{2,6},{3,7},{4,0},{5,1},{6,2},{7,3},{8,12},{9,13},{10,... | collective-permute-start | bytes 122888 | tf_op jit(solution)/shard_map/ppermute | solution.py:36
  74.3 4.9 %collective-permute-start.32 = (bf16[8,2560]{1,0:T(8,128)(2,1)S(1)}, bf16[8,2560]{1,0:T(8,128)(2,1)S(1)}, u32[]{:S(2)}, u32[]{:S(2)}) collective-permute-start(bf16[8,2560]{1,0:T(8,128)(2,1)S(1)} %folded_sums.6.refs_0_), channel_id=1, source_target_pairs={{0,2},{1,3},{2,0},{3,1},{4,6},{5,7},{6,4},{7,5},{8,10},{9,11},{10,... | collective-permute-start | bytes 122888 | tf_op jit(solution)/shard_map/ppermute | solution.py:36
  80.5 5.5 %collective-permute-start.34 = (bf16[8,640]{1,0:T(8,128)(2,1)S(1)}, bf16[8,640]{1,0:T(8,128)(2,1)S(1)}, u32[]{:S(2)}, u32[]{:S(2)}) collective-permute-start(bf16[8,640]{1,0:T(8,128)(2,1)S(1)} %sep_rows.21), channel_id=1, source_target_pairs={{0,6},{1,7},{2,4},{3,5},{4,2},{5,3},{6,0},{7,1},{8,14},{9,15},{10,... | collective-permute-start | bytes 30728 | tf_op jit(solution)/shard_map/ppermute | solution.py:36
  82.6 4.6 %collective-permute-start.35 = (bf16[8,640]{1,0:T(8,128)(2,1)S(1)}, bf16[8,640]{1,0:T(8,128)(2,1)S(1)}, u32[]{:S(2)}, u32[]{:S(2)}) collective-permute-start(bf16[8,640]{1,0:T(8,128)(2,1)S(1)} %sep_rows.21), channel_id=1, source_target_pairs={{0,4},{1,5},{2,6},{3,7},{4,0},{5,1},{6,2},{7,3},{8,12},{9,13},{10,... | collective-permute-start | bytes 30728 | tf_op jit(solution)/shard_map/ppermute | solution.py:36
  82.7 4.5 %collective-permute-start.36 = (bf16[8,640]{1,0:T(8,128)(2,1)S(1)}, bf16[8,640]{1,0:T(8,128)(2,1)S(1)}, u32[]{:S(2)}, u32[]{:S(2)}) collective-permute-start(bf16[8,640]{1,0:T(8,128)(2,1)S(1)} %sep_rows.21), channel_id=1, source_target_pairs={{0,2},{1,3},{2,0},{3,1},{4,6},{5,7},{6,4},{7,5},{8,10},{9,11},{10,... | collective-permute-start | bytes 30728 | tf_op jit(solution)/shard_map/ppermute | solution.py:36
  87.2 4.3 %collective-permute-start.37 = (f32[8,256]{1,0:T(8,128)S(1)}, f32[8,256]{1,0:T(8,128)S(1)}, u32[]{:S(2)}, u32[]{:S(2)}) collective-permute-start(f32[8,256]{1,0:T(8,128)S(1)} %get-tuple-element.58), channel_id=1, source_target_pairs={{24,16},{25,17},{26,18},{27,19},{28,20},{29,21},{30,22},{31,23},{1... | collective-permute-start | bytes 24584 | tf_op jit(solution)/shard_map/ppermute | solution.py:58
  92.7 6.1 %collective-permute-start.39 = (bf16[8,2560]{1,0:T(8,128)(2,1)S(1)}, bf16[8,2560]{1,0:T(8,128)(2,1)S(1)}, u32[]{:S(2)}, u32[]{:S(2)}) collective-permute-start(bf16[8,2560]{1,0:T(8,128)(2,1)S(1)} %folded_sums.7.refs_0_), channel_id=1, source_target_pairs={{0,6},{1,7},{2,4},{3,5},{4,2},{5,3},{6,0},{7,1},{8,14},{9,15},{10,... | collective-permute-start | bytes 122888 | tf_op jit(solution)/shard_map/ppermute | solution.py:36
  94.2 5.8 %collective-permute-start.40 = (bf16[8,2560]{1,0:T(8,128)(2,1)S(1)}, bf16[8,2560]{1,0:T(8,128)(2,1)S(1)}, u32[]{:S(2)}, u32[]{:S(2)}) collective-permute-start(bf16[8,2560]{1,0:T(8,128)(2,1)S(1)} %folded_sums.7.refs_0_), channel_id=1, source_target_pairs={{0,4},{1,5},{2,6},{3,7},{4,0},{5,1},{6,2},{7,3},{8,12},{9,13},{10,... | collective-permute-start | bytes 122888 | tf_op jit(solution)/shard_map/ppermute | solution.py:36
  95.2 4.8 %collective-permute-start.41 = (bf16[8,2560]{1,0:T(8,128)(2,1)S(1)}, bf16[8,2560]{1,0:T(8,128)(2,1)S(1)}, u32[]{:S(2)}, u32[]{:S(2)}) collective-permute-start(bf16[8,2560]{1,0:T(8,128)(2,1)S(1)} %folded_sums.7.refs_0_), channel_id=1, source_target_pairs={{0,2},{1,3},{2,0},{3,1},{4,6},{5,7},{6,4},{7,5},{8,10},{9,11},{10,... | collective-permute-start | bytes 122888 | tf_op jit(solution)/shard_map/ppermute | solution.py:36
  101.3 5.6 %collective-permute-start.43 = (bf16[8,640]{1,0:T(8,128)(2,1)S(1)}, bf16[8,640]{1,0:T(8,128)(2,1)S(1)}, u32[]{:S(2)}, u32[]{:S(2)}) collective-permute-start(bf16[8,640]{1,0:T(8,128)(2,1)S(1)} %sep_rows.23), channel_id=1, source_target_pairs={{0,6},{1,7},{2,4},{3,5},{4,2},{5,3},{6,0},{7,1},{8,14},{9,15},{10,... | collective-permute-start | bytes 30728 | tf_op jit(solution)/shard_map/ppermute | solution.py:36
  103.7 4.6 %collective-permute-start.44 = (bf16[8,640]{1,0:T(8,128)(2,1)S(1)}, bf16[8,640]{1,0:T(8,128)(2,1)S(1)}, u32[]{:S(2)}, u32[]{:S(2)}) collective-permute-start(bf16[8,640]{1,0:T(8,128)(2,1)S(1)} %sep_rows.23), channel_id=1, source_target_pairs={{0,4},{1,5},{2,6},{3,7},{4,0},{5,1},{6,2},{7,3},{8,12},{9,13},{10,... | collective-permute-start | bytes 30728 | tf_op jit(solution)/shard_map/ppermute | solution.py:36
  103.8 4.4 %collective-permute-start.45 = (bf16[8,640]{1,0:T(8,128)(2,1)S(1)}, bf16[8,640]{1,0:T(8,128)(2,1)S(1)}, u32[]{:S(2)}, u32[]{:S(2)}) collective-permute-start(bf16[8,640]{1,0:T(8,128)(2,1)S(1)} %sep_rows.23), channel_id=1, source_target_pairs={{0,2},{1,3},{2,0},{3,1},{4,6},{5,7},{6,4},{7,5},{8,10},{9,11},{10,... | collective-permute-start | bytes 30728 | tf_op jit(solution)/shard_map/ppermute | solution.py:36
  112.7 6.1 %collective-permute-start.49 = (bf16[8,2560]{1,0:T(8,128)(2,1)S(1)}, bf16[8,2560]{1,0:T(8,128)(2,1)S(1)}, u32[]{:S(2)}, u32[]{:S(2)}) collective-permute-start(bf16[8,2560]{1,0:T(8,128)(2,1)S(1)} %folded_sums.8.refs_0_), channel_id=1, source_target_pairs={{0,6},{1,7},{2,4},{3,5},{4,2},{5,3},{6,0},{7,1},{8,14},{9,15},{10,... | collective-permute-start | bytes 122888 | tf_op jit(solution)/shard_map/ppermute | solution.py:36
  114.4 6.0 %collective-permute-start.50 = (bf16[8,2560]{1,0:T(8,128)(2,1)S(1)}, bf16[8,2560]{1,0:T(8,128)(2,1)S(1)}, u32[]{:S(2)}, u32[]{:S(2)}) collective-permute-start(bf16[8,2560]{1,0:T(8,128)(2,1)S(1)} %folded_sums.8.refs_0_), channel_id=1, source_target_pairs={{0,4},{1,5},{2,6},{3,7},{4,0},{5,1},{6,2},{7,3},{8,12},{9,13},{10,... | collective-permute-start | bytes 122888 | tf_op jit(solution)/shard_map/ppermute | solution.py:36
  115.5 5.0 %collective-permute-start.51 = (bf16[8,2560]{1,0:T(8,128)(2,1)S(1)}, bf16[8,2560]{1,0:T(8,128)(2,1)S(1)}, u32[]{:S(2)}, u32[]{:S(2)}) collective-permute-start(bf16[8,2560]{1,0:T(8,128)(2,1)S(1)} %folded_sums.8.refs_0_), channel_id=1, source_target_pairs={{0,2},{1,3},{2,0},{3,1},{4,6},{5,7},{6,4},{7,5},{8,10},{9,11},{10,... | collective-permute-start | bytes 122888 | tf_op jit(solution)/shard_map/ppermute | solution.py:36
  121.7 5.5 %collective-permute-start.53 = (bf16[8,640]{1,0:T(8,128)(2,1)S(1)}, bf16[8,640]{1,0:T(8,128)(2,1)S(1)}, u32[]{:S(2)}, u32[]{:S(2)}) collective-permute-start(bf16[8,640]{1,0:T(8,128)(2,1)S(1)} %sep_rows.25), channel_id=1, source_target_pairs={{0,6},{1,7},{2,4},{3,5},{4,2},{5,3},{6,0},{7,1},{8,14},{9,15},{10,... | collective-permute-start | bytes 30728 | tf_op jit(solution)/shard_map/ppermute | solution.py:36
  123.8 4.6 %collective-permute-start.54 = (bf16[8,640]{1,0:T(8,128)(2,1)S(1)}, bf16[8,640]{1,0:T(8,128)(2,1)S(1)}, u32[]{:S(2)}, u32[]{:S(2)}) collective-permute-start(bf16[8,640]{1,0:T(8,128)(2,1)S(1)} %sep_rows.25), channel_id=1, source_target_pairs={{0,4},{1,5},{2,6},{3,7},{4,0},{5,1},{6,2},{7,3},{8,12},{9,13},{10,... | collective-permute-start | bytes 30728 | tf_op jit(solution)/shard_map/ppermute | solution.py:36
  123.9 4.5 %collective-permute-start.55 = (bf16[8,640]{1,0:T(8,128)(2,1)S(1)}, bf16[8,640]{1,0:T(8,128)(2,1)S(1)}, u32[]{:S(2)}, u32[]{:S(2)}) collective-permute-start(bf16[8,640]{1,0:T(8,128)(2,1)S(1)} %sep_rows.25), channel_id=1, source_target_pairs={{0,2},{1,3},{2,0},{3,1},{4,6},{5,7},{6,4},{7,5},{8,10},{9,11},{10,... | collective-permute-start | bytes 30728 | tf_op jit(solution)/shard_map/ppermute | solution.py:36
  128.4 5.0 %collective-permute-start.56 = (f32[8,256]{1,0:T(8,128)S(1)}, f32[8,256]{1,0:T(8,128)S(1)}, u32[]{:S(2)}, u32[]{:S(2)}) collective-permute-start(f32[8,256]{1,0:T(8,128)S(1)} %get-tuple-element.64), channel_id=1, source_target_pairs={{8,0},{9,1},{10,2},{11,3},{12,4},{13,5},{14,6},{15,7},{0,16},{1,17... | collective-permute-start | bytes 24584 | tf_op jit(solution)/shard_map/ppermute | solution.py:58
  133.9 6.3 %collective-permute-start.58 = (bf16[8,2560]{1,0:T(8,128)(2,1)S(1)}, bf16[8,2560]{1,0:T(8,128)(2,1)S(1)}, u32[]{:S(2)}, u32[]{:S(2)}) collective-permute-start(bf16[8,2560]{1,0:T(8,128)(2,1)S(1)} %folded_sums.9.refs_0_), channel_id=1, source_target_pairs={{0,6},{1,7},{2,4},{3,5},{4,2},{5,3},{6,0},{7,1},{8,14},{9,15},{10,... | collective-permute-start | bytes 122888 | tf_op jit(solution)/shard_map/ppermute | solution.py:36
  135.4 5.6 %collective-permute-start.59 = (bf16[8,2560]{1,0:T(8,128)(2,1)S(1)}, bf16[8,2560]{1,0:T(8,128)(2,1)S(1)}, u32[]{:S(2)}, u32[]{:S(2)}) collective-permute-start(bf16[8,2560]{1,0:T(8,128)(2,1)S(1)} %folded_sums.9.refs_0_), channel_id=1, source_target_pairs={{0,4},{1,5},{2,6},{3,7},{4,0},{5,1},{6,2},{7,3},{8,12},{9,13},{10,... | collective-permute-start | bytes 122888 | tf_op jit(solution)/shard_map/ppermute | solution.py:36
  136.4 4.6 %collective-permute-start.60 = (bf16[8,2560]{1,0:T(8,128)(2,1)S(1)}, bf16[8,2560]{1,0:T(8,128)(2,1)S(1)}, u32[]{:S(2)}, u32[]{:S(2)}) collective-permute-start(bf16[8,2560]{1,0:T(8,128)(2,1)S(1)} %folded_sums.9.refs_0_), channel_id=1, source_target_pairs={{0,2},{1,3},{2,0},{3,1},{4,6},{5,7},{6,4},{7,5},{8,10},{9,11},{10,... | collective-permute-start | bytes 122888 | tf_op jit(solution)/shard_map/ppermute | solution.py:36
  143.3 5.5 %collective-permute-start.62 = (bf16[8,640]{1,0:T(8,128)(2,1)S(1)}, bf16[8,640]{1,0:T(8,128)(2,1)S(1)}, u32[]{:S(2)}, u32[]{:S(2)}) collective-permute-start(bf16[8,640]{1,0:T(8,128)(2,1)S(1)} %sep_rows.27), channel_id=1, source_target_pairs={{0,6},{1,7},{2,4},{3,5},{4,2},{5,3},{6,0},{7,1},{8,14},{9,15},{10,... | collective-permute-start | bytes 30728 | tf_op jit(solution)/shard_map/ppermute | solution.py:36
  145.8 4.6 %collective-permute-start.63 = (bf16[8,640]{1,0:T(8,128)(2,1)S(1)}, bf16[8,640]{1,0:T(8,128)(2,1)S(1)}, u32[]{:S(2)}, u32[]{:S(2)}) collective-permute-start(bf16[8,640]{1,0:T(8,128)(2,1)S(1)} %sep_rows.27), channel_id=1, source_target_pairs={{0,4},{1,5},{2,6},{3,7},{4,0},{5,1},{6,2},{7,3},{8,12},{9,13},{10,... | collective-permute-start | bytes 30728 | tf_op jit(solution)/shard_map/ppermute | solution.py:36
  146.1 4.3 %collective-permute-start.64 = (bf16[8,640]{1,0:T(8,128)(2,1)S(1)}, bf16[8,640]{1,0:T(8,128)(2,1)S(1)}, u32[]{:S(2)}, u32[]{:S(2)}) collective-permute-start(bf16[8,640]{1,0:T(8,128)(2,1)S(1)} %sep_rows.27), channel_id=1, source_target_pairs={{0,2},{1,3},{2,0},{3,1},{4,6},{5,7},{6,4},{7,5},{8,10},{9,11},{10,... | collective-permute-start | bytes 30728 | tf_op jit(solution)/shard_map/ppermute | solution.py:36
  (19 other events, 46.3 us)

commit v9 on v8

--- a/solution.py
+++ b/solution.py
@@ -277,27 +277,21 @@
     )(*parts, in_vmem(after))
 
 
-def first_leaf_and_gather(sources, gather, maps):
+def first_leaf_and_gather(sources, leaf, gather):
     cells = gather.shape[2]
     half = gather.shape[1] // 2
-    starts = [sum(block.shape[2] for block in maps[:index]) for index in range(len(maps))]
-    width = sum(block.shape[2] for block in maps)
-
-    def kernel(*refs):
-        sources_hbm, gather_hbm, *maps_hbm = refs[: 2 + len(maps)]
-        keep, give, gather_ref, maps_ref, sources_ref, done = refs[2 + len(maps) :]
+
+    def kernel(*refs):
+        sources_hbm, leaf_hbm, gather_hbm, keep, give, gather_ref = refs[:6]
+        sources_ref, leaf_ref, done = refs[6:]
         core = lax.axis_index("front") % 2
         layer = lax.axis_index("layer")
         sides = [pl.ds(pl.multiple_of(side * half, half), half) for side in (1 - core, core)]
-        leaf_at = pl.ds(starts[1], cells)
         values_at, sources_at = pl.ds(half, cells), pl.ds(half + cells, cells)
-        pieces = [(sources_hbm, sources_ref), (maps_hbm[1], maps_ref.at[:, :, leaf_at])]
+        pieces = [(sources_hbm, sources_ref), (leaf_hbm, leaf_ref)]
         for rows in sides:
             for part in range(2):
                 pieces.append((gather_hbm.at[part, rows], gather_ref.at[part, rows]))
-        for index in (0, 2, 3):
-            columns = pl.ds(starts[index], maps[index].shape[2])
-            pieces.append((maps_hbm[index], maps_ref.at[:, :, columns]))
         copies = [
             pltpu.make_async_copy(source, target, done.at[index])
             for index, (source, target) in enumerate(pieces)
@@ -312,7 +306,7 @@
 
         @pl.when(layer == 0)
         def _():
-            leaf_values = times(source, maps_ref[0, :, leaf_at], maps_ref[1, :, leaf_at], 1)
+            leaf_values = times(source, leaf_ref[0], leaf_ref[1], 1)
             for out in (give, keep):
                 out[:, values_at] = leaf_values
 
@@ -327,24 +321,52 @@
                     leaf_values, gather_ref[0, rows, :], gather_ref[1, rows, :], 1
                 )
 
-        for copy in copies[6:]:
-            copy.wait()
-
-    return pl.pallas_call(
-        kernel,
-        in_specs=[ANY] * (2 + len(maps)),
-        out_specs=[VMEM] * 4,
+    return pl.pallas_call(
+        kernel,
+        in_specs=[ANY] * 3,
+        out_specs=[VMEM] * 3,
         out_shape=[
             jax.ShapeDtypeStruct((8, half + 2 * cells), F32),
             jax.ShapeDtypeStruct((8, half + 2 * cells), F32),
             pltpu.VMEM(gather.shape, BF16),
-            pltpu.VMEM((2, cells, width), BF16),
         ],
-        scratch_shapes=[pltpu.VMEM(sources.shape, F32), pltpu.SemaphoreType.DMA((9,))],
+        scratch_shapes=[
+            pltpu.VMEM(sources.shape, F32),
+            pltpu.VMEM(leaf.shape, BF16),
+            pltpu.SemaphoreType.DMA((6,)),
+        ],
         compiler_params=params(16),
         cost_estimate=cost(16 * gather.size, 2 * gather.size),
         name="first_leaf_and_gather",
-    )(in_hbm(sources), in_hbm(gather), *[in_hbm(block) for block in maps])
+    )(in_hbm(sources), in_hbm(leaf), in_hbm(gather))
+
+
+def load_maps(maps, after):
+    widths = [block.shape[2] for block in maps]
+
+    def kernel(*refs):
+        out, done = refs[-2:]
+        copies = []
+        for index, width in enumerate(widths):
+            columns = pl.ds(sum(widths[:index]), width)
+            copies.append(
+                pltpu.make_async_copy(refs[index], out.at[:, :, columns], done.at[index])
+            )
+        for copy in copies:
+            copy.start()
+        for copy in copies:
+            copy.wait()
+
+    return pl.pallas_call(
+        kernel,
+        in_specs=[ANY] * (len(maps) + 1),
+        out_specs=VMEM,
+        out_shape=pltpu.VMEM((*maps[0].shape[:2], sum(widths)), BF16),
+        scratch_shapes=[pltpu.SemaphoreType.DMA((len(maps),))],
+        compiler_params=params(16),
+        cost_estimate=cost(0, 4 * maps[0].size),
+        name="load_maps",
+    )(*[in_hbm(block) for block in maps], after)
 
 
 def leaf_and_gather(level, blocks, gather, arrived, sources=None):
@@ -637,8 +659,9 @@
     rows = sep_inverse.shape[2]
 
     maps = [sep_spread[0], leaf_inverse[0], couple_above[0], couple_below[0]]
-    keep, give, own_gather, own_maps = first_leaf_and_gather(right_sides[0], sep_gather[0], maps)
+    keep, give, own_gather = first_leaf_and_gather(right_sides[0], leaf_inverse[0], sep_gather[0])
     got = pair(give)
+    own_maps = load_maps(maps, give)
     half = sep_gather.shape[2] // 2
     first_sums = (keep[:, :half] + got[:, :half]).astype(BF16)
     first_values, sources = (

time: 153 us -> 153 us (level)
    pallas_call x1 -> x2, Pallas kernels: 2.67 us -> 4.08 us  [the longest x1 2.3 us: first_leaf_and_gather(): pl.pallas_call(kernel, in_specs=[ANY] * 3, out_specs=[VMEM] * 3, out_shap...]
  transfers between devices with their start and end apart: 66 -> 66, of which waited for: 44 -> 43; matrix products, arithmetic and copies ran while one was open for 0% -> 0% of each run, Pallas kernels for 9% -> 10%
where the time goes in v9:
time: 153 us
  starting transfers between devices  75.9 us (50%)
  waiting for transfers between devices  56.7 us (37%)
  Pallas kernels  19.9 us (13%)
    ppermute x42, starting transfers between devices, from_chips(): lax.ppermute(block, 'front', xor_route('front', 2 * (chips - step)))  62.5 us
    ppermute x42, waiting for transfers between devices, from_chips(): lax.ppermute(block, 'front', xor_route('front', 2 * (chips - step)))  33.2 us
    ppermute x12, waiting for transfers between devices, hop(): lax.ppermute(block, ('layer', 'front'), [(i * slots + j, target[i] * slot...  14.7 us
    ppermute x12, starting transfers between devices, hop(): lax.ppermute(block, ('layer', 'front'), [(i * slots + j, target[i] * slot...  11.6 us
    ppermute x12, waiting for transfers between devices, pair(): return lax.ppermute(block, 'front', xor_route('front', 1))  8.69 us
    pallas_call x1, Pallas kernels, transpose_sep(): pl.pallas_call(kernel, in_specs=[ANY, ANY], out_specs=VMEM, out_shape=plt...  5.35 us
    pallas_call x14, Pallas kernels, sep_rows(): pl.pallas_call(kernel, in_specs=[VMEM] * (len(given) + 1), out_specs=VMEM...  3.91 us
  transfers between devices with their start and end apart: 66, of which 43 were waited for; matrix products, arithmetic and copies ran while one was open for 0% of the time, Pallas kernels for 10%

profile of v9, /device:TPU:0, one launch (start us, length us, event | category | flops | bytes accessed | tf_op | source)
XLA Modules:
  0.0 152.8 jit_solution(14669645603639740099)
XLA Ops:
  0.0 2.3 %first_leaf_and_gather.1 = (f32[8,2816]{1,0:T(8,128)S(1)}, f32[8,2816]{1,0:T(8,128)S(1)}, bf16[2,5120,128]{2,1,0:T(8,128)(2,1)S(1)}) custom-call(f32[2,4,128]{2,1,0:T(4,128)} %bitcast.16, bf16[2,128,128]{2,1,0:T(8,128)(2,1)} %bitcast.12, bf16[2,5120,128]{2,1,0:T(8,128)(2,1)} %bitcast.10), custom_call_target="tpu_custom_call" | custom-call | flops 20971520 | bytes 2621440 | tf_op jit(solution)/shard_map/first_leaf_and_gather/pallas_call | solution.py:324
  2.8 1.8 %load_maps.1.refs_1_ = bf16[2,128,5504]{2,1,0:T(8,128)(2,1)S(1)} custom-call(bf16[2,128,5120]{2,1,0:T(8,128)(2,1)} %bitcast.11, bf16[2,128,128]{2,1,0:T(8,128)(2,1)} %bitcast.13, bf16[2,128,128]{2,1,0:T(8,128)(2,1)} %bitcast.14, bf16[2,128,128]{2,1,0:T(8,128)(2,1)} %bitcast.15, f32[8,2816]{1,0:T(8,128)S(1)} %get-tuple-element.37.refs_4_), custom_call_target="tpu_custom_call" | custom-call | bytes 5242880 | tf_op jit(solution)/shard_map/load_maps/pallas_call | solution.py:360
  5.2 4.7 %collective-permute-start.1 = (bf16[8,2560]{1,0:T(8,128)(2,1)S(1)}, bf16[8,2560]{1,0:T(8,128)(2,1)S(1)}, u32[]{:S(2)}, u32[]{:S(2)}) collective-permute-start(bf16[8,2560]{1,0:T(8,128)(2,1)S(1)} %fusion._.refs_0_.refs_2_), channel_id=1, source_target_pairs={{0,6},{1,7},{2,4},{3,5},{4,2},{5,3},{6,0},{7,1},{8,14},{9,15},{10,... | collective-permute-start | bytes 122888 | tf_op jit(solution)/shard_map/ppermute | solution.py:36
  10.5 5.3 %transpose_sep.1.refs_4_.refs_1_.refs_2_ = bf16[2,5120,640]{2,1,0:T(8,128)(2,1)S(1)} custom-call(bf16[2,640,5120]{2,1,0:T(8,128)(2,1)} %bitcast.9, bf16[8,2560]{1,0:T(8,128)(2,1)S(1)} %fusion._.refs_0_.refs_2_), custom_call_target="tpu_custom_call" | custom-call | bytes 26214400 | tf_op jit(solution)/shard_map/transpose_sep/pallas_call | solution.py:127
  18.1 3.9 %collective-permute-start.5 = (bf16[8,640]{1,0:T(8,128)(2,1)S(1)}, bf16[8,640]{1,0:T(8,128)(2,1)S(1)}, u32[]{:S(2)}, u32[]{:S(2)}) collective-permute-start(bf16[8,640]{1,0:T(8,128)(2,1)S(1)} %sep_rows.15._.refs_0_), channel_id=1, source_target_pairs={{0,6},{1,7},{2,4},{3,5},{4,2},{5,3},{6,0},{7,1},{8,14},{9,15},{10,... | collective-permute-start | bytes 30728 | tf_op jit(solution)/shard_map/ppermute | solution.py:36
  24.0 2.6 %collective-permute-done.6.refs_2_ = bf16[8,640]{1,0:T(8,128)(2,1)S(1)} collective-permute-done((bf16[8,640]{1,0:T(8,128)(2,1)S(1)}, bf16[8,640]{1,0:T(8,128)(2,1)S(1)}, u32[]{:S(2)}, u32[]{:S(2)}) %collective-permute-start.6) | collective-permute-done | bytes 10272 | tf_op jit(solution)/shard_map/ppermute | solution.py:36
  27.9 3.2 %collective-permute-done.10.refs_1_ = f32[8,256]{1,0:T(8,128)S(1)} collective-permute-done((f32[8,256]{1,0:T(8,128)S(1)}, f32[8,256]{1,0:T(8,128)S(1)}, u32[]{:S(2)}, u32[]{:S(2)}) %collective-permute-start.10) | collective-permute-done | bytes 8224 | tf_op jit(solution)/shard_map/ppermute | solution.py:58
  31.7 1.4 collective-permute-start.12
  33.7 2.4 %collective-permute-start.14 = (bf16[8,2560]{1,0:T(8,128)(2,1)S(1)}, bf16[8,2560]{1,0:T(8,128)(2,1)S(1)}, u32[]{:S(2)}, u32[]{:S(2)}) collective-permute-start(bf16[8,2560]{1,0:T(8,128)(2,1)S(1)} %get-tuple-element.44.refs_0_), channel_id=1, source_target_pairs={{0,2},{1,3},{2,0},{3,1},{4,6},{5,7},{6,4},{7,5},{8,10},{9,11},{10,... | collective-permute-start | bytes 122888 | tf_op jit(solution)/shard_map/ppermute | solution.py:36
  36.0 1.9 %collective-permute-done.12.refs_1_ = bf16[8,2560]{1,0:T(8,128)(2,1)S(1)} collective-permute-done((bf16[8,2560]{1,0:T(8,128)(2,1)S(1)}, bf16[8,2560]{1,0:T(8,128)(2,1)S(1)}, u32[]{:S(2)}, u32[]{:S(2)}) %collective-permute-start.12) | collective-permute-done | bytes 40992 | tf_op jit(solution)/shard_map/ppermute | solution.py:36
  39.9 2.2 %collective-permute-start.16 = (bf16[8,640]{1,0:T(8,128)(2,1)S(1)}, bf16[8,640]{1,0:T(8,128)(2,1)S(1)}, u32[]{:S(2)}, u32[]{:S(2)}) collective-permute-start(bf16[8,640]{1,0:T(8,128)(2,1)S(1)} %sep_rows.17), channel_id=1, source_target_pairs={{0,6},{1,7},{2,4},{3,5},{4,2},{5,3},{6,0},{7,1},{8,14},{9,15},{10,... | collective-permute-start | bytes 30728 | tf_op jit(solution)/shard_map/ppermute | solution.py:36
  42.8 1.5 collective-permute-start.18
  48.2 2.3 %collective-permute-done.19.refs_0_ = f32[8,256]{1,0:T(8,128)S(1)} collective-permute-done((f32[8,256]{1,0:T(8,128)S(1)}, f32[8,256]{1,0:T(8,128)S(1)}, u32[]{:S(2)}, u32[]{:S(2)}) %collective-permute-start.19) | collective-permute-done | bytes 8224 | tf_op jit(solution)/shard_map/ppermute | solution.py:58
  50.7 1.8 %collective-permute-start.21 = (bf16[8,2560]{1,0:T(8,128)(2,1)S(1)}, bf16[8,2560]{1,0:T(8,128)(2,1)S(1)}, u32[]{:S(2)}, u32[]{:S(2)}) collective-permute-start(bf16[8,2560]{1,0:T(8,128)(2,1)S(1)} %folded_sums.5.refs_0_), channel_id=1, source_target_pairs={{0,6},{1,7},{2,4},{3,5},{4,2},{5,3},{6,0},{7,1},{8,14},{9,15},{10,... | collective-permute-start | bytes 122888 | tf_op jit(solution)/shard_map/ppermute | solution.py:36
  53.6 1.5 collective-permute-start.23
  55.1 1.8 %collective-permute-done.21.refs_1_ = bf16[8,2560]{1,0:T(8,128)(2,1)S(1)} collective-permute-done((bf16[8,2560]{1,0:T(8,128)(2,1)S(1)}, bf16[8,2560]{1,0:T(8,128)(2,1)S(1)}, u32[]{:S(2)}, u32[]{:S(2)}) %collective-permute-start.21) | collective-permute-done | bytes 40992 | tf_op jit(solution)/shard_map/ppermute | solution.py:36
  56.9 1.4 collective-permute-done.22.refs_2_
  59.6 1.8 %collective-permute-start.25 = (bf16[8,640]{1,0:T(8,128)(2,1)S(1)}, bf16[8,640]{1,0:T(8,128)(2,1)S(1)}, u32[]{:S(2)}, u32[]{:S(2)}) collective-permute-start(bf16[8,640]{1,0:T(8,128)(2,1)S(1)} %sep_rows.19), channel_id=1, source_target_pairs={{0,6},{1,7},{2,4},{3,5},{4,2},{5,3},{6,0},{7,1},{8,14},{9,15},{10,... | collective-permute-start | bytes 30728 | tf_op jit(solution)/shard_map/ppermute | solution.py:36
  61.9 2.1 %collective-permute-start.27 = (bf16[8,640]{1,0:T(8,128)(2,1)S(1)}, bf16[8,640]{1,0:T(8,128)(2,1)S(1)}, u32[]{:S(2)}, u32[]{:S(2)}) collective-permute-start(bf16[8,640]{1,0:T(8,128)(2,1)S(1)} %sep_rows.19), channel_id=1, source_target_pairs={{0,2},{1,3},{2,0},{3,1},{4,6},{5,7},{6,4},{7,5},{8,10},{9,11},{10,... | collective-permute-start | bytes 30728 | tf_op jit(solution)/shard_map/ppermute | solution.py:36
  66.0 1.7 %collective-permute-start.28 = (f32[8,256]{1,0:T(8,128)S(1)}, f32[8,256]{1,0:T(8,128)S(1)}, u32[]{:S(2)}, u32[]{:S(2)}) collective-permute-start(f32[8,256]{1,0:T(8,128)S(1)} %get-tuple-element.53._), channel_id=1, source_target_pairs={{16,24},{17,25},{18,26},{19,27},{20,28},{21,29},{22,30},{23,31},{2... | collective-permute-start | bytes 24584 | tf_op jit(solution)/shard_map/ppermute | solution.py:58
  67.7 1.9 %collective-permute-start.29 = (f32[8,256]{1,0:T(8,128)S(1)}, f32[8,256]{1,0:T(8,128)S(1)}, u32[]{:S(2)}, u32[]{:S(2)}) collective-permute-start(f32[8,256]{1,0:T(8,128)S(1)} %get-tuple-element.53._), channel_id=1, source_target_pairs={{16,25},{17,24},{18,27},{19,26},{20,29},{21,28},{22,31},{23,30},{2... | collective-permute-start | bytes 24584 | tf_op jit(solution)/shard_map/ppermute | solution.py:58
  71.7 1.5 collective-permute-start.30
  74.2 1.9 %collective-permute-start.32 = (bf16[8,2560]{1,0:T(8,128)(2,1)S(1)}, bf16[8,2560]{1,0:T(8,128)(2,1)S(1)}, u32[]{:S(2)}, u32[]{:S(2)}) collective-permute-start(bf16[8,2560]{1,0:T(8,128)(2,1)S(1)} %folded_sums.6.refs_0_), channel_id=1, source_target_pairs={{0,2},{1,3},{2,0},{3,1},{4,6},{5,7},{6,4},{7,5},{8,10},{9,11},{10,... | collective-permute-start | bytes 122888 | tf_op jit(solution)/shard_map/ppermute | solution.py:36
  76.1 1.7 %collective-permute-done.30.refs_1_ = bf16[8,2560]{1,0:T(8,128)(2,1)S(1)} collective-permute-done((bf16[8,2560]{1,0:T(8,128)(2,1)S(1)}, bf16[8,2560]{1,0:T(8,128)(2,1)S(1)}, u32[]{:S(2)}, u32[]{:S(2)}) %collective-permute-start.30) | collective-permute-done | bytes 40992 | tf_op jit(solution)/shard_map/ppermute | solution.py:36
  77.8 1.6 %collective-permute-done.31.refs_2_ = bf16[8,2560]{1,0:T(8,128)(2,1)S(1)} collective-permute-done((bf16[8,2560]{1,0:T(8,128)(2,1)S(1)}, bf16[8,2560]{1,0:T(8,128)(2,1)S(1)}, u32[]{:S(2)}, u32[]{:S(2)}) %collective-permute-start.31) | collective-permute-done | bytes 40992 | tf_op jit(solution)/shard_map/ppermute | solution.py:36
  80.7 2.1 %collective-permute-start.34 = (bf16[8,640]{1,0:T(8,128)(2,1)S(1)}, bf16[8,640]{1,0:T(8,128)(2,1)S(1)}, u32[]{:S(2)}, u32[]{:S(2)}) collective-permute-start(bf16[8,640]{1,0:T(8,128)(2,1)S(1)} %sep_rows.21), channel_id=1, source_target_pairs={{0,6},{1,7},{2,4},{3,5},{4,2},{5,3},{6,0},{7,1},{8,14},{9,15},{10,... | collective-permute-start | bytes 30728 | tf_op jit(solution)/shard_map/ppermute | solution.py:36
  82.9 2.2 %collective-permute-start.36 = (bf16[8,640]{1,0:T(8,128)(2,1)S(1)}, bf16[8,640]{1,0:T(8,128)(2,1)S(1)}, u32[]{:S(2)}, u32[]{:S(2)}) collective-permute-start(bf16[8,640]{1,0:T(8,128)(2,1)S(1)} %sep_rows.21), channel_id=1, source_target_pairs={{0,2},{1,3},{2,0},{3,1},{4,6},{5,7},{6,4},{7,5},{8,10},{9,11},{10,... | collective-permute-start | bytes 30728 | tf_op jit(solution)/shard_map/ppermute | solution.py:36
  87.5 2.4 %collective-permute-start.37 = (f32[8,256]{1,0:T(8,128)S(1)}, f32[8,256]{1,0:T(8,128)S(1)}, u32[]{:S(2)}, u32[]{:S(2)}) collective-permute-start(f32[8,256]{1,0:T(8,128)S(1)} %get-tuple-element.56), channel_id=1, source_target_pairs={{24,16},{25,17},{26,18},{27,19},{28,20},{29,21},{30,22},{31,23},{1... | collective-permute-start | bytes 24584 | tf_op jit(solution)/shard_map/ppermute | solution.py:58
  89.8 1.9 %folded.3.refs_2_ = bf16[2,256,2560]{2,1,0:T(8,128)(2,1)S(1)} custom-call(bf16[2,3,2,128,128]{4,3,2,1,0:T(8,128)(2,1)S(1)} %get-tuple-element.42.refs_3_.blocks_ref.refs_2_, bf16[2,256,2560]{2,1,0:T(8,128)(2,1)S(1)} %transpose_gather.1.refs_4_.gather_ref, f32[8,256]{1,0:T(8,128)S(1)} %get-tuple-element.53._), custom_call_target="tpu_custom_call" | custom-call | flops 1342177280 | bytes 5242880 | tf_op jit(solution)/shard_map/folded/pallas_call | solution.py:444
  92.9 1.6 %collective-permute-start.39 = (bf16[8,2560]{1,0:T(8,128)(2,1)S(1)}, bf16[8,2560]{1,0:T(8,128)(2,1)S(1)}, u32[]{:S(2)}, u32[]{:S(2)}) collective-permute-start(bf16[8,2560]{1,0:T(8,128)(2,1)S(1)} %folded_sums.7.refs_0_), channel_id=1, source_target_pairs={{0,6},{1,7},{2,4},{3,5},{4,2},{5,3},{6,0},{7,1},{8,14},{9,15},{10,... | collective-permute-start | bytes 122888 | tf_op jit(solution)/shard_map/ppermute | solution.py:36
  95.4 1.9 %collective-permute-start.41 = (bf16[8,2560]{1,0:T(8,128)(2,1)S(1)}, bf16[8,2560]{1,0:T(8,128)(2,1)S(1)}, u32[]{:S(2)}, u32[]{:S(2)}) collective-permute-start(bf16[8,2560]{1,0:T(8,128)(2,1)S(1)} %folded_sums.7.refs_0_), channel_id=1, source_target_pairs={{0,2},{1,3},{2,0},{3,1},{4,6},{5,7},{6,4},{7,5},{8,10},{9,11},{10,... | collective-permute-start | bytes 122888 | tf_op jit(solution)/shard_map/ppermute | solution.py:36
  97.3 1.7 %collective-permute-done.39.refs_1_ = bf16[8,2560]{1,0:T(8,128)(2,1)S(1)} collective-permute-done((bf16[8,2560]{1,0:T(8,128)(2,1)S(1)}, bf16[8,2560]{1,0:T(8,128)(2,1)S(1)}, u32[]{:S(2)}, u32[]{:S(2)}) %collective-permute-start.39) | collective-permute-done | bytes 40992 | tf_op jit(solution)/shard_map/ppermute | solution.py:36
  101.6 2.4 %collective-permute-start.43 = (bf16[8,640]{1,0:T(8,128)(2,1)S(1)}, bf16[8,640]{1,0:T(8,128)(2,1)S(1)}, u32[]{:S(2)}, u32[]{:S(2)}) collective-permute-start(bf16[8,640]{1,0:T(8,128)(2,1)S(1)} %sep_rows.23), channel_id=1, source_target_pairs={{0,6},{1,7},{2,4},{3,5},{4,2},{5,3},{6,0},{7,1},{8,14},{9,15},{10,... | collective-permute-start | bytes 30728 | tf_op jit(solution)/shard_map/ppermute | solution.py:36
  104.1 1.9 %collective-permute-start.45 = (bf16[8,640]{1,0:T(8,128)(2,1)S(1)}, bf16[8,640]{1,0:T(8,128)(2,1)S(1)}, u32[]{:S(2)}, u32[]{:S(2)}) collective-permute-start(bf16[8,640]{1,0:T(8,128)(2,1)S(1)} %sep_rows.23), channel_id=1, source_target_pairs={{0,2},{1,3},{2,0},{3,1},{4,6},{5,7},{6,4},{7,5},{8,10},{9,11},{10,... | collective-permute-start | bytes 30728 | tf_op jit(solution)/shard_map/ppermute | solution.py:36
  112.9 1.7 %collective-permute-start.49 = (bf16[8,2560]{1,0:T(8,128)(2,1)S(1)}, bf16[8,2560]{1,0:T(8,128)(2,1)S(1)}, u32[]{:S(2)}, u32[]{:S(2)}) collective-permute-start(bf16[8,2560]{1,0:T(8,128)(2,1)S(1)} %folded_sums.8.refs_0_), channel_id=1, source_target_pairs={{0,6},{1,7},{2,4},{3,5},{4,2},{5,3},{6,0},{7,1},{8,14},{9,15},{10,... | collective-permute-start | bytes 122888 | tf_op jit(solution)/shard_map/ppermute | solution.py:36
  115.7 1.7 %collective-permute-start.51 = (bf16[8,2560]{1,0:T(8,128)(2,1)S(1)}, bf16[8,2560]{1,0:T(8,128)(2,1)S(1)}, u32[]{:S(2)}, u32[]{:S(2)}) collective-permute-start(bf16[8,2560]{1,0:T(8,128)(2,1)S(1)} %folded_sums.8.refs_0_), channel_id=1, source_target_pairs={{0,2},{1,3},{2,0},{3,1},{4,6},{5,7},{6,4},{7,5},{8,10},{9,11},{10,... | collective-permute-start | bytes 122888 | tf_op jit(solution)/shard_map/ppermute | solution.py:36
  117.4 1.7 %collective-permute-done.49.refs_1_ = bf16[8,2560]{1,0:T(8,128)(2,1)S(1)} collective-permute-done((bf16[8,2560]{1,0:T(8,128)(2,1)S(1)}, bf16[8,2560]{1,0:T(8,128)(2,1)S(1)}, u32[]{:S(2)}, u32[]{:S(2)}) %collective-permute-start.49) | collective-permute-done | bytes 40992 | tf_op jit(solution)/shard_map/ppermute | solution.py:36
  119.0 1.6 %collective-permute-done.50.refs_2_ = bf16[8,2560]{1,0:T(8,128)(2,1)S(1)} collective-permute-done((bf16[8,2560]{1,0:T(8,128)(2,1)S(1)}, bf16[8,2560]{1,0:T(8,128)(2,1)S(1)}, u32[]{:S(2)}, u32[]{:S(2)}) %collective-permute-start.50) | collective-permute-done | bytes 40992 | tf_op jit(solution)/shard_map/ppermute | solution.py:36
  122.0 2.1 %collective-permute-start.53 = (bf16[8,640]{1,0:T(8,128)(2,1)S(1)}, bf16[8,640]{1,0:T(8,128)(2,1)S(1)}, u32[]{:S(2)}, u32[]{:S(2)}) collective-permute-start(bf16[8,640]{1,0:T(8,128)(2,1)S(1)} %sep_rows.25), channel_id=1, source_target_pairs={{0,6},{1,7},{2,4},{3,5},{4,2},{5,3},{6,0},{7,1},{8,14},{9,15},{10,... | collective-permute-start | bytes 30728 | tf_op jit(solution)/shard_map/ppermute | solution.py:36
  124.1 2.2 %collective-permute-start.55 = (bf16[8,640]{1,0:T(8,128)(2,1)S(1)}, bf16[8,640]{1,0:T(8,128)(2,1)S(1)}, u32[]{:S(2)}, u32[]{:S(2)}) collective-permute-start(bf16[8,640]{1,0:T(8,128)(2,1)S(1)} %sep_rows.25), channel_id=1, source_target_pairs={{0,2},{1,3},{2,0},{3,1},{4,6},{5,7},{6,4},{7,5},{8,10},{9,11},{10,... | collective-permute-start | bytes 30728 | tf_op jit(solution)/shard_map/ppermute | solution.py:36
  128.7 1.8 %collective-permute-start.56 = (f32[8,256]{1,0:T(8,128)S(1)}, f32[8,256]{1,0:T(8,128)S(1)}, u32[]{:S(2)}, u32[]{:S(2)}) collective-permute-start(f32[8,256]{1,0:T(8,128)S(1)} %get-tuple-element.62), channel_id=1, source_target_pairs={{8,0},{9,1},{10,2},{11,3},{12,4},{13,5},{14,6},{15,7},{0,16},{1,17... | collective-permute-start | bytes 24584 | tf_op jit(solution)/shard_map/ppermute | solution.py:58
  130.5 3.1 %collective-permute-done.56.refs_0_ = f32[8,256]{1,0:T(8,128)S(1)} collective-permute-done((f32[8,256]{1,0:T(8,128)S(1)}, f32[8,256]{1,0:T(8,128)S(1)}, u32[]{:S(2)}, u32[]{:S(2)}) %collective-permute-start.56) | collective-permute-done | bytes 8224 | tf_op jit(solution)/shard_map/ppermute | solution.py:58
  134.1 1.5 collective-permute-start.58
  136.6 1.9 %collective-permute-start.60 = (bf16[8,2560]{1,0:T(8,128)(2,1)S(1)}, bf16[8,2560]{1,0:T(8,128)(2,1)S(1)}, u32[]{:S(2)}, u32[]{:S(2)}) collective-permute-start(bf16[8,2560]{1,0:T(8,128)(2,1)S(1)} %folded_sums.9.refs_0_), channel_id=1, source_target_pairs={{0,2},{1,3},{2,0},{3,1},{4,6},{5,7},{6,4},{7,5},{8,10},{9,11},{10,... | collective-permute-start | bytes 122888 | tf_op jit(solution)/shard_map/ppermute | solution.py:36
  138.8 1.6 %collective-permute-done.58.refs_1_ = bf16[8,2560]{1,0:T(8,128)(2,1)S(1)} collective-permute-done((bf16[8,2560]{1,0:T(8,128)(2,1)S(1)}, bf16[8,2560]{1,0:T(8,128)(2,1)S(1)}, u32[]{:S(2)}, u32[]{:S(2)}) %collective-permute-start.58) | collective-permute-done | bytes 40992 | tf_op jit(solution)/shard_map/ppermute | solution.py:36
  143.5 2.5 %collective-permute-start.62 = (bf16[8,640]{1,0:T(8,128)(2,1)S(1)}, bf16[8,640]{1,0:T(8,128)(2,1)S(1)}, u32[]{:S(2)}, u32[]{:S(2)}) collective-permute-start(bf16[8,640]{1,0:T(8,128)(2,1)S(1)} %sep_rows.27), channel_id=1, source_target_pairs={{0,6},{1,7},{2,4},{3,5},{4,2},{5,3},{6,0},{7,1},{8,14},{9,15},{10,... | collective-permute-start | bytes 30728 | tf_op jit(solution)/shard_map/ppermute | solution.py:36
  146.3 1.7 %collective-permute-start.64 = (bf16[8,640]{1,0:T(8,128)(2,1)S(1)}, bf16[8,640]{1,0:T(8,128)(2,1)S(1)}, u32[]{:S(2)}, u32[]{:S(2)}) collective-permute-start(bf16[8,640]{1,0:T(8,128)(2,1)S(1)} %sep_rows.27), channel_id=1, source_target_pairs={{0,2},{1,3},{2,0},{3,1},{4,6},{5,7},{6,4},{7,5},{8,10},{9,11},{10,... | collective-permute-start | bytes 30728 | tf_op jit(solution)/shard_map/ppermute | solution.py:36
  149.1 1.5 collective-permute-done.63
  (148 shorter events, 52.0 us)
Async XLA Ops:
  4.7 18.0 %collective-permute-start.8 = (bf16[2,128,5504]{2,1,0:T(8,128)(2,1)S(1)}, bf16[2,128,5504]{2,1,0:T(8,128)(2,1)S(1)}, u32[]{:S(2)}, u32[]{:S(2)}) collective-permute-start(bf16[2,128,5504]{2,1,0:T(8,128)(2,1)S(1)} %get-tuple-element.39.own_ref), channel_id=1, source_target_pairs={{0,1},{1,0},{2,3},{3,2},{4,5},{5,4},{6,7},{7,6},{8,9},{9,8},{10,11... | collective-permute-start | bytes 8454152 | tf_op jit(solution)/shard_map/ppermute | solution.py:21
  4.8 22.3 %collective-permute-start.11 = (bf16[2,5120,128]{2,1,0:T(8,128)(2,1)S(1)}, bf16[2,5120,128]{2,1,0:T(8,128)(2,1)S(1)}, u32[]{:S(2)}, u32[]{:S(2)}) collective-permute-start(bf16[2,5120,128]{2,1,0:T(8,128)(2,1)S(1)} %get-tuple-element.43.own_ref), channel_id=1, source_target_pairs={{0,1},{1,0},{2,3},{3,2},{4,5},{5,4},{6,7},{7,6},{8,9},{9,8},{10,11... | collective-permute-start | bytes 7864328 | tf_op jit(solution)/shard_map/ppermute | solution.py:21
  5.2 10.6 %collective-permute-start.1 = (bf16[8,2560]{1,0:T(8,128)(2,1)S(1)}, bf16[8,2560]{1,0:T(8,128)(2,1)S(1)}, u32[]{:S(2)}, u32[]{:S(2)}) collective-permute-start(bf16[8,2560]{1,0:T(8,128)(2,1)S(1)} %fusion._.refs_0_.refs_2_), channel_id=1, source_target_pairs={{0,6},{1,7},{2,4},{3,5},{4,2},{5,3},{6,0},{7,1},{8,14},{9,15},{10,... | collective-permute-start | bytes 122888 | tf_op jit(solution)/shard_map/ppermute | solution.py:36
  9.9 5.9 %collective-permute-start.2 = (bf16[8,2560]{1,0:T(8,128)(2,1)S(1)}, bf16[8,2560]{1,0:T(8,128)(2,1)S(1)}, u32[]{:S(2)}, u32[]{:S(2)}) collective-permute-start(bf16[8,2560]{1,0:T(8,128)(2,1)S(1)} %fusion._.refs_0_.refs_2_), channel_id=1, source_target_pairs={{0,4},{1,5},{2,6},{3,7},{4,0},{5,1},{6,2},{7,3},{8,12},{9,13},{10,... | collective-permute-start | bytes 122888 | tf_op jit(solution)/shard_map/ppermute | solution.py:36
  9.9 5.9 %collective-permute-start.3 = (bf16[8,2560]{1,0:T(8,128)(2,1)S(1)}, bf16[8,2560]{1,0:T(8,128)(2,1)S(1)}, u32[]{:S(2)}, u32[]{:S(2)}) collective-permute-start(bf16[8,2560]{1,0:T(8,128)(2,1)S(1)} %fusion._.refs_0_.refs_2_), channel_id=1, source_target_pairs={{0,2},{1,3},{2,0},{3,1},{4,6},{5,7},{6,4},{7,5},{8,10},{9,11},{10,... | collective-permute-start | bytes 122888 | tf_op jit(solution)/shard_map/ppermute | solution.py:36
  18.1 5.8 %collective-permute-start.5 = (bf16[8,640]{1,0:T(8,128)(2,1)S(1)}, bf16[8,640]{1,0:T(8,128)(2,1)S(1)}, u32[]{:S(2)}, u32[]{:S(2)}) collective-permute-start(bf16[8,640]{1,0:T(8,128)(2,1)S(1)} %sep_rows.15._.refs_0_), channel_id=1, source_target_pairs={{0,6},{1,7},{2,4},{3,5},{4,2},{5,3},{6,0},{7,1},{8,14},{9,15},{10,... | collective-permute-start | bytes 30728 | tf_op jit(solution)/shard_map/ppermute | solution.py:36
  22.0 4.6 %collective-permute-start.6 = (bf16[8,640]{1,0:T(8,128)(2,1)S(1)}, bf16[8,640]{1,0:T(8,128)(2,1)S(1)}, u32[]{:S(2)}, u32[]{:S(2)}) collective-permute-start(bf16[8,640]{1,0:T(8,128)(2,1)S(1)} %sep_rows.15._.refs_0_), channel_id=1, source_target_pairs={{0,4},{1,5},{2,6},{3,7},{4,0},{5,1},{6,2},{7,3},{8,12},{9,13},{10,... | collective-permute-start | bytes 30728 | tf_op jit(solution)/shard_map/ppermute | solution.py:36
  22.0 4.6 %collective-permute-start.7 = (bf16[8,640]{1,0:T(8,128)(2,1)S(1)}, bf16[8,640]{1,0:T(8,128)(2,1)S(1)}, u32[]{:S(2)}, u32[]{:S(2)}) collective-permute-start(bf16[8,640]{1,0:T(8,128)(2,1)S(1)} %sep_rows.15._.refs_0_), channel_id=1, source_target_pairs={{0,2},{1,3},{2,0},{3,1},{4,6},{5,7},{6,4},{7,5},{8,10},{9,11},{10,... | collective-permute-start | bytes 30728 | tf_op jit(solution)/shard_map/ppermute | solution.py:36
  27.1 4.0 %collective-permute-start.10 = (f32[8,256]{1,0:T(8,128)S(1)}, f32[8,256]{1,0:T(8,128)S(1)}, u32[]{:S(2)}, u32[]{:S(2)}) collective-permute-start(f32[8,256]{1,0:T(8,128)S(1)} %get-tuple-element.41._), channel_id=1, source_target_pairs={{0,9},{1,8},{2,11},{3,10},{4,13},{5,12},{6,15},{7,14},{8,17},{9,16... | collective-permute-start | bytes 24584 | tf_op jit(solution)/shard_map/ppermute | solution.py:58
  27.1 4.6 %collective-permute-start.9 = (f32[8,256]{1,0:T(8,128)S(1)}, f32[8,256]{1,0:T(8,128)S(1)}, u32[]{:S(2)}, u32[]{:S(2)}) collective-permute-start(f32[8,256]{1,0:T(8,128)S(1)} %get-tuple-element.41._), channel_id=1, source_target_pairs={{0,8},{1,9},{2,10},{3,11},{4,12},{5,13},{6,14},{7,15},{8,16},{9,17... | collective-permute-start | bytes 24584 | tf_op jit(solution)/shard_map/ppermute | solution.py:58
  31.7 6.3 %collective-permute-start.12 = (bf16[8,2560]{1,0:T(8,128)(2,1)S(1)}, bf16[8,2560]{1,0:T(8,128)(2,1)S(1)}, u32[]{:S(2)}, u32[]{:S(2)}) collective-permute-start(bf16[8,2560]{1,0:T(8,128)(2,1)S(1)} %get-tuple-element.44.refs_0_), channel_id=1, source_target_pairs={{0,6},{1,7},{2,4},{3,5},{4,2},{5,3},{6,0},{7,1},{8,14},{9,15},{10,... | collective-permute-start | bytes 122888 | tf_op jit(solution)/shard_map/ppermute | solution.py:36
  33.1 5.5 %collective-permute-start.13 = (bf16[8,2560]{1,0:T(8,128)(2,1)S(1)}, bf16[8,2560]{1,0:T(8,128)(2,1)S(1)}, u32[]{:S(2)}, u32[]{:S(2)}) collective-permute-start(bf16[8,2560]{1,0:T(8,128)(2,1)S(1)} %get-tuple-element.44.refs_0_), channel_id=1, source_target_pairs={{0,4},{1,5},{2,6},{3,7},{4,0},{5,1},{6,2},{7,3},{8,12},{9,13},{10,... | collective-permute-start | bytes 122888 | tf_op jit(solution)/shard_map/ppermute | solution.py:36
  33.7 4.9 %collective-permute-start.14 = (bf16[8,2560]{1,0:T(8,128)(2,1)S(1)}, bf16[8,2560]{1,0:T(8,128)(2,1)S(1)}, u32[]{:S(2)}, u32[]{:S(2)}) collective-permute-start(bf16[8,2560]{1,0:T(8,128)(2,1)S(1)} %get-tuple-element.44.refs_0_), channel_id=1, source_target_pairs={{0,2},{1,3},{2,0},{3,1},{4,6},{5,7},{6,4},{7,5},{8,10},{9,11},{10,... | collective-permute-start | bytes 122888 | tf_op jit(solution)/shard_map/ppermute | solution.py:36
  39.9 5.5 %collective-permute-start.16 = (bf16[8,640]{1,0:T(8,128)(2,1)S(1)}, bf16[8,640]{1,0:T(8,128)(2,1)S(1)}, u32[]{:S(2)}, u32[]{:S(2)}) collective-permute-start(bf16[8,640]{1,0:T(8,128)(2,1)S(1)} %sep_rows.17), channel_id=1, source_target_pairs={{0,6},{1,7},{2,4},{3,5},{4,2},{5,3},{6,0},{7,1},{8,14},{9,15},{10,... | collective-permute-start | bytes 30728 | tf_op jit(solution)/shard_map/ppermute | solution.py:36
  42.1 4.6 %collective-permute-start.17 = (bf16[8,640]{1,0:T(8,128)(2,1)S(1)}, bf16[8,640]{1,0:T(8,128)(2,1)S(1)}, u32[]{:S(2)}, u32[]{:S(2)}) collective-permute-start(bf16[8,640]{1,0:T(8,128)(2,1)S(1)} %sep_rows.17), channel_id=1, source_target_pairs={{0,4},{1,5},{2,6},{3,7},{4,0},{5,1},{6,2},{7,3},{8,12},{9,13},{10,... | collective-permute-start | bytes 30728 | tf_op jit(solution)/shard_map/ppermute | solution.py:36
  50.7 6.2 %collective-permute-start.21 = (bf16[8,2560]{1,0:T(8,128)(2,1)S(1)}, bf16[8,2560]{1,0:T(8,128)(2,1)S(1)}, u32[]{:S(2)}, u32[]{:S(2)}) collective-permute-start(bf16[8,2560]{1,0:T(8,128)(2,1)S(1)} %folded_sums.5.refs_0_), channel_id=1, source_target_pairs={{0,6},{1,7},{2,4},{3,5},{4,2},{5,3},{6,0},{7,1},{8,14},{9,15},{10,... | collective-permute-start | bytes 122888 | tf_op jit(solution)/shard_map/ppermute | solution.py:36
  52.5 5.7 %collective-permute-start.22 = (bf16[8,2560]{1,0:T(8,128)(2,1)S(1)}, bf16[8,2560]{1,0:T(8,128)(2,1)S(1)}, u32[]{:S(2)}, u32[]{:S(2)}) collective-permute-start(bf16[8,2560]{1,0:T(8,128)(2,1)S(1)} %folded_sums.5.refs_0_), channel_id=1, source_target_pairs={{0,4},{1,5},{2,6},{3,7},{4,0},{5,1},{6,2},{7,3},{8,12},{9,13},{10,... | collective-permute-start | bytes 122888 | tf_op jit(solution)/shard_map/ppermute | solution.py:36
  53.6 4.6 %collective-permute-start.23 = (bf16[8,2560]{1,0:T(8,128)(2,1)S(1)}, bf16[8,2560]{1,0:T(8,128)(2,1)S(1)}, u32[]{:S(2)}, u32[]{:S(2)}) collective-permute-start(bf16[8,2560]{1,0:T(8,128)(2,1)S(1)} %folded_sums.5.refs_0_), channel_id=1, source_target_pairs={{0,2},{1,3},{2,0},{3,1},{4,6},{5,7},{6,4},{7,5},{8,10},{9,11},{10,... | collective-permute-start | bytes 122888 | tf_op jit(solution)/shard_map/ppermute | solution.py:36
  59.6 5.5 %collective-permute-start.25 = (bf16[8,640]{1,0:T(8,128)(2,1)S(1)}, bf16[8,640]{1,0:T(8,128)(2,1)S(1)}, u32[]{:S(2)}, u32[]{:S(2)}) collective-permute-start(bf16[8,640]{1,0:T(8,128)(2,1)S(1)} %sep_rows.19), channel_id=1, source_target_pairs={{0,6},{1,7},{2,4},{3,5},{4,2},{5,3},{6,0},{7,1},{8,14},{9,15},{10,... | collective-permute-start | bytes 30728 | tf_op jit(solution)/shard_map/ppermute | solution.py:36
  61.4 4.6 %collective-permute-start.26 = (bf16[8,640]{1,0:T(8,128)(2,1)S(1)}, bf16[8,640]{1,0:T(8,128)(2,1)S(1)}, u32[]{:S(2)}, u32[]{:S(2)}) collective-permute-start(bf16[8,640]{1,0:T(8,128)(2,1)S(1)} %sep_rows.19), channel_id=1, source_target_pairs={{0,4},{1,5},{2,6},{3,7},{4,0},{5,1},{6,2},{7,3},{8,12},{9,13},{10,... | collective-permute-start | bytes 30728 | tf_op jit(solution)/shard_map/ppermute | solution.py:36
  61.9 4.1 %collective-permute-start.27 = (bf16[8,640]{1,0:T(8,128)(2,1)S(1)}, bf16[8,640]{1,0:T(8,128)(2,1)S(1)}, u32[]{:S(2)}, u32[]{:S(2)}) collective-permute-start(bf16[8,640]{1,0:T(8,128)(2,1)S(1)} %sep_rows.19), channel_id=1, source_target_pairs={{0,2},{1,3},{2,0},{3,1},{4,6},{5,7},{6,4},{7,5},{8,10},{9,11},{10,... | collective-permute-start | bytes 30728 | tf_op jit(solution)/shard_map/ppermute | solution.py:36
  66.0 4.8 %collective-permute-start.28 = (f32[8,256]{1,0:T(8,128)S(1)}, f32[8,256]{1,0:T(8,128)S(1)}, u32[]{:S(2)}, u32[]{:S(2)}) collective-permute-start(f32[8,256]{1,0:T(8,128)S(1)} %get-tuple-element.53._), channel_id=1, source_target_pairs={{16,24},{17,25},{18,26},{19,27},{20,28},{21,29},{22,30},{23,31},{2... | collective-permute-start | bytes 24584 | tf_op jit(solution)/shard_map/ppermute | solution.py:58
  71.7 6.1 %collective-permute-start.30 = (bf16[8,2560]{1,0:T(8,128)(2,1)S(1)}, bf16[8,2560]{1,0:T(8,128)(2,1)S(1)}, u32[]{:S(2)}, u32[]{:S(2)}) collective-permute-start(bf16[8,2560]{1,0:T(8,128)(2,1)S(1)} %folded_sums.6.refs_0_), channel_id=1, source_target_pairs={{0,6},{1,7},{2,4},{3,5},{4,2},{5,3},{6,0},{7,1},{8,14},{9,15},{10,... | collective-permute-start | bytes 122888 | tf_op jit(solution)/shard_map/ppermute | solution.py:36
  73.2 6.2 %collective-permute-start.31 = (bf16[8,2560]{1,0:T(8,128)(2,1)S(1)}, bf16[8,2560]{1,0:T(8,128)(2,1)S(1)}, u32[]{:S(2)}, u32[]{:S(2)}) collective-permute-start(bf16[8,2560]{1,0:T(8,128)(2,1)S(1)} %folded_sums.6.refs_0_), channel_id=1, source_target_pairs={{0,4},{1,5},{2,6},{3,7},{4,0},{5,1},{6,2},{7,3},{8,12},{9,13},{10,... | collective-permute-start | bytes 122888 | tf_op jit(solution)/shard_map/ppermute | solution.py:36
  74.2 5.2 %collective-permute-start.32 = (bf16[8,2560]{1,0:T(8,128)(2,1)S(1)}, bf16[8,2560]{1,0:T(8,128)(2,1)S(1)}, u32[]{:S(2)}, u32[]{:S(2)}) collective-permute-start(bf16[8,2560]{1,0:T(8,128)(2,1)S(1)} %folded_sums.6.refs_0_), channel_id=1, source_target_pairs={{0,2},{1,3},{2,0},{3,1},{4,6},{5,7},{6,4},{7,5},{8,10},{9,11},{10,... | collective-permute-start | bytes 122888 | tf_op jit(solution)/shard_map/ppermute | solution.py:36
  80.7 5.5 %collective-permute-start.34 = (bf16[8,640]{1,0:T(8,128)(2,1)S(1)}, bf16[8,640]{1,0:T(8,128)(2,1)S(1)}, u32[]{:S(2)}, u32[]{:S(2)}) collective-permute-start(bf16[8,640]{1,0:T(8,128)(2,1)S(1)} %sep_rows.21), channel_id=1, source_target_pairs={{0,6},{1,7},{2,4},{3,5},{4,2},{5,3},{6,0},{7,1},{8,14},{9,15},{10,... | collective-permute-start | bytes 30728 | tf_op jit(solution)/shard_map/ppermute | solution.py:36
  82.8 4.6 %collective-permute-start.35 = (bf16[8,640]{1,0:T(8,128)(2,1)S(1)}, bf16[8,640]{1,0:T(8,128)(2,1)S(1)}, u32[]{:S(2)}, u32[]{:S(2)}) collective-permute-start(bf16[8,640]{1,0:T(8,128)(2,1)S(1)} %sep_rows.21), channel_id=1, source_target_pairs={{0,4},{1,5},{2,6},{3,7},{4,0},{5,1},{6,2},{7,3},{8,12},{9,13},{10,... | collective-permute-start | bytes 30728 | tf_op jit(solution)/shard_map/ppermute | solution.py:36
  82.9 4.5 %collective-permute-start.36 = (bf16[8,640]{1,0:T(8,128)(2,1)S(1)}, bf16[8,640]{1,0:T(8,128)(2,1)S(1)}, u32[]{:S(2)}, u32[]{:S(2)}) collective-permute-start(bf16[8,640]{1,0:T(8,128)(2,1)S(1)} %sep_rows.21), channel_id=1, source_target_pairs={{0,2},{1,3},{2,0},{3,1},{4,6},{5,7},{6,4},{7,5},{8,10},{9,11},{10,... | collective-permute-start | bytes 30728 | tf_op jit(solution)/shard_map/ppermute | solution.py:36
  87.5 4.3 %collective-permute-start.37 = (f32[8,256]{1,0:T(8,128)S(1)}, f32[8,256]{1,0:T(8,128)S(1)}, u32[]{:S(2)}, u32[]{:S(2)}) collective-permute-start(f32[8,256]{1,0:T(8,128)S(1)} %get-tuple-element.56), channel_id=1, source_target_pairs={{24,16},{25,17},{26,18},{27,19},{28,20},{29,21},{30,22},{31,23},{1... | collective-permute-start | bytes 24584 | tf_op jit(solution)/shard_map/ppermute | solution.py:58
  92.9 6.1 %collective-permute-start.39 = (bf16[8,2560]{1,0:T(8,128)(2,1)S(1)}, bf16[8,2560]{1,0:T(8,128)(2,1)S(1)}, u32[]{:S(2)}, u32[]{:S(2)}) collective-permute-start(bf16[8,2560]{1,0:T(8,128)(2,1)S(1)} %folded_sums.7.refs_0_), channel_id=1, source_target_pairs={{0,6},{1,7},{2,4},{3,5},{4,2},{5,3},{6,0},{7,1},{8,14},{9,15},{10,... | collective-permute-start | bytes 122888 | tf_op jit(solution)/shard_map/ppermute | solution.py:36
  94.5 5.8 %collective-permute-start.40 = (bf16[8,2560]{1,0:T(8,128)(2,1)S(1)}, bf16[8,2560]{1,0:T(8,128)(2,1)S(1)}, u32[]{:S(2)}, u32[]{:S(2)}) collective-permute-start(bf16[8,2560]{1,0:T(8,128)(2,1)S(1)} %folded_sums.7.refs_0_), channel_id=1, source_target_pairs={{0,4},{1,5},{2,6},{3,7},{4,0},{5,1},{6,2},{7,3},{8,12},{9,13},{10,... | collective-permute-start | bytes 122888 | tf_op jit(solution)/shard_map/ppermute | solution.py:36
  95.4 4.8 %collective-permute-start.41 = (bf16[8,2560]{1,0:T(8,128)(2,1)S(1)}, bf16[8,2560]{1,0:T(8,128)(2,1)S(1)}, u32[]{:S(2)}, u32[]{:S(2)}) collective-permute-start(bf16[8,2560]{1,0:T(8,128)(2,1)S(1)} %folded_sums.7.refs_0_), channel_id=1, source_target_pairs={{0,2},{1,3},{2,0},{3,1},{4,6},{5,7},{6,4},{7,5},{8,10},{9,11},{10,... | collective-permute-start | bytes 122888 | tf_op jit(solution)/shard_map/ppermute | solution.py:36
  101.6 5.6 %collective-permute-start.43 = (bf16[8,640]{1,0:T(8,128)(2,1)S(1)}, bf16[8,640]{1,0:T(8,128)(2,1)S(1)}, u32[]{:S(2)}, u32[]{:S(2)}) collective-permute-start(bf16[8,640]{1,0:T(8,128)(2,1)S(1)} %sep_rows.23), channel_id=1, source_target_pairs={{0,6},{1,7},{2,4},{3,5},{4,2},{5,3},{6,0},{7,1},{8,14},{9,15},{10,... | collective-permute-start | bytes 30728 | tf_op jit(solution)/shard_map/ppermute | solution.py:36
  103.9 4.6 %collective-permute-start.44 = (bf16[8,640]{1,0:T(8,128)(2,1)S(1)}, bf16[8,640]{1,0:T(8,128)(2,1)S(1)}, u32[]{:S(2)}, u32[]{:S(2)}) collective-permute-start(bf16[8,640]{1,0:T(8,128)(2,1)S(1)} %sep_rows.23), channel_id=1, source_target_pairs={{0,4},{1,5},{2,6},{3,7},{4,0},{5,1},{6,2},{7,3},{8,12},{9,13},{10,... | collective-permute-start | bytes 30728 | tf_op jit(solution)/shard_map/ppermute | solution.py:36
  104.1 4.4 %collective-permute-start.45 = (bf16[8,640]{1,0:T(8,128)(2,1)S(1)}, bf16[8,640]{1,0:T(8,128)(2,1)S(1)}, u32[]{:S(2)}, u32[]{:S(2)}) collective-permute-start(bf16[8,640]{1,0:T(8,128)(2,1)S(1)} %sep_rows.23), channel_id=1, source_target_pairs={{0,2},{1,3},{2,0},{3,1},{4,6},{5,7},{6,4},{7,5},{8,10},{9,11},{10,... | collective-permute-start | bytes 30728 | tf_op jit(solution)/shard_map/ppermute | solution.py:36
  112.9 6.1 %collective-permute-start.49 = (bf16[8,2560]{1,0:T(8,128)(2,1)S(1)}, bf16[8,2560]{1,0:T(8,128)(2,1)S(1)}, u32[]{:S(2)}, u32[]{:S(2)}) collective-permute-start(bf16[8,2560]{1,0:T(8,128)(2,1)S(1)} %folded_sums.8.refs_0_), channel_id=1, source_target_pairs={{0,6},{1,7},{2,4},{3,5},{4,2},{5,3},{6,0},{7,1},{8,14},{9,15},{10,... | collective-permute-start | bytes 122888 | tf_op jit(solution)/shard_map/ppermute | solution.py:36
  114.6 6.0 %collective-permute-start.50 = (bf16[8,2560]{1,0:T(8,128)(2,1)S(1)}, bf16[8,2560]{1,0:T(8,128)(2,1)S(1)}, u32[]{:S(2)}, u32[]{:S(2)}) collective-permute-start(bf16[8,2560]{1,0:T(8,128)(2,1)S(1)} %folded_sums.8.refs_0_), channel_id=1, source_target_pairs={{0,4},{1,5},{2,6},{3,7},{4,0},{5,1},{6,2},{7,3},{8,12},{9,13},{10,... | collective-permute-start | bytes 122888 | tf_op jit(solution)/shard_map/ppermute | solution.py:36
  115.7 5.0 %collective-permute-start.51 = (bf16[8,2560]{1,0:T(8,128)(2,1)S(1)}, bf16[8,2560]{1,0:T(8,128)(2,1)S(1)}, u32[]{:S(2)}, u32[]{:S(2)}) collective-permute-start(bf16[8,2560]{1,0:T(8,128)(2,1)S(1)} %folded_sums.8.refs_0_), channel_id=1, source_target_pairs={{0,2},{1,3},{2,0},{3,1},{4,6},{5,7},{6,4},{7,5},{8,10},{9,11},{10,... | collective-permute-start | bytes 122888 | tf_op jit(solution)/shard_map/ppermute | solution.py:36
  122.0 5.5 %collective-permute-start.53 = (bf16[8,640]{1,0:T(8,128)(2,1)S(1)}, bf16[8,640]{1,0:T(8,128)(2,1)S(1)}, u32[]{:S(2)}, u32[]{:S(2)}) collective-permute-start(bf16[8,640]{1,0:T(8,128)(2,1)S(1)} %sep_rows.25), channel_id=1, source_target_pairs={{0,6},{1,7},{2,4},{3,5},{4,2},{5,3},{6,0},{7,1},{8,14},{9,15},{10,... | collective-permute-start | bytes 30728 | tf_op jit(solution)/shard_map/ppermute | solution.py:36
  124.0 4.6 %collective-permute-start.54 = (bf16[8,640]{1,0:T(8,128)(2,1)S(1)}, bf16[8,640]{1,0:T(8,128)(2,1)S(1)}, u32[]{:S(2)}, u32[]{:S(2)}) collective-permute-start(bf16[8,640]{1,0:T(8,128)(2,1)S(1)} %sep_rows.25), channel_id=1, source_target_pairs={{0,4},{1,5},{2,6},{3,7},{4,0},{5,1},{6,2},{7,3},{8,12},{9,13},{10,... | collective-permute-start | bytes 30728 | tf_op jit(solution)/shard_map/ppermute | solution.py:36
  124.1 4.5 %collective-permute-start.55 = (bf16[8,640]{1,0:T(8,128)(2,1)S(1)}, bf16[8,640]{1,0:T(8,128)(2,1)S(1)}, u32[]{:S(2)}, u32[]{:S(2)}) collective-permute-start(bf16[8,640]{1,0:T(8,128)(2,1)S(1)} %sep_rows.25), channel_id=1, source_target_pairs={{0,2},{1,3},{2,0},{3,1},{4,6},{5,7},{6,4},{7,5},{8,10},{9,11},{10,... | collective-permute-start | bytes 30728 | tf_op jit(solution)/shard_map/ppermute | solution.py:36
  128.7 5.0 %collective-permute-start.56 = (f32[8,256]{1,0:T(8,128)S(1)}, f32[8,256]{1,0:T(8,128)S(1)}, u32[]{:S(2)}, u32[]{:S(2)}) collective-permute-start(f32[8,256]{1,0:T(8,128)S(1)} %get-tuple-element.62), channel_id=1, source_target_pairs={{8,0},{9,1},{10,2},{11,3},{12,4},{13,5},{14,6},{15,7},{0,16},{1,17... | collective-permute-start | bytes 24584 | tf_op jit(solution)/shard_map/ppermute | solution.py:58
  134.1 6.3 %collective-permute-start.58 = (bf16[8,2560]{1,0:T(8,128)(2,1)S(1)}, bf16[8,2560]{1,0:T(8,128)(2,1)S(1)}, u32[]{:S(2)}, u32[]{:S(2)}) collective-permute-start(bf16[8,2560]{1,0:T(8,128)(2,1)S(1)} %folded_sums.9.refs_0_), channel_id=1, source_target_pairs={{0,6},{1,7},{2,4},{3,5},{4,2},{5,3},{6,0},{7,1},{8,14},{9,15},{10,... | collective-permute-start | bytes 122888 | tf_op jit(solution)/shard_map/ppermute | solution.py:36
  135.6 5.6 %collective-permute-start.59 = (bf16[8,2560]{1,0:T(8,128)(2,1)S(1)}, bf16[8,2560]{1,0:T(8,128)(2,1)S(1)}, u32[]{:S(2)}, u32[]{:S(2)}) collective-permute-start(bf16[8,2560]{1,0:T(8,128)(2,1)S(1)} %folded_sums.9.refs_0_), channel_id=1, source_target_pairs={{0,4},{1,5},{2,6},{3,7},{4,0},{5,1},{6,2},{7,3},{8,12},{9,13},{10,... | collective-permute-start | bytes 122888 | tf_op jit(solution)/shard_map/ppermute | solution.py:36
  136.6 4.6 %collective-permute-start.60 = (bf16[8,2560]{1,0:T(8,128)(2,1)S(1)}, bf16[8,2560]{1,0:T(8,128)(2,1)S(1)}, u32[]{:S(2)}, u32[]{:S(2)}) collective-permute-start(bf16[8,2560]{1,0:T(8,128)(2,1)S(1)} %folded_sums.9.refs_0_), channel_id=1, source_target_pairs={{0,2},{1,3},{2,0},{3,1},{4,6},{5,7},{6,4},{7,5},{8,10},{9,11},{10,... | collective-permute-start | bytes 122888 | tf_op jit(solution)/shard_map/ppermute | solution.py:36
  143.5 5.5 %collective-permute-start.62 = (bf16[8,640]{1,0:T(8,128)(2,1)S(1)}, bf16[8,640]{1,0:T(8,128)(2,1)S(1)}, u32[]{:S(2)}, u32[]{:S(2)}) collective-permute-start(bf16[8,640]{1,0:T(8,128)(2,1)S(1)} %sep_rows.27), channel_id=1, source_target_pairs={{0,6},{1,7},{2,4},{3,5},{4,2},{5,3},{6,0},{7,1},{8,14},{9,15},{10,... | collective-permute-start | bytes 30728 | tf_op jit(solution)/shard_map/ppermute | solution.py:36
  146.0 4.6 %collective-permute-start.63 = (bf16[8,640]{1,0:T(8,128)(2,1)S(1)}, bf16[8,640]{1,0:T(8,128)(2,1)S(1)}, u32[]{:S(2)}, u32[]{:S(2)}) collective-permute-start(bf16[8,640]{1,0:T(8,128)(2,1)S(1)} %sep_rows.27), channel_id=1, source_target_pairs={{0,4},{1,5},{2,6},{3,7},{4,0},{5,1},{6,2},{7,3},{8,12},{9,13},{10,... | collective-permute-start | bytes 30728 | tf_op jit(solution)/shard_map/ppermute | solution.py:36
  146.3 4.3 %collective-permute-start.64 = (bf16[8,640]{1,0:T(8,128)(2,1)S(1)}, bf16[8,640]{1,0:T(8,128)(2,1)S(1)}, u32[]{:S(2)}, u32[]{:S(2)}) collective-permute-start(bf16[8,640]{1,0:T(8,128)(2,1)S(1)} %sep_rows.27), channel_id=1, source_target_pairs={{0,2},{1,3},{2,0},{3,1},{4,6},{5,7},{6,4},{7,5},{8,10},{9,11},{10,... | collective-permute-start | bytes 30728 | tf_op jit(solution)/shard_map/ppermute | solution.py:36
  (19 other events, 47.1 us)
